TPU v7x, 32 devices: a whole 2x2x4 slice. The times are simulated.
32 devices in a mesh: group: 2 (over y), mrow: 4 (over z), mcol: 2 (over x), sub: 2 (over core).
Axes of the slice: x: 2, y: 2, z: 4, core: 2. Of those that a mesh axis runs over, the one named last changes fastest.
Arguments:
- tokens: bfloat16 [1024, 6144], P(('group', 'mrow'), ('mcol', 'sub')), parts along dimension 0, may hold values from -8 to 8
- ln_gain: float32 [6144], P(('mcol', 'sub')), may hold values from 0.1 to 1.9
- w_in: bfloat16 [6144, 24576], P(('mcol', 'sub'), 'mrow'), may hold values from -0.078125 to 0.078125
- b_in: float32 [24576], P('mrow'), may hold values from -3 to 3
- w_out: bfloat16 [24576, 6144], P('mrow', ('mcol', 'sub')), may hold values from -0.0390625 to 0.0390625
- b_out: float32 [6144], replicated, may hold values from -0.6 to 0.6
- captions: bfloat16 [2048, 6144], P(('group', 'mrow', 'mcol', 'sub')), parts along dimension 0, may hold values from -6 to 6
- pairs: int32 [2048], P(('group', 'mrow', 'mcol', 'sub')), parts along dimension 0, may hold values from 0 to 1
Outputs:
- scores: float32 [2048], P(('group', 'mrow', 'mcol', 'sub')), parts along dimension 0
There are 2 independent parts, one for each index of `group`. A program takes and returns all parts, laid end to end along the dimension named above; an argument that names none is the same for every part. Nothing has to cross between parts.
All inputs are finite; a program needn't handle non-finite values.
Results may differ from a plain program's by a relative error of at most 0.0065.
Values may be sent and summed in bfloat16 or wider, within the bound.
No kernel may reach another device: no remote copies, remote signals or barrier semaphores. Data moves between devices by JAX's collectives and lax.ppermute only.
A program may use at most 128 MiB of HBM per device.

v0:
```python
import jax
import jax.numpy as jnp
from jax import lax
from jax.sharding import PartitionSpec as P

D = 6144
PATCHES = 256
IMAGES = 2


def image_table(first_row, count):
    positions = first_row + jnp.arange(count, dtype=jnp.int32)
    return (positions[None, :] // PATCHES == jnp.arange(IMAGES, dtype=jnp.int32)[:, None]).astype(
        jnp.bfloat16
    )


def shards(tokens, ln_gain, w_in, b_in, w_out, b_out, captions, pairs):
    values = tokens.astype(jnp.float32)
    totals, squares = lax.psum(
        (jnp.sum(values, axis=1), jnp.sum(values * values, axis=1)), ("mcol", "sub")
    )
    average = totals / D
    variance = squares / D - average * average
    normed = (
        (values - average[:, None]) * lax.rsqrt(variance + 1e-06)[:, None] * ln_gain[None, :]
    ).astype(jnp.bfloat16)
    gathered = lax.all_gather(normed, "mrow", axis=0, tiled=True)
    rows_local = tokens.shape[0]
    columns = tokens.shape[1]
    col_index = lax.axis_index(("mcol", "sub"))
    row_index = lax.axis_index("mrow")
    resid_pool = jnp.dot(
        image_table(row_index * rows_local, rows_local), tokens, preferred_element_type=jnp.float32
    )
    empty = jnp.zeros((IMAGES, D), jnp.float32)
    offset = col_index * columns
    out_weights = w_out.astype(jnp.float32)
    full_preact = jnp.dot(gathered, w_in, preferred_element_type=jnp.float32)
    preact = lax.psum_scatter(
        full_preact.astype(jnp.bfloat16), ("mcol", "sub"), scatter_dimension=1, tiled=True
    ).astype(jnp.float32)
    units = preact.shape[1]
    unit_bias = lax.dynamic_slice_in_dim(b_in, col_index * units, units, 0)
    hidden = jax.nn.gelu(preact + unit_bias[None, :], approximate=True).astype(jnp.bfloat16)
    local_pool = jnp.dot(
        image_table(0, hidden.shape[0]), hidden, preferred_element_type=jnp.float32
    )
    pooled_hidden = lax.all_gather(local_pool, ("mcol", "sub"), axis=1, tiled=True) / PATCHES
    mixed = jnp.dot(pooled_hidden, out_weights, precision=lax.Precision.HIGHEST)
    placed = lax.dynamic_update_slice(empty, resid_pool / PATCHES + mixed, (0, offset))
    pooled = lax.psum(placed, ("mrow", "mcol", "sub")) + b_out[None, :]
    embedding = (
        pooled * lax.rsqrt(jnp.mean(pooled * pooled, axis=1, keepdims=True) + 1e-06)
    ).astype(jnp.bfloat16)
    similar = jnp.dot(captions, embedding.T, preferred_element_type=jnp.float32)
    chosen = pairs[:, None] == jnp.arange(IMAGES, dtype=jnp.int32)[None, :]
    picked = jnp.sum(jnp.where(chosen, similar, 0.0), axis=1)
    text_vals = captions.astype(jnp.float32)
    text_scale = lax.rsqrt(jnp.mean(text_vals * text_vals, axis=1) + 1e-06)
    return 100.0 * picked * text_scale / D


def solution(mesh):
    placed = (
        P(("group", "mrow"), ("mcol", "sub")),
        P(("mcol", "sub")),
        P(("mcol", "sub"), "mrow"),
        P("mrow"),
        P("mrow", ("mcol", "sub")),
        P(),
        P(("group", "mrow", "mcol", "sub"), None),
        P(("group", "mrow", "mcol", "sub")),
    )
    return jax.shard_map(
        shards,
        mesh=mesh,
        in_specs=placed,
        out_specs=P(("group", "mrow", "mcol", "sub")),
        check_vma=False,
    )
```

profile of v0, /device:TPU:0, one launch (start us, length us, event | category | flops | bytes accessed | tf_op | source)
XLA Modules:
  0.0 216.4 jit_solution(13078012652072766389)
XLA Ops:
  6.5 0.0 all-gather.2.cloned.1.call-start
  6.5 1.2 convert_reduce_fusion
  7.7 8.3 %all-reduce = (f32[128]{0:T(128)S(1)}, f32[128]{0:T(128)S(1)}) all-reduce(f32[128]{0:T(128)S(1)} %get-tuple-element.6, f32[128]{0:T(128)S(1)} %get-tuple-element.5), channel_id=1, replica_groups=mesh['group'=2,'mrow'=4,'mcol'=2,'sub'=2] {'mcol','sub'}, use_global_device_ids=true, to_apply=%region_3.0 | all-reduce | flops 256 | bytes 2048 | tf_op jit(solution)/shard_map/psum | solution.py:20
  16.1 2.0 fusion.15
  18.1 0.0 all-gather.2.cloned.1.call-update
  18.1 0.0 reduce-scatter.2.cloned.1.call-start
  18.2 37.5 %all-gather.2.cloned.1.call-done = bf16[512,1536]{1,0:T(8,128)(2,1)} async-done(((bf16[128,1536]{1,0:T(8,128)(2,1)}), bf16[512,1536]{1,0:T(8,128)(2,1)}) %all-gather.2.cloned.1.call-update) | async-done | bytes 1572880 | tf_op jit(solution)/shard_map/all_gather | solution.py:28
  55.7 15.9 %convolution_convert_fusion = bf16[512,6144]{1,0:T(8,128)(2,1)} fusion(bf16[512,1536]{1,0:T(8,128)(2,1)} %all-gather.2.cloned.1.call-done, bf16[1536,6144]{1,0:T(8,128)(2,1)} %param.10), kind=kOutput, calls=%fused_computation | convolution fusion | flops 9666822144 | bytes 26738688 | tf_op jit(solution)/shard_map/dot_general | solution.py:39
  71.6 0.0 copy-start.1
  71.6 0.0 copy-start
  71.6 0.0 reduce-scatter.2.cloned.1.call-update
  71.6 0.9 dynamic_slice.3
  72.5 0.2 copy-done.1
  72.7 0.3 multiply_reduce_fusion
  73.0 0.0 copy-done
  73.0 0.2 convolution_multiply_fusion
  73.1 55.9 %reduce-scatter.2.cloned.1.call-done = bf16[512,1536]{1,0:T(8,128)(2,1)} async-done(((bf16[512,6144]{1,0:T(8,128)(2,1)}), bf16[512,1536]{1,0:T(8,128)(2,1)}) %reduce-scatter.2.cloned.1.call-update) | async-done | bytes 1572880 | tf_op jit(solution)/shard_map/reduce_scatter | solution.py:40
  129.0 2.7 %fusion.9 = f32[2,1536]{1,0:T(2,128)S(1)} fusion(bf16[512,1536]{1,0:T(8,128)(2,1)} %reduce-scatter.2.cloned.1.call-done, f32[1536]{0:T(1024)S(1)} %dynamic_slice.3, s32[512]{0:T(512)S(1)} %add_select_fusion), kind=kOutput, calls=%fused_computation.14 | convolution fusion | flops 11797504 | bytes 1593344 | tf_op jit(solution)/shard_map/dot_general | solution.py:46
  131.7 5.2 %all_gather.7 = f32[2,6144]{1,0:T(2,128)S(1)} all-gather(f32[2,1536]{1,0:T(2,128)S(1)} %fusion.9), channel_id=1, replica_groups=mesh['group'=2,'mrow'=4,'mcol'=2,'sub'=2] {'mcol','sub'}, dimensions={1}, use_global_device_ids=true | all-gather | bytes 61440 | tf_op jit(solution)/shard_map/all_gather | solution.py:49
  136.9 0.0 copy-start.2
  136.9 0.0 copy-start.3
  137.0 10.7 %fusion.8 = f32[2,6144]{1,0:T(2,128)S(1)} fusion(f32[2,6144]{1,0:T(2,128)S(1)} %broadcast_in_dim.5, s32[]{:T(128)S(6)} %select_n.30, f32[2,1536]{1,0:T(2,128)S(1)} %convolution_multiply_fusion, bf16[6144,1536]{1,0:T(8,128)(2,1)} %param.12, f32[2,6144]{1,0:T(2,128)S(1)} %all_gather.7), kind=kOutput, calls=%fused_computation.11 | convolution fusion | flops 226507776 | bytes 18948100 | tf_op jit(solution)/shard_map/dot_general | solution.py:50
  147.6 60.9 %psum.23 = f32[2,6144]{1,0:T(2,128)S(1)} all-reduce(f32[2,6144]{1,0:T(2,128)S(1)} %fusion.8), channel_id=1, replica_groups=mesh['group'=2,'mrow'=4,'mcol'=2,'sub'=2] {'mrow','mcol','sub'}, use_global_device_ids=true, to_apply=%region_5.6 | all-reduce | flops 12288 | bytes 98304 | tf_op jit(solution)/shard_map/psum | solution.py:52
  208.5 0.0 copy-done.2
  208.5 0.2 multiply_reduce_fusion.1
  208.7 0.0 copy-done.3
  208.7 0.4 fusion.12
  209.0 0.5 multiply_multiply_fusion.1
  (5 shorter events, 0.0 us)
Async XLA Ops:
  6.5 49.2 %all-gather.2.cloned.1.call-start = ((), (), s32[]{:S(2)}) async-start(), calls=%async_computation.1 | async-start | bytes 1966080 | tf_op jit(solution)/shard_map/all_gather | solution.py:28
  18.1 110.9 %reduce-scatter.2.cloned.1.call-start = ((), (), s32[]{:S(2)}) async-start(), calls=%async_computation.2 | async-start | bytes 7864320 | tf_op jit(solution)/shard_map/reduce_scatter | solution.py:40
  71.6 1.1 copy-start.1
  71.6 1.4 copy-start
  136.9 71.5 %copy-start.2 = (f32[6144]{0:T(1024)S(1)}, f32[6144]{0:T(1024)}, u32[]{:S(2)}) copy-start(f32[6144]{0:T(1024)} %param.13) | copy-start | bytes 73732
  136.9 71.7 %copy-start.3 = (s32[64]{0:T(128)S(1)}, s32[64]{0:T(128)}, u32[]{:S(2)}) copy-start(s32[64]{0:T(128)} %param.15) | copy-start | bytes 772
Sparse Core Ops, SparseCore 0:
  18.2 37.4 all-gather.1
  71.7 57.2 reduce-scatter.1
where the time goes:
time: 217 us; the launch traced here: 216 us
  waiting for transfers between devices  93.4 us (43%)
  blocking collectives  74.4 us (34%)
  matrix products  29.8 us (14%)
  between operations  13.5 us (6%)
  other arithmetic  4.19 us (2%)
    psum x1, blocking collectives, shards(): pooled = lax.psum(placed, ('mrow', 'mcol', 'sub')) + b_out[None, :]  60.9 us
    reduce_scatter x1, waiting for transfers between devices, shards(): lax.psum_scatter(full_preact.astype(jnp.bfloat16), ('mcol', 'sub'), scatt...  55.9 us
    all_gather x1, waiting for transfers between devices, shards(): gathered = lax.all_gather(normed, 'mrow', axis=0, tiled=True)  37.5 us
    dot_general x1, matrix products, shards(): full_preact = jnp.dot(gathered, w_in, preferred_element_type=jnp.float32)  15.9 us
    dot_general x1, matrix products, shards(): mixed = jnp.dot(pooled_hidden, out_weights, precision=lax.Precision.HIGHEST)  10.7 us
    psum x1, blocking collectives, shards(): lax.psum((jnp.sum(values, axis=1), jnp.sum(values * values, axis=1)), ('m...  8.34 us
    all_gather x1, blocking collectives, shards(): lax.all_gather(local_pool, ('mcol', 'sub'), axis=1, tiled=True) / PATCHES  5.21 us
  transfers between devices with their start and end apart: 2, of which 2 were waited for; matrix products, arithmetic and copies ran while one was open for 1% of the time, Pallas kernels for 0%

commit v1 on v0

v1 whole, which is shorter than its diff:
```python
import jax
import jax.numpy as jnp
from jax import lax
from jax.experimental import pallas as pl
from jax.experimental.pallas import tpu as pltpu
from jax.sharding import PartitionSpec as P

PATCHES = 256
IMAGES = 2
F32 = jnp.float32
BF16 = jnp.bfloat16
VMEM = pltpu.VMEM
WHOLE = pl.BlockSpec(memory_space=VMEM)
IN_HBM = pl.BlockSpec(memory_space=pltpu.HBM)
MIB = 1 << 20


def params(mib):
    return pltpu.CompilerParams(vmem_limit_bytes=mib * MIB)


def cost(flops, moved):
    return pl.CostEstimate(flops=int(flops), bytes_accessed=int(moved), transcendentals=0)


def struct(shape, dtype=F32):
    return jax.ShapeDtypeStruct(shape, dtype)


def image_table(first_row, count):
    positions = first_row + jnp.arange(count, dtype=jnp.int32)
    return (positions[None, :] // PATCHES == jnp.arange(IMAGES, dtype=jnp.int32)[:, None]).astype(BF16)


def plain(tokens, ln_gain, w_in, b_in, w_out, b_out, captions, pairs):
    width = b_out.shape[0]
    values = tokens.astype(F32)
    totals, squares = lax.psum((jnp.sum(values, axis=1), jnp.sum(values * values, axis=1)), ("mcol", "sub"))
    average = totals / width
    variance = squares / width - average * average
    normed = ((values - average[:, None]) * lax.rsqrt(variance + 1e-06)[:, None] * ln_gain[None, :]).astype(BF16)
    gathered = lax.all_gather(normed, "mrow", axis=0, tiled=True)
    rows = tokens.shape[0]
    col_index = lax.axis_index(("mcol", "sub"))
    resid = jnp.dot(image_table(lax.axis_index("mrow") * rows, rows), tokens, preferred_element_type=F32)
    partial = jnp.dot(gathered, w_in, preferred_element_type=F32).astype(BF16)
    preact = lax.psum_scatter(partial, ("mcol", "sub"), scatter_dimension=1, tiled=True).astype(F32)
    units = preact.shape[1]
    bias = lax.dynamic_slice_in_dim(b_in, col_index * units, units, 0)
    hidden = jax.nn.gelu(preact + bias[None, :], approximate=True).astype(BF16)
    local_pool = jnp.dot(image_table(0, hidden.shape[0]), hidden, preferred_element_type=F32)
    pooled_hidden = lax.all_gather(local_pool, ("mcol", "sub"), axis=1, tiled=True) / PATCHES
    mixed = jnp.dot(pooled_hidden, w_out.astype(F32), precision=lax.Precision.HIGHEST)
    own = lax.psum(resid / PATCHES + mixed, "mrow")
    pooled = lax.all_gather(own, ("mcol", "sub"), axis=1, tiled=True) + b_out[None, :]
    embedding = (pooled * lax.rsqrt(jnp.mean(pooled * pooled, axis=1, keepdims=True) + 1e-06)).astype(BF16)
    similar = jnp.dot(captions, embedding.T, preferred_element_type=F32)
    chosen = pairs[:, None] == jnp.arange(IMAGES, dtype=jnp.int32)[None, :]
    picked = jnp.sum(jnp.where(chosen, similar, 0.0), axis=1)
    text_vals = captions.astype(F32)
    text_scale = lax.rsqrt(jnp.mean(text_vals * text_vals, axis=1) + 1e-06)
    return 100.0 * picked * text_scale / width


def sums_kernel(tokens, stats, resid):
    values = tokens[...].astype(F32)
    rows = values.shape[0]
    totals = jnp.sum(values, axis=1, keepdims=True)
    squares = jnp.sum(values * values, axis=1, keepdims=True)
    lane = lax.broadcasted_iota(jnp.int32, (rows, 128), 1)
    both = jnp.where(lane == 0, totals, jnp.where(lane == 1, squares, 0.0))
    stats[...] = both.T[:8]
    resid[...] = jnp.sum(values, axis=0, keepdims=True) / PATCHES


def normalize(values, stats, gain, width):
    rows = values.shape[0]
    padded = jnp.concatenate([stats, jnp.zeros((120, rows), F32)], axis=0).T
    average = padded[:, 0:1] / width
    variance = padded[:, 1:2] / width - average * average
    return ((values - average) * lax.rsqrt(variance + 1e-06) * gain).astype(BF16)


def quarters():
    across, core = lax.axis_index("mcol"), lax.axis_index("sub")
    return (
        (1 - core) * 2 + (1 - across),
        core * 2 + (1 - across),
        (1 - core) * 2 + across,
        core * 2 + across,
    )


def first_kernel(width, which, pieces, tokens, stats, gain, w, give, keep, held, sems):
    share = keep.shape[1]
    step = share // pieces
    copies = []
    for part in range(2):
        start = quarters()[which * 2 + part] * share
        for piece in range(pieces):
            copies.append(
                pltpu.make_async_copy(
                    w.at[:, pl.ds(pl.multiple_of(start + piece * step, 128), step)],
                    held.at[part, :, pl.ds(piece * step, step)],
                    sems.at[part * pieces + piece],
                )
            )
    for copy in copies:
        copy.start()
    normed = normalize(tokens[...].astype(F32), stats[...], gain[...], width)
    for part in range(2):
        for piece in range(pieces):
            copies[part * pieces + piece].wait()
            cols = pl.ds(piece * step, step)
            out = jnp.dot(normed, held[part, :, cols], preferred_element_type=F32)
            if part == 0:
                give[:, cols] = out.astype(BF16)
            else:
                keep[:, cols] = out


def first_block(width, which, tokens, stats, gain, w):
    rows, depth = tokens.shape
    share = w.shape[1] // 4
    pieces = 2
    return pl.pallas_call(
        lambda *refs: first_kernel(width, which, pieces, *refs),
        name="first_block",
        out_shape=(struct((rows, share), BF16), struct((rows, share)), pltpu.VMEM((2, depth, share), BF16)),
        in_specs=[WHOLE, WHOLE, WHOLE, IN_HBM],
        out_specs=(WHOLE, WHOLE, WHOLE),
        scratch_shapes=[pltpu.SemaphoreType.DMA((2 * pieces,))],
        compiler_params=params(8),
        cost_estimate=cost(4 * rows * depth * share, 4 * depth * share),
    )(tokens, stats, gain, w)


def later_kernel(width, count, *refs):
    blocks, (stats, gain, held, give, keep) = refs[:count], refs[count:]
    values = blocks[0][...].astype(F32)
    for other in blocks[1:]:
        values = values + other[...].astype(F32)
    normed = normalize(values, stats[...], gain[...], width)
    share = keep.shape[1]
    step = share // 2
    for piece in range(2):
        cols = pl.ds(piece * step, step)
        give[:, cols] = jnp.dot(normed, held[0, :, cols], preferred_element_type=F32).astype(BF16)
    for piece in range(2):
        cols = pl.ds(piece * step, step)
        keep[:, cols] = jnp.dot(normed, held[1, :, cols], preferred_element_type=F32)


def later_block(width, blocks, stats, gain, held):
    rows = blocks[0].shape[0]
    depth, share = held.shape[1:]
    return pl.pallas_call(
        lambda *refs: later_kernel(width, len(blocks), *refs),
        name="later_block",
        out_shape=(struct((rows, share), BF16), struct((rows, share))),
        in_specs=[WHOLE] * (len(blocks) + 3),
        out_specs=(WHOLE, WHOLE),
        compiler_params=params(8),
        cost_estimate=cost(4 * rows * depth * share, 4 * rows * depth),
    )(*blocks, stats, gain, held)


def chip_sum_kernel(kept, got, out):
    out[...] = (kept[...] + got[...].astype(F32)).astype(BF16)


def chip_sum(kept, got):
    return pl.pallas_call(
        chip_sum_kernel,
        name="chip_sum",
        out_shape=struct(kept.shape, BF16),
        in_specs=[WHOLE, WHOLE],
        out_specs=WHOLE,
        compiler_params=params(4),
        cost_estimate=cost(kept.size, 8 * kept.size),
    )(kept, got)


def pool_kernel(kept, near, far, bias, out):
    share = kept.shape[1]
    start = pl.multiple_of(quarters()[3] * share, 128)
    step = 256 if share % 256 == 0 else 128
    for piece in range(share // step):
        cols = pl.ds(piece * step, step)
        v = kept[:, cols] + near[:, cols].astype(F32) + far[:, cols].astype(F32)
        v = v + bias[:, pl.ds(pl.multiple_of(start + piece * step, 128), step)]
        inner = 0.7978845608028654 * (v + 0.044715 * (v * v * v))
        hidden = (0.5 * v * (1.0 + jnp.tanh(inner))).astype(BF16).astype(F32)
        out[:, cols] = jnp.sum(hidden, axis=0, keepdims=True)


def pool(kept, near, far, bias):
    share = kept.shape[1]
    return pl.pallas_call(
        pool_kernel,
        name="pool",
        out_shape=struct((1, share)),
        in_specs=[WHOLE] * 4,
        out_specs=WHOLE,
        compiler_params=params(4),
        cost_estimate=cost(20 * kept.size, 8 * kept.size),
    )(kept, near, far, bias)


def mix_kernel(rows, own, core, across, both, resid, w, out):
    share = own.shape[1]
    mine_x, mine_c = lax.axis_index("mcol"), lax.axis_index("sub")
    total = jnp.zeros((16, w.shape[1]), F32)
    order = ((own, 0, 0), (core, 0, 1), (across, 1, 0), (both, 1, 1))
    for ref, dx, dc in order:
        x, c = (1 - mine_x if dx else mine_x), (1 - mine_c if dc else mine_c)
        start = pl.multiple_of((c * 2 + x) * share, 128)
        value = ref[...] / PATCHES
        high = value.astype(BF16)
        rest = value - high.astype(F32)
        middle = rest.astype(BF16)
        low = (rest - middle.astype(F32)).astype(BF16)
        terms = jnp.concatenate([high, middle, low, jnp.zeros((10, share), BF16)], axis=0)
        total = total + jnp.dot(terms, w[pl.ds(start, share), :], preferred_element_type=F32)
    mixed = total[0:2] + (total[2:4] + total[4:6])
    image = lax.axis_index("mrow") * rows // PATCHES
    row = lax.broadcasted_iota(jnp.int32, mixed.shape, 0)
    out[...] = mixed + jnp.where(row == image, resid[...], 0.0)


def mix(rows, own, core, across, both, resid, w):
    return pl.pallas_call(
        lambda *refs: mix_kernel(rows, *refs),
        name="mix",
        out_shape=struct((IMAGES, w.shape[1])),
        in_specs=[WHOLE] * 6,
        out_specs=WHOLE,
        compiler_params=params(8),
        cost_estimate=cost(32 * w.size, 16 * w.shape[0]),
    )(own, core, across, both, resid, w)


def score_kernel(own, core, across, both, bias, captions, text_scale, pairs, out):
    depth = own.shape[1]
    width = captions.shape[1]
    mine_x, mine_c = lax.axis_index("mcol"), lax.axis_index("sub")
    pieces = []
    total = jnp.zeros((IMAGES, 1), F32)
    for ref, dx, dc in ((own, 0, 0), (core, 0, 1), (across, 1, 0), (both, 1, 1)):
        x, c = (1 - mine_x if dx else mine_x), (1 - mine_c if dc else mine_c)
        start = pl.multiple_of((x * 2 + c) * depth, 128)
        pooled = ref[...] + bias[:, pl.ds(start, depth)]
        total = total + jnp.sum(pooled * pooled, axis=1, keepdims=True)
        pieces.append((start, pooled))
    scale = lax.rsqrt(total / width + 1e-06)
    similar = jnp.zeros((IMAGES, captions.shape[0]), F32)
    for start, pooled in pieces:
        embedding = (pooled * scale).astype(BF16)
        similar = similar + lax.dot_general(
            embedding, captions[:, pl.ds(start, depth)], (((1,), (1,)), ((), ())), preferred_element_type=F32
        )
    chosen = lax.broadcasted_iota(jnp.int32, similar.shape, 0) == pairs[...]
    picked = jnp.sum(jnp.where(chosen, similar, 0.0), axis=0, keepdims=True)
    out[...] = 100.0 * picked * text_scale[...] / width


def score(own, core, across, both, bias, captions, text_scale, pairs):
    count = captions.shape[0]
    return pl.pallas_call(
        score_kernel,
        name="score",
        out_shape=struct((1, count)),
        in_specs=[WHOLE] * 8,
        out_specs=WHOLE,
        compiler_params=params(8),
        cost_estimate=cost(4 * captions.size, 2 * captions.size),
    )(own, core, across, both, bias, captions, text_scale, pairs)


def other_core(value):
    return lax.ppermute(value, "sub", [(0, 1), (1, 0)])


def other_chip(value):
    return lax.ppermute(value, "mcol", [(0, 1), (1, 0)])


def other_both(value):
    return lax.ppermute(value, ("mcol", "sub"), [(0, 3), (1, 2), (2, 1), (3, 0)])


def along(value, *pairs):
    return lax.ppermute(value, "mrow", list(pairs))


SWAP = ((0, 1), (1, 0), (2, 3), (3, 2))
MIDDLE = ((1, 2), (2, 1))
OUTWARD = ((1, 0), (2, 3))
SKIP = ((0, 2), (2, 0), (1, 3), (3, 1))
ENDS = ((0, 3), (3, 0), (1, 2), (2, 1))


def staged(tokens, ln_gain, w_in, b_in, w_out, b_out, captions, pairs):
    width = b_out.shape[0]
    rows, depth = tokens.shape
    gain = ln_gain.reshape(1, depth)
    bias = b_in.reshape(1, -1)
    near = along(tokens, *SWAP)
    middle = along(tokens, *MIDDLE)
    passed = along(middle, *OUTWARD)
    crossed = along(near, *MIDDLE)
    last = along(crossed, *OUTWARD)

    stats, resid = pl.pallas_call(
        sums_kernel,
        name="sums",
        out_shape=(struct((8, rows)), struct((1, depth))),
        in_specs=[WHOLE],
        out_specs=(WHOLE, WHOLE),
        compiler_params=params(4),
        cost_estimate=cost(4 * tokens.size, 2 * tokens.size),
    )(tokens)
    stats = stats + other_core(stats)
    stats = stats + other_chip(stats)
    near_stats = along(stats, *SWAP)
    pair = jnp.stack([stats, near_stats])
    far_pair = along(pair, *SKIP)
    row = lax.axis_index("mrow")
    at_end = (row == 0) | (row == 3)
    second_stats = jnp.where(at_end, far_pair[0], far_pair[1])
    third_stats = jnp.where(at_end, far_pair[1], far_pair[0])

    give_a, keep_a, held_a = first_block(width, 0, tokens, stats, gain, w_in)
    got_a = other_core(give_a)
    sums = [chip_sum(keep_a, got_a)]
    give_b, keep_b, held_b = first_block(width, 1, tokens, stats, gain, w_in)
    kept = [(keep_b, other_core(give_b))]
    for blocks, block_stats in (
        ((near,), near_stats),
        ((middle, passed), second_stats),
        ((crossed, last), third_stats),
    ):
        give_a, keep_a = later_block(width, blocks, block_stats, gain, held_a)
        got_a = other_core(give_a)
        give_b, keep_b = later_block(width, blocks, block_stats, gain, held_b)
        sums.append(chip_sum(keep_a, got_a))
        kept.append((keep_b, other_core(give_b)))
    parts = [pool(mine, core, other_chip(sent), bias) for (mine, core), sent in zip(kept, sums)]
    sources = (row, row ^ 1, jnp.where(row < 2, 2, 1), jnp.where(row < 2, 3, 0))
    ids = jnp.arange(IMAGES, dtype=jnp.int32)[:, None]
    pooled = sum(jnp.where(ids == source * rows // PATCHES, part, 0.0) for part, source in zip(parts, sources))

    mixed = mix(rows, pooled, other_core(pooled), other_chip(pooled), other_both(pooled), resid, w_out)
    own = mixed + along(mixed, *SWAP) + along(mixed, *SKIP) + along(mixed, *ENDS)
    text_vals = captions.astype(F32)
    text_scale = lax.rsqrt(jnp.mean(text_vals * text_vals, axis=1) + 1e-06)
    scores = score(
        own,
        other_core(own),
        other_chip(own),
        other_both(own),
        b_out.reshape(1, -1),
        captions,
        text_scale.reshape(1, -1),
        pairs.reshape(1, -1),
    )
    return scores.reshape(-1)


def solution(mesh):
    sizes = dict(mesh.shape)

    def shards(tokens, ln_gain, w_in, *rest):
        rows, depth = tokens.shape
        fits = (
            (sizes["mrow"], sizes["mcol"], sizes["sub"]) == (4, 2, 2)
            and rows == 128
            and PATCHES % rows == 0
            and depth % 256 == 0
            and w_in.shape[1] % 1024 == 0
        )
        return (staged if fits else plain)(tokens, ln_gain, w_in, *rest)

    placed = (
        P(("group", "mrow"), ("mcol", "sub")),
        P(("mcol", "sub")),
        P(("mcol", "sub"), "mrow"),
        P("mrow"),
        P("mrow", ("mcol", "sub")),
        P(),
        P(("group", "mrow", "mcol", "sub"), None),
        P(("group", "mrow", "mcol", "sub")),
    )
    return jax.shard_map(
        shards,
        mesh=mesh,
        in_specs=placed,
        out_specs=P(("group", "mrow", "mcol", "sub")),
        check_vma=False,
    )
```

time: 217 us -> 129 us (0.59)
  blocking collectives: 74.4 us -> 0 us
  waiting for transfers between devices: 93.4 us -> 43.1 us
  starting transfers between devices: 0.04 us -> 30.8 us
  Pallas kernels: 0 us -> 30.7 us
  matrix products: 29.8 us -> 0 us
  local copies, waits for them, and re-layouts: 1.12 us -> 21.4 us
  between operations: 13.5 us -> 0.32 us
    psum x2 -> x0, blocking collectives: 69.2 us -> none  [the longest x1 60.9 us: shards(): pooled = lax.psum(placed, ('mrow', 'mcol', 'sub')) + b_out[None, :]]
    reduce_scatter x1 -> x0, waiting for transfers between devices: 55.9 us -> none  [shards(): lax.psum_scatter(full_preact.astype(jnp.bfloat16), ('mcol', 'sub'), scatt...]
    ppermute x0 -> x30, waiting for transfers between devices: none -> 43.1 us  [the longest x10 22.7 us: along(): return lax.ppermute(value, 'mrow', list(pairs))]
    all_gather x1 -> x0, waiting for transfers between devices: 37.5 us -> none  [shards(): gathered = lax.all_gather(normed, 'mrow', axis=0, tiled=True)]
    ppermute x0 -> x30, starting transfers between devices: none -> 30.8 us  [the longest x10 18.7 us: along(): return lax.ppermute(value, 'mrow', list(pairs))]
    pallas_call x0 -> x19, Pallas kernels: none -> 30.7 us  [the longest x6 11.4 us: later_block(): pl.pallas_call(lambda *refs: later_kernel(width, len(blocks), *refs), nam...]
    dot_general x5 -> x0, matrix products: 29.8 us -> none  [the longest x1 15.9 us: shards(): full_preact = jnp.dot(gathered, w_in, preferred_element_type=jnp.float32)]
    unnamed x8 -> x30, local copies, waits for them, and re-layouts: 0.23 us -> 20.7 us
  transfers between devices with their start and end apart: 2 -> 30, of which waited for: 2 -> 16; matrix products, arithmetic and copies ran while one was open for 1% -> 2% of each run, Pallas kernels for 0% -> 20%
where the time goes in v1:
time: 129 us
  waiting for transfers between devices  43.1 us (33%)
  starting transfers between devices  30.8 us (24%)
  Pallas kernels  30.7 us (24%)
  local copies, waits for them, and re-layouts  21.4 us (17%)
  other arithmetic  2.32 us (2%)
    ppermute x10, waiting for transfers between devices, along(): return lax.ppermute(value, 'mrow', list(pairs))  22.7 us
    unnamed x30, local copies, waits for them, and re-layouts  20.7 us
    ppermute x10, starting transfers between devices, along(): return lax.ppermute(value, 'mrow', list(pairs))  18.7 us
    ppermute x7, waiting for transfers between devices, other_chip(): return lax.ppermute(value, 'mcol', [(0, 1), (1, 0)])  16.6 us
    pallas_call x6, Pallas kernels, later_block(): pl.pallas_call(lambda *refs: later_kernel(width, len(blocks), *refs), nam...  11.4 us
    ppermute x7, starting transfers between devices, other_chip(): return lax.ppermute(value, 'mcol', [(0, 1), (1, 0)])  9.47 us
    pallas_call x2, Pallas kernels, first_block(): pl.pallas_call(lambda *refs: first_kernel(width, which, pieces, *refs), n...  8.34 us
    pallas_call x4, Pallas kernels, pool(): pl.pallas_call(pool_kernel, name='pool', out_shape=struct((1, share)), in...  5.33 us
  transfers between devices with their start and end apart: 30, of which 16 were waited for; matrix products, arithmetic and copies ran while one was open for 2% of the time, Pallas kernels for 20%

profile of v1, /device:TPU:0, one launch (start us, length us, event | category | flops | bytes accessed | tf_op | source)
XLA Modules:
  0.0 128.7 jit_solution(7966133930520667545)
XLA Ops:
  0.0 3.0 %collective-permute-start.5 = (bf16[128,1536]{1,0:T(8,128)(2,1)}, bf16[128,1536]{1,0:T(8,128)(2,1)S(1)}, u32[]{:S(2)}, u32[]{:S(2)}) collective-permute-start(bf16[128,1536]{1,0:T(8,128)(2,1)} %refs_0_.3), channel_id=1, source_target_pairs={{0,4},{4,0},{8,12},{12,8},{1,5},{5,1},{9,13},{13,9},{2,6},{6,2},{1... | collective-permute-start | bytes 1179656 | tf_op jit(solution)/shard_map/ppermute | solution.py:293
  3.0 0.7 collective-permute-start.10
  3.7 8.6 %collective-permute-done.5.refs_0_ = bf16[128,1536]{1,0:T(8,128)(2,1)S(1)} collective-permute-done((bf16[128,1536]{1,0:T(8,128)(2,1)}, bf16[128,1536]{1,0:T(8,128)(2,1)S(1)}, u32[]{:S(2)}, u32[]{:S(2)}) %collective-permute-start.5) | collective-permute-done | bytes 393248 | tf_op jit(solution)/shard_map/ppermute | solution.py:293
  12.3 0.7 collective-permute-start.16
  13.0 1.0 copy-done.2
  14.3 1.2 collective-permute-done
  15.5 1.7 %collective-permute-start.1 = (f32[8,128]{1,0:T(8,128)S(1)}, f32[8,128]{1,0:T(8,128)S(1)}, u32[]{:S(2)}, u32[]{:S(2)}) collective-permute-start(f32[8,128]{1,0:T(8,128)S(1)} %add.42), channel_id=1, source_target_pairs={{0,2},{2,0},{1,3},{3,1},{4,6},{6,4},{5,7},{7,5},{8,10},{10,8},{9,1... | collective-permute-start | bytes 12296 | tf_op jit(solution)/shard_map/ppermute | solution.py:285
  17.1 0.7 reshape.58.refs_2_.refs_3_
  17.8 1.2 collective-permute-done.1
  19.1 4.5 %collective-permute-start.6 = (f32[8,128]{1,0:T(8,128)S(1)}, f32[8,128]{1,0:T(8,128)S(1)}, u32[]{:S(2)}, u32[]{:S(2)}) collective-permute-start(f32[8,128]{1,0:T(8,128)S(1)} %add.43.refs_1_), channel_id=1, source_target_pairs={{0,4},{4,0},{8,12},{12,8},{1,5},{5,1},{9,13},{13,9},{2,6},{6,2},{1... | collective-permute-start | bytes 12296 | tf_op jit(solution)/shard_map/ppermute | solution.py:293
  23.6 6.4 %copy-done = bf16[1536,6144]{1,0:T(8,128)(2,1)S(1)} copy-done((bf16[1536,6144]{1,0:T(8,128)(2,1)S(1)}, bf16[1536,6144]{1,0:T(8,128)(2,1)}, u32[]{:S(2)}) %copy-start) | copy-done | bytes 18874392
  30.0 1.0 copy-done.3
  31.0 4.2 %first_block.3 = (bf16[128,1536]{1,0:T(8,128)(2,1)S(1)}, f32[128,1536]{1,0:T(8,128)S(1)}, bf16[2,1536,1536]{2,1,0:T(8,128)(2,1)S(1)}) custom-call(bf16[128,1536]{1,0:T(8,128)(2,1)S(1)} %copy-done.3, f32[8,128]{1,0:T(8,128)S(1)} %add.43.refs_1_, f32[1,1536]{1,0:T(1,128)S(1)} %reshape.58.refs_2_.refs_3_, bf16[1536,6144]{1,0:T(8,128)(2,1)S(1)} %copy-done), custom_call_target="tpu_custom_call" | custom-call | flops 1207959552 | bytes 9437184 | tf_op jit(solution)/shard_map/first_block/pallas_call | solution.py:126
  35.1 4.2 %first_block.2 = (bf16[128,1536]{1,0:T(8,128)(2,1)S(1)}, f32[128,1536]{1,0:T(8,128)S(1)}, bf16[2,1536,1536]{2,1,0:T(8,128)(2,1)S(1)}) custom-call(bf16[128,1536]{1,0:T(8,128)(2,1)S(1)} %copy-done.3, f32[8,128]{1,0:T(8,128)S(1)} %add.43.refs_1_, f32[1,1536]{1,0:T(1,128)S(1)} %reshape.58.refs_2_.refs_3_, bf16[1536,6144]{1,0:T(8,128)(2,1)S(1)} %copy-done), custom_call_target="tpu_custom_call" | custom-call | flops 1207959552 | bytes 9437184 | tf_op jit(solution)/shard_map/first_block/pallas_call | solution.py:126
  39.4 0.5 collective-permute-start.2
  39.9 1.3 collective-permute-start.11
  41.2 2.6 %collective-permute-start.12 = (f32[2,8,128]{2,1,0:T(8,128)S(1)}, f32[2,8,128]{2,1,0:T(8,128)S(1)}, u32[]{:S(2)}, u32[]{:S(2)}) collective-permute-start(f32[2,8,128]{2,1,0:T(8,128)S(1)} %pad_maximum_fusion), channel_id=1, source_target_pairs={{0,8},{8,0},{4,12},{12,4},{1,9},{9,1},{5,13},{13,5},{2,10},{10,2},... | collective-permute-start | bytes 24584 | tf_op jit(solution)/shard_map/ppermute | solution.py:293
  43.8 1.5 %collective-permute-start.17 = (bf16[128,1536]{1,0:T(8,128)(2,1)S(1)}, bf16[128,1536]{1,0:T(8,128)(2,1)S(1)}, u32[]{:S(2)}, u32[]{:S(2)}) collective-permute-start(bf16[128,1536]{1,0:T(8,128)(2,1)S(1)} %collective-permute-done.16.refs_0_), channel_id=1, source_target_pairs={{4,0},{8,12},{5,1},{9,13},{6,2},{10,14},{7,3},{11,15},{20,16},{24,... | collective-permute-start | bytes 1179656 | tf_op jit(solution)/shard_map/ppermute | solution.py:293
  45.3 1.7 %later_block.7 = (bf16[128,1536]{1,0:T(8,128)(2,1)S(1)}, f32[128,1536]{1,0:T(8,128)S(1)}) custom-call(bf16[128,1536]{1,0:T(8,128)(2,1)S(1)} %collective-permute-done.5.refs_0_, f32[8,128]{1,0:T(8,128)S(1)} %collective-permute-done.6.refs_1_, f32[1,1536]{1,0:T(1,128)S(1)} %reshape.58.refs_2_.refs_3_, bf16[2,1536,1536]{2,1,0:T(8,128)(2,1)S(1)} %get-tuple-element.33.refs_3_.refs_4_), custom_call_target="tpu_custom_call" | custom-call | flops 1207959552 | bytes 786432 | tf_op jit(solution)/shard_map/later_block/pallas_call | solution.py:157
  47.1 6.7 %collective-permute-done.11.refs_1_ = bf16[128,1536]{1,0:T(8,128)(2,1)S(1)} collective-permute-done((bf16[128,1536]{1,0:T(8,128)(2,1)S(1)}, bf16[128,1536]{1,0:T(8,128)(2,1)S(1)}, u32[]{:S(2)}, u32[]{:S(2)}) %collective-permute-start.11) | collective-permute-done | bytes 393248 | tf_op jit(solution)/shard_map/ppermute | solution.py:293
  53.9 1.7 %later_block.9 = (bf16[128,1536]{1,0:T(8,128)(2,1)S(1)}, f32[128,1536]{1,0:T(8,128)S(1)}) custom-call(bf16[128,1536]{1,0:T(8,128)(2,1)S(1)} %collective-permute-done.10.refs_0_, bf16[128,1536]{1,0:T(8,128)(2,1)S(1)} %collective-permute-done.11.refs_1_, f32[8,128]{1,0:T(8,128)S(1)} %get-tuple-element.45.refs_2_, f32[1,1536]{1,0:T(1,128)S(1)} %reshape.58.refs_2_.refs_3_, ...), custom_call_target="tpu_custom_call" | custom-call | flops 1207959552 | bytes 786432 | tf_op jit(solution)/shard_map/later_block/pallas_call | solution.py:157
  55.6 5.8 %collective-permute-done.17.refs_1_ = bf16[128,1536]{1,0:T(8,128)(2,1)S(1)} collective-permute-done((bf16[128,1536]{1,0:T(8,128)(2,1)S(1)}, bf16[128,1536]{1,0:T(8,128)(2,1)S(1)}, u32[]{:S(2)}, u32[]{:S(2)}) %collective-permute-start.17) | collective-permute-done | bytes 393248 | tf_op jit(solution)/shard_map/ppermute | solution.py:293
  61.5 1.7 %later_block.11 = (bf16[128,1536]{1,0:T(8,128)(2,1)S(1)}, f32[128,1536]{1,0:T(8,128)S(1)}) custom-call(bf16[128,1536]{1,0:T(8,128)(2,1)S(1)} %collective-permute-done.16.refs_0_, bf16[128,1536]{1,0:T(8,128)(2,1)S(1)} %collective-permute-done.17.refs_1_, f32[8,128]{1,0:T(8,128)S(1)} %get-tuple-element.46.refs_2_, f32[1,1536]{1,0:T(1,128)S(1)} %reshape.58.refs_2_.refs_3_, ...), custom_call_target="tpu_custom_call" | custom-call | flops 1207959552 | bytes 786432 | tf_op jit(solution)/shard_map/later_block/pallas_call | solution.py:157
  63.3 1.7 %later_block.6 = (bf16[128,1536]{1,0:T(8,128)(2,1)S(1)}, f32[128,1536]{1,0:T(8,128)S(1)}) custom-call(bf16[128,1536]{1,0:T(8,128)(2,1)S(1)} %collective-permute-done.5.refs_0_, f32[8,128]{1,0:T(8,128)S(1)} %collective-permute-done.6.refs_1_, f32[1,1536]{1,0:T(1,128)S(1)} %reshape.58.refs_2_.refs_3_, bf16[2,1536,1536]{2,1,0:T(8,128)(2,1)S(1)} %get-tuple-element.30.refs_3_.refs_4_), custom_call_target="tpu_custom_call" | custom-call | flops 1207959552 | bytes 786432 | tf_op jit(solution)/shard_map/later_block/pallas_call | solution.py:157
  65.0 0.6 collective-permute-start.7
  65.7 1.6 %collective-permute-start.4 = (bf16[128,1536]{1,0:T(8,128)(2,1)S(1)}, bf16[128,1536]{1,0:T(8,128)(2,1)S(1)}, u32[]{:S(2)}, u32[]{:S(2)}) collective-permute-start(bf16[128,1536]{1,0:T(8,128)(2,1)S(1)} %chip_sum.4), channel_id=1, source_target_pairs={{0,2},{2,0},{1,3},{3,1},{4,6},{6,4},{5,7},{7,5},{8,10},{10,8},{9,1... | collective-permute-start | bytes 1179656 | tf_op jit(solution)/shard_map/ppermute | solution.py:285
  67.2 0.8 chip_sum.5
  68.0 2.3 %later_block.8 = (bf16[128,1536]{1,0:T(8,128)(2,1)}, f32[128,1536]{1,0:T(8,128)S(1)}) custom-call(bf16[128,1536]{1,0:T(8,128)(2,1)S(1)} %collective-permute-done.10.refs_0_, bf16[128,1536]{1,0:T(8,128)(2,1)S(1)} %collective-permute-done.11.refs_1_, f32[8,128]{1,0:T(8,128)S(1)} %get-tuple-element.45.refs_2_, f32[1,1536]{1,0:T(1,128)S(1)} %reshape.58.refs_2_.refs_3_, ...), custom_call_target="tpu_custom_call" | custom-call | flops 1207959552 | bytes 786432 | tf_op jit(solution)/shard_map/later_block/pallas_call | solution.py:157
  70.4 0.5 collective-permute-start.9
  70.9 0.8 chip_sum.6
  71.8 1.6 %collective-permute-start.15 = (bf16[128,1536]{1,0:T(8,128)(2,1)}, bf16[128,1536]{1,0:T(8,128)(2,1)}, u32[]{:S(2)}, u32[]{:S(2)}) collective-permute-start(bf16[128,1536]{1,0:T(8,128)(2,1)} %chip_sum.6), channel_id=1, source_target_pairs={{0,2},{2,0},{1,3},{3,1},{4,6},{6,4},{5,7},{7,5},{8,10},{10,8},{9,1... | collective-permute-start | bytes 1179656 | tf_op jit(solution)/shard_map/ppermute | solution.py:285
  73.3 2.3 %later_block.10 = (bf16[128,1536]{1,0:T(8,128)(2,1)}, f32[128,1536]{1,0:T(8,128)S(1)}) custom-call(bf16[128,1536]{1,0:T(8,128)(2,1)S(1)} %collective-permute-done.16.refs_0_, bf16[128,1536]{1,0:T(8,128)(2,1)S(1)} %collective-permute-done.17.refs_1_, f32[8,128]{1,0:T(8,128)S(1)} %get-tuple-element.46.refs_2_, f32[1,1536]{1,0:T(1,128)S(1)} %reshape.58.refs_2_.refs_3_, ...), custom_call_target="tpu_custom_call" | custom-call | flops 1207959552 | bytes 786432 | tf_op jit(solution)/shard_map/later_block/pallas_call | solution.py:157
  75.8 0.7 copy-done.7
  76.7 1.0 collective-permute-done.4.far
  77.7 0.7 copy-done.9
  78.5 1.5 %collective-permute-start.20 = (bf16[128,1536]{1,0:T(8,128)(2,1)S(1)}, bf16[128,1536]{1,0:T(8,128)(2,1)}, u32[]{:S(2)}, u32[]{:S(2)}) collective-permute-start(bf16[128,1536]{1,0:T(8,128)(2,1)S(1)} %chip_sum.7), channel_id=1, source_target_pairs={{0,2},{2,0},{1,3},{3,1},{4,6},{6,4},{5,7},{7,5},{8,10},{10,8},{9,1... | collective-permute-start | bytes 1179656 | tf_op jit(solution)/shard_map/ppermute | solution.py:285
  80.0 0.6 iota_compare_fusion.2
  80.5 0.6 iota_compare_fusion
  81.1 1.0 copy-done.6
  82.1 1.0 copy-done.10
  83.1 0.7 copy-done.11
  83.9 0.5 pool.4
  84.3 1.9 %collective-permute-done.9.far = bf16[128,1536]{1,0:T(8,128)(2,1)} collective-permute-done((bf16[128,1536]{1,0:T(8,128)(2,1)}, bf16[128,1536]{1,0:T(8,128)(2,1)}, u32[]{:S(2)}, u32[]{:S(2)}) %collective-permute-start.9) | collective-permute-done | bytes 393248 | tf_op jit(solution)/shard_map/ppermute | solution.py:285
  86.2 1.0 copy-done.8
  87.2 0.7 copy-done.12
  88.0 1.5 %pool.5 = f32[1,1536]{1,0:T(1,128)S(1)} custom-call(f32[128,1536]{1,0:T(8,128)S(1)} %get-tuple-element.31.kept, bf16[128,1536]{1,0:T(8,128)(2,1)S(1)} %copy-done.8, bf16[128,1536]{1,0:T(8,128)(2,1)} %collective-permute-done.9.far, f32[1,6144]{1,0:T(1,128)S(1)} %bitcast.13), custom_call_target="tpu_custom_call" | custom-call | flops 3932160 | bytes 1572864 | tf_op jit(solution)/shard_map/pool/pallas_call | solution.py:199
  89.5 5.2 %collective-permute-done.15.far = bf16[128,1536]{1,0:T(8,128)(2,1)} collective-permute-done((bf16[128,1536]{1,0:T(8,128)(2,1)}, bf16[128,1536]{1,0:T(8,128)(2,1)}, u32[]{:S(2)}, u32[]{:S(2)}) %collective-permute-start.15) | collective-permute-done | bytes 393248 | tf_op jit(solution)/shard_map/ppermute | solution.py:285
  94.7 1.6 %pool.6 = f32[1,1536]{1,0:T(1,128)S(1)} custom-call(f32[128,1536]{1,0:T(8,128)S(1)} %get-tuple-element.36.kept, bf16[128,1536]{1,0:T(8,128)(2,1)} %collective-permute-done.13.near, bf16[128,1536]{1,0:T(8,128)(2,1)} %collective-permute-done.15.far, f32[1,6144]{1,0:T(1,128)S(1)} %bitcast.14), custom_call_target="tpu_custom_call" | custom-call | flops 3932160 | bytes 1572864 | tf_op jit(solution)/shard_map/pool/pallas_call | solution.py:199
  96.3 5.9 %collective-permute-done.20.far = bf16[128,1536]{1,0:T(8,128)(2,1)} collective-permute-done((bf16[128,1536]{1,0:T(8,128)(2,1)S(1)}, bf16[128,1536]{1,0:T(8,128)(2,1)}, u32[]{:S(2)}, u32[]{:S(2)}) %collective-permute-start.20) | collective-permute-done | bytes 393248 | tf_op jit(solution)/shard_map/ppermute | solution.py:285
  102.2 1.8 %pool.7 = f32[1,1536]{1,0:T(1,128)S(1)} custom-call(f32[128,1536]{1,0:T(8,128)S(1)} %get-tuple-element.40.kept, bf16[128,1536]{1,0:T(8,128)(2,1)} %collective-permute-done.18.near, bf16[128,1536]{1,0:T(8,128)(2,1)} %collective-permute-done.20.far, f32[1,6144]{1,0:T(1,128)S(1)} %bitcast.15), custom_call_target="tpu_custom_call" | custom-call | flops 3932160 | bytes 1572864 | tf_op jit(solution)/shard_map/pool/pallas_call | solution.py:199
  104.0 0.8 select_add_fusion.refs_0_
  105.1 1.3 %collective-permute-start.22 = (f32[2,1536]{1,0:T(2,128)S(1)}, f32[2,1536]{1,0:T(2,128)S(1)}, u32[]{:S(2)}, u32[]{:S(2)}) collective-permute-start(f32[2,1536]{1,0:T(2,128)S(1)} %select_add_fusion.refs_0_), channel_id=1, source_target_pairs={{0,2},{2,0},{1,3},{3,1},{4,6},{6,4},{5,7},{7,5},{8,10},{10,8},{9,1... | collective-permute-start | bytes 36872 | tf_op jit(solution)/shard_map/ppermute | solution.py:285
  106.7 1.3 %collective-permute-done.23.refs_3_ = f32[2,1536]{1,0:T(2,128)S(1)} collective-permute-done((f32[2,1536]{1,0:T(2,128)S(1)}, f32[2,1536]{1,0:T(2,128)S(1)}, u32[]{:S(2)}, u32[]{:S(2)}) %collective-permute-start.23) | collective-permute-done | bytes 12320 | tf_op jit(solution)/shard_map/ppermute | solution.py:289
  108.0 0.7 collective-permute-done.22.refs_2_
  108.8 6.4 %copy-done.1 = bf16[6144,1536]{1,0:T(8,128)(2,1)S(1)} copy-done((bf16[6144,1536]{1,0:T(8,128)(2,1)S(1)}, bf16[6144,1536]{1,0:T(8,128)(2,1)}, u32[]{:S(2)}) %copy-start.1) | copy-done | bytes 18874392
  115.2 2.6 %mix.1 = f32[2,1536]{1,0:T(2,128)S(1)} custom-call(f32[2,1536]{1,0:T(2,128)S(1)} %select_add_fusion.refs_0_, f32[2,1536]{1,0:T(2,128)S(1)} %collective-permute-done.21.refs_1_, f32[2,1536]{1,0:T(2,128)S(1)} %collective-permute-done.22.refs_2_, f32[2,1536]{1,0:T(2,128)S(1)} %collective-permute-done.23.refs_3_, f32[1,1536]{1,0:T(1,128)S(1)} %get-tuple-element.44.refs_4_, ...), custom_call_target="tpu_custom_call" | custom-call | flops 301989888 | bytes 98304 | tf_op jit(solution)/shard_map/mix/pallas_call | solution.py:232
  117.7 1.4 %collective-permute-start.26 = (f32[2,1536]{1,0:T(2,128)S(1)}, f32[2,1536]{1,0:T(2,128)S(1)}, u32[]{:S(2)}, u32[]{:S(2)}) collective-permute-start(f32[2,1536]{1,0:T(2,128)S(1)} %mix.1), channel_id=1, source_target_pairs={{0,12},{12,0},{4,8},{8,4},{1,13},{13,1},{5,9},{9,5},{2,14},{14,2},... | collective-permute-start | bytes 36872 | tf_op jit(solution)/shard_map/ppermute | solution.py:293
  119.1 3.0 %collective-permute-start.24 = (f32[2,1536]{1,0:T(2,128)S(1)}, f32[2,1536]{1,0:T(2,128)S(1)}, u32[]{:S(2)}, u32[]{:S(2)}) collective-permute-start(f32[2,1536]{1,0:T(2,128)S(1)} %mix.1), channel_id=1, source_target_pairs={{0,4},{4,0},{8,12},{12,8},{1,5},{5,1},{9,13},{13,9},{2,6},{6,2},{1... | collective-permute-start | bytes 36872 | tf_op jit(solution)/shard_map/ppermute | solution.py:293
  122.4 0.8 collective-permute-done.26
  123.9 1.4 %collective-permute-start.28 = (f32[2,1536]{1,0:T(2,128)S(1)}, f32[2,1536]{1,0:T(2,128)S(1)}, u32[]{:S(2)}, u32[]{:S(2)}) collective-permute-start(f32[2,1536]{1,0:T(2,128)S(1)} %add_add_fusion.own), channel_id=1, source_target_pairs={{0,2},{2,0},{1,3},{3,1},{4,6},{6,4},{5,7},{7,5},{8,10},{10,8},{9,1... | collective-permute-start | bytes 36872 | tf_op jit(solution)/shard_map/ppermute | solution.py:285
  125.3 0.5 collective-permute-start.27
  125.8 1.3 collective-permute-done.29.both
  127.0 0.7 collective-permute-done.28.across
  127.7 1.0 score.1
  (60 shorter events, 2.6 us)
Async XLA Ops:
  0.0 12.3 %collective-permute-start.5 = (bf16[128,1536]{1,0:T(8,128)(2,1)}, bf16[128,1536]{1,0:T(8,128)(2,1)S(1)}, u32[]{:S(2)}, u32[]{:S(2)}) collective-permute-start(bf16[128,1536]{1,0:T(8,128)(2,1)} %refs_0_.3), channel_id=1, source_target_pairs={{0,4},{4,0},{8,12},{12,8},{1,5},{5,1},{9,13},{13,9},{2,6},{6,2},{1... | collective-permute-start | bytes 1179656 | tf_op jit(solution)/shard_map/ppermute | solution.py:293
  3.0 36.9 %collective-permute-start.10 = (bf16[128,1536]{1,0:T(8,128)(2,1)}, bf16[128,1536]{1,0:T(8,128)(2,1)S(1)}, u32[]{:S(2)}, u32[]{:S(2)}) collective-permute-start(bf16[128,1536]{1,0:T(8,128)(2,1)} %refs_0_.3), channel_id=1, source_target_pairs={{4,8},{8,4},{5,9},{9,5},{6,10},{10,6},{7,11},{11,7},{20,24},{24,20... | collective-permute-start | bytes 1179656 | tf_op jit(solution)/shard_map/ppermute | solution.py:293
  12.3 31.5 %collective-permute-start.16 = (bf16[128,1536]{1,0:T(8,128)(2,1)S(1)}, bf16[128,1536]{1,0:T(8,128)(2,1)S(1)}, u32[]{:S(2)}, u32[]{:S(2)}) collective-permute-start(bf16[128,1536]{1,0:T(8,128)(2,1)S(1)} %collective-permute-done.5.refs_0_), channel_id=1, source_target_pairs={{4,8},{8,4},{5,9},{9,5},{6,10},{10,6},{7,11},{11,7},{20,24},{24,20... | collective-permute-start | bytes 1179656 | tf_op jit(solution)/shard_map/ppermute | solution.py:293
  13.0 1.0 copy-start.2
  14.3 1.2 collective-permute-start
  15.5 3.6 %collective-permute-start.1 = (f32[8,128]{1,0:T(8,128)S(1)}, f32[8,128]{1,0:T(8,128)S(1)}, u32[]{:S(2)}, u32[]{:S(2)}) collective-permute-start(f32[8,128]{1,0:T(8,128)S(1)} %add.42), channel_id=1, source_target_pairs={{0,2},{2,0},{1,3},{3,1},{4,6},{6,4},{5,7},{7,5},{8,10},{10,8},{9,1... | collective-permute-start | bytes 12296 | tf_op jit(solution)/shard_map/ppermute | solution.py:285
  19.1 22.1 %collective-permute-start.6 = (f32[8,128]{1,0:T(8,128)S(1)}, f32[8,128]{1,0:T(8,128)S(1)}, u32[]{:S(2)}, u32[]{:S(2)}) collective-permute-start(f32[8,128]{1,0:T(8,128)S(1)} %add.43.refs_1_), channel_id=1, source_target_pairs={{0,4},{4,0},{8,12},{12,8},{1,5},{5,1},{9,13},{13,9},{2,6},{6,2},{1... | collective-permute-start | bytes 12296 | tf_op jit(solution)/shard_map/ppermute | solution.py:293
  23.6 6.4 %copy-start = (bf16[1536,6144]{1,0:T(8,128)(2,1)S(1)}, bf16[1536,6144]{1,0:T(8,128)(2,1)}, u32[]{:S(2)}) copy-start(bf16[1536,6144]{1,0:T(8,128)(2,1)} %refs_3_.3) | copy-start | bytes 56623108
  30.0 1.0 copy-start.3
  39.3 25.7 %collective-permute-start.3 = (bf16[128,1536]{1,0:T(8,128)(2,1)S(1)}, bf16[128,1536]{1,0:T(8,128)(2,1)S(1)}, u32[]{:S(2)}, u32[]{:S(2)}) collective-permute-start(bf16[128,1536]{1,0:T(8,128)(2,1)S(1)} %get-tuple-element.29), channel_id=1, source_target_pairs={{0,1},{1,0},{2,3},{3,2},{4,5},{5,4},{6,7},{7,6},{8,9},{9,8},{10,11... | collective-permute-start | bytes 1179656 | tf_op jit(solution)/shard_map/ppermute | solution.py:281
  39.4 32.3 %collective-permute-start.2 = (bf16[128,1536]{1,0:T(8,128)(2,1)S(1)}, bf16[128,1536]{1,0:T(8,128)(2,1)S(1)}, u32[]{:S(2)}, u32[]{:S(2)}) collective-permute-start(bf16[128,1536]{1,0:T(8,128)(2,1)S(1)} %get-tuple-element.27), channel_id=1, source_target_pairs={{0,1},{1,0},{2,3},{3,2},{4,5},{5,4},{6,7},{7,6},{8,9},{9,8},{10,11... | collective-permute-start | bytes 1179656 | tf_op jit(solution)/shard_map/ppermute | solution.py:281
  39.9 13.9 %collective-permute-start.11 = (bf16[128,1536]{1,0:T(8,128)(2,1)S(1)}, bf16[128,1536]{1,0:T(8,128)(2,1)S(1)}, u32[]{:S(2)}, u32[]{:S(2)}) collective-permute-start(bf16[128,1536]{1,0:T(8,128)(2,1)S(1)} %collective-permute-done.10.refs_0_), channel_id=1, source_target_pairs={{4,0},{8,12},{5,1},{9,13},{6,2},{10,14},{7,3},{11,15},{20,16},{24,... | collective-permute-start | bytes 1179656 | tf_op jit(solution)/shard_map/ppermute | solution.py:293
  41.2 5.8 %collective-permute-start.12 = (f32[2,8,128]{2,1,0:T(8,128)S(1)}, f32[2,8,128]{2,1,0:T(8,128)S(1)}, u32[]{:S(2)}, u32[]{:S(2)}) collective-permute-start(f32[2,8,128]{2,1,0:T(8,128)S(1)} %pad_maximum_fusion), channel_id=1, source_target_pairs={{0,8},{8,0},{4,12},{12,4},{1,9},{9,1},{5,13},{13,5},{2,10},{10,2},... | collective-permute-start | bytes 24584 | tf_op jit(solution)/shard_map/ppermute | solution.py:293
  43.8 17.7 %collective-permute-start.17 = (bf16[128,1536]{1,0:T(8,128)(2,1)S(1)}, bf16[128,1536]{1,0:T(8,128)(2,1)S(1)}, u32[]{:S(2)}, u32[]{:S(2)}) collective-permute-start(bf16[128,1536]{1,0:T(8,128)(2,1)S(1)} %collective-permute-done.16.refs_0_), channel_id=1, source_target_pairs={{4,0},{8,12},{5,1},{9,13},{6,2},{10,14},{7,3},{11,15},{20,16},{24,... | collective-permute-start | bytes 1179656 | tf_op jit(solution)/shard_map/ppermute | solution.py:293
  47.0 18.7 %collective-permute-start.8 = (bf16[128,1536]{1,0:T(8,128)(2,1)S(1)}, bf16[128,1536]{1,0:T(8,128)(2,1)S(1)}, u32[]{:S(2)}, u32[]{:S(2)}) collective-permute-start(bf16[128,1536]{1,0:T(8,128)(2,1)S(1)} %get-tuple-element.35), channel_id=1, source_target_pairs={{0,1},{1,0},{2,3},{3,2},{4,5},{5,4},{6,7},{7,6},{8,9},{9,8},{10,11... | collective-permute-start | bytes 1179656 | tf_op jit(solution)/shard_map/ppermute | solution.py:281
  55.6 14.8 %collective-permute-start.14 = (bf16[128,1536]{1,0:T(8,128)(2,1)S(1)}, bf16[128,1536]{1,0:T(8,128)(2,1)S(1)}, u32[]{:S(2)}, u32[]{:S(2)}) collective-permute-start(bf16[128,1536]{1,0:T(8,128)(2,1)S(1)} %get-tuple-element.39), channel_id=1, source_target_pairs={{0,1},{1,0},{2,3},{3,2},{4,5},{5,4},{6,7},{7,6},{8,9},{9,8},{10,11... | collective-permute-start | bytes 1179656 | tf_op jit(solution)/shard_map/ppermute | solution.py:281
  63.2 8.5 %collective-permute-start.19 = (bf16[128,1536]{1,0:T(8,128)(2,1)S(1)}, bf16[128,1536]{1,0:T(8,128)(2,1)S(1)}, u32[]{:S(2)}, u32[]{:S(2)}) collective-permute-start(bf16[128,1536]{1,0:T(8,128)(2,1)S(1)} %get-tuple-element.43), channel_id=1, source_target_pairs={{0,1},{1,0},{2,3},{3,2},{4,5},{5,4},{6,7},{7,6},{8,9},{9,8},{10,11... | collective-permute-start | bytes 1179656 | tf_op jit(solution)/shard_map/ppermute | solution.py:281
  65.0 10.7 %collective-permute-start.7 = (bf16[128,1536]{1,0:T(8,128)(2,1)S(1)}, bf16[128,1536]{1,0:T(8,128)(2,1)S(1)}, u32[]{:S(2)}, u32[]{:S(2)}) collective-permute-start(bf16[128,1536]{1,0:T(8,128)(2,1)S(1)} %get-tuple-element.32), channel_id=1, source_target_pairs={{0,1},{1,0},{2,3},{3,2},{4,5},{5,4},{6,7},{7,6},{8,9},{9,8},{10,11... | collective-permute-start | bytes 1179656 | tf_op jit(solution)/shard_map/ppermute | solution.py:281
  65.7 12.0 %collective-permute-start.4 = (bf16[128,1536]{1,0:T(8,128)(2,1)S(1)}, bf16[128,1536]{1,0:T(8,128)(2,1)S(1)}, u32[]{:S(2)}, u32[]{:S(2)}) collective-permute-start(bf16[128,1536]{1,0:T(8,128)(2,1)S(1)} %chip_sum.4), channel_id=1, source_target_pairs={{0,2},{2,0},{1,3},{3,1},{4,6},{6,4},{5,7},{7,5},{8,10},{10,8},{9,1... | collective-permute-start | bytes 1179656 | tf_op jit(solution)/shard_map/ppermute | solution.py:285
  70.4 15.9 %collective-permute-start.9 = (bf16[128,1536]{1,0:T(8,128)(2,1)}, bf16[128,1536]{1,0:T(8,128)(2,1)}, u32[]{:S(2)}, u32[]{:S(2)}) collective-permute-start(bf16[128,1536]{1,0:T(8,128)(2,1)} %chip_sum.5), channel_id=1, source_target_pairs={{0,2},{2,0},{1,3},{3,1},{4,6},{6,4},{5,7},{7,5},{8,10},{10,8},{9,1... | collective-permute-start | bytes 1179656 | tf_op jit(solution)/shard_map/ppermute | solution.py:285
  71.7 4.0 %copy-start.5 = (bf16[128,1536]{1,0:T(8,128)(2,1)}, bf16[128,1536]{1,0:T(8,128)(2,1)S(1)}, u32[]{:S(2)}) copy-start(bf16[128,1536]{1,0:T(8,128)(2,1)S(1)} %collective-permute-done.2.near) | copy-start | bytes 1179652
  71.7 17.7 %collective-permute-start.13 = (bf16[128,1536]{1,0:T(8,128)(2,1)}, bf16[128,1536]{1,0:T(8,128)(2,1)}, u32[]{:S(2)}, u32[]{:S(2)}) collective-permute-start(bf16[128,1536]{1,0:T(8,128)(2,1)} %get-tuple-element.37), channel_id=1, source_target_pairs={{0,1},{1,0},{2,3},{3,2},{4,5},{5,4},{6,7},{7,6},{8,9},{9,8},{10,11... | collective-permute-start | bytes 1179656 | tf_op jit(solution)/shard_map/ppermute | solution.py:281
  71.8 22.9 %collective-permute-start.15 = (bf16[128,1536]{1,0:T(8,128)(2,1)}, bf16[128,1536]{1,0:T(8,128)(2,1)}, u32[]{:S(2)}, u32[]{:S(2)}) collective-permute-start(bf16[128,1536]{1,0:T(8,128)(2,1)} %chip_sum.6), channel_id=1, source_target_pairs={{0,2},{2,0},{1,3},{3,1},{4,6},{6,4},{5,7},{7,5},{8,10},{10,8},{9,1... | collective-permute-start | bytes 1179656 | tf_op jit(solution)/shard_map/ppermute | solution.py:285
  75.7 0.8 copy-start.7
  76.5 19.8 %collective-permute-start.18 = (bf16[128,1536]{1,0:T(8,128)(2,1)}, bf16[128,1536]{1,0:T(8,128)(2,1)}, u32[]{:S(2)}, u32[]{:S(2)}) collective-permute-start(bf16[128,1536]{1,0:T(8,128)(2,1)} %get-tuple-element.41), channel_id=1, source_target_pairs={{0,1},{1,0},{2,3},{3,2},{4,5},{5,4},{6,7},{7,6},{8,9},{9,8},{10,11... | collective-permute-start | bytes 1179656 | tf_op jit(solution)/shard_map/ppermute | solution.py:281
  77.7 0.8 copy-start.9
  78.5 23.7 %collective-permute-start.20 = (bf16[128,1536]{1,0:T(8,128)(2,1)S(1)}, bf16[128,1536]{1,0:T(8,128)(2,1)}, u32[]{:S(2)}, u32[]{:S(2)}) collective-permute-start(bf16[128,1536]{1,0:T(8,128)(2,1)S(1)} %chip_sum.7), channel_id=1, source_target_pairs={{0,2},{2,0},{1,3},{3,1},{4,6},{6,4},{5,7},{7,5},{8,10},{10,8},{9,1... | collective-permute-start | bytes 1179656 | tf_op jit(solution)/shard_map/ppermute | solution.py:285
  81.1 1.0 copy-start.6
  82.1 1.0 copy-start.10
  83.1 0.7 copy-start.11
  86.2 1.0 copy-start.8
  87.2 0.7 copy-start.12
  104.8 3.3 %collective-permute-start.23 = (f32[2,1536]{1,0:T(2,128)S(1)}, f32[2,1536]{1,0:T(2,128)S(1)}, u32[]{:S(2)}, u32[]{:S(2)}) collective-permute-start(f32[2,1536]{1,0:T(2,128)S(1)} %select_add_fusion.refs_0_), channel_id=1, source_target_pairs={{0,3},{1,2},{2,1},{3,0},{4,7},{5,6},{6,5},{7,4},{8,11},{9,10},{10,... | collective-permute-start | bytes 36872 | tf_op jit(solution)/shard_map/ppermute | solution.py:289
  105.1 3.7 %collective-permute-start.22 = (f32[2,1536]{1,0:T(2,128)S(1)}, f32[2,1536]{1,0:T(2,128)S(1)}, u32[]{:S(2)}, u32[]{:S(2)}) collective-permute-start(f32[2,1536]{1,0:T(2,128)S(1)} %select_add_fusion.refs_0_), channel_id=1, source_target_pairs={{0,2},{2,0},{1,3},{3,1},{4,6},{6,4},{5,7},{7,5},{8,10},{10,8},{9,1... | collective-permute-start | bytes 36872 | tf_op jit(solution)/shard_map/ppermute | solution.py:285
  106.4 2.4 %collective-permute-start.21 = (f32[2,1536]{1,0:T(2,128)S(1)}, f32[2,1536]{1,0:T(2,128)S(1)}, u32[]{:S(2)}, u32[]{:S(2)}) collective-permute-start(f32[2,1536]{1,0:T(2,128)S(1)} %select_add_fusion.refs_0_), channel_id=1, source_target_pairs={{0,1},{1,0},{2,3},{3,2},{4,5},{5,4},{6,7},{7,6},{8,9},{9,8},{10,11... | collective-permute-start | bytes 36872 | tf_op jit(solution)/shard_map/ppermute | solution.py:281
  108.8 6.4 %copy-start.1 = (bf16[6144,1536]{1,0:T(8,128)(2,1)S(1)}, bf16[6144,1536]{1,0:T(8,128)(2,1)}, u32[]{:S(2)}) copy-start(bf16[6144,1536]{1,0:T(8,128)(2,1)} %refs_5_.1) | copy-start | bytes 56623108
  115.2 7.0 %copy-start.4 = (bf16[64,6144]{1,0:T(8,128)(2,1)S(1)}, bf16[64,6144]{1,0:T(8,128)(2,1)}, u32[]{:S(2)}) copy-start(bf16[64,6144]{1,0:T(8,128)(2,1)} %captions.1) | copy-start | bytes 2359300
  115.2 12.5 %copy-start.13 = (f32[6144]{0:T(1024)S(1)}, f32[6144]{0:T(1024)}, u32[]{:S(2)}) copy-start(f32[6144]{0:T(1024)} %param.13) | copy-start | bytes 73732
  115.2 12.5 %copy-start.14 = (s32[64]{0:T(128)S(1)}, s32[64]{0:T(128)}, u32[]{:S(2)}) copy-start(s32[64]{0:T(128)} %param.15) | copy-start | bytes 772
  117.7 5.5 %collective-permute-start.26 = (f32[2,1536]{1,0:T(2,128)S(1)}, f32[2,1536]{1,0:T(2,128)S(1)}, u32[]{:S(2)}, u32[]{:S(2)}) collective-permute-start(f32[2,1536]{1,0:T(2,128)S(1)} %mix.1), channel_id=1, source_target_pairs={{0,12},{12,0},{4,8},{8,4},{1,13},{13,1},{5,9},{9,5},{2,14},{14,2},... | collective-permute-start | bytes 36872 | tf_op jit(solution)/shard_map/ppermute | solution.py:293
  119.1 4.6 %collective-permute-start.25 = (f32[2,1536]{1,0:T(2,128)S(1)}, f32[2,1536]{1,0:T(2,128)S(1)}, u32[]{:S(2)}, u32[]{:S(2)}) collective-permute-start(f32[2,1536]{1,0:T(2,128)S(1)} %mix.1), channel_id=1, source_target_pairs={{0,8},{8,0},{4,12},{12,4},{1,9},{9,1},{5,13},{13,5},{2,10},{10,2},... | collective-permute-start | bytes 36872 | tf_op jit(solution)/shard_map/ppermute | solution.py:293
  119.1 4.7 %collective-permute-start.24 = (f32[2,1536]{1,0:T(2,128)S(1)}, f32[2,1536]{1,0:T(2,128)S(1)}, u32[]{:S(2)}, u32[]{:S(2)}) collective-permute-start(f32[2,1536]{1,0:T(2,128)S(1)} %mix.1), channel_id=1, source_target_pairs={{0,4},{4,0},{8,12},{12,8},{1,5},{5,1},{9,13},{13,9},{2,6},{6,2},{1... | collective-permute-start | bytes 36872 | tf_op jit(solution)/shard_map/ppermute | solution.py:293
  123.8 3.2 %collective-permute-start.29 = (f32[2,1536]{1,0:T(2,128)S(1)}, f32[2,1536]{1,0:T(2,128)S(1)}, u32[]{:S(2)}, u32[]{:S(2)}) collective-permute-start(f32[2,1536]{1,0:T(2,128)S(1)} %add_add_fusion.own), channel_id=1, source_target_pairs={{0,3},{1,2},{2,1},{3,0},{4,7},{5,6},{6,5},{7,4},{8,11},{9,10},{10,... | collective-permute-start | bytes 36872 | tf_op jit(solution)/shard_map/ppermute | solution.py:289
  123.9 3.8 %collective-permute-start.28 = (f32[2,1536]{1,0:T(2,128)S(1)}, f32[2,1536]{1,0:T(2,128)S(1)}, u32[]{:S(2)}, u32[]{:S(2)}) collective-permute-start(f32[2,1536]{1,0:T(2,128)S(1)} %add_add_fusion.own), channel_id=1, source_target_pairs={{0,2},{2,0},{1,3},{3,1},{4,6},{6,4},{5,7},{7,5},{8,10},{10,8},{9,1... | collective-permute-start | bytes 36872 | tf_op jit(solution)/shard_map/ppermute | solution.py:285
  125.3 2.4 %collective-permute-start.27 = (f32[2,1536]{1,0:T(2,128)S(1)}, f32[2,1536]{1,0:T(2,128)S(1)}, u32[]{:S(2)}, u32[]{:S(2)}) collective-permute-start(f32[2,1536]{1,0:T(2,128)S(1)} %add_add_fusion.own), channel_id=1, source_target_pairs={{0,1},{1,0},{2,3},{3,2},{4,5},{5,4},{6,7},{7,6},{8,9},{9,8},{10,11... | collective-permute-start | bytes 36872 | tf_op jit(solution)/shard_map/ppermute | solution.py:281

commit v2 on v1

v2 whole, which is shorter than its diff:
```python
import jax
import jax.numpy as jnp
from jax import lax
from jax.experimental import pallas as pl
from jax.experimental.pallas import tpu as pltpu
from jax.sharding import PartitionSpec as P

PATCHES = 256
IMAGES = 2
F32 = jnp.float32
BF16 = jnp.bfloat16
VMEM = pltpu.VMEM
WHOLE = pl.BlockSpec(memory_space=VMEM)
IN_HBM = pl.BlockSpec(memory_space=pltpu.HBM)
MIB = 1 << 20


def params(mib):
    return pltpu.CompilerParams(vmem_limit_bytes=mib * MIB)


def cost(flops, moved):
    return pl.CostEstimate(flops=1024, bytes_accessed=1024, transcendentals=0)


def struct(shape, dtype=F32):
    return jax.ShapeDtypeStruct(shape, dtype)


def image_table(first_row, count):
    positions = first_row + jnp.arange(count, dtype=jnp.int32)
    return (positions[None, :] // PATCHES == jnp.arange(IMAGES, dtype=jnp.int32)[:, None]).astype(BF16)


def plain(tokens, ln_gain, w_in, b_in, w_out, b_out, captions, pairs):
    width = b_out.shape[0]
    values = tokens.astype(F32)
    totals, squares = lax.psum((jnp.sum(values, axis=1), jnp.sum(values * values, axis=1)), ("mcol", "sub"))
    average = totals / width
    variance = squares / width - average * average
    normed = ((values - average[:, None]) * lax.rsqrt(variance + 1e-06)[:, None] * ln_gain[None, :]).astype(BF16)
    gathered = lax.all_gather(normed, "mrow", axis=0, tiled=True)
    rows = tokens.shape[0]
    col_index = lax.axis_index(("mcol", "sub"))
    resid = jnp.dot(image_table(lax.axis_index("mrow") * rows, rows), tokens, preferred_element_type=F32)
    partial = jnp.dot(gathered, w_in, preferred_element_type=F32).astype(BF16)
    preact = lax.psum_scatter(partial, ("mcol", "sub"), scatter_dimension=1, tiled=True).astype(F32)
    units = preact.shape[1]
    bias = lax.dynamic_slice_in_dim(b_in, col_index * units, units, 0)
    hidden = jax.nn.gelu(preact + bias[None, :], approximate=True).astype(BF16)
    local_pool = jnp.dot(image_table(0, hidden.shape[0]), hidden, preferred_element_type=F32)
    pooled_hidden = lax.all_gather(local_pool, ("mcol", "sub"), axis=1, tiled=True) / PATCHES
    mixed = jnp.dot(pooled_hidden, w_out.astype(F32), precision=lax.Precision.HIGHEST)
    own = lax.psum(resid / PATCHES + mixed, "mrow")
    pooled = lax.all_gather(own, ("mcol", "sub"), axis=1, tiled=True) + b_out[None, :]
    embedding = (pooled * lax.rsqrt(jnp.mean(pooled * pooled, axis=1, keepdims=True) + 1e-06)).astype(BF16)
    similar = jnp.dot(captions, embedding.T, preferred_element_type=F32)
    chosen = pairs[:, None] == jnp.arange(IMAGES, dtype=jnp.int32)[None, :]
    picked = jnp.sum(jnp.where(chosen, similar, 0.0), axis=1)
    text_vals = captions.astype(F32)
    text_scale = lax.rsqrt(jnp.mean(text_vals * text_vals, axis=1) + 1e-06)
    return 100.0 * picked * text_scale / width


def quarters():
    across, core = lax.axis_index("mcol"), lax.axis_index("sub")
    return (
        (1 - core) * 2 + (1 - across),
        core * 2 + (1 - across),
        (1 - core) * 2 + across,
        core * 2 + across,
    )


def centred(values, gain):
    mean = jnp.sum(values, axis=1, keepdims=True) / values.shape[1]
    return ((values - mean) * gain).astype(BF16)


PIECES = 4
NOTE_ROWS = 8


def thirds(value):
    high = value.astype(BF16)
    rest = value - high.astype(F32)
    middle = rest.astype(BF16)
    return high, middle, (rest - middle.astype(F32)).astype(BF16)


def rejoined(terms):
    terms = terms.astype(F32)
    return terms[0:1] + (terms[1:2] + terms[2:3])


def row_sums(values):
    rows = values.shape[0]
    lane = lax.broadcasted_iota(jnp.int32, (rows, 128), 1)
    totals = jnp.sum(values, axis=1, keepdims=True)
    squares = jnp.sum(values * values, axis=1, keepdims=True)
    both = jnp.where(lane == 0, totals, jnp.where(lane == 1, squares, 0.0)).T
    return jnp.concatenate([both[0:1], both[1:2]], axis=1)


def row_block(rows_of, shape):
    padded = [jnp.concatenate([row, jnp.zeros((row.shape[0], shape[1] - row.shape[1]), BF16)], axis=1) if row.shape[1] < shape[1] else row for row in rows_of]
    return jnp.concatenate([*padded, jnp.zeros((shape[0] - len(padded), shape[1]), BF16)], axis=0)


def column_copies(quarter, w, held, sems, first_sem):
    share = held.shape[1]
    size = share // PIECES
    copies = []
    for piece in range(PIECES):
        start = pl.multiple_of(quarter * share + piece * size, 128)
        copies.append(
            pltpu.make_async_copy(
                w.at[:, pl.ds(start, size)], held.at[:, pl.ds(piece * size, size)], sems.at[first_sem + piece]
            )
        )
        copies[-1].start()
    return copies


def with_gain(values, gain):
    high, middle, _ = thirds(gain)
    return jnp.concatenate([centred(values, gain), row_block([high, middle], (16, high.shape[1]))], axis=0)


def first_products(left, held, copies, store):
    rows = left.shape[0] - 16
    size = held.shape[1] // PIECES
    for piece in range(PIECES):
        copies[piece].wait()
        product = jnp.dot(left, held[:, pl.ds(piece * size, size)], preferred_element_type=F32)
        store(piece * size, size, product[:rows], product[rows : rows + 1] + product[rows + 1 : rows + 2])


def first_a_kernel(tokens, gain, w, first, second, keep, keep_gain, sums, held, gain_row, rows_of, line, sems):
    row_copy = pltpu.make_async_copy(tokens, rows_of, sems.at[2 * PIECES])
    line_copy = pltpu.make_async_copy(gain, line, sems.at[2 * PIECES + 1])
    row_copy.start()
    line_copy.start()
    to_give, to_send = quarters()[:2]
    give_copies = column_copies(to_give, w, held.at[0], sems, 0)
    keep_copies = column_copies(to_send, w, held.at[1], sems, PIECES)
    line_copy.wait()
    gain_row[...] = line[...].reshape(gain_row.shape)
    row_copy.wait()
    values = rows_of[...].astype(F32)
    left = with_gain(values, gain_row[...])
    own = row_sums(values)
    sums[...] = own
    rows, half = rows_of.shape[0], first.shape[1]

    def give_store(at, size, product, of_gain):
        ref, cols = (first, second)[at // half], pl.ds(at % half, size)
        ref[0:rows, cols] = product.astype(BF16)
        told = own if at == 0 else jnp.zeros((1, size), F32)
        ref[rows:, cols] = row_block([*thirds(told), *thirds(of_gain)], (16, size))

    def keep_store(at, size, product, of_gain):
        keep[:, pl.ds(at, size)] = product
        keep_gain[:, pl.ds(at, size)] = of_gain

    first_products(left, held.at[0], give_copies, give_store)
    first_products(left, held.at[1], keep_copies, keep_store)


def first_a(tokens, gain, w):
    rows, depth = tokens.shape
    share = w.shape[1] // 4
    return pl.pallas_call(
        first_a_kernel,
        name="first_a",
        out_shape=(
            struct((rows + 16, share // 2), BF16),
            struct((rows + 16, share // 2), BF16),
            struct((rows, share)),
            struct((1, share)),
            struct((1, 2 * rows)),
            pltpu.VMEM((2, depth, share), BF16),
            struct((1, depth)),
        ),
        in_specs=[IN_HBM] * 3,
        out_specs=(WHOLE,) * 7,
        scratch_shapes=[VMEM((rows, depth), BF16), VMEM((depth,), F32), pltpu.SemaphoreType.DMA((2 * PIECES + 2,))],
        compiler_params=params(8),
        cost_estimate=cost(4 * rows * depth * share, 4 * depth * share),
    )(*(pltpu.with_memory_space_constraint(value, pltpu.HBM) for value in (tokens, gain, w)))


def first_give_kernel(tokens, gain, w, give, held, resid, sems):
    copies = column_copies(quarters()[2], w, held, sems, 0)
    values = tokens[...].astype(F32)
    rows = values.shape[0]
    resid[...] = jnp.sum(values, axis=0, keepdims=True) / PATCHES

    def store(at, size, product, of_gain):
        give[0:rows, pl.ds(at, size)] = product.astype(BF16)
        give[rows:, pl.ds(at, size)] = row_block(thirds(of_gain), (16, size))

    first_products(with_gain(values, gain[...]), held, copies, store)


def first_keep_kernel(tokens, gain, w, keep, keep_gain, held, sems):
    copies = column_copies(quarters()[3], w, held, sems, 0)

    def store(at, size, product, of_gain):
        keep[:, pl.ds(at, size)] = product
        keep_gain[:, pl.ds(at, size)] = of_gain

    first_products(with_gain(tokens[...].astype(F32), gain[...]), held, copies, store)


def first_part(kernel, name, tokens, gain, w, shapes):
    rows, depth = tokens.shape
    share = w.shape[1] // 4
    return pl.pallas_call(
        kernel,
        name=name,
        out_shape=shapes,
        in_specs=[WHOLE, WHOLE, IN_HBM],
        out_specs=(WHOLE,) * len(shapes),
        scratch_shapes=[pltpu.SemaphoreType.DMA((PIECES,))],
        compiler_params=params(8),
        cost_estimate=cost(2 * rows * depth * share, 2 * depth * share),
    )(tokens, gain, pltpu.with_memory_space_constraint(w, pltpu.HBM))


def later_a_kernel(count, *refs):
    blocks, gain, held, (first, second, keep, ready, sums) = refs[:count], refs[count], refs[count + 1], refs[count + 2 :]
    values = blocks[0][...].astype(F32)
    for other in blocks[1:]:
        values = values + other[...].astype(F32)
    rows = values.shape[0]
    left = centred(values, gain[...])
    ready[...] = left
    later_products(left, (held.at[0], held.at[1]), (first, second), keep)
    own = row_sums(values)
    sums[...] = own
    first[rows:, :] = row_block(thirds(own), (16, first.shape[1]))


def later_b_kernel(left, give_held, keep_held, *refs):
    later_products(left[...], (give_held, keep_held), refs[:-1], refs[-1])


def later_products(left, held, gives, keep):
    rows = left.shape[0]
    step = keep.shape[1] // 2
    size = gives[0].shape[1]
    for part in range(2):
        for first in range(0, keep.shape[1], step):
            product = jnp.dot(left, held[part][:, pl.ds(first, step)], preferred_element_type=F32)
            if part == 0:
                gives[first // size][0:rows, pl.ds(first % size, step)] = product.astype(BF16)
            else:
                keep[:, pl.ds(first, step)] = product


def later_block(kernel, args, out, flops=1024):
    rows, share = out[-1].shape if len(out) < 4 else out[2].shape
    depth = args[0].shape[1]
    return pl.pallas_call(
        kernel,
        name="later_block",
        out_shape=out,
        in_specs=[WHOLE] * len(args),
        out_specs=(WHOLE,) * len(out),
        compiler_params=params(8),
        cost_estimate=pl.CostEstimate(flops=flops, bytes_accessed=1024, transcendentals=0),
    )(*args)


def chip_sum_kernel(kept, first, second, own, *refs):
    kept_gain, (out, note) = refs[:-2], refs[-2:]
    rows, share = kept.shape
    half = share // 2
    for index, got in enumerate((first, second)):
        cols = pl.ds(index * half, half)
        out[0:rows, cols] = (kept[:, cols] + got[0:rows, :].astype(F32)).astype(BF16)
    sums = jnp.concatenate([own[...], rejoined(first[rows : rows + 3, 0 : 2 * rows])], axis=1)
    note[...] = sums
    below = list(thirds(sums))
    if kept_gain:
        below.extend(thirds(kept_gain[0][...])[:2])
        got_gain = jnp.concatenate([rejoined(got[rows + 3 : rows + 6, :]) for got in (first, second)], axis=1)
        below.extend(thirds(got_gain)[:2])
    out[rows:, :] = row_block(below, (NOTE_ROWS, share))


def all_gains_kernel(rows, kept, near, far, gains):
    gains[...] = jnp.zeros(gains.shape, F32)
    gains[0:1, :] = kept[...]
    gains[1:2, :] = rejoined(near[rows : rows + 3, :])
    for index in range(2):
        terms = far[rows + 3 + 2 * index : rows + 5 + 2 * index, :].astype(F32)
        gains[2 + index : 3 + index, :] = terms[0:1] + terms[1:2]


def small(kernel, name, out, *args):
    return pl.pallas_call(
        kernel,
        name=name,
        out_shape=out,
        in_specs=[WHOLE] * len(args),
        out_specs=jax.tree.map(lambda _: WHOLE, out),
        compiler_params=params(4),
        cost_estimate=cost(0, 0),
    )(*args)


def pool_pieces(width, kept, nears, far, bias, gains, note, out):
    rows, share = kept.shape
    depth = width // 4
    all_sums = jnp.concatenate([note[...], rejoined(far[rows : rows + 3, 0 : 4 * rows])], axis=1)
    lines = [all_sums[:, index * rows : (index + 1) * rows] for index in range(8)]
    columns = jnp.concatenate([*lines, jnp.zeros((120, rows), F32)], axis=0).T
    totals = [columns[:, 2 * k : 2 * k + 1] for k in range(4)]
    squares = [columns[:, 2 * k + 1 : 2 * k + 2] for k in range(4)]
    average = (totals[0] + totals[1] + totals[2] + totals[3]) / width
    variance = (squares[0] + squares[1] + squares[2] + squares[3]) / width - average * average
    scale = lax.rsqrt(variance + 1e-06)
    shifts = [(total / depth - average) * scale for total in totals]
    start = pl.multiple_of(quarters()[3] * share, 128)
    step = 256
    for first in range(0, share, step):
        cols = pl.ds(first, step)
        v = kept[:, cols] + far[0:rows, cols].astype(F32)
        size = share // len(nears)
        v = v + nears[first // size][0:rows, pl.ds(first % size, step)].astype(F32)
        v = v * scale + bias[:, pl.ds(pl.multiple_of(start + first, 128), step)]
        for k in range(4):
            v = v + shifts[k] * gains[k : k + 1, cols]
        inner = 0.7978845608028654 * (v + 0.044715 * (v * v * v))
        hidden = (0.5 * v * (1.0 + jnp.tanh(inner))).astype(BF16).astype(F32)
        out[:, cols] = jnp.sum(hidden, axis=0, keepdims=True)


def pool_kernel(width, count, kept, *refs):
    pool_pieces(width, kept, refs[:count], *refs[count:])


def pool(width, kept, nears, far, bias, gains, note):
    share = kept.shape[1]
    args = (kept, *nears, far, bias, gains, note)
    return pl.pallas_call(
        lambda *refs: pool_kernel(width, len(nears), *refs),
        name="pool",
        out_shape=struct((1, share)),
        in_specs=[WHOLE] * len(args),
        out_specs=WHOLE,
        compiler_params=params(6),
        cost_estimate=cost(20 * kept.size, 8 * kept.size),
    )(*args)


def pool_all_kernel(width, count, kept, *refs):
    nears, (far, bias, gains, note, first, second, third, out, part) = refs[:count], refs[count:]
    pool_pieces(width, kept, nears, far, bias, gains, note, part)
    z = lax.axis_index("mrow")
    sources = (z, z ^ 1, jnp.where(z < 2, 2, 1), jnp.where(z < 2, 3, 0))
    image = lax.broadcasted_iota(jnp.int32, out.shape, 0)
    total = jnp.zeros(out.shape, F32)
    for source, ref in zip(sources, (first, second, third, part)):
        total = total + jnp.where(image == source * kept.shape[0] // PATCHES, ref[...], 0.0)
    out[...] = total


def pool_all(width, kept, nears, far, bias, gains, note, parts):
    share = kept.shape[1]
    args = (kept, *nears, far, bias, gains, note, *parts)
    return pl.pallas_call(
        lambda *refs: pool_all_kernel(width, len(nears), *refs),
        name="pool_all",
        out_shape=struct((IMAGES, share)),
        in_specs=[WHOLE] * len(args),
        out_specs=WHOLE,
        scratch_shapes=[VMEM((1, share), F32)],
        compiler_params=params(6),
        cost_estimate=cost(20 * kept.size, 8 * kept.size),
    )(*args)


def mix_kernel(rows, own, core, across, both, resid, w, out):
    share = own.shape[1]
    mine_x, mine_c = lax.axis_index("mcol"), lax.axis_index("sub")
    total = jnp.zeros((16, w.shape[1]), F32)
    order = ((own, 0, 0), (core, 0, 1), (across, 1, 0), (both, 1, 1))
    for ref, dx, dc in order:
        x, c = (1 - mine_x if dx else mine_x), (1 - mine_c if dc else mine_c)
        start = pl.multiple_of((c * 2 + x) * share, 128)
        value = ref[...] / PATCHES
        high, middle, low = thirds(value)
        terms = jnp.concatenate([high, middle, low, jnp.zeros((10, share), BF16)], axis=0)
        total = total + jnp.dot(terms, w[pl.ds(start, share), :], preferred_element_type=F32)
    mixed = total[0:2] + (total[2:4] + total[4:6])
    image = lax.axis_index("mrow") * rows // PATCHES
    row = lax.broadcasted_iota(jnp.int32, mixed.shape, 0)
    out[...] = mixed + jnp.where(row == image, resid[...], 0.0)


def mix(rows, own, core, across, both, resid, w):
    return pl.pallas_call(
        lambda *refs: mix_kernel(rows, *refs),
        name="mix",
        out_shape=struct((IMAGES, w.shape[1])),
        in_specs=[WHOLE] * 6,
        out_specs=WHOLE,
        compiler_params=params(8),
        cost_estimate=cost(32 * w.size, 16 * w.shape[0]),
    )(own, core, across, both, resid, w)


def score_kernel(own, core, across, both, bias, captions, text_scale, pairs, out):
    depth = own.shape[1]
    width = captions.shape[1]
    mine_x, mine_c = lax.axis_index("mcol"), lax.axis_index("sub")
    pieces = []
    total = jnp.zeros((IMAGES, 1), F32)
    for ref, dx, dc in ((own, 0, 0), (core, 0, 1), (across, 1, 0), (both, 1, 1)):
        x, c = (1 - mine_x if dx else mine_x), (1 - mine_c if dc else mine_c)
        start = pl.multiple_of((x * 2 + c) * depth, 128)
        pooled = ref[...] + bias[:, pl.ds(start, depth)]
        total = total + jnp.sum(pooled * pooled, axis=1, keepdims=True)
        pieces.append((start, pooled))
    scale = lax.rsqrt(total / width + 1e-06)
    similar = jnp.zeros((IMAGES, captions.shape[0]), F32)
    for start, pooled in pieces:
        embedding = (pooled * scale).astype(BF16)
        similar = similar + lax.dot_general(
            embedding, captions[:, pl.ds(start, depth)], (((1,), (1,)), ((), ())), preferred_element_type=F32
        )
    chosen = lax.broadcasted_iota(jnp.int32, similar.shape, 0) == pairs[...]
    picked = jnp.sum(jnp.where(chosen, similar, 0.0), axis=0, keepdims=True)
    out[...] = 100.0 * picked * text_scale[...] / width


def score(own, core, across, both, bias, captions, text_scale, pairs):
    count = captions.shape[0]
    return pl.pallas_call(
        score_kernel,
        name="score",
        out_shape=struct((1, count)),
        in_specs=[WHOLE] * 8,
        out_specs=WHOLE,
        compiler_params=params(8),
        cost_estimate=cost(4 * captions.size, 2 * captions.size),
    )(own, core, across, both, bias, captions, text_scale, pairs)


def other_core(name, value):
    with jax.named_scope(name):
        return lax.ppermute(value, "sub", [(0, 1), (1, 0)])


def other_chip(name, value):
    with jax.named_scope(name):
        return lax.ppermute(value, "mcol", [(0, 1), (1, 0)])


def other_both(name, value):
    with jax.named_scope(name):
        return lax.ppermute(value, ("mcol", "sub"), [(0, 3), (1, 2), (2, 1), (3, 0)])


def along(name, value, pairs):
    with jax.named_scope(name):
        return lax.ppermute(value, "mrow", list(pairs))


SWAP = ((0, 1), (1, 0), (2, 3), (3, 2))
MIDDLE = ((1, 2), (2, 1))
OUTWARD = ((1, 0), (2, 3))
INWARD = ((0, 2), (3, 1))
OUTER = ((0, 3), (3, 0))
SKIP = ((0, 2), (2, 0), (1, 3), (3, 1))
ENDS = ((0, 3), (3, 0), (1, 2), (2, 1))


def after(values, *others):
    return lax.optimization_barrier((values, others))[0]


def staged(tokens, ln_gain, w_in, b_in, w_out, b_out, captions, pairs):
    width = b_out.shape[0]
    rows, depth = tokens.shape
    share = w_in.shape[1] // 4
    bias = b_in.reshape(1, -1)

    near = along("near_rows", tokens, SWAP)
    middle = along("middle_rows", tokens, MIDDLE)

    def chip_sum(index, keep, gots, *others):
        chip, note = small(
            chip_sum_kernel,
            "chip_sum",
            (struct((rows + NOTE_ROWS, share), BF16), struct((1, 4 * rows))),
            keep,
            *gots,
            *others,
        )
        return chip, note, other_chip(f"chip_sum_{index}", chip)

    *gives_a, keep_a, keep_gain, sums, held_a, gain = first_a(tokens, ln_gain, w_in)
    gots_a = [other_core("core_sum_0a", give_a) for give_a in gives_a]
    chip_0, note_0, far_0 = chip_sum(0, keep_a, gots_a, sums, keep_gain)
    inward = along("inward_rows", after(tokens, chip_0), INWARD)
    give_0, give_held, resid = first_part(
        first_give_kernel,
        "first_give",
        after(tokens, chip_0),
        gain,
        w_in,
        (struct((rows + 16, share), BF16), pltpu.VMEM((depth, share), BF16), struct((1, depth))),
    )
    near, middle = after((near, middle), give_0)
    passed = along("passed_rows", middle, OUTWARD)

    def later_a(index, rows_of, ready_after, sums_after=()):
        halves = (struct((rows + 16, share // 2), BF16), struct((rows, share // 2), BF16))
        *gives, keep, ready, own = later_block(
            lambda *refs: later_a_kernel(len(rows_of), *refs),
            (*rows_of, after(gain, ready_after), held_a),
            (*halves, struct((rows, share)), struct((rows, depth), BF16), struct((1, 2 * rows))),
        )
        gots = after([other_core(f"core_sum_{index}a", give) for give in gives], sums_after)
        return ready, *chip_sum(index, keep, gots, own)

    def later_b(index, ready, *others):
        ready = lax.optimization_barrier((ready, others))[0]
        pieces = 2 if index == 3 else 1
        return later_block(
            later_b_kernel,
            (ready, give_held, keep_held),
            (struct((rows, share // pieces), BF16),) * pieces + (struct((rows, share)),),
            4 * rows * depth * share,
        )

    def send(index, gives):
        return [other_core(f"core_sum_{index}b", give) for give in gives]

    ready_1, chip_1, note_1, far_1 = later_a(1, (near,), (near, middle))
    keep_0, keep_gain, keep_held = first_part(
        first_keep_kernel,
        "first_keep",
        after(tokens, chip_1),
        gain,
        w_in,
        (struct((rows, share)), struct((1, share)), pltpu.VMEM((depth, share), BF16)),
    )
    far_0, inward, passed = after((far_0, inward, passed), keep_0)
    give_1, keep_1 = later_b(1, ready_1, far_0, inward, passed)

    outer = along("outer_rows", after(tokens, chip_1), OUTER)
    ready_2, chip_2, note_2, far_2 = later_a(2, (middle, passed), give_1, far_1)
    outer = after(outer, chip_2)
    give_2, keep_2 = later_b(2, ready_2, chip_2, outer)

    ready_3, chip_3, note_3, far_3 = later_a(3, (inward, outer), give_2, far_2)
    *gives_3, keep_3 = later_b(3, ready_3, chip_3)
    nears_0, nears_1, nears_2, nears_3 = send(0, [give_0]), send(1, [give_1]), send(2, [give_2]), send(3, gives_3)
    gains = small(
        lambda *refs: all_gains_kernel(rows, *refs),
        "all_gains",
        struct((8, share)),
        after(keep_gain, keep_3),
        *nears_0,
        far_0,
    )
    parts = [
        pool(width, keep_0, nears_0, far_0, bias, gains, note_0),
        pool(width, keep_1, nears_1, far_1, bias, gains, note_1),
        pool(width, keep_2, nears_2, far_2, bias, gains, note_2),
    ]
    pooled = pool_all(width, keep_3, nears_3, far_3, bias, gains, note_3, parts)

    mixed = mix(
        rows,
        pooled,
        other_core("core_pool", pooled),
        other_chip("chip_pool", pooled),
        other_both("both_pool", pooled),
        resid,
        w_out,
    )
    own = mixed + along("swap_mixed", mixed, SWAP) + along("skip_mixed", mixed, SKIP) + along("ends_mixed", mixed, ENDS)
    text_vals = captions.astype(F32)
    text_scale = lax.rsqrt(jnp.mean(text_vals * text_vals, axis=1) + 1e-06)
    scores = score(
        own,
        other_core("core_embed", own),
        other_chip("chip_embed", own),
        other_both("both_embed", own),
        b_out.reshape(1, -1),
        captions,
        text_scale.reshape(1, -1),
        pairs.reshape(1, -1),
    )
    return scores.reshape(-1)


def solution(mesh):
    sizes = dict(mesh.shape)

    def shards(tokens, ln_gain, w_in, *rest):
        rows, depth = tokens.shape
        fits = (
            (sizes["mrow"], sizes["mcol"], sizes["sub"]) == (4, 2, 2)
            and rows == 128
            and PATCHES % rows == 0
            and depth % 256 == 0
            and w_in.shape[1] % 1024 == 0
        )
        return (staged if fits else plain)(tokens, ln_gain, w_in, *rest)

    placed = (
        P(("group", "mrow"), ("mcol", "sub")),
        P(("mcol", "sub")),
        P(("mcol", "sub"), "mrow"),
        P("mrow"),
        P("mrow", ("mcol", "sub")),
        P(),
        P(("group", "mrow", "mcol", "sub"), None),
        P(("group", "mrow", "mcol", "sub")),
    )
    return jax.shard_map(
        shards,
        mesh=mesh,
        in_specs=placed,
        out_specs=P(("group", "mrow", "mcol", "sub")),
        check_vma=False,
    )
```

time: 129 us -> 83.9 us (0.65)
  local copies, waits for them, and re-layouts: 21.4 us -> 0.05 us
  waiting for transfers between devices: 43.1 us -> 22.3 us
  Pallas kernels: 30.7 us -> 28 us
  other arithmetic: 2.32 us -> 0.27 us
  starting transfers between devices: 30.8 us -> 32.7 us
    unnamed x30 -> x20, local copies, waits for them, and re-layouts: 20.7 us -> 0.05 us
    ppermute x10 -> x8, waiting for transfers between devices: 22.7 us -> 6.56 us  [along(): return lax.ppermute(value, 'mrow', list(pairs))]
    ppermute x7 -> x6, waiting for transfers between devices: 16.6 us -> 9.17 us  [other_chip(): return lax.ppermute(value, 'mcol', [(0, 1), (1, 0)])]
    ppermute x11 -> x15, waiting for transfers between devices: 1.18 us -> 5.6 us  [other_core(): return lax.ppermute(value, 'sub', [(0, 1), (1, 0)])]
    pallas_call x17 -> x18, Pallas kernels: 27.2 us -> 24.5 us  [the longest x6 9.02 us: later_block(): pl.pallas_call(kernel, name='later_block', out_shape=out, in_specs=[WHOLE...]
    ppermute x7 -> x6, starting transfers between devices: 9.47 us -> 7.55 us  [other_chip(): return lax.ppermute(value, 'mcol', [(0, 1), (1, 0)])]
    ppermute x2, waiting for transfers between devices: 2.6 us -> 1.02 us  [other_both(): lax.ppermute(value, ('mcol', 'sub'), [(0, 3), (1, 2), (2, 1), (3, 0)])]
    ppermute x10 -> x8, starting transfers between devices: 18.7 us -> 20.1 us  [along(): return lax.ppermute(value, 'mrow', list(pairs))]
  transfers between devices with their start and end apart: 30 -> 31, of which waited for: 16 -> 14; matrix products, arithmetic and copies ran while one was open for 2% -> 0% of each run, Pallas kernels for 20% -> 28%
where the time goes in v2:
time: 83.9 us; the launch traced here: 83.7 us
  starting transfers between devices  32.7 us (39%)
  Pallas kernels  28 us (33%)
  waiting for transfers between devices  22.3 us (27%)
    ppermute x8, starting transfers between devices, along(): return lax.ppermute(value, 'mrow', list(pairs))  20.1 us
    ppermute x6, waiting for transfers between devices, other_chip(): return lax.ppermute(value, 'mcol', [(0, 1), (1, 0)])  9.17 us
    pallas_call x6, Pallas kernels, later_block(): pl.pallas_call(kernel, name='later_block', out_shape=out, in_specs=[WHOLE...  9.02 us
    ppermute x6, starting transfers between devices, other_chip(): return lax.ppermute(value, 'mcol', [(0, 1), (1, 0)])  7.55 us
    ppermute x8, waiting for transfers between devices, along(): return lax.ppermute(value, 'mrow', list(pairs))  6.56 us
    pallas_call x2, Pallas kernels, first_part(): pl.pallas_call(kernel, name=name, out_shape=shapes, in_specs=[WHOLE, WHOL...  6.01 us
    ppermute x15, waiting for transfers between devices, other_core(): return lax.ppermute(value, 'sub', [(0, 1), (1, 0)])  5.6 us
    pallas_call x1, Pallas kernels, first_a(): pl.pallas_call(first_a_kernel, name='first_a', out_shape=(struct((rows +...  4.77 us
  transfers between devices with their start and end apart: 31, of which 14 were waited for; matrix products, arithmetic and copies ran while one was open for 0% of the time, Pallas kernels for 28%

profile of v2, /device:TPU:0, one launch (start us, length us, event | category | flops | bytes accessed | tf_op | source)
XLA Modules:
  0.0 83.7 jit_solution(9264753042189525344)
XLA Ops:
  0.0 3.0 %collective-permute-start.4 = (bf16[128,1536]{1,0:T(8,128)(2,1)}, bf16[128,1536]{1,0:T(8,128)(2,1)S(1)}, u32[]{:S(2)}, u32[]{:S(2)}) collective-permute-start(bf16[128,1536]{1,0:T(8,128)(2,1)} %tokens.3), channel_id=1, source_target_pairs={{0,4},{4,0},{8,12},{12,8},{1,5},{5,1},{9,13},{13,9},{2,6},{6,2},{1... | collective-permute-start | bytes 1179656 | tf_op jit(solution)/shard_map/near_rows/ppermute | solution.py:470
  3.0 0.7 collective-permute-start.5
  3.7 4.8 %first_a.1 = (bf16[144,768]{1,0:T(8,128)(2,1)S(1)}, bf16[144,768]{1,0:T(8,128)(2,1)S(1)}, f32[128,1536]{1,0:T(8,128)S(1)}, f32[1,1536]{1,0:T(1,128)S(1)}, f32[1,...) custom-call(bf16[128,1536]{1,0:T(8,128)(2,1)} %tokens.3, f32[1536]{0:T(1024)} %gain.1, ...), custom_call_target="tpu_custom_call" | custom-call | flops 1024 | bytes 1024 | tf_op jit(solution)/shard_map/first_a/pallas_call | solution.py:173
  8.5 0.1 collective-permute-start
  8.6 0.5 collective-permute-start.1
  9.1 1.0 %collective-permute-done.first = bf16[144,768]{1,0:T(8,128)(2,1)S(1)} collective-permute-done((bf16[144,768]{1,0:T(8,128)(2,1)S(1)}, bf16[144,768]{1,0:T(8,128)(2,1)S(1)}, u32[]{:S(2)}, u32[]{:S(2)}) %collective-permute-start) | collective-permute-done | bytes 221216 | tf_op jit(solution)/shard_map/core_sum_0a/ppermute | solution.py:455
  10.0 0.3 collective-permute-done.1.second
  10.3 0.1 chip_sum.4
  10.5 1.6 %collective-permute-start.2 = (bf16[136,1536]{1,0:T(8,128)(2,1)S(1)}, bf16[136,1536]{1,0:T(8,128)(2,1)S(1)}, u32[]{:S(2)}, u32[]{:S(2)}) collective-permute-start(bf16[136,1536]{1,0:T(8,128)(2,1)S(1)} %get-tuple-element.74), channel_id=1, source_target_pairs={{0,2},{2,0},{1,3},{3,1},{4,6},{6,4},{5,7},{7,5},{8,10},{10,8},{9,1... | collective-permute-start | bytes 1253384 | tf_op jit(solution)/shard_map/chip_sum_0/ppermute | solution.py:460
  12.0 5.7 %collective-permute-start.3 = (bf16[128,1536]{1,0:T(8,128)(2,1)S(1)}, bf16[128,1536]{1,0:T(8,128)(2,1)S(1)}, u32[]{:S(2)}, u32[]{:S(2)}) collective-permute-start(bf16[128,1536]{1,0:T(8,128)(2,1)S(1)} %copy-done), channel_id=1, source_target_pairs={{0,8},{12,4},{1,9},{13,5},{2,10},{14,6},{3,11},{15,7},{16,24},{28,... | collective-permute-start | bytes 1179656 | tf_op jit(solution)/shard_map/inward_rows/ppermute | solution.py:470
  17.8 3.1 %first_give.1 = (bf16[144,1536]{1,0:T(8,128)(2,1)S(1)}, bf16[1536,1536]{1,0:T(8,128)(2,1)S(1)}, f32[1,1536]{1,0:T(1,128)S(1)}) custom-call(bf16[128,1536]{1,0:T(8,128)(2,1)S(1)} %copy-done, f32[1,1536]{1,0:T(1,128)S(1)} %get-tuple-element.111.gain.refs_1_.refs_2_, bf16[1536,6144]{1,0:T(8,128)(2,1)} %w.5), custom_call_target="tpu_custom_call" | custom-call | flops 1024 | bytes 1024 | tf_op jit(solution)/shard_map/first_give/pallas_call | solution.py:219
  20.9 1.3 %collective-permute-start.6 = (bf16[128,1536]{1,0:T(8,128)(2,1)S(1)}, bf16[128,1536]{1,0:T(8,128)(2,1)S(1)}, u32[]{:S(2)}, u32[]{:S(2)}) collective-permute-start(bf16[128,1536]{1,0:T(8,128)(2,1)S(1)} %collective-permute-done.5.refs_0_), channel_id=1, source_target_pairs={{4,0},{8,12},{5,1},{9,13},{6,2},{10,14},{7,3},{11,15},{20,16},{24,... | collective-permute-start | bytes 1179656 | tf_op jit(solution)/shard_map/passed_rows/ppermute | solution.py:470
  22.2 1.6 %later_block.6 = (bf16[144,768]{1,0:T(8,128)(2,1)S(1)}, bf16[128,768]{1,0:T(8,128)(2,1)S(1)}, f32[128,1536]{1,0:T(8,128)S(1)}, bf16[128,1536]{1,0:T(8,128)(2,1)S(1)}, f32[1,256]{1,0:T(1,128)S(1)}) custom-call(bf16[128,1536]{1,0:T(8,128)(2,1)S(1)} %collective-permute-done.4.refs_0_, f32[1,1536]{1,0:T(1,128)S(1)} %get-tuple-element.111.gain.refs_1_.refs_2_, ...), custom_call_target="tpu_custom_call" | custom-call | flops 1024 | bytes 1024 | tf_op jit(solution)/shard_map/later_block/pallas_call | solution.py:265
  23.8 0.1 collective-permute-start.7
  23.9 0.5 collective-permute-start.8
  24.4 1.2 %collective-permute-done.8.second = bf16[128,768]{1,0:T(8,128)(2,1)S(1)} collective-permute-done((bf16[128,768]{1,0:T(8,128)(2,1)S(1)}, bf16[128,768]{1,0:T(8,128)(2,1)S(1)}, u32[]{:S(2)}, u32[]{:S(2)}) %collective-permute-start.8) | collective-permute-done | bytes 196640 | tf_op jit(solution)/shard_map/core_sum_1a/ppermute | solution.py:455
  25.6 0.1 chip_sum.5
  25.7 0.6 collective-permute-start.12
  26.3 2.9 %first_keep.1 = (f32[128,1536]{1,0:T(8,128)S(1)}, f32[1,1536]{1,0:T(1,128)S(1)}, bf16[1536,1536]{1,0:T(8,128)(2,1)S(1)}) custom-call(bf16[128,1536]{1,0:T(8,128)(2,1)S(1)} %copy-done, f32[1,1536]{1,0:T(1,128)S(1)} %get-tuple-element.111.gain.refs_1_.refs_2_, bf16[1536,6144]{1,0:T(8,128)(2,1)} %w.5), custom_call_target="tpu_custom_call" | custom-call | flops 1024 | bytes 1024 | tf_op jit(solution)/shard_map/first_keep/pallas_call | solution.py:219
  29.3 5.0 %collective-permute-start.9 = (bf16[128,1536]{1,0:T(8,128)(2,1)S(1)}, bf16[128,1536]{1,0:T(8,128)(2,1)S(1)}, u32[]{:S(2)}, u32[]{:S(2)}) collective-permute-start(bf16[128,1536]{1,0:T(8,128)(2,1)S(1)} %copy-done), channel_id=1, source_target_pairs={{0,12},{12,0},{1,13},{13,1},{2,14},{14,2},{3,15},{15,3},{16,28},{2... | collective-permute-start | bytes 1179656 | tf_op jit(solution)/shard_map/outer_rows/ppermute | solution.py:470
  34.3 1.4 %later_block.7 = (bf16[128,1536]{1,0:T(8,128)(2,1)S(1)}, f32[128,1536]{1,0:T(8,128)S(1)}) custom-call(bf16[128,1536]{1,0:T(8,128)(2,1)S(1)} %get-tuple-element.95.left, bf16[1536,1536]{1,0:T(8,128)(2,1)S(1)} %get-tuple-element.96.give_held, bf16[1536,1536]{1,0:T(8,128)(2,1)S(1)} %get-tuple-element.97.keep_held), custom_call_target="tpu_custom_call" | custom-call | flops 1207959552 | bytes 1024 | tf_op jit(solution)/shard_map/later_block/pallas_call | solution.py:265
  35.7 1.6 %later_block.8 = (bf16[144,768]{1,0:T(8,128)(2,1)S(1)}, bf16[128,768]{1,0:T(8,128)(2,1)S(1)}, f32[128,1536]{1,0:T(8,128)S(1)}, bf16[128,1536]{1,0:T(8,128)(2,1)S(1)}, f32[1,256]{1,0:T(1,128)S(1)}) custom-call(bf16[128,1536]{1,0:T(8,128)(2,1)S(1)} %collective-permute-done.5.refs_0_, bf16[128,1536]{1,0:T(8,128)(2,1)S(1)} %collective-permute-done.6.refs_1_, ...), custom_call_target="tpu_custom_call" | custom-call | flops 1024 | bytes 1024 | tf_op jit(solution)/shard_map/later_block/pallas_call | solution.py:265
  37.3 0.1 collective-permute-start.10
  37.4 0.5 collective-permute-start.11
  37.9 1.2 %collective-permute-done.11.second = bf16[128,768]{1,0:T(8,128)(2,1)S(1)} collective-permute-done((bf16[128,768]{1,0:T(8,128)(2,1)S(1)}, bf16[128,768]{1,0:T(8,128)(2,1)S(1)}, u32[]{:S(2)}, u32[]{:S(2)}) %collective-permute-start.11) | collective-permute-done | bytes 196640 | tf_op jit(solution)/shard_map/core_sum_2a/ppermute | solution.py:455
  39.2 0.1 chip_sum.6
  39.3 1.6 %collective-permute-start.15 = (bf16[136,1536]{1,0:T(8,128)(2,1)S(1)}, bf16[136,1536]{1,0:T(8,128)(2,1)S(1)}, u32[]{:S(2)}, u32[]{:S(2)}) collective-permute-start(bf16[136,1536]{1,0:T(8,128)(2,1)S(1)} %get-tuple-element.106), channel_id=1, source_target_pairs={{0,2},{2,0},{1,3},{3,1},{4,6},{6,4},{5,7},{7,5},{8,10},{10,8},{9,1... | collective-permute-start | bytes 1253384 | tf_op jit(solution)/shard_map/chip_sum_2/ppermute | solution.py:460
  40.8 3.1 %collective-permute-done.9.refs_1_ = bf16[128,1536]{1,0:T(8,128)(2,1)S(1)} collective-permute-done((bf16[128,1536]{1,0:T(8,128)(2,1)S(1)}, bf16[128,1536]{1,0:T(8,128)(2,1)S(1)}, u32[]{:S(2)}, u32[]{:S(2)}) %collective-permute-start.9) | collective-permute-done | bytes 393248 | tf_op jit(solution)/shard_map/outer_rows/ppermute | solution.py:470
  43.9 1.4 %later_block.9 = (bf16[128,1536]{1,0:T(8,128)(2,1)S(1)}, f32[128,1536]{1,0:T(8,128)S(1)}) custom-call(bf16[128,1536]{1,0:T(8,128)(2,1)S(1)} %get-tuple-element.109.left, bf16[1536,1536]{1,0:T(8,128)(2,1)S(1)} %get-tuple-element.96.give_held, bf16[1536,1536]{1,0:T(8,128)(2,1)S(1)} %get-tuple-element.97.keep_held), custom_call_target="tpu_custom_call" | custom-call | flops 1207959552 | bytes 1024 | tf_op jit(solution)/shard_map/later_block/pallas_call | solution.py:265
  45.3 1.6 %later_block.10 = (bf16[144,768]{1,0:T(8,128)(2,1)S(1)}, bf16[128,768]{1,0:T(8,128)(2,1)S(1)}, f32[128,1536]{1,0:T(8,128)S(1)}, bf16[128,1536]{1,0:T(8,128)(2,1)S(1)}, f32[1,256]{1,0:T(1,128)S(1)}) custom-call(bf16[128,1536]{1,0:T(8,128)(2,1)S(1)} %collective-permute-done.3.refs_0_, bf16[128,1536]{1,0:T(8,128)(2,1)S(1)} %collective-permute-done.9.refs_1_, ...), custom_call_target="tpu_custom_call" | custom-call | flops 1024 | bytes 1024 | tf_op jit(solution)/shard_map/later_block/pallas_call | solution.py:265
  46.9 0.1 collective-permute-start.13
  47.0 0.5 collective-permute-start.19
  47.5 0.1 collective-permute-start.14
  47.6 1.8 %collective-permute-done.14.second = bf16[128,768]{1,0:T(8,128)(2,1)S(1)} collective-permute-done((bf16[128,768]{1,0:T(8,128)(2,1)S(1)}, bf16[128,768]{1,0:T(8,128)(2,1)S(1)}, u32[]{:S(2)}, u32[]{:S(2)}) %collective-permute-start.14) | collective-permute-done | bytes 196640 | tf_op jit(solution)/shard_map/core_sum_3a/ppermute | solution.py:455
  49.4 1.7 %collective-permute-done.15.refs_2_ = bf16[136,1536]{1,0:T(8,128)(2,1)S(1)} collective-permute-done((bf16[136,1536]{1,0:T(8,128)(2,1)S(1)}, bf16[136,1536]{1,0:T(8,128)(2,1)S(1)}, u32[]{:S(2)}, u32[]{:S(2)}) %collective-permute-start.15) | collective-permute-done | bytes 417824 | tf_op jit(solution)/shard_map/chip_sum_2/ppermute | solution.py:460
  51.1 0.1 chip_sum.7
  51.2 1.6 %collective-permute-start.18 = (bf16[136,1536]{1,0:T(8,128)(2,1)S(1)}, bf16[136,1536]{1,0:T(8,128)(2,1)S(1)}, u32[]{:S(2)}, u32[]{:S(2)}) collective-permute-start(bf16[136,1536]{1,0:T(8,128)(2,1)S(1)} %get-tuple-element.119), channel_id=1, source_target_pairs={{0,2},{2,0},{1,3},{3,1},{4,6},{6,4},{5,7},{7,5},{8,10},{10,8},{9,1... | collective-permute-start | bytes 1253384 | tf_op jit(solution)/shard_map/chip_sum_3/ppermute | solution.py:460
  52.7 0.5 collective-permute-start.20
  53.2 1.4 %later_block.11 = (bf16[128,768]{1,0:T(8,128)(2,1)S(1)}, bf16[128,768]{1,0:T(8,128)(2,1)S(1)}, f32[128,1536]{1,0:T(8,128)S(1)}) custom-call(bf16[128,1536]{1,0:T(8,128)(2,1)S(1)} %get-tuple-element.120.left, bf16[1536,1536]{1,0:T(8,128)(2,1)S(1)} %get-tuple-element.96.give_held, bf16[1536,1536]{1,0:T(8,128)(2,1)S(1)} %get-tuple-element.97.keep_held), custom_call_target="tpu_custom_call" | custom-call | flops 1207959552 | bytes 1024 | tf_op jit(solution)/shard_map/later_block/pallas_call | solution.py:265
  54.6 0.1 collective-permute-start.16
  54.7 0.5 collective-permute-start.17
  55.3 1.1 %pool.3.refs_7_ = f32[1,1536]{1,0:T(1,128)S(1)} custom-call(f32[128,1536]{1,0:T(8,128)S(1)} %get-tuple-element.90.refs_0_, bf16[144,1536]{1,0:T(8,128)(2,1)S(1)} %collective-permute-done.19.refs_1_, bf16[136,1536]{1,0:T(8,128)(2,1)S(1)} %collective-permute-done.2.refs_2_, f32[1,6144]{1,0:T(1,128)S(1)} %bitcast.8, f32[8,1536]{1,0:T(8,128)S(1)} %all_gains.1.refs_4_.refs_5_, ...), custom_call_target="tpu_custom_call" | custom-call | flops 1024 | bytes 1024 | tf_op jit(solution)/shard_map/pool/pallas_call | solution.py:348
  56.3 1.0 %pool.5.refs_9_ = f32[1,1536]{1,0:T(1,128)S(1)} custom-call(f32[128,1536]{1,0:T(8,128)S(1)} %get-tuple-element.130.refs_0_, bf16[128,1536]{1,0:T(8,128)(2,1)S(1)} %collective-permute-done.21.refs_1_, bf16[136,1536]{1,0:T(8,128)(2,1)S(1)} %collective-permute-done.15.refs_2_, f32[1,6144]{1,0:T(1,128)S(1)} %bitcast.9, f32[8,1536]{1,0:T(8,128)S(1)} %all_gains.1.refs_4_.refs_5_, ...), custom_call_target="tpu_custom_call" | custom-call | flops 1024 | bytes 1024 | tf_op jit(solution)/shard_map/pool/pallas_call | solution.py:348
  57.4 1.0 %pool.4.refs_8_ = f32[1,1536]{1,0:T(1,128)S(1)} custom-call(f32[128,1536]{1,0:T(8,128)S(1)} %get-tuple-element.128.refs_0_, bf16[128,1536]{1,0:T(8,128)(2,1)S(1)} %collective-permute-done.20.refs_1_, bf16[136,1536]{1,0:T(8,128)(2,1)S(1)} %collective-permute-done.12.refs_2_, f32[1,6144]{1,0:T(1,128)S(1)} %bitcast.10, f32[8,1536]{1,0:T(8,128)S(1)} %all_gains.1.refs_4_.refs_5_, ...), custom_call_target="tpu_custom_call" | custom-call | flops 1024 | bytes 1024 | tf_op jit(solution)/shard_map/pool/pallas_call | solution.py:348
  58.5 3.7 %collective-permute-done.18.refs_3_ = bf16[136,1536]{1,0:T(8,128)(2,1)S(1)} collective-permute-done((bf16[136,1536]{1,0:T(8,128)(2,1)S(1)}, bf16[136,1536]{1,0:T(8,128)(2,1)S(1)}, u32[]{:S(2)}, u32[]{:S(2)}) %collective-permute-start.18) | collective-permute-done | bytes 417824 | tf_op jit(solution)/shard_map/chip_sum_3/ppermute | solution.py:460
  62.1 1.1 %pool_all.1.refs_0_ = f32[2,1536]{1,0:T(2,128)S(1)} custom-call(f32[128,1536]{1,0:T(8,128)S(1)} %get-tuple-element.121.refs_0_, bf16[128,768]{1,0:T(8,128)(2,1)S(1)} %collective-permute-done.16.refs_1_, bf16[128,768]{1,0:T(8,128)(2,1)S(1)} %collective-permute-done.17.refs_2_, bf16[136,1536]{1,0:T(8,128)(2,1)S(1)} %collective-permute-done.18.refs_3_, ...), custom_call_target="tpu_custom_call" | custom-call | flops 1024 | bytes 1024 | tf_op jit(solution)/shard_map/pool_all/pallas_call | solution.py:374
  63.2 0.1 collective-permute-start.22
  63.3 1.6 %collective-permute-start.23 = (f32[2,1536]{1,0:T(2,128)S(1)}, f32[2,1536]{1,0:T(2,128)S(1)}, u32[]{:S(2)}, u32[]{:S(2)}) collective-permute-start(f32[2,1536]{1,0:T(2,128)S(1)} %pool_all.1.refs_0_), channel_id=1, source_target_pairs={{0,2},{2,0},{1,3},{3,1},{4,6},{6,4},{5,7},{7,5},{8,10},{10,8},{9,1... | collective-permute-start | bytes 36872 | tf_op jit(solution)/shard_map/chip_pool/ppermute | solution.py:460
  64.8 0.3 collective-permute-start.24
  65.2 1.9 %collective-permute-done.23.refs_2_ = f32[2,1536]{1,0:T(2,128)S(1)} collective-permute-done((f32[2,1536]{1,0:T(2,128)S(1)}, f32[2,1536]{1,0:T(2,128)S(1)}, u32[]{:S(2)}, u32[]{:S(2)}) %collective-permute-start.23) | collective-permute-done | bytes 12320 | tf_op jit(solution)/shard_map/chip_pool/ppermute | solution.py:460
  67.1 0.9 %collective-permute-done.24.refs_3_ = f32[2,1536]{1,0:T(2,128)S(1)} collective-permute-done((f32[2,1536]{1,0:T(2,128)S(1)}, f32[2,1536]{1,0:T(2,128)S(1)}, u32[]{:S(2)}, u32[]{:S(2)}) %collective-permute-start.24) | collective-permute-done | bytes 12320 | tf_op jit(solution)/shard_map/both_pool/ppermute | solution.py:465
  68.0 2.6 %mix.1 = f32[2,1536]{1,0:T(2,128)S(1)} custom-call(f32[2,1536]{1,0:T(2,128)S(1)} %pool_all.1.refs_0_, f32[2,1536]{1,0:T(2,128)S(1)} %collective-permute-done.22.refs_1_, f32[2,1536]{1,0:T(2,128)S(1)} %collective-permute-done.23.refs_2_, f32[2,1536]{1,0:T(2,128)S(1)} %collective-permute-done.24.refs_3_, f32[1,1536]{1,0:T(1,128)S(1)} %get-tuple-element.132.refs_4_, ...), custom_call_target="tpu_custom_call" | custom-call | flops 1024 | bytes 1024 | tf_op jit(solution)/shard_map/mix/pallas_call | solution.py:405
  70.6 0.0 collective-permute-start.25
  70.6 2.6 %collective-permute-start.26 = (f32[2,1536]{1,0:T(2,128)S(1)}, f32[2,1536]{1,0:T(2,128)S(1)}, u32[]{:S(2)}, u32[]{:S(2)}) collective-permute-start(f32[2,1536]{1,0:T(2,128)S(1)} %mix.1), channel_id=1, source_target_pairs={{0,8},{8,0},{4,12},{12,4},{1,9},{9,1},{5,13},{13,5},{2,10},{10,2},... | collective-permute-start | bytes 36872 | tf_op jit(solution)/shard_map/skip_mixed/ppermute | solution.py:470
  73.2 1.8 %collective-permute-start.27 = (f32[2,1536]{1,0:T(2,128)S(1)}, f32[2,1536]{1,0:T(2,128)S(1)}, u32[]{:S(2)}, u32[]{:S(2)}) collective-permute-start(f32[2,1536]{1,0:T(2,128)S(1)} %mix.1), channel_id=1, source_target_pairs={{0,12},{12,0},{4,8},{8,4},{1,13},{13,1},{5,9},{9,5},{2,14},{14,2},... | collective-permute-start | bytes 36872 | tf_op jit(solution)/shard_map/ends_mixed/ppermute | solution.py:470
  75.0 0.3 multiply_reduce_fusion
  75.3 0.1 collective-permute-done.26
  75.3 3.4 %collective-permute-done.27 = f32[2,1536]{1,0:T(2,128)S(1)} collective-permute-done((f32[2,1536]{1,0:T(2,128)S(1)}, f32[2,1536]{1,0:T(2,128)S(1)}, u32[]{:S(2)}, u32[]{:S(2)}) %collective-permute-start.27) | collective-permute-done | bytes 12320 | tf_op jit(solution)/shard_map/ends_mixed/ppermute | solution.py:470
  78.8 0.1 collective-permute-start.28
  78.8 0.7 collective-permute-start.29
  79.6 1.1 %collective-permute-start.30 = (f32[2,1536]{1,0:T(2,128)S(1)}, f32[2,1536]{1,0:T(2,128)S(1)}, u32[]{:S(2)}, u32[]{:S(2)}) collective-permute-start(f32[2,1536]{1,0:T(2,128)S(1)} %add_add_fusion.own), channel_id=1, source_target_pairs={{0,3},{1,2},{2,1},{3,0},{4,7},{5,6},{6,5},{7,4},{8,11},{9,10},{10,... | collective-permute-start | bytes 36872 | tf_op jit(solution)/shard_map/both_embed/ppermute | solution.py:465
  80.7 1.9 %collective-permute-done.29.across = f32[2,1536]{1,0:T(2,128)S(1)} collective-permute-done((f32[2,1536]{1,0:T(2,128)S(1)}, f32[2,1536]{1,0:T(2,128)S(1)}, u32[]{:S(2)}, u32[]{:S(2)}) %collective-permute-start.29) | collective-permute-done | bytes 12320 | tf_op jit(solution)/shard_map/chip_embed/ppermute | solution.py:460
  82.6 0.1 collective-permute-done.30.both
  82.7 1.0 %score.1 = f32[1,64]{1,0:T(1,128)} custom-call(f32[2,1536]{1,0:T(2,128)S(1)} %add_add_fusion.own, f32[2,1536]{1,0:T(2,128)S(1)} %collective-permute-done.28.core, f32[2,1536]{1,0:T(2,128)S(1)} %collective-permute-done.29.across, f32[2,1536]{1,0:T(2,128)S(1)} %collective-permute-done.30.both, f32[1,6144]{1,0:T(1,128)S(1)} %bitcast.12, ...), custom_call_target="tpu_custom_call" | custom-call | flops 1024 | bytes 1024 | tf_op jit(solution)/shard_map/score/pallas_call | solution.py:442
  (42 shorter events, 0.1 us)
Async XLA Ops:
  0.0 12.0 %copy-start = (bf16[128,1536]{1,0:T(8,128)(2,1)S(1)}, bf16[128,1536]{1,0:T(8,128)(2,1)}, u32[]{:S(2)}) copy-start(bf16[128,1536]{1,0:T(8,128)(2,1)} %tokens.3) | copy-start | bytes 1179652
  0.0 20.9 %collective-permute-start.4 = (bf16[128,1536]{1,0:T(8,128)(2,1)}, bf16[128,1536]{1,0:T(8,128)(2,1)S(1)}, u32[]{:S(2)}, u32[]{:S(2)}) collective-permute-start(bf16[128,1536]{1,0:T(8,128)(2,1)} %tokens.3), channel_id=1, source_target_pairs={{0,4},{4,0},{8,12},{12,8},{1,5},{5,1},{9,13},{13,9},{2,6},{6,2},{1... | collective-permute-start | bytes 1179656 | tf_op jit(solution)/shard_map/near_rows/ppermute | solution.py:470
  3.0 17.9 %collective-permute-start.5 = (bf16[128,1536]{1,0:T(8,128)(2,1)}, bf16[128,1536]{1,0:T(8,128)(2,1)S(1)}, u32[]{:S(2)}, u32[]{:S(2)}) collective-permute-start(bf16[128,1536]{1,0:T(8,128)(2,1)} %tokens.3), channel_id=1, source_target_pairs={{4,8},{8,4},{5,9},{9,5},{6,10},{10,6},{7,11},{11,7},{20,24},{24,20... | collective-permute-start | bytes 1179656 | tf_op jit(solution)/shard_map/middle_rows/ppermute | solution.py:470
  8.5 1.5 %collective-permute-start = (bf16[144,768]{1,0:T(8,128)(2,1)S(1)}, bf16[144,768]{1,0:T(8,128)(2,1)S(1)}, u32[]{:S(2)}, u32[]{:S(2)}) collective-permute-start(bf16[144,768]{1,0:T(8,128)(2,1)S(1)} %get-tuple-element.70), channel_id=1, source_target_pairs={{0,1},{1,0},{2,3},{3,2},{4,5},{5,4},{6,7},{7,6},{8,9},{9,8},{10,11... | collective-permute-start | bytes 663560 | tf_op jit(solution)/shard_map/core_sum_0a/ppermute | solution.py:455
  8.6 1.8 %collective-permute-start.1 = (bf16[144,768]{1,0:T(8,128)(2,1)S(1)}, bf16[144,768]{1,0:T(8,128)(2,1)S(1)}, u32[]{:S(2)}, u32[]{:S(2)}) collective-permute-start(bf16[144,768]{1,0:T(8,128)(2,1)S(1)} %get-tuple-element.71), channel_id=1, source_target_pairs={{0,1},{1,0},{2,3},{3,2},{4,5},{5,4},{6,7},{7,6},{8,9},{9,8},{10,11... | collective-permute-start | bytes 663560 | tf_op jit(solution)/shard_map/core_sum_0a/ppermute | solution.py:455
  10.5 23.8 %collective-permute-start.2 = (bf16[136,1536]{1,0:T(8,128)(2,1)S(1)}, bf16[136,1536]{1,0:T(8,128)(2,1)S(1)}, u32[]{:S(2)}, u32[]{:S(2)}) collective-permute-start(bf16[136,1536]{1,0:T(8,128)(2,1)S(1)} %get-tuple-element.74), channel_id=1, source_target_pairs={{0,2},{2,0},{1,3},{3,1},{4,6},{6,4},{5,7},{7,5},{8,10},{10,8},{9,1... | collective-permute-start | bytes 1253384 | tf_op jit(solution)/shard_map/chip_sum_0/ppermute | solution.py:460
  12.0 22.2 %collective-permute-start.3 = (bf16[128,1536]{1,0:T(8,128)(2,1)S(1)}, bf16[128,1536]{1,0:T(8,128)(2,1)S(1)}, u32[]{:S(2)}, u32[]{:S(2)}) collective-permute-start(bf16[128,1536]{1,0:T(8,128)(2,1)S(1)} %copy-done), channel_id=1, source_target_pairs={{0,8},{12,4},{1,9},{13,5},{2,10},{14,6},{3,11},{15,7},{16,24},{28,... | collective-permute-start | bytes 1179656 | tf_op jit(solution)/shard_map/inward_rows/ppermute | solution.py:470
  20.9 13.4 %collective-permute-start.6 = (bf16[128,1536]{1,0:T(8,128)(2,1)S(1)}, bf16[128,1536]{1,0:T(8,128)(2,1)S(1)}, u32[]{:S(2)}, u32[]{:S(2)}) collective-permute-start(bf16[128,1536]{1,0:T(8,128)(2,1)S(1)} %collective-permute-done.5.refs_0_), channel_id=1, source_target_pairs={{4,0},{8,12},{5,1},{9,13},{6,2},{10,14},{7,3},{11,15},{20,16},{24,... | collective-permute-start | bytes 1179656 | tf_op jit(solution)/shard_map/passed_rows/ppermute | solution.py:470
  23.8 1.8 %collective-permute-start.7 = (bf16[144,768]{1,0:T(8,128)(2,1)S(1)}, bf16[144,768]{1,0:T(8,128)(2,1)S(1)}, u32[]{:S(2)}, u32[]{:S(2)}) collective-permute-start(bf16[144,768]{1,0:T(8,128)(2,1)S(1)} %get-tuple-element.83), channel_id=1, source_target_pairs={{0,1},{1,0},{2,3},{3,2},{4,5},{5,4},{6,7},{7,6},{8,9},{9,8},{10,11... | collective-permute-start | bytes 663560 | tf_op jit(solution)/shard_map/core_sum_1a/ppermute | solution.py:455
  23.9 1.7 %collective-permute-start.8 = (bf16[128,768]{1,0:T(8,128)(2,1)S(1)}, bf16[128,768]{1,0:T(8,128)(2,1)S(1)}, u32[]{:S(2)}, u32[]{:S(2)}) collective-permute-start(bf16[128,768]{1,0:T(8,128)(2,1)S(1)} %get-tuple-element.84), channel_id=1, source_target_pairs={{0,1},{1,0},{2,3},{3,2},{4,5},{5,4},{6,7},{7,6},{8,9},{9,8},{10,11... | collective-permute-start | bytes 589832 | tf_op jit(solution)/shard_map/core_sum_1a/ppermute | solution.py:455
  25.7 13.4 %collective-permute-start.12 = (bf16[136,1536]{1,0:T(8,128)(2,1)S(1)}, bf16[136,1536]{1,0:T(8,128)(2,1)S(1)}, u32[]{:S(2)}, u32[]{:S(2)}) collective-permute-start(bf16[136,1536]{1,0:T(8,128)(2,1)S(1)} %get-tuple-element.88), channel_id=1, source_target_pairs={{0,2},{2,0},{1,3},{3,1},{4,6},{6,4},{5,7},{7,5},{8,10},{10,8},{9,1... | collective-permute-start | bytes 1253384 | tf_op jit(solution)/shard_map/chip_sum_1/ppermute | solution.py:460
  29.3 14.6 %collective-permute-start.9 = (bf16[128,1536]{1,0:T(8,128)(2,1)S(1)}, bf16[128,1536]{1,0:T(8,128)(2,1)S(1)}, u32[]{:S(2)}, u32[]{:S(2)}) collective-permute-start(bf16[128,1536]{1,0:T(8,128)(2,1)S(1)} %copy-done), channel_id=1, source_target_pairs={{0,12},{12,0},{1,13},{13,1},{2,14},{14,2},{3,15},{15,3},{16,28},{2... | collective-permute-start | bytes 1179656 | tf_op jit(solution)/shard_map/outer_rows/ppermute | solution.py:470
  37.3 1.8 %collective-permute-start.10 = (bf16[144,768]{1,0:T(8,128)(2,1)S(1)}, bf16[144,768]{1,0:T(8,128)(2,1)S(1)}, u32[]{:S(2)}, u32[]{:S(2)}) collective-permute-start(bf16[144,768]{1,0:T(8,128)(2,1)S(1)} %get-tuple-element.101), channel_id=1, source_target_pairs={{0,1},{1,0},{2,3},{3,2},{4,5},{5,4},{6,7},{7,6},{8,9},{9,8},{10,11... | collective-permute-start | bytes 663560 | tf_op jit(solution)/shard_map/core_sum_2a/ppermute | solution.py:455
  37.4 1.7 %collective-permute-start.11 = (bf16[128,768]{1,0:T(8,128)(2,1)S(1)}, bf16[128,768]{1,0:T(8,128)(2,1)S(1)}, u32[]{:S(2)}, u32[]{:S(2)}) collective-permute-start(bf16[128,768]{1,0:T(8,128)(2,1)S(1)} %get-tuple-element.102), channel_id=1, source_target_pairs={{0,1},{1,0},{2,3},{3,2},{4,5},{5,4},{6,7},{7,6},{8,9},{9,8},{10,11... | collective-permute-start | bytes 589832 | tf_op jit(solution)/shard_map/core_sum_2a/ppermute | solution.py:455
  39.3 11.8 %collective-permute-start.15 = (bf16[136,1536]{1,0:T(8,128)(2,1)S(1)}, bf16[136,1536]{1,0:T(8,128)(2,1)S(1)}, u32[]{:S(2)}, u32[]{:S(2)}) collective-permute-start(bf16[136,1536]{1,0:T(8,128)(2,1)S(1)} %get-tuple-element.106), channel_id=1, source_target_pairs={{0,2},{2,0},{1,3},{3,1},{4,6},{6,4},{5,7},{7,5},{8,10},{10,8},{9,1... | collective-permute-start | bytes 1253384 | tf_op jit(solution)/shard_map/chip_sum_2/ppermute | solution.py:460
  43.9 24.1 %slice-start = ((s8[18874368]{0:T(1024)(128)(4,1)}), s8[4194304]{0:T(1024)(128)(4,1)S(1)}, s32[]{:S(2)}) async-start(s8[18874368]{0:T(1024)(128)(4,1)} %bitcast.6), calls=%async_computation | async-start | bytes 8388608
  43.9 24.1 %slice-start.1 = ((s8[18874368]{0:T(1024)(128)(4,1)}), s8[4194304]{0:T(1024)(128)(4,1)S(1)}, s32[]{:S(2)}) async-start(s8[18874368]{0:T(1024)(128)(4,1)} %bitcast.6), calls=%async_computation.1 | async-start | bytes 8388608
  45.3 22.7 %slice-start.2 = ((s8[18874368]{0:T(1024)(128)(4,1)}), s8[4194304]{0:T(1024)(128)(4,1)S(1)}, s32[]{:S(2)}) async-start(s8[18874368]{0:T(1024)(128)(4,1)} %bitcast.6), calls=%async_computation.2 | async-start | bytes 8388608
  46.9 2.5 %collective-permute-start.13 = (bf16[144,768]{1,0:T(8,128)(2,1)S(1)}, bf16[144,768]{1,0:T(8,128)(2,1)S(1)}, u32[]{:S(2)}, u32[]{:S(2)}) collective-permute-start(bf16[144,768]{1,0:T(8,128)(2,1)S(1)} %get-tuple-element.114), channel_id=1, source_target_pairs={{0,1},{1,0},{2,3},{3,2},{4,5},{5,4},{6,7},{7,6},{8,9},{9,8},{10,11... | collective-permute-start | bytes 663560 | tf_op jit(solution)/shard_map/core_sum_3a/ppermute | solution.py:455
  47.0 7.7 %collective-permute-start.19 = (bf16[144,1536]{1,0:T(8,128)(2,1)S(1)}, bf16[144,1536]{1,0:T(8,128)(2,1)S(1)}, u32[]{:S(2)}, u32[]{:S(2)}) collective-permute-start(bf16[144,1536]{1,0:T(8,128)(2,1)S(1)} %get-tuple-element.77), channel_id=1, source_target_pairs={{0,1},{1,0},{2,3},{3,2},{4,5},{5,4},{6,7},{7,6},{8,9},{9,8},{10,11... | collective-permute-start | bytes 1327112 | tf_op jit(solution)/shard_map/core_sum_0b/ppermute | solution.py:455
  47.5 1.9 %collective-permute-start.14 = (bf16[128,768]{1,0:T(8,128)(2,1)S(1)}, bf16[128,768]{1,0:T(8,128)(2,1)S(1)}, u32[]{:S(2)}, u32[]{:S(2)}) collective-permute-start(bf16[128,768]{1,0:T(8,128)(2,1)S(1)} %get-tuple-element.115), channel_id=1, source_target_pairs={{0,1},{1,0},{2,3},{3,2},{4,5},{5,4},{6,7},{7,6},{8,9},{9,8},{10,11... | collective-permute-start | bytes 589832 | tf_op jit(solution)/shard_map/core_sum_3a/ppermute | solution.py:455
  51.2 11.0 %collective-permute-start.18 = (bf16[136,1536]{1,0:T(8,128)(2,1)S(1)}, bf16[136,1536]{1,0:T(8,128)(2,1)S(1)}, u32[]{:S(2)}, u32[]{:S(2)}) collective-permute-start(bf16[136,1536]{1,0:T(8,128)(2,1)S(1)} %get-tuple-element.119), channel_id=1, source_target_pairs={{0,2},{2,0},{1,3},{3,1},{4,6},{6,4},{5,7},{7,5},{8,10},{10,8},{9,1... | collective-permute-start | bytes 1253384 | tf_op jit(solution)/shard_map/chip_sum_3/ppermute | solution.py:460
  52.7 3.6 %collective-permute-start.21 = (bf16[128,1536]{1,0:T(8,128)(2,1)S(1)}, bf16[128,1536]{1,0:T(8,128)(2,1)S(1)}, u32[]{:S(2)}, u32[]{:S(2)}) collective-permute-start(bf16[128,1536]{1,0:T(8,128)(2,1)S(1)} %get-tuple-element.110), channel_id=1, source_target_pairs={{0,1},{1,0},{2,3},{3,2},{4,5},{5,4},{6,7},{7,6},{8,9},{9,8},{10,11... | collective-permute-start | bytes 1179656 | tf_op jit(solution)/shard_map/core_sum_2b/ppermute | solution.py:455
  52.7 4.7 %collective-permute-start.20 = (bf16[128,1536]{1,0:T(8,128)(2,1)S(1)}, bf16[128,1536]{1,0:T(8,128)(2,1)S(1)}, u32[]{:S(2)}, u32[]{:S(2)}) collective-permute-start(bf16[128,1536]{1,0:T(8,128)(2,1)S(1)} %get-tuple-element.98), channel_id=1, source_target_pairs={{0,1},{1,0},{2,3},{3,2},{4,5},{5,4},{6,7},{7,6},{8,9},{9,8},{10,11... | collective-permute-start | bytes 1179656 | tf_op jit(solution)/shard_map/core_sum_1b/ppermute | solution.py:455
  53.2 2.0 %copy-start.2 = (f32[6144]{0:T(1024)S(1)}, f32[6144]{0:T(1024)}, u32[]{:S(2)}) copy-start(f32[6144]{0:T(1024)} %param.11) | copy-start | bytes 73732
  53.2 14.8 %slice-start.3 = ((s8[18874368]{0:T(1024)(128)(4,1)}), s8[4194304]{0:T(1024)(128)(4,1)S(1)}, s32[]{:S(2)}) async-start(s8[18874368]{0:T(1024)(128)(4,1)} %bitcast.6), calls=%async_computation.3 | async-start | bytes 8388608
  53.2 14.8 %slice-start.4 = ((s8[18874368]{0:T(1024)(128)(4,1)}), s8[2097152]{0:T(1024)(128)(4,1)S(1)}, s32[]{:S(2)}) async-start(s8[18874368]{0:T(1024)(128)(4,1)} %bitcast.6), calls=%async_computation.4 | async-start | bytes 4194304
  54.6 3.8 %collective-permute-start.16 = (bf16[128,768]{1,0:T(8,128)(2,1)S(1)}, bf16[128,768]{1,0:T(8,128)(2,1)S(1)}, u32[]{:S(2)}, u32[]{:S(2)}) collective-permute-start(bf16[128,768]{1,0:T(8,128)(2,1)S(1)} %get-tuple-element.122), channel_id=1, source_target_pairs={{0,1},{1,0},{2,3},{3,2},{4,5},{5,4},{6,7},{7,6},{8,9},{9,8},{10,11... | collective-permute-start | bytes 589832 | tf_op jit(solution)/shard_map/core_sum_3b/ppermute | solution.py:455
  54.7 3.7 %collective-permute-start.17 = (bf16[128,768]{1,0:T(8,128)(2,1)S(1)}, bf16[128,768]{1,0:T(8,128)(2,1)S(1)}, u32[]{:S(2)}, u32[]{:S(2)}) collective-permute-start(bf16[128,768]{1,0:T(8,128)(2,1)S(1)} %get-tuple-element.123), channel_id=1, source_target_pairs={{0,1},{1,0},{2,3},{3,2},{4,5},{5,4},{6,7},{7,6},{8,9},{9,8},{10,11... | collective-permute-start | bytes 589832 | tf_op jit(solution)/shard_map/core_sum_3b/ppermute | solution.py:455
  63.2 1.9 %collective-permute-start.22 = (f32[2,1536]{1,0:T(2,128)S(1)}, f32[2,1536]{1,0:T(2,128)S(1)}, u32[]{:S(2)}, u32[]{:S(2)}) collective-permute-start(f32[2,1536]{1,0:T(2,128)S(1)} %pool_all.1.refs_0_), channel_id=1, source_target_pairs={{0,1},{1,0},{2,3},{3,2},{4,5},{5,4},{6,7},{7,6},{8,9},{9,8},{10,11... | collective-permute-start | bytes 36872 | tf_op jit(solution)/shard_map/core_pool/ppermute | solution.py:455
  63.3 3.8 %collective-permute-start.23 = (f32[2,1536]{1,0:T(2,128)S(1)}, f32[2,1536]{1,0:T(2,128)S(1)}, u32[]{:S(2)}, u32[]{:S(2)}) collective-permute-start(f32[2,1536]{1,0:T(2,128)S(1)} %pool_all.1.refs_0_), channel_id=1, source_target_pairs={{0,2},{2,0},{1,3},{3,1},{4,6},{6,4},{5,7},{7,5},{8,10},{10,8},{9,1... | collective-permute-start | bytes 36872 | tf_op jit(solution)/shard_map/chip_pool/ppermute | solution.py:460
  64.8 3.1 %collective-permute-start.24 = (f32[2,1536]{1,0:T(2,128)S(1)}, f32[2,1536]{1,0:T(2,128)S(1)}, u32[]{:S(2)}, u32[]{:S(2)}) collective-permute-start(f32[2,1536]{1,0:T(2,128)S(1)} %pool_all.1.refs_0_), channel_id=1, source_target_pairs={{0,3},{1,2},{2,1},{3,0},{4,7},{5,6},{6,5},{7,4},{8,11},{9,10},{10,... | collective-permute-start | bytes 36872 | tf_op jit(solution)/shard_map/both_pool/ppermute | solution.py:465
  68.0 7.0 %copy-start.1 = (bf16[64,6144]{1,0:T(8,128)(2,1)S(1)}, bf16[64,6144]{1,0:T(8,128)(2,1)}, u32[]{:S(2)}) copy-start(bf16[64,6144]{1,0:T(8,128)(2,1)} %captions.1) | copy-start | bytes 2359300
  68.0 14.7 %copy-start.3 = (f32[6144]{0:T(1024)S(1)}, f32[6144]{0:T(1024)}, u32[]{:S(2)}) copy-start(f32[6144]{0:T(1024)} %param.13) | copy-start | bytes 73732
  68.0 14.7 %copy-start.4 = (s32[64]{0:T(128)S(1)}, s32[64]{0:T(128)}, u32[]{:S(2)}) copy-start(s32[64]{0:T(128)} %param.15) | copy-start | bytes 772
  70.6 4.7 %collective-permute-start.25 = (f32[2,1536]{1,0:T(2,128)S(1)}, f32[2,1536]{1,0:T(2,128)S(1)}, u32[]{:S(2)}, u32[]{:S(2)}) collective-permute-start(f32[2,1536]{1,0:T(2,128)S(1)} %mix.1), channel_id=1, source_target_pairs={{0,4},{4,0},{8,12},{12,8},{1,5},{5,1},{9,13},{13,9},{2,6},{6,2},{1... | collective-permute-start | bytes 36872 | tf_op jit(solution)/shard_map/swap_mixed/ppermute | solution.py:470
  70.6 4.7 %collective-permute-start.26 = (f32[2,1536]{1,0:T(2,128)S(1)}, f32[2,1536]{1,0:T(2,128)S(1)}, u32[]{:S(2)}, u32[]{:S(2)}) collective-permute-start(f32[2,1536]{1,0:T(2,128)S(1)} %mix.1), channel_id=1, source_target_pairs={{0,8},{8,0},{4,12},{12,4},{1,9},{9,1},{5,13},{13,5},{2,10},{10,2},... | collective-permute-start | bytes 36872 | tf_op jit(solution)/shard_map/skip_mixed/ppermute | solution.py:470
  73.2 5.5 %collective-permute-start.27 = (f32[2,1536]{1,0:T(2,128)S(1)}, f32[2,1536]{1,0:T(2,128)S(1)}, u32[]{:S(2)}, u32[]{:S(2)}) collective-permute-start(f32[2,1536]{1,0:T(2,128)S(1)} %mix.1), channel_id=1, source_target_pairs={{0,12},{12,0},{4,8},{8,4},{1,13},{13,1},{5,9},{9,5},{2,14},{14,2},... | collective-permute-start | bytes 36872 | tf_op jit(solution)/shard_map/ends_mixed/ppermute | solution.py:470
  78.8 1.9 %collective-permute-start.28 = (f32[2,1536]{1,0:T(2,128)S(1)}, f32[2,1536]{1,0:T(2,128)S(1)}, u32[]{:S(2)}, u32[]{:S(2)}) collective-permute-start(f32[2,1536]{1,0:T(2,128)S(1)} %add_add_fusion.own), channel_id=1, source_target_pairs={{0,1},{1,0},{2,3},{3,2},{4,5},{5,4},{6,7},{7,6},{8,9},{9,8},{10,11... | collective-permute-start | bytes 36872 | tf_op jit(solution)/shard_map/core_embed/ppermute | solution.py:455
  78.8 3.8 %collective-permute-start.29 = (f32[2,1536]{1,0:T(2,128)S(1)}, f32[2,1536]{1,0:T(2,128)S(1)}, u32[]{:S(2)}, u32[]{:S(2)}) collective-permute-start(f32[2,1536]{1,0:T(2,128)S(1)} %add_add_fusion.own), channel_id=1, source_target_pairs={{0,2},{2,0},{1,3},{3,1},{4,6},{6,4},{5,7},{7,5},{8,10},{10,8},{9,1... | collective-permute-start | bytes 36872 | tf_op jit(solution)/shard_map/chip_embed/ppermute | solution.py:460
  79.6 3.1 %collective-permute-start.30 = (f32[2,1536]{1,0:T(2,128)S(1)}, f32[2,1536]{1,0:T(2,128)S(1)}, u32[]{:S(2)}, u32[]{:S(2)}) collective-permute-start(f32[2,1536]{1,0:T(2,128)S(1)} %add_add_fusion.own), channel_id=1, source_target_pairs={{0,3},{1,2},{2,1},{3,0},{4,7},{5,6},{6,5},{7,4},{8,11},{9,10},{10,... | collective-permute-start | bytes 36872 | tf_op jit(solution)/shard_map/both_embed/ppermute | solution.py:465

commit v3 on v2

--- a/solution.py
+++ b/solution.py
@@ -190,41 +190,47 @@
     )(*(pltpu.with_memory_space_constraint(value, pltpu.HBM) for value in (tokens, gain, w)))
 
 
-def first_give_kernel(tokens, gain, w, give, held, resid, sems):
-    copies = column_copies(quarters()[2], w, held, sems, 0)
+def first_b_kernel(tokens, gain, w, give, keep, keep_gain, give_held, keep_held, resid, sems):
+    to_give, own = quarters()[2:]
+    give_copies = column_copies(to_give, w, give_held, sems, 0)
+    keep_copies = column_copies(own, w, keep_held, sems, PIECES)
     values = tokens[...].astype(F32)
     rows = values.shape[0]
+    left = with_gain(values, gain[...])
     resid[...] = jnp.sum(values, axis=0, keepdims=True) / PATCHES
 
-    def store(at, size, product, of_gain):
+    def give_store(at, size, product, of_gain):
         give[0:rows, pl.ds(at, size)] = product.astype(BF16)
         give[rows:, pl.ds(at, size)] = row_block(thirds(of_gain), (16, size))
 
-    first_products(with_gain(values, gain[...]), held, copies, store)
-
-
-def first_keep_kernel(tokens, gain, w, keep, keep_gain, held, sems):
-    copies = column_copies(quarters()[3], w, held, sems, 0)
-
-    def store(at, size, product, of_gain):
+    def keep_store(at, size, product, of_gain):
         keep[:, pl.ds(at, size)] = product
         keep_gain[:, pl.ds(at, size)] = of_gain
 
-    first_products(with_gain(tokens[...].astype(F32), gain[...]), held, copies, store)
-
-
-def first_part(kernel, name, tokens, gain, w, shapes):
+    first_products(left, give_held, give_copies, give_store)
+    first_products(left, keep_held, keep_copies, keep_store)
+
+
+def first_b(tokens, gain, w):
     rows, depth = tokens.shape
     share = w.shape[1] // 4
-    return pl.pallas_call(
-        kernel,
-        name=name,
-        out_shape=shapes,
+    held = pltpu.VMEM((depth, share), BF16)
+    return pl.pallas_call(
+        first_b_kernel,
+        name="first_b",
+        out_shape=(
+            struct((rows + 16, share), BF16),
+            struct((rows, share)),
+            struct((1, share)),
+            held,
+            held,
+            struct((1, depth)),
+        ),
         in_specs=[WHOLE, WHOLE, IN_HBM],
-        out_specs=(WHOLE,) * len(shapes),
-        scratch_shapes=[pltpu.SemaphoreType.DMA((PIECES,))],
+        out_specs=(WHOLE,) * 6,
+        scratch_shapes=[pltpu.SemaphoreType.DMA((2 * PIECES,))],
         compiler_params=params(8),
-        cost_estimate=cost(2 * rows * depth * share, 2 * depth * share),
+        cost_estimate=cost(4 * rows * depth * share, 4 * depth * share),
     )(tokens, gain, pltpu.with_memory_space_constraint(w, pltpu.HBM))
 
 
@@ -259,7 +265,7 @@
                 keep[:, pl.ds(first, step)] = product
 
 
-def later_block(kernel, args, out, flops=1024):
+def later_block(kernel, args, out, flops):
     rows, share = out[-1].shape if len(out) < 4 else out[2].shape
     depth = args[0].shape[1]
     return pl.pallas_call(
@@ -383,34 +389,35 @@
     )(*args)
 
 
-def mix_kernel(rows, own, core, across, both, resid, w, out):
-    share = own.shape[1]
+def mix_kernel(rows, distant, *refs):
+    *shares, other, w, out = refs
+    share = shares[0].shape[1]
     mine_x, mine_c = lax.axis_index("mcol"), lax.axis_index("sub")
+    x = 1 - mine_x if distant else mine_x
     total = jnp.zeros((16, w.shape[1]), F32)
-    order = ((own, 0, 0), (core, 0, 1), (across, 1, 0), (both, 1, 1))
-    for ref, dx, dc in order:
-        x, c = (1 - mine_x if dx else mine_x), (1 - mine_c if dc else mine_c)
+    for ref, c in zip(shares, (mine_c, 1 - mine_c)):
         start = pl.multiple_of((c * 2 + x) * share, 128)
-        value = ref[...] / PATCHES
-        high, middle, low = thirds(value)
-        terms = jnp.concatenate([high, middle, low, jnp.zeros((10, share), BF16)], axis=0)
+        terms = jnp.concatenate([*thirds(ref[...] / PATCHES), jnp.zeros((10, share), BF16)], axis=0)
         total = total + jnp.dot(terms, w[pl.ds(start, share), :], preferred_element_type=F32)
     mixed = total[0:2] + (total[2:4] + total[4:6])
-    image = lax.axis_index("mrow") * rows // PATCHES
-    row = lax.broadcasted_iota(jnp.int32, mixed.shape, 0)
-    out[...] = mixed + jnp.where(row == image, resid[...], 0.0)
-
-
-def mix(rows, own, core, across, both, resid, w):
-    return pl.pallas_call(
-        lambda *refs: mix_kernel(rows, *refs),
+    if distant:
+        out[...] = mixed + other[...]
+    else:
+        image = lax.axis_index("mrow") * rows // PATCHES
+        row = lax.broadcasted_iota(jnp.int32, mixed.shape, 0)
+        out[...] = mixed + jnp.where(row == image, other[...], 0.0)
+
+
+def mix(rows, distant, first, second, other, w):
+    return pl.pallas_call(
+        lambda *refs: mix_kernel(rows, distant, *refs),
         name="mix",
         out_shape=struct((IMAGES, w.shape[1])),
-        in_specs=[WHOLE] * 6,
+        in_specs=[WHOLE] * 4,
         out_specs=WHOLE,
         compiler_params=params(8),
-        cost_estimate=cost(32 * w.size, 16 * w.shape[0]),
-    )(own, core, across, both, resid, w)
+        cost_estimate=cost(16 * w.size, 8 * w.shape[0]),
+    )(first, second, other, w)
 
 
 def score_kernel(own, core, across, both, bias, captions, text_scale, pairs, out):
@@ -473,8 +480,6 @@
 SWAP = ((0, 1), (1, 0), (2, 3), (3, 2))
 MIDDLE = ((1, 2), (2, 1))
 OUTWARD = ((1, 0), (2, 3))
-INWARD = ((0, 2), (3, 1))
-OUTER = ((0, 3), (3, 0))
 SKIP = ((0, 2), (2, 0), (1, 3), (3, 1))
 ENDS = ((0, 3), (3, 0), (1, 2), (2, 1))
 
@@ -506,17 +511,9 @@
     *gives_a, keep_a, keep_gain, sums, held_a, gain = first_a(tokens, ln_gain, w_in)
     gots_a = [other_core("core_sum_0a", give_a) for give_a in gives_a]
     chip_0, note_0, far_0 = chip_sum(0, keep_a, gots_a, sums, keep_gain)
-    inward = along("inward_rows", after(tokens, chip_0), INWARD)
-    give_0, give_held, resid = first_part(
-        first_give_kernel,
-        "first_give",
-        after(tokens, chip_0),
-        gain,
-        w_in,
-        (struct((rows + 16, share), BF16), pltpu.VMEM((depth, share), BF16), struct((1, depth))),
-    )
-    near, middle = after((near, middle), give_0)
+    near, middle = after(near, chip_0), after(middle, chip_0)
     passed = along("passed_rows", middle, OUTWARD)
+    crossed = along("crossed_rows", near, MIDDLE)
 
     def later_a(index, rows_of, ready_after, sums_after=()):
         halves = (struct((rows + 16, share // 2), BF16), struct((rows, share // 2), BF16))
@@ -524,6 +521,7 @@
             lambda *refs: later_a_kernel(len(rows_of), *refs),
             (*rows_of, after(gain, ready_after), held_a),
             (*halves, struct((rows, share)), struct((rows, depth), BF16), struct((1, 2 * rows))),
+            1024,
         )
         gots = after([other_core(f"core_sum_{index}a", give) for give in gives], sums_after)
         return ready, *chip_sum(index, keep, gots, own)
@@ -541,24 +539,17 @@
     def send(index, gives):
         return [other_core(f"core_sum_{index}b", give) for give in gives]
 
-    ready_1, chip_1, note_1, far_1 = later_a(1, (near,), (near, middle))
-    keep_0, keep_gain, keep_held = first_part(
-        first_keep_kernel,
-        "first_keep",
-        after(tokens, chip_1),
-        gain,
-        w_in,
-        (struct((rows, share)), struct((1, share)), pltpu.VMEM((depth, share), BF16)),
-    )
-    far_0, inward, passed = after((far_0, inward, passed), keep_0)
-    give_1, keep_1 = later_b(1, ready_1, far_0, inward, passed)
-
-    outer = along("outer_rows", after(tokens, chip_1), OUTER)
+    ready_1, chip_1, note_1, far_1 = later_a(1, (near,), ())
+    give_0, keep_0, keep_gain, give_held, keep_held, resid = first_b(after(tokens, chip_1), gain, w_in)
+    far_0, crossed = after((far_0, crossed), keep_0)
+    give_1, keep_1 = later_b(1, ready_1, far_0, crossed)
+    last = along("last_rows", crossed, OUTWARD)
+
     ready_2, chip_2, note_2, far_2 = later_a(2, (middle, passed), give_1, far_1)
-    outer = after(outer, chip_2)
-    give_2, keep_2 = later_b(2, ready_2, chip_2, outer)
-
-    ready_3, chip_3, note_3, far_3 = later_a(3, (inward, outer), give_2, far_2)
+    last = after(last, chip_2)
+    give_2, keep_2 = later_b(2, ready_2, chip_2, last)
+
+    ready_3, chip_3, note_3, far_3 = later_a(3, (crossed, last), give_2, far_2)
     *gives_3, keep_3 = later_b(3, ready_3, chip_3)
     nears_0, nears_1, nears_2, nears_3 = send(0, [give_0]), send(1, [give_1]), send(2, [give_2]), send(3, gives_3)
     gains = small(
@@ -576,15 +567,10 @@
     ]
     pooled = pool_all(width, keep_3, nears_3, far_3, bias, gains, note_3, parts)
 
-    mixed = mix(
-        rows,
-        pooled,
-        other_core("core_pool", pooled),
-        other_chip("chip_pool", pooled),
-        other_both("both_pool", pooled),
-        resid,
-        w_out,
-    )
+    core, across, both = other_core("core_pool", pooled), other_chip("chip_pool", pooled), other_both("both_pool", pooled)
+    near_mix = mix(rows, False, pooled, core, resid, w_out)
+    across, both = after((across, both), near_mix)
+    mixed = mix(rows, True, across, both, near_mix, w_out)
     own = mixed + along("swap_mixed", mixed, SWAP) + along("skip_mixed", mixed, SKIP) + along("ends_mixed", mixed, ENDS)
     text_vals = captions.astype(F32)
     text_scale = lax.rsqrt(jnp.mean(text_vals * text_vals, axis=1) + 1e-06)

time: 83.9 us -> 79.3 us (0.945)
  starting transfers between devices: 32.7 us -> 23.7 us
  waiting for transfers between devices: 22.3 us -> 28.1 us
  Pallas kernels: 28 us -> 26.7 us
    ppermute x8, starting transfers between devices: 20.1 us -> 11.5 us  [along(): return lax.ppermute(value, 'mrow', list(pairs))]
    ppermute x8, waiting for transfers between devices: 6.56 us -> 13.9 us  [along(): return lax.ppermute(value, 'mrow', list(pairs))]
    ppermute x15, waiting for transfers between devices: 5.6 us -> 4.36 us  [other_core(): return lax.ppermute(value, 'sub', [(0, 1), (1, 0)])]
    pallas_call x3, Pallas kernels: 8.56 us -> 7.33 us  [the longest x1 4.65 us: first_b(): pl.pallas_call(first_b_kernel, name='first_b', out_shape=(struct((rows +...]
  transfers between devices with their start and end apart: 31 -> 31, of which waited for: 14 -> 15; matrix products, arithmetic and copies ran while one was open for 0% -> 0% of each run, Pallas kernels for 28% -> 29%
where the time goes in v3:
time: 79.3 us; the launch traced here: 79.1 us
  waiting for transfers between devices  28.1 us (35%)
  Pallas kernels  26.7 us (34%)
  starting transfers between devices  23.7 us (30%)
    ppermute x8, waiting for transfers between devices, along(): return lax.ppermute(value, 'mrow', list(pairs))  13.9 us
    ppermute x8, starting transfers between devices, along(): return lax.ppermute(value, 'mrow', list(pairs))  11.5 us
    pallas_call x6, Pallas kernels, later_block(): pl.pallas_call(kernel, name='later_block', out_shape=out, in_specs=[WHOLE...  8.94 us
    ppermute x6, waiting for transfers between devices, other_chip(): return lax.ppermute(value, 'mcol', [(0, 1), (1, 0)])  8.86 us
    ppermute x6, starting transfers between devices, other_chip(): return lax.ppermute(value, 'mcol', [(0, 1), (1, 0)])  7.06 us
    pallas_call x1, Pallas kernels, first_a(): pl.pallas_call(first_a_kernel, name='first_a', out_shape=(struct((rows +...  4.77 us
    pallas_call x1, Pallas kernels, first_b(): pl.pallas_call(first_b_kernel, name='first_b', out_shape=(struct((rows +...  4.65 us
    ppermute x15, waiting for transfers between devices, other_core(): return lax.ppermute(value, 'sub', [(0, 1), (1, 0)])  4.36 us
  transfers between devices with their start and end apart: 31, of which 15 were waited for; matrix products, arithmetic and copies ran while one was open for 0% of the time, Pallas kernels for 29%

profile of v3, /device:TPU:0, one launch (start us, length us, event | category | flops | bytes accessed | tf_op | source)
XLA Modules:
  0.0 79.1 jit_solution(7082554989465853605)
XLA Ops:
  0.0 3.0 %collective-permute-start.3 = (bf16[128,1536]{1,0:T(8,128)(2,1)}, bf16[128,1536]{1,0:T(8,128)(2,1)S(1)}, u32[]{:S(2)}, u32[]{:S(2)}) collective-permute-start(bf16[128,1536]{1,0:T(8,128)(2,1)} %tokens.2), channel_id=1, source_target_pairs={{0,4},{4,0},{8,12},{12,8},{1,5},{5,1},{9,13},{13,9},{2,6},{6,2},{1... | collective-permute-start | bytes 1179656 | tf_op jit(solution)/shard_map/near_rows/ppermute | solution.py:477
  3.0 0.7 collective-permute-start.8
  3.7 4.8 %first_a.1 = (bf16[144,768]{1,0:T(8,128)(2,1)S(1)}, bf16[144,768]{1,0:T(8,128)(2,1)S(1)}, f32[128,1536]{1,0:T(8,128)S(1)}, f32[1,1536]{1,0:T(1,128)S(1)}, f32[1,...) custom-call(bf16[128,1536]{1,0:T(8,128)(2,1)} %tokens.2, f32[1536]{0:T(1024)} %gain.1, ...), custom_call_target="tpu_custom_call" | custom-call | flops 1024 | bytes 1024 | tf_op jit(solution)/shard_map/first_a/pallas_call | solution.py:173
  8.5 0.1 collective-permute-start
  8.6 0.5 collective-permute-start.1
  9.1 1.0 %collective-permute-done.first = bf16[144,768]{1,0:T(8,128)(2,1)S(1)} collective-permute-done((bf16[144,768]{1,0:T(8,128)(2,1)S(1)}, bf16[144,768]{1,0:T(8,128)(2,1)S(1)}, u32[]{:S(2)}, u32[]{:S(2)}) %collective-permute-start) | collective-permute-done | bytes 221216 | tf_op jit(solution)/shard_map/core_sum_0a/ppermute | solution.py:462
  10.0 0.3 collective-permute-done.1.second
  10.3 0.1 chip_sum.4
  10.5 1.6 %collective-permute-start.2 = (bf16[136,1536]{1,0:T(8,128)(2,1)S(1)}, bf16[136,1536]{1,0:T(8,128)(2,1)S(1)}, u32[]{:S(2)}, u32[]{:S(2)}) collective-permute-start(bf16[136,1536]{1,0:T(8,128)(2,1)S(1)} %get-tuple-element.73), channel_id=1, source_target_pairs={{0,2},{2,0},{1,3},{3,1},{4,6},{6,4},{5,7},{7,5},{8,10},{10,8},{9,1... | collective-permute-start | bytes 1253384 | tf_op jit(solution)/shard_map/chip_sum_0/ppermute | solution.py:467
  12.0 0.3 collective-permute-done.3.refs_0_
  12.3 0.7 collective-permute-start.4
  13.0 1.6 %later_block.6 = (bf16[144,768]{1,0:T(8,128)(2,1)S(1)}, bf16[128,768]{1,0:T(8,128)(2,1)S(1)}, f32[128,1536]{1,0:T(8,128)S(1)}, bf16[128,1536]{1,0:T(8,128)(2,1)S(1)}, f32[1,256]{1,0:T(1,128)S(1)}) custom-call(bf16[128,1536]{1,0:T(8,128)(2,1)S(1)} %collective-permute-done.3.refs_0_, f32[1,1536]{1,0:T(1,128)S(1)} %get-tuple-element.106.refs_1_.gain.refs_2_, ...), custom_call_target="tpu_custom_call" | custom-call | flops 1024 | bytes 1024 | tf_op jit(solution)/shard_map/later_block/pallas_call | solution.py:271
  14.6 0.1 collective-permute-start.5
  14.7 0.5 collective-permute-start.6
  15.2 1.3 %collective-permute-start.9 = (bf16[128,1536]{1,0:T(8,128)(2,1)S(1)}, bf16[128,1536]{1,0:T(8,128)(2,1)S(1)}, u32[]{:S(2)}, u32[]{:S(2)}) collective-permute-start(bf16[128,1536]{1,0:T(8,128)(2,1)S(1)} %collective-permute-done.8.refs_0_), channel_id=1, source_target_pairs={{4,0},{8,12},{5,1},{9,13},{6,2},{10,14},{7,3},{11,15},{20,16},{24,... | collective-permute-start | bytes 1179656 | tf_op jit(solution)/shard_map/passed_rows/ppermute | solution.py:477
  16.5 0.1 chip_sum.5
  16.6 1.7 %collective-permute-start.12 = (bf16[136,1536]{1,0:T(8,128)(2,1)S(1)}, bf16[136,1536]{1,0:T(8,128)(2,1)S(1)}, u32[]{:S(2)}, u32[]{:S(2)}) collective-permute-start(bf16[136,1536]{1,0:T(8,128)(2,1)S(1)} %get-tuple-element.83), channel_id=1, source_target_pairs={{0,2},{2,0},{1,3},{3,1},{4,6},{6,4},{5,7},{7,5},{8,10},{10,8},{9,1... | collective-permute-start | bytes 1253384 | tf_op jit(solution)/shard_map/chip_sum_1/ppermute | solution.py:467
  18.3 4.7 %first_b.1 = (bf16[144,1536]{1,0:T(8,128)(2,1)S(1)}, f32[128,1536]{1,0:T(8,128)S(1)}, f32[1,1536]{1,0:T(1,128)S(1)}, bf16[1536,1536]{1,0:T(8,128)(2,1)S(1)}, bf1...) custom-call(bf16[128,1536]{1,0:T(8,128)(2,1)S(1)} %copy-done.1, ...), custom_call_target="tpu_custom_call" | custom-call | flops 1024 | bytes 1024 | tf_op jit(solution)/shard_map/first_b/pallas_call | solution.py:218
  23.0 1.5 %collective-permute-start.7 = (bf16[128,1536]{1,0:T(8,128)(2,1)S(1)}, bf16[128,1536]{1,0:T(8,128)(2,1)S(1)}, u32[]{:S(2)}, u32[]{:S(2)}) collective-permute-start(bf16[128,1536]{1,0:T(8,128)(2,1)S(1)} %collective-permute-done.4.refs_0_), channel_id=1, source_target_pairs={{4,0},{8,12},{5,1},{9,13},{6,2},{10,14},{7,3},{11,15},{20,16},{24,... | collective-permute-start | bytes 1179656 | tf_op jit(solution)/shard_map/last_rows/ppermute | solution.py:477
  24.5 1.4 %later_block.7 = (bf16[128,1536]{1,0:T(8,128)(2,1)S(1)}, f32[128,1536]{1,0:T(8,128)S(1)}) custom-call(bf16[128,1536]{1,0:T(8,128)(2,1)S(1)} %get-tuple-element.90.left, bf16[1536,1536]{1,0:T(8,128)(2,1)S(1)} %get-tuple-element.91.give_held, bf16[1536,1536]{1,0:T(8,128)(2,1)S(1)} %get-tuple-element.92.keep_held), custom_call_target="tpu_custom_call" | custom-call | flops 1207959552 | bytes 1024 | tf_op jit(solution)/shard_map/later_block/pallas_call | solution.py:271
  25.9 5.8 %collective-permute-done.9.refs_1_ = bf16[128,1536]{1,0:T(8,128)(2,1)S(1)} collective-permute-done((bf16[128,1536]{1,0:T(8,128)(2,1)S(1)}, bf16[128,1536]{1,0:T(8,128)(2,1)S(1)}, u32[]{:S(2)}, u32[]{:S(2)}) %collective-permute-start.9) | collective-permute-done | bytes 393248 | tf_op jit(solution)/shard_map/passed_rows/ppermute | solution.py:477
  31.7 1.6 %later_block.8 = (bf16[144,768]{1,0:T(8,128)(2,1)S(1)}, bf16[128,768]{1,0:T(8,128)(2,1)S(1)}, f32[128,1536]{1,0:T(8,128)S(1)}, bf16[128,1536]{1,0:T(8,128)(2,1)S(1)}, f32[1,256]{1,0:T(1,128)S(1)}) custom-call(bf16[128,1536]{1,0:T(8,128)(2,1)S(1)} %collective-permute-done.8.refs_0_, bf16[128,1536]{1,0:T(8,128)(2,1)S(1)} %collective-permute-done.9.refs_1_, ...), custom_call_target="tpu_custom_call" | custom-call | flops 1024 | bytes 1024 | tf_op jit(solution)/shard_map/later_block/pallas_call | solution.py:271
  33.3 0.1 collective-permute-start.10
  33.4 0.5 collective-permute-start.11
  33.9 1.2 %collective-permute-done.11.second = bf16[128,768]{1,0:T(8,128)(2,1)S(1)} collective-permute-done((bf16[128,768]{1,0:T(8,128)(2,1)S(1)}, bf16[128,768]{1,0:T(8,128)(2,1)S(1)}, u32[]{:S(2)}, u32[]{:S(2)}) %collective-permute-start.11) | collective-permute-done | bytes 196640 | tf_op jit(solution)/shard_map/core_sum_2a/ppermute | solution.py:462
  35.1 0.1 chip_sum.6
  35.2 0.8 collective-permute-start.15
  36.0 3.5 %collective-permute-done.7.refs_1_ = bf16[128,1536]{1,0:T(8,128)(2,1)S(1)} collective-permute-done((bf16[128,1536]{1,0:T(8,128)(2,1)S(1)}, bf16[128,1536]{1,0:T(8,128)(2,1)S(1)}, u32[]{:S(2)}, u32[]{:S(2)}) %collective-permute-start.7) | collective-permute-done | bytes 393248 | tf_op jit(solution)/shard_map/last_rows/ppermute | solution.py:477
  39.6 1.4 %later_block.9 = (bf16[128,1536]{1,0:T(8,128)(2,1)S(1)}, f32[128,1536]{1,0:T(8,128)S(1)}) custom-call(bf16[128,1536]{1,0:T(8,128)(2,1)S(1)} %get-tuple-element.104.left, bf16[1536,1536]{1,0:T(8,128)(2,1)S(1)} %get-tuple-element.91.give_held, bf16[1536,1536]{1,0:T(8,128)(2,1)S(1)} %get-tuple-element.92.keep_held), custom_call_target="tpu_custom_call" | custom-call | flops 1207959552 | bytes 1024 | tf_op jit(solution)/shard_map/later_block/pallas_call | solution.py:271
  41.0 1.6 %later_block.10 = (bf16[144,768]{1,0:T(8,128)(2,1)S(1)}, bf16[128,768]{1,0:T(8,128)(2,1)S(1)}, f32[128,1536]{1,0:T(8,128)S(1)}, bf16[128,1536]{1,0:T(8,128)(2,1)S(1)}, f32[1,256]{1,0:T(1,128)S(1)}) custom-call(bf16[128,1536]{1,0:T(8,128)(2,1)S(1)} %collective-permute-done.4.refs_0_, bf16[128,1536]{1,0:T(8,128)(2,1)S(1)} %collective-permute-done.7.refs_1_, ...), custom_call_target="tpu_custom_call" | custom-call | flops 1024 | bytes 1024 | tf_op jit(solution)/shard_map/later_block/pallas_call | solution.py:271
  42.6 0.1 collective-permute-start.13
  42.7 0.5 collective-permute-start.19
  43.2 0.1 collective-permute-start.14
  43.2 1.8 %collective-permute-done.14.second = bf16[128,768]{1,0:T(8,128)(2,1)S(1)} collective-permute-done((bf16[128,768]{1,0:T(8,128)(2,1)S(1)}, bf16[128,768]{1,0:T(8,128)(2,1)S(1)}, u32[]{:S(2)}, u32[]{:S(2)}) %collective-permute-start.14) | collective-permute-done | bytes 196640 | tf_op jit(solution)/shard_map/core_sum_3a/ppermute | solution.py:462
  45.0 2.0 %collective-permute-done.15.refs_2_ = bf16[136,1536]{1,0:T(8,128)(2,1)S(1)} collective-permute-done((bf16[136,1536]{1,0:T(8,128)(2,1)S(1)}, bf16[136,1536]{1,0:T(8,128)(2,1)S(1)}, u32[]{:S(2)}, u32[]{:S(2)}) %collective-permute-start.15) | collective-permute-done | bytes 417824 | tf_op jit(solution)/shard_map/chip_sum_2/ppermute | solution.py:467
  47.1 0.1 chip_sum.7
  47.2 0.8 collective-permute-start.18
  48.0 0.5 collective-permute-start.21
  48.5 1.4 %later_block.11 = (bf16[128,768]{1,0:T(8,128)(2,1)S(1)}, bf16[128,768]{1,0:T(8,128)(2,1)S(1)}, f32[128,1536]{1,0:T(8,128)S(1)}) custom-call(bf16[128,1536]{1,0:T(8,128)(2,1)S(1)} %get-tuple-element.115.left, bf16[1536,1536]{1,0:T(8,128)(2,1)S(1)} %get-tuple-element.91.give_held, bf16[1536,1536]{1,0:T(8,128)(2,1)S(1)} %get-tuple-element.92.keep_held), custom_call_target="tpu_custom_call" | custom-call | flops 1207959552 | bytes 1024 | tf_op jit(solution)/shard_map/later_block/pallas_call | solution.py:271
  49.9 0.1 collective-permute-start.16
  50.0 0.5 collective-permute-start.17
  50.5 1.1 %pool.3.refs_7_ = f32[1,1536]{1,0:T(1,128)S(1)} custom-call(f32[128,1536]{1,0:T(8,128)S(1)} %get-tuple-element.85.refs_0_, bf16[144,1536]{1,0:T(8,128)(2,1)S(1)} %collective-permute-done.19.refs_1_, bf16[136,1536]{1,0:T(8,128)(2,1)S(1)} %collective-permute-done.2.refs_2_, f32[1,6144]{1,0:T(1,128)S(1)} %bitcast.8, f32[8,1536]{1,0:T(8,128)S(1)} %all_gains.1.refs_4_.refs_5_, ...), custom_call_target="tpu_custom_call" | custom-call | flops 1024 | bytes 1024 | tf_op jit(solution)/shard_map/pool/pallas_call | solution.py:354
  51.6 1.0 %pool.4.refs_8_ = f32[1,1536]{1,0:T(1,128)S(1)} custom-call(f32[128,1536]{1,0:T(8,128)S(1)} %get-tuple-element.124.refs_0_, bf16[128,1536]{1,0:T(8,128)(2,1)S(1)} %collective-permute-done.20.refs_1_, bf16[136,1536]{1,0:T(8,128)(2,1)S(1)} %collective-permute-done.12.refs_2_, f32[1,6144]{1,0:T(1,128)S(1)} %bitcast.9, f32[8,1536]{1,0:T(8,128)S(1)} %all_gains.1.refs_4_.refs_5_, ...), custom_call_target="tpu_custom_call" | custom-call | flops 1024 | bytes 1024 | tf_op jit(solution)/shard_map/pool/pallas_call | solution.py:354
  52.6 1.1 %pool.5.refs_9_ = f32[1,1536]{1,0:T(1,128)S(1)} custom-call(f32[128,1536]{1,0:T(8,128)S(1)} %get-tuple-element.126.refs_0_, bf16[128,1536]{1,0:T(8,128)(2,1)S(1)} %collective-permute-done.21.refs_1_, bf16[136,1536]{1,0:T(8,128)(2,1)S(1)} %collective-permute-done.15.refs_2_, f32[1,6144]{1,0:T(1,128)S(1)} %bitcast.10, f32[8,1536]{1,0:T(8,128)S(1)} %all_gains.1.refs_4_.refs_5_, ...), custom_call_target="tpu_custom_call" | custom-call | flops 1024 | bytes 1024 | tf_op jit(solution)/shard_map/pool/pallas_call | solution.py:354
  53.7 4.5 %collective-permute-done.18.refs_3_ = bf16[136,1536]{1,0:T(8,128)(2,1)S(1)} collective-permute-done((bf16[136,1536]{1,0:T(8,128)(2,1)S(1)}, bf16[136,1536]{1,0:T(8,128)(2,1)S(1)}, u32[]{:S(2)}, u32[]{:S(2)}) %collective-permute-start.18) | collective-permute-done | bytes 417824 | tf_op jit(solution)/shard_map/chip_sum_3/ppermute | solution.py:467
  58.1 1.1 %pool_all.1.refs_0_ = f32[2,1536]{1,0:T(2,128)S(1)} custom-call(f32[128,1536]{1,0:T(8,128)S(1)} %get-tuple-element.116.refs_0_, bf16[128,768]{1,0:T(8,128)(2,1)S(1)} %collective-permute-done.16.refs_1_, bf16[128,768]{1,0:T(8,128)(2,1)S(1)} %collective-permute-done.17.refs_2_, bf16[136,1536]{1,0:T(8,128)(2,1)S(1)} %collective-permute-done.18.refs_3_, ...), custom_call_target="tpu_custom_call" | custom-call | flops 1024 | bytes 1024 | tf_op jit(solution)/shard_map/pool_all/pallas_call | solution.py:380
  59.3 0.8 collective-permute-start.22
  60.1 1.1 %collective-permute-start.23 = (f32[2,1536]{1,0:T(2,128)S(1)}, f32[2,1536]{1,0:T(2,128)S(1)}, u32[]{:S(2)}, u32[]{:S(2)}) collective-permute-start(f32[2,1536]{1,0:T(2,128)S(1)} %pool_all.1.refs_0_), channel_id=1, source_target_pairs={{0,3},{1,2},{2,1},{3,0},{4,7},{5,6},{6,5},{7,4},{8,11},{9,10},{10,... | collective-permute-start | bytes 36872 | tf_op jit(solution)/shard_map/both_pool/ppermute | solution.py:472
  61.2 1.3 %mix.2.refs_2_ = f32[2,1536]{1,0:T(2,128)S(1)} custom-call(f32[2,1536]{1,0:T(2,128)S(1)} %pool_all.1.refs_0_, f32[2,1536]{1,0:T(2,128)S(1)} %collective-permute-done.24.refs_1_, f32[1,1536]{1,0:T(1,128)S(1)} %get-tuple-element.128.refs_2_, bf16[6144,1536]{1,0:T(8,128)(2,1)S(1)} %bitcast.7), custom_call_target="tpu_custom_call" | custom-call | flops 1024 | bytes 1024 | tf_op jit(solution)/shard_map/mix/pallas_call | solution.py:412
  62.6 0.5 collective-permute-done.22.refs_0_
  63.1 0.1 collective-permute-done.23.refs_1_
  63.2 1.3 %mix.3 = f32[2,1536]{1,0:T(2,128)S(1)} custom-call(f32[2,1536]{1,0:T(2,128)S(1)} %collective-permute-done.22.refs_0_, f32[2,1536]{1,0:T(2,128)S(1)} %collective-permute-done.23.refs_1_, f32[2,1536]{1,0:T(2,128)S(1)} %mix.2.refs_2_, bf16[6144,1536]{1,0:T(8,128)(2,1)S(1)} %bitcast.7), custom_call_target="tpu_custom_call" | custom-call | flops 1024 | bytes 1024 | tf_op jit(solution)/shard_map/mix/pallas_call | solution.py:412
  64.5 0.2 collective-permute-start.25
  64.8 3.2 %collective-permute-start.26 = (f32[2,1536]{1,0:T(2,128)S(1)}, f32[2,1536]{1,0:T(2,128)S(1)}, u32[]{:S(2)}, u32[]{:S(2)}) collective-permute-start(f32[2,1536]{1,0:T(2,128)S(1)} %mix.3), channel_id=1, source_target_pairs={{0,8},{8,0},{4,12},{12,4},{1,9},{9,1},{5,13},{13,5},{2,10},{10,2},... | collective-permute-start | bytes 36872 | tf_op jit(solution)/shard_map/skip_mixed/ppermute | solution.py:477
  68.0 1.0 %collective-permute-start.27 = (f32[2,1536]{1,0:T(2,128)S(1)}, f32[2,1536]{1,0:T(2,128)S(1)}, u32[]{:S(2)}, u32[]{:S(2)}) collective-permute-start(f32[2,1536]{1,0:T(2,128)S(1)} %mix.3), channel_id=1, source_target_pairs={{0,12},{12,0},{4,8},{8,4},{1,13},{13,1},{5,9},{9,5},{2,14},{14,2},... | collective-permute-start | bytes 36872 | tf_op jit(solution)/shard_map/ends_mixed/ppermute | solution.py:477
  68.9 0.3 multiply_reduce_fusion
  69.2 0.5 collective-permute-done.26
  69.7 3.8 %collective-permute-done.27 = f32[2,1536]{1,0:T(2,128)S(1)} collective-permute-done((f32[2,1536]{1,0:T(2,128)S(1)}, f32[2,1536]{1,0:T(2,128)S(1)}, u32[]{:S(2)}, u32[]{:S(2)}) %collective-permute-start.27) | collective-permute-done | bytes 12320 | tf_op jit(solution)/shard_map/ends_mixed/ppermute | solution.py:477
  73.5 0.1 collective-permute-start.28
  73.6 1.4 %collective-permute-start.29 = (f32[2,1536]{1,0:T(2,128)S(1)}, f32[2,1536]{1,0:T(2,128)S(1)}, u32[]{:S(2)}, u32[]{:S(2)}) collective-permute-start(f32[2,1536]{1,0:T(2,128)S(1)} %add_add_fusion.own), channel_id=1, source_target_pairs={{0,2},{2,0},{1,3},{3,1},{4,6},{6,4},{5,7},{7,5},{8,10},{10,8},{9,1... | collective-permute-start | bytes 36872 | tf_op jit(solution)/shard_map/chip_embed/ppermute | solution.py:467
  75.0 0.4 collective-permute-start.30
  75.4 1.9 %collective-permute-done.29.across = f32[2,1536]{1,0:T(2,128)S(1)} collective-permute-done((f32[2,1536]{1,0:T(2,128)S(1)}, f32[2,1536]{1,0:T(2,128)S(1)}, u32[]{:S(2)}, u32[]{:S(2)}) %collective-permute-start.29) | collective-permute-done | bytes 12320 | tf_op jit(solution)/shard_map/chip_embed/ppermute | solution.py:467
  77.3 0.8 collective-permute-done.30.both
  78.1 1.0 %score.1 = f32[1,64]{1,0:T(1,128)} custom-call(f32[2,1536]{1,0:T(2,128)S(1)} %add_add_fusion.own, f32[2,1536]{1,0:T(2,128)S(1)} %collective-permute-done.28.core, f32[2,1536]{1,0:T(2,128)S(1)} %collective-permute-done.29.across, f32[2,1536]{1,0:T(2,128)S(1)} %collective-permute-done.30.both, f32[1,6144]{1,0:T(1,128)S(1)} %bitcast.12, ...), custom_call_target="tpu_custom_call" | custom-call | flops 1024 | bytes 1024 | tf_op jit(solution)/shard_map/score/pallas_call | solution.py:449
  (42 shorter events, 0.2 us)
Async XLA Ops:
  0.0 12.3 %collective-permute-start.3 = (bf16[128,1536]{1,0:T(8,128)(2,1)}, bf16[128,1536]{1,0:T(8,128)(2,1)S(1)}, u32[]{:S(2)}, u32[]{:S(2)}) collective-permute-start(bf16[128,1536]{1,0:T(8,128)(2,1)} %tokens.2), channel_id=1, source_target_pairs={{0,4},{4,0},{8,12},{12,8},{1,5},{5,1},{9,13},{13,9},{2,6},{6,2},{1... | collective-permute-start | bytes 1179656 | tf_op jit(solution)/shard_map/near_rows/ppermute | solution.py:477
  3.0 12.2 %collective-permute-start.8 = (bf16[128,1536]{1,0:T(8,128)(2,1)}, bf16[128,1536]{1,0:T(8,128)(2,1)S(1)}, u32[]{:S(2)}, u32[]{:S(2)}) collective-permute-start(bf16[128,1536]{1,0:T(8,128)(2,1)} %tokens.2), channel_id=1, source_target_pairs={{4,8},{8,4},{5,9},{9,5},{6,10},{10,6},{7,11},{11,7},{20,24},{24,20... | collective-permute-start | bytes 1179656 | tf_op jit(solution)/shard_map/middle_rows/ppermute | solution.py:477
  8.5 1.5 %collective-permute-start = (bf16[144,768]{1,0:T(8,128)(2,1)S(1)}, bf16[144,768]{1,0:T(8,128)(2,1)S(1)}, u32[]{:S(2)}, u32[]{:S(2)}) collective-permute-start(bf16[144,768]{1,0:T(8,128)(2,1)S(1)} %get-tuple-element.69), channel_id=1, source_target_pairs={{0,1},{1,0},{2,3},{3,2},{4,5},{5,4},{6,7},{7,6},{8,9},{9,8},{10,11... | collective-permute-start | bytes 663560 | tf_op jit(solution)/shard_map/core_sum_0a/ppermute | solution.py:462
  8.6 1.8 %collective-permute-start.1 = (bf16[144,768]{1,0:T(8,128)(2,1)S(1)}, bf16[144,768]{1,0:T(8,128)(2,1)S(1)}, u32[]{:S(2)}, u32[]{:S(2)}) collective-permute-start(bf16[144,768]{1,0:T(8,128)(2,1)S(1)} %get-tuple-element.70), channel_id=1, source_target_pairs={{0,1},{1,0},{2,3},{3,2},{4,5},{5,4},{6,7},{7,6},{8,9},{9,8},{10,11... | collective-permute-start | bytes 663560 | tf_op jit(solution)/shard_map/core_sum_0a/ppermute | solution.py:462
  10.5 12.5 %collective-permute-start.2 = (bf16[136,1536]{1,0:T(8,128)(2,1)S(1)}, bf16[136,1536]{1,0:T(8,128)(2,1)S(1)}, u32[]{:S(2)}, u32[]{:S(2)}) collective-permute-start(bf16[136,1536]{1,0:T(8,128)(2,1)S(1)} %get-tuple-element.73), channel_id=1, source_target_pairs={{0,2},{2,0},{1,3},{3,1},{4,6},{6,4},{5,7},{7,5},{8,10},{10,8},{9,1... | collective-permute-start | bytes 1253384 | tf_op jit(solution)/shard_map/chip_sum_0/ppermute | solution.py:467
  12.3 10.7 %collective-permute-start.4 = (bf16[128,1536]{1,0:T(8,128)(2,1)S(1)}, bf16[128,1536]{1,0:T(8,128)(2,1)S(1)}, u32[]{:S(2)}, u32[]{:S(2)}) collective-permute-start(bf16[128,1536]{1,0:T(8,128)(2,1)S(1)} %collective-permute-done.3.refs_0_), channel_id=1, source_target_pairs={{4,8},{8,4},{5,9},{9,5},{6,10},{10,6},{7,11},{11,7},{20,24},{24,20... | collective-permute-start | bytes 1179656 | tf_op jit(solution)/shard_map/crossed_rows/ppermute | solution.py:477
  13.0 5.3 %copy-start.1 = (bf16[128,1536]{1,0:T(8,128)(2,1)S(1)}, bf16[128,1536]{1,0:T(8,128)(2,1)}, u32[]{:S(2)}) copy-start(bf16[128,1536]{1,0:T(8,128)(2,1)} %tokens.2) | copy-start | bytes 1179652
  14.6 1.9 %collective-permute-start.5 = (bf16[144,768]{1,0:T(8,128)(2,1)S(1)}, bf16[144,768]{1,0:T(8,128)(2,1)S(1)}, u32[]{:S(2)}, u32[]{:S(2)}) collective-permute-start(bf16[144,768]{1,0:T(8,128)(2,1)S(1)} %get-tuple-element.78), channel_id=1, source_target_pairs={{0,1},{1,0},{2,3},{3,2},{4,5},{5,4},{6,7},{7,6},{8,9},{9,8},{10,11... | collective-permute-start | bytes 663560 | tf_op jit(solution)/shard_map/core_sum_1a/ppermute | solution.py:462
  14.7 1.8 %collective-permute-start.6 = (bf16[128,768]{1,0:T(8,128)(2,1)S(1)}, bf16[128,768]{1,0:T(8,128)(2,1)S(1)}, u32[]{:S(2)}, u32[]{:S(2)}) collective-permute-start(bf16[128,768]{1,0:T(8,128)(2,1)S(1)} %get-tuple-element.79), channel_id=1, source_target_pairs={{0,1},{1,0},{2,3},{3,2},{4,5},{5,4},{6,7},{7,6},{8,9},{9,8},{10,11... | collective-permute-start | bytes 589832 | tf_op jit(solution)/shard_map/core_sum_1a/ppermute | solution.py:462
  15.2 16.5 %collective-permute-start.9 = (bf16[128,1536]{1,0:T(8,128)(2,1)S(1)}, bf16[128,1536]{1,0:T(8,128)(2,1)S(1)}, u32[]{:S(2)}, u32[]{:S(2)}) collective-permute-start(bf16[128,1536]{1,0:T(8,128)(2,1)S(1)} %collective-permute-done.8.refs_0_), channel_id=1, source_target_pairs={{4,0},{8,12},{5,1},{9,13},{6,2},{10,14},{7,3},{11,15},{20,16},{24,... | collective-permute-start | bytes 1179656 | tf_op jit(solution)/shard_map/passed_rows/ppermute | solution.py:477
  16.6 18.5 %collective-permute-start.12 = (bf16[136,1536]{1,0:T(8,128)(2,1)S(1)}, bf16[136,1536]{1,0:T(8,128)(2,1)S(1)}, u32[]{:S(2)}, u32[]{:S(2)}) collective-permute-start(bf16[136,1536]{1,0:T(8,128)(2,1)S(1)} %get-tuple-element.83), channel_id=1, source_target_pairs={{0,2},{2,0},{1,3},{3,1},{4,6},{6,4},{5,7},{7,5},{8,10},{10,8},{9,1... | collective-permute-start | bytes 1253384 | tf_op jit(solution)/shard_map/chip_sum_1/ppermute | solution.py:467
  23.0 16.5 %collective-permute-start.7 = (bf16[128,1536]{1,0:T(8,128)(2,1)S(1)}, bf16[128,1536]{1,0:T(8,128)(2,1)S(1)}, u32[]{:S(2)}, u32[]{:S(2)}) collective-permute-start(bf16[128,1536]{1,0:T(8,128)(2,1)S(1)} %collective-permute-done.4.refs_0_), channel_id=1, source_target_pairs={{4,0},{8,12},{5,1},{9,13},{6,2},{10,14},{7,3},{11,15},{20,16},{24,... | collective-permute-start | bytes 1179656 | tf_op jit(solution)/shard_map/last_rows/ppermute | solution.py:477
  33.3 1.8 %collective-permute-start.10 = (bf16[144,768]{1,0:T(8,128)(2,1)S(1)}, bf16[144,768]{1,0:T(8,128)(2,1)S(1)}, u32[]{:S(2)}, u32[]{:S(2)}) collective-permute-start(bf16[144,768]{1,0:T(8,128)(2,1)S(1)} %get-tuple-element.96), channel_id=1, source_target_pairs={{0,1},{1,0},{2,3},{3,2},{4,5},{5,4},{6,7},{7,6},{8,9},{9,8},{10,11... | collective-permute-start | bytes 663560 | tf_op jit(solution)/shard_map/core_sum_2a/ppermute | solution.py:462
  33.4 1.7 %collective-permute-start.11 = (bf16[128,768]{1,0:T(8,128)(2,1)S(1)}, bf16[128,768]{1,0:T(8,128)(2,1)S(1)}, u32[]{:S(2)}, u32[]{:S(2)}) collective-permute-start(bf16[128,768]{1,0:T(8,128)(2,1)S(1)} %get-tuple-element.97), channel_id=1, source_target_pairs={{0,1},{1,0},{2,3},{3,2},{4,5},{5,4},{6,7},{7,6},{8,9},{9,8},{10,11... | collective-permute-start | bytes 589832 | tf_op jit(solution)/shard_map/core_sum_2a/ppermute | solution.py:462
  35.2 11.8 %collective-permute-start.15 = (bf16[136,1536]{1,0:T(8,128)(2,1)S(1)}, bf16[136,1536]{1,0:T(8,128)(2,1)S(1)}, u32[]{:S(2)}, u32[]{:S(2)}) collective-permute-start(bf16[136,1536]{1,0:T(8,128)(2,1)S(1)} %get-tuple-element.101), channel_id=1, source_target_pairs={{0,2},{2,0},{1,3},{3,1},{4,6},{6,4},{5,7},{7,5},{8,10},{10,8},{9,1... | collective-permute-start | bytes 1253384 | tf_op jit(solution)/shard_map/chip_sum_2/ppermute | solution.py:467
  39.6 21.6 %slice-start = ((s8[18874368]{0:T(1024)(128)(4,1)}), s8[2097152]{0:T(1024)(128)(4,1)S(1)}, s32[]{:S(2)}) async-start(s8[18874368]{0:T(1024)(128)(4,1)} %bitcast.6), calls=%async_computation | async-start | bytes 4194304
  39.6 21.6 %slice-start.1 = ((s8[18874368]{0:T(1024)(128)(4,1)}), s8[4194304]{0:T(1024)(128)(4,1)S(1)}, s32[]{:S(2)}) async-start(s8[18874368]{0:T(1024)(128)(4,1)} %bitcast.6), calls=%async_computation.1 | async-start | bytes 8388608
  41.0 20.2 %slice-start.2 = ((s8[18874368]{0:T(1024)(128)(4,1)}), s8[4194304]{0:T(1024)(128)(4,1)S(1)}, s32[]{:S(2)}) async-start(s8[18874368]{0:T(1024)(128)(4,1)} %bitcast.6), calls=%async_computation.2 | async-start | bytes 8388608
  42.6 2.5 %collective-permute-start.13 = (bf16[144,768]{1,0:T(8,128)(2,1)S(1)}, bf16[144,768]{1,0:T(8,128)(2,1)S(1)}, u32[]{:S(2)}, u32[]{:S(2)}) collective-permute-start(bf16[144,768]{1,0:T(8,128)(2,1)S(1)} %get-tuple-element.109), channel_id=1, source_target_pairs={{0,1},{1,0},{2,3},{3,2},{4,5},{5,4},{6,7},{7,6},{8,9},{9,8},{10,11... | collective-permute-start | bytes 663560 | tf_op jit(solution)/shard_map/core_sum_3a/ppermute | solution.py:462
  42.7 7.3 %collective-permute-start.19 = (bf16[144,1536]{1,0:T(8,128)(2,1)S(1)}, bf16[144,1536]{1,0:T(8,128)(2,1)S(1)}, u32[]{:S(2)}, u32[]{:S(2)}) collective-permute-start(bf16[144,1536]{1,0:T(8,128)(2,1)S(1)} %get-tuple-element.121), channel_id=1, source_target_pairs={{0,1},{1,0},{2,3},{3,2},{4,5},{5,4},{6,7},{7,6},{8,9},{9,8},{10,11... | collective-permute-start | bytes 1327112 | tf_op jit(solution)/shard_map/core_sum_0b/ppermute | solution.py:462
  43.2 1.9 %collective-permute-start.14 = (bf16[128,768]{1,0:T(8,128)(2,1)S(1)}, bf16[128,768]{1,0:T(8,128)(2,1)S(1)}, u32[]{:S(2)}, u32[]{:S(2)}) collective-permute-start(bf16[128,768]{1,0:T(8,128)(2,1)S(1)} %get-tuple-element.110), channel_id=1, source_target_pairs={{0,1},{1,0},{2,3},{3,2},{4,5},{5,4},{6,7},{7,6},{8,9},{9,8},{10,11... | collective-permute-start | bytes 589832 | tf_op jit(solution)/shard_map/core_sum_3a/ppermute | solution.py:462
  47.2 11.0 %collective-permute-start.18 = (bf16[136,1536]{1,0:T(8,128)(2,1)S(1)}, bf16[136,1536]{1,0:T(8,128)(2,1)S(1)}, u32[]{:S(2)}, u32[]{:S(2)}) collective-permute-start(bf16[136,1536]{1,0:T(8,128)(2,1)S(1)} %get-tuple-element.114), channel_id=1, source_target_pairs={{0,2},{2,0},{1,3},{3,1},{4,6},{6,4},{5,7},{7,5},{8,10},{10,8},{9,1... | collective-permute-start | bytes 1253384 | tf_op jit(solution)/shard_map/chip_sum_3/ppermute | solution.py:467
  48.0 3.6 %collective-permute-start.20 = (bf16[128,1536]{1,0:T(8,128)(2,1)S(1)}, bf16[128,1536]{1,0:T(8,128)(2,1)S(1)}, u32[]{:S(2)}, u32[]{:S(2)}) collective-permute-start(bf16[128,1536]{1,0:T(8,128)(2,1)S(1)} %get-tuple-element.93), channel_id=1, source_target_pairs={{0,1},{1,0},{2,3},{3,2},{4,5},{5,4},{6,7},{7,6},{8,9},{9,8},{10,11... | collective-permute-start | bytes 1179656 | tf_op jit(solution)/shard_map/core_sum_1b/ppermute | solution.py:462
  48.0 4.6 %collective-permute-start.21 = (bf16[128,1536]{1,0:T(8,128)(2,1)S(1)}, bf16[128,1536]{1,0:T(8,128)(2,1)S(1)}, u32[]{:S(2)}, u32[]{:S(2)}) collective-permute-start(bf16[128,1536]{1,0:T(8,128)(2,1)S(1)} %get-tuple-element.105), channel_id=1, source_target_pairs={{0,1},{1,0},{2,3},{3,2},{4,5},{5,4},{6,7},{7,6},{8,9},{9,8},{10,11... | collective-permute-start | bytes 1179656 | tf_op jit(solution)/shard_map/core_sum_2b/ppermute | solution.py:462
  48.5 2.0 %copy-start.2 = (f32[6144]{0:T(1024)S(1)}, f32[6144]{0:T(1024)}, u32[]{:S(2)}) copy-start(f32[6144]{0:T(1024)} %param.11) | copy-start | bytes 73732
  48.5 12.7 %slice-start.3 = ((s8[18874368]{0:T(1024)(128)(4,1)}), s8[4194304]{0:T(1024)(128)(4,1)S(1)}, s32[]{:S(2)}) async-start(s8[18874368]{0:T(1024)(128)(4,1)} %bitcast.6), calls=%async_computation.3 | async-start | bytes 8388608
  48.5 12.7 %slice-start.4 = ((s8[18874368]{0:T(1024)(128)(4,1)}), s8[4194304]{0:T(1024)(128)(4,1)S(1)}, s32[]{:S(2)}) async-start(s8[18874368]{0:T(1024)(128)(4,1)} %bitcast.6), calls=%async_computation.4 | async-start | bytes 8388608
  49.9 3.8 %collective-permute-start.16 = (bf16[128,768]{1,0:T(8,128)(2,1)S(1)}, bf16[128,768]{1,0:T(8,128)(2,1)S(1)}, u32[]{:S(2)}, u32[]{:S(2)}) collective-permute-start(bf16[128,768]{1,0:T(8,128)(2,1)S(1)} %get-tuple-element.117), channel_id=1, source_target_pairs={{0,1},{1,0},{2,3},{3,2},{4,5},{5,4},{6,7},{7,6},{8,9},{9,8},{10,11... | collective-permute-start | bytes 589832 | tf_op jit(solution)/shard_map/core_sum_3b/ppermute | solution.py:462
  50.0 3.7 %collective-permute-start.17 = (bf16[128,768]{1,0:T(8,128)(2,1)S(1)}, bf16[128,768]{1,0:T(8,128)(2,1)S(1)}, u32[]{:S(2)}, u32[]{:S(2)}) collective-permute-start(bf16[128,768]{1,0:T(8,128)(2,1)S(1)} %get-tuple-element.118), channel_id=1, source_target_pairs={{0,1},{1,0},{2,3},{3,2},{4,5},{5,4},{6,7},{7,6},{8,9},{9,8},{10,11... | collective-permute-start | bytes 589832 | tf_op jit(solution)/shard_map/core_sum_3b/ppermute | solution.py:462
  59.2 1.9 %collective-permute-start.24 = (f32[2,1536]{1,0:T(2,128)S(1)}, f32[2,1536]{1,0:T(2,128)S(1)}, u32[]{:S(2)}, u32[]{:S(2)}) collective-permute-start(f32[2,1536]{1,0:T(2,128)S(1)} %pool_all.1.refs_0_), channel_id=1, source_target_pairs={{0,1},{1,0},{2,3},{3,2},{4,5},{5,4},{6,7},{7,6},{8,9},{9,8},{10,11... | collective-permute-start | bytes 36872 | tf_op jit(solution)/shard_map/core_pool/ppermute | solution.py:462
  59.3 3.8 %collective-permute-start.22 = (f32[2,1536]{1,0:T(2,128)S(1)}, f32[2,1536]{1,0:T(2,128)S(1)}, u32[]{:S(2)}, u32[]{:S(2)}) collective-permute-start(f32[2,1536]{1,0:T(2,128)S(1)} %pool_all.1.refs_0_), channel_id=1, source_target_pairs={{0,2},{2,0},{1,3},{3,1},{4,6},{6,4},{5,7},{7,5},{8,10},{10,8},{9,1... | collective-permute-start | bytes 36872 | tf_op jit(solution)/shard_map/chip_pool/ppermute | solution.py:467
  60.1 3.1 %collective-permute-start.23 = (f32[2,1536]{1,0:T(2,128)S(1)}, f32[2,1536]{1,0:T(2,128)S(1)}, u32[]{:S(2)}, u32[]{:S(2)}) collective-permute-start(f32[2,1536]{1,0:T(2,128)S(1)} %pool_all.1.refs_0_), channel_id=1, source_target_pairs={{0,3},{1,2},{2,1},{3,0},{4,7},{5,6},{6,5},{7,4},{8,11},{9,10},{10,... | collective-permute-start | bytes 36872 | tf_op jit(solution)/shard_map/both_pool/ppermute | solution.py:472
  62.5 6.4 %copy-start = (bf16[64,6144]{1,0:T(8,128)(2,1)S(1)}, bf16[64,6144]{1,0:T(8,128)(2,1)}, u32[]{:S(2)}) copy-start(bf16[64,6144]{1,0:T(8,128)(2,1)} %captions.1) | copy-start | bytes 2359300
  62.6 15.6 %copy-start.3 = (f32[6144]{0:T(1024)S(1)}, f32[6144]{0:T(1024)}, u32[]{:S(2)}) copy-start(f32[6144]{0:T(1024)} %param.13) | copy-start | bytes 73732
  62.6 15.5 %copy-start.4 = (s32[64]{0:T(128)S(1)}, s32[64]{0:T(128)}, u32[]{:S(2)}) copy-start(s32[64]{0:T(128)} %param.15) | copy-start | bytes 772
  64.5 4.7 %collective-permute-start.25 = (f32[2,1536]{1,0:T(2,128)S(1)}, f32[2,1536]{1,0:T(2,128)S(1)}, u32[]{:S(2)}, u32[]{:S(2)}) collective-permute-start(f32[2,1536]{1,0:T(2,128)S(1)} %mix.3), channel_id=1, source_target_pairs={{0,4},{4,0},{8,12},{12,8},{1,5},{5,1},{9,13},{13,9},{2,6},{6,2},{1... | collective-permute-start | bytes 36872 | tf_op jit(solution)/shard_map/swap_mixed/ppermute | solution.py:477
  64.8 4.9 %collective-permute-start.26 = (f32[2,1536]{1,0:T(2,128)S(1)}, f32[2,1536]{1,0:T(2,128)S(1)}, u32[]{:S(2)}, u32[]{:S(2)}) collective-permute-start(f32[2,1536]{1,0:T(2,128)S(1)} %mix.3), channel_id=1, source_target_pairs={{0,8},{8,0},{4,12},{12,4},{1,9},{9,1},{5,13},{13,5},{2,10},{10,2},... | collective-permute-start | bytes 36872 | tf_op jit(solution)/shard_map/skip_mixed/ppermute | solution.py:477
  68.0 5.5 %collective-permute-start.27 = (f32[2,1536]{1,0:T(2,128)S(1)}, f32[2,1536]{1,0:T(2,128)S(1)}, u32[]{:S(2)}, u32[]{:S(2)}) collective-permute-start(f32[2,1536]{1,0:T(2,128)S(1)} %mix.3), channel_id=1, source_target_pairs={{0,12},{12,0},{4,8},{8,4},{1,13},{13,1},{5,9},{9,5},{2,14},{14,2},... | collective-permute-start | bytes 36872 | tf_op jit(solution)/shard_map/ends_mixed/ppermute | solution.py:477
  73.5 1.9 %collective-permute-start.28 = (f32[2,1536]{1,0:T(2,128)S(1)}, f32[2,1536]{1,0:T(2,128)S(1)}, u32[]{:S(2)}, u32[]{:S(2)}) collective-permute-start(f32[2,1536]{1,0:T(2,128)S(1)} %add_add_fusion.own), channel_id=1, source_target_pairs={{0,1},{1,0},{2,3},{3,2},{4,5},{5,4},{6,7},{7,6},{8,9},{9,8},{10,11... | collective-permute-start | bytes 36872 | tf_op jit(solution)/shard_map/core_embed/ppermute | solution.py:462
  73.6 3.8 %collective-permute-start.29 = (f32[2,1536]{1,0:T(2,128)S(1)}, f32[2,1536]{1,0:T(2,128)S(1)}, u32[]{:S(2)}, u32[]{:S(2)}) collective-permute-start(f32[2,1536]{1,0:T(2,128)S(1)} %add_add_fusion.own), channel_id=1, source_target_pairs={{0,2},{2,0},{1,3},{3,1},{4,6},{6,4},{5,7},{7,5},{8,10},{10,8},{9,1... | collective-permute-start | bytes 36872 | tf_op jit(solution)/shard_map/chip_embed/ppermute | solution.py:467
  75.0 3.1 %collective-permute-start.30 = (f32[2,1536]{1,0:T(2,128)S(1)}, f32[2,1536]{1,0:T(2,128)S(1)}, u32[]{:S(2)}, u32[]{:S(2)}) collective-permute-start(f32[2,1536]{1,0:T(2,128)S(1)} %add_add_fusion.own), channel_id=1, source_target_pairs={{0,3},{1,2},{2,1},{3,0},{4,7},{5,6},{6,5},{7,4},{8,11},{9,10},{10,... | collective-permute-start | bytes 36872 | tf_op jit(solution)/shard_map/both_embed/ppermute | solution.py:472

commit v4 on v3

--- a/solution.py
+++ b/solution.py
@@ -190,47 +190,41 @@
     )(*(pltpu.with_memory_space_constraint(value, pltpu.HBM) for value in (tokens, gain, w)))
 
 
-def first_b_kernel(tokens, gain, w, give, keep, keep_gain, give_held, keep_held, resid, sems):
-    to_give, own = quarters()[2:]
-    give_copies = column_copies(to_give, w, give_held, sems, 0)
-    keep_copies = column_copies(own, w, keep_held, sems, PIECES)
+def first_give_kernel(tokens, gain, w, give, held, resid, sems):
+    copies = column_copies(quarters()[2], w, held, sems, 0)
     values = tokens[...].astype(F32)
     rows = values.shape[0]
-    left = with_gain(values, gain[...])
     resid[...] = jnp.sum(values, axis=0, keepdims=True) / PATCHES
 
-    def give_store(at, size, product, of_gain):
+    def store(at, size, product, of_gain):
         give[0:rows, pl.ds(at, size)] = product.astype(BF16)
         give[rows:, pl.ds(at, size)] = row_block(thirds(of_gain), (16, size))
 
-    def keep_store(at, size, product, of_gain):
+    first_products(with_gain(values, gain[...]), held, copies, store)
+
+
+def first_keep_kernel(tokens, gain, w, keep, keep_gain, held, sems):
+    copies = column_copies(quarters()[3], w, held, sems, 0)
+
+    def store(at, size, product, of_gain):
         keep[:, pl.ds(at, size)] = product
         keep_gain[:, pl.ds(at, size)] = of_gain
 
-    first_products(left, give_held, give_copies, give_store)
-    first_products(left, keep_held, keep_copies, keep_store)
-
-
-def first_b(tokens, gain, w):
+    first_products(with_gain(tokens[...].astype(F32), gain[...]), held, copies, store)
+
+
+def first_part(kernel, name, tokens, gain, w, shapes):
     rows, depth = tokens.shape
     share = w.shape[1] // 4
-    held = pltpu.VMEM((depth, share), BF16)
-    return pl.pallas_call(
-        first_b_kernel,
-        name="first_b",
-        out_shape=(
-            struct((rows + 16, share), BF16),
-            struct((rows, share)),
-            struct((1, share)),
-            held,
-            held,
-            struct((1, depth)),
-        ),
+    return pl.pallas_call(
+        kernel,
+        name=name,
+        out_shape=shapes,
         in_specs=[WHOLE, WHOLE, IN_HBM],
-        out_specs=(WHOLE,) * 6,
-        scratch_shapes=[pltpu.SemaphoreType.DMA((2 * PIECES,))],
+        out_specs=(WHOLE,) * len(shapes),
+        scratch_shapes=[pltpu.SemaphoreType.DMA((PIECES,))],
         compiler_params=params(8),
-        cost_estimate=cost(4 * rows * depth * share, 4 * depth * share),
+        cost_estimate=cost(2 * rows * depth * share, 2 * depth * share),
     )(tokens, gain, pltpu.with_memory_space_constraint(w, pltpu.HBM))
 
 
@@ -521,7 +515,7 @@
             lambda *refs: later_a_kernel(len(rows_of), *refs),
             (*rows_of, after(gain, ready_after), held_a),
             (*halves, struct((rows, share)), struct((rows, depth), BF16), struct((1, 2 * rows))),
-            1024,
+            4 * rows * depth * share,
         )
         gots = after([other_core(f"core_sum_{index}a", give) for give in gives], sums_after)
         return ready, *chip_sum(index, keep, gots, own)
@@ -540,17 +534,33 @@
         return [other_core(f"core_sum_{index}b", give) for give in gives]
 
     ready_1, chip_1, note_1, far_1 = later_a(1, (near,), ())
-    give_0, keep_0, keep_gain, give_held, keep_held, resid = first_b(after(tokens, chip_1), gain, w_in)
-    far_0, crossed = after((far_0, crossed), keep_0)
-    give_1, keep_1 = later_b(1, ready_1, far_0, crossed)
+    keep_0, keep_gain, keep_held = first_part(
+        first_keep_kernel,
+        "first_keep",
+        after(tokens, chip_1),
+        gain,
+        w_in,
+        (struct((rows, share)), struct((1, share)), pltpu.VMEM((depth, share), BF16)),
+    )
+    passed, crossed, far_0 = after(passed, keep_0), after(crossed, keep_0), after(far_0, keep_0)
     last = along("last_rows", crossed, OUTWARD)
 
-    ready_2, chip_2, note_2, far_2 = later_a(2, (middle, passed), give_1, far_1)
-    last = after(last, chip_2)
-    give_2, keep_2 = later_b(2, ready_2, chip_2, last)
-
-    ready_3, chip_3, note_3, far_3 = later_a(3, (crossed, last), give_2, far_2)
-    *gives_3, keep_3 = later_b(3, ready_3, chip_3)
+    ready_2, chip_2, note_2, far_2 = later_a(2, (middle, passed), far_0)
+    give_0, give_held, resid = first_part(
+        first_give_kernel,
+        "first_give",
+        after(tokens, chip_2),
+        gain,
+        w_in,
+        (struct((rows + 16, share), BF16), pltpu.VMEM((depth, share), BF16), struct((1, depth))),
+    )
+    far_1 = after(far_1, give_0)
+    give_1, keep_1 = later_b(1, ready_1, far_1)
+
+    ready_3, chip_3, note_3, far_3 = later_a(3, (crossed, last), give_1)
+    far_2 = after(far_2, chip_3)
+    give_2, keep_2 = later_b(2, ready_2, far_2)
+    *gives_3, keep_3 = later_b(3, ready_3, give_2)
     nears_0, nears_1, nears_2, nears_3 = send(0, [give_0]), send(1, [give_1]), send(2, [give_2]), send(3, gives_3)
     gains = small(
         lambda *refs: all_gains_kernel(rows, *refs),

time: 79.3 us -> 75.6 us (0.953)
  waiting for transfers between devices: 28.1 us -> 22.4 us
  Pallas kernels: 26.7 us -> 28.3 us
    ppermute x8, waiting for transfers between devices: 13.9 us -> 9.83 us  [along(): return lax.ppermute(value, 'mrow', list(pairs))]
    ppermute x6, waiting for transfers between devices: 8.86 us -> 7.38 us  [other_chip(): return lax.ppermute(value, 'mcol', [(0, 1), (1, 0)])]
    pallas_call x1 -> x2, Pallas kernels: 4.65 us -> 5.99 us  [first_part(): pl.pallas_call(kernel, name=name, out_shape=shapes, in_specs=[WHOLE, WHOL...]
  transfers between devices with their start and end apart: 31 -> 31, of which waited for: 15 -> 15; matrix products, arithmetic and copies ran while one was open for 0% -> 0% of each run, Pallas kernels for 29% -> 33%
where the time goes in v4:
time: 75.6 us; the launch traced here: 75.4 us
  Pallas kernels  28.3 us (37%)
  starting transfers between devices  24 us (32%)
  waiting for transfers between devices  22.4 us (30%)
    ppermute x8, starting transfers between devices, along(): return lax.ppermute(value, 'mrow', list(pairs))  11.5 us
    ppermute x8, waiting for transfers between devices, along(): return lax.ppermute(value, 'mrow', list(pairs))  9.83 us
    pallas_call x6, Pallas kernels, later_block(): pl.pallas_call(kernel, name='later_block', out_shape=out, in_specs=[WHOLE...  8.94 us
    ppermute x6, waiting for transfers between devices, other_chip(): return lax.ppermute(value, 'mcol', [(0, 1), (1, 0)])  7.38 us
    ppermute x6, starting transfers between devices, other_chip(): return lax.ppermute(value, 'mcol', [(0, 1), (1, 0)])  7.06 us
    pallas_call x2, Pallas kernels, first_part(): pl.pallas_call(kernel, name=name, out_shape=shapes, in_specs=[WHOLE, WHOL...  5.99 us
    pallas_call x1, Pallas kernels, first_a(): pl.pallas_call(first_a_kernel, name='first_a', out_shape=(struct((rows +...  4.77 us
    ppermute x15, waiting for transfers between devices, other_core(): return lax.ppermute(value, 'sub', [(0, 1), (1, 0)])  4.54 us
  transfers between devices with their start and end apart: 31, of which 15 were waited for; matrix products, arithmetic and copies ran while one was open for 0% of the time, Pallas kernels for 33%

profile of v4, /device:TPU:0, one launch (start us, length us, event | category | flops | bytes accessed | tf_op | source)
XLA Modules:
  0.0 75.4 jit_solution(5414792946333991974)
XLA Ops:
  0.0 3.0 %collective-permute-start = (bf16[128,1536]{1,0:T(8,128)(2,1)}, bf16[128,1536]{1,0:T(8,128)(2,1)S(1)}, u32[]{:S(2)}, u32[]{:S(2)}) collective-permute-start(bf16[128,1536]{1,0:T(8,128)(2,1)} %tokens.3), channel_id=1, source_target_pairs={{0,4},{4,0},{8,12},{12,8},{1,5},{5,1},{9,13},{13,9},{2,6},{6,2},{1... | collective-permute-start | bytes 1179656 | tf_op jit(solution)/shard_map/near_rows/ppermute | solution.py:471
  3.0 0.7 collective-permute-start.8
  3.7 4.8 %first_a.1 = (bf16[144,768]{1,0:T(8,128)(2,1)S(1)}, bf16[144,768]{1,0:T(8,128)(2,1)S(1)}, f32[128,1536]{1,0:T(8,128)S(1)}, f32[1,1536]{1,0:T(1,128)S(1)}, f32[1,...) custom-call(bf16[128,1536]{1,0:T(8,128)(2,1)} %tokens.3, f32[1536]{0:T(1024)} %gain.1, ...), custom_call_target="tpu_custom_call" | custom-call | flops 1024 | bytes 1024 | tf_op jit(solution)/shard_map/first_a/pallas_call | solution.py:173
  8.5 0.1 collective-permute-start.1
  8.6 0.5 collective-permute-start.2
  9.1 1.0 %collective-permute-done.1.first = bf16[144,768]{1,0:T(8,128)(2,1)S(1)} collective-permute-done((bf16[144,768]{1,0:T(8,128)(2,1)S(1)}, bf16[144,768]{1,0:T(8,128)(2,1)S(1)}, u32[]{:S(2)}, u32[]{:S(2)}) %collective-permute-start.1) | collective-permute-done | bytes 221216 | tf_op jit(solution)/shard_map/core_sum_0a/ppermute | solution.py:456
  10.0 0.3 collective-permute-done.2.second
  10.3 0.1 chip_sum.4
  10.5 1.6 %collective-permute-start.10 = (bf16[136,1536]{1,0:T(8,128)(2,1)S(1)}, bf16[136,1536]{1,0:T(8,128)(2,1)S(1)}, u32[]{:S(2)}, u32[]{:S(2)}) collective-permute-start(bf16[136,1536]{1,0:T(8,128)(2,1)S(1)} %get-tuple-element.76), channel_id=1, source_target_pairs={{0,2},{2,0},{1,3},{3,1},{4,6},{6,4},{5,7},{7,5},{8,10},{10,8},{9,1... | collective-permute-start | bytes 1253384 | tf_op jit(solution)/shard_map/chip_sum_0/ppermute | solution.py:461
  12.0 0.3 collective-permute-done.refs_0_
  12.3 1.3 %collective-permute-start.9 = (bf16[128,1536]{1,0:T(8,128)(2,1)S(1)}, bf16[128,1536]{1,0:T(8,128)(2,1)S(1)}, u32[]{:S(2)}, u32[]{:S(2)}) collective-permute-start(bf16[128,1536]{1,0:T(8,128)(2,1)S(1)} %collective-permute-done.8.refs_0_), channel_id=1, source_target_pairs={{4,0},{8,12},{5,1},{9,13},{6,2},{10,14},{7,3},{11,15},{20,16},{24,... | collective-permute-start | bytes 1179656 | tf_op jit(solution)/shard_map/passed_rows/ppermute | solution.py:471
  13.6 0.7 collective-permute-start.3
  14.3 1.6 %later_block.6 = (bf16[144,768]{1,0:T(8,128)(2,1)S(1)}, bf16[128,768]{1,0:T(8,128)(2,1)S(1)}, f32[128,1536]{1,0:T(8,128)S(1)}, bf16[128,1536]{1,0:T(8,128)(2,1)S(1)}, f32[1,256]{1,0:T(1,128)S(1)}) custom-call(bf16[128,1536]{1,0:T(8,128)(2,1)S(1)} %collective-permute-done.refs_0_, f32[1,1536]{1,0:T(1,128)S(1)} %get-tuple-element.109.refs_1_.gain.refs_2_, ...), custom_call_target="tpu_custom_call" | custom-call | flops 1207959552 | bytes 1024 | tf_op jit(solution)/shard_map/later_block/pallas_call | solution.py:265
  15.9 0.1 collective-permute-start.4
  16.0 0.5 collective-permute-start.5
  16.5 1.2 %collective-permute-done.5.second = bf16[128,768]{1,0:T(8,128)(2,1)S(1)} collective-permute-done((bf16[128,768]{1,0:T(8,128)(2,1)S(1)}, bf16[128,768]{1,0:T(8,128)(2,1)S(1)}, u32[]{:S(2)}, u32[]{:S(2)}) %collective-permute-start.5) | collective-permute-done | bytes 196640 | tf_op jit(solution)/shard_map/core_sum_1a/ppermute | solution.py:456
  17.8 0.1 chip_sum.5
  17.9 1.7 %collective-permute-start.7 = (bf16[136,1536]{1,0:T(8,128)(2,1)S(1)}, bf16[136,1536]{1,0:T(8,128)(2,1)S(1)}, u32[]{:S(2)}, u32[]{:S(2)}) collective-permute-start(bf16[136,1536]{1,0:T(8,128)(2,1)S(1)} %get-tuple-element.86), channel_id=1, source_target_pairs={{0,2},{2,0},{1,3},{3,1},{4,6},{6,4},{5,7},{7,5},{8,10},{10,8},{9,1... | collective-permute-start | bytes 1253384 | tf_op jit(solution)/shard_map/chip_sum_1/ppermute | solution.py:461
  19.6 2.9 %first_keep.1 = (f32[128,1536]{1,0:T(8,128)S(1)}, f32[1,1536]{1,0:T(1,128)S(1)}, bf16[1536,1536]{1,0:T(8,128)(2,1)S(1)}) custom-call(bf16[128,1536]{1,0:T(8,128)(2,1)S(1)} %copy-done, f32[1,1536]{1,0:T(1,128)S(1)} %get-tuple-element.109.refs_1_.gain.refs_2_, bf16[1536,6144]{1,0:T(8,128)(2,1)} %w.5), custom_call_target="tpu_custom_call" | custom-call | flops 1024 | bytes 1024 | tf_op jit(solution)/shard_map/first_keep/pallas_call | solution.py:219
  22.5 0.5 collective-permute-done.10.refs_2_
  23.0 3.9 %collective-permute-done.9.refs_1_ = bf16[128,1536]{1,0:T(8,128)(2,1)S(1)} collective-permute-done((bf16[128,1536]{1,0:T(8,128)(2,1)S(1)}, bf16[128,1536]{1,0:T(8,128)(2,1)S(1)}, u32[]{:S(2)}, u32[]{:S(2)}) %collective-permute-start.9) | collective-permute-done | bytes 393248 | tf_op jit(solution)/shard_map/passed_rows/ppermute | solution.py:471
  26.9 1.5 %collective-permute-start.6 = (bf16[128,1536]{1,0:T(8,128)(2,1)S(1)}, bf16[128,1536]{1,0:T(8,128)(2,1)S(1)}, u32[]{:S(2)}, u32[]{:S(2)}) collective-permute-start(bf16[128,1536]{1,0:T(8,128)(2,1)S(1)} %collective-permute-done.3.refs_0_), channel_id=1, source_target_pairs={{4,0},{8,12},{5,1},{9,13},{6,2},{10,14},{7,3},{11,15},{20,16},{24,... | collective-permute-start | bytes 1179656 | tf_op jit(solution)/shard_map/last_rows/ppermute | solution.py:471
  28.4 1.6 %later_block.7 = (bf16[144,768]{1,0:T(8,128)(2,1)S(1)}, bf16[128,768]{1,0:T(8,128)(2,1)S(1)}, f32[128,1536]{1,0:T(8,128)S(1)}, bf16[128,1536]{1,0:T(8,128)(2,1)S(1)}, f32[1,256]{1,0:T(1,128)S(1)}) custom-call(bf16[128,1536]{1,0:T(8,128)(2,1)S(1)} %collective-permute-done.8.refs_0_, bf16[128,1536]{1,0:T(8,128)(2,1)S(1)} %collective-permute-done.9.refs_1_, ...), custom_call_target="tpu_custom_call" | custom-call | flops 1207959552 | bytes 1024 | tf_op jit(solution)/shard_map/later_block/pallas_call | solution.py:265
  30.0 0.1 collective-permute-start.11
  30.0 0.5 collective-permute-start.12
  30.5 1.2 %collective-permute-done.12.second = bf16[128,768]{1,0:T(8,128)(2,1)S(1)} collective-permute-done((bf16[128,768]{1,0:T(8,128)(2,1)S(1)}, bf16[128,768]{1,0:T(8,128)(2,1)S(1)}, u32[]{:S(2)}, u32[]{:S(2)}) %collective-permute-start.12) | collective-permute-done | bytes 196640 | tf_op jit(solution)/shard_map/core_sum_2a/ppermute | solution.py:456
  31.8 0.1 chip_sum.6
  31.9 1.3 %collective-permute-start.13 = (bf16[136,1536]{1,0:T(8,128)(2,1)S(1)}, bf16[136,1536]{1,0:T(8,128)(2,1)S(1)}, u32[]{:S(2)}, u32[]{:S(2)}) collective-permute-start(bf16[136,1536]{1,0:T(8,128)(2,1)S(1)} %get-tuple-element.101), channel_id=1, source_target_pairs={{0,2},{2,0},{1,3},{3,1},{4,6},{6,4},{5,7},{7,5},{8,10},{10,8},{9,1... | collective-permute-start | bytes 1253384 | tf_op jit(solution)/shard_map/chip_sum_2/ppermute | solution.py:461
  33.2 3.1 %first_give.1 = (bf16[144,1536]{1,0:T(8,128)(2,1)S(1)}, bf16[1536,1536]{1,0:T(8,128)(2,1)S(1)}, f32[1,1536]{1,0:T(1,128)S(1)}) custom-call(bf16[128,1536]{1,0:T(8,128)(2,1)S(1)} %copy-done, f32[1,1536]{1,0:T(1,128)S(1)} %get-tuple-element.109.refs_1_.gain.refs_2_, bf16[1536,6144]{1,0:T(8,128)(2,1)} %w.5), custom_call_target="tpu_custom_call" | custom-call | flops 1024 | bytes 1024 | tf_op jit(solution)/shard_map/first_give/pallas_call | solution.py:219
  36.3 1.4 %later_block.8 = (bf16[128,1536]{1,0:T(8,128)(2,1)S(1)}, f32[128,1536]{1,0:T(8,128)S(1)}) custom-call(bf16[128,1536]{1,0:T(8,128)(2,1)S(1)} %get-tuple-element.105.left, bf16[1536,1536]{1,0:T(8,128)(2,1)S(1)} %get-tuple-element.106.give_held, bf16[1536,1536]{1,0:T(8,128)(2,1)S(1)} %get-tuple-element.107.keep_held), custom_call_target="tpu_custom_call" | custom-call | flops 1207959552 | bytes 1024 | tf_op jit(solution)/shard_map/later_block/pallas_call | solution.py:265
  37.7 2.9 %collective-permute-done.6.refs_1_ = bf16[128,1536]{1,0:T(8,128)(2,1)S(1)} collective-permute-done((bf16[128,1536]{1,0:T(8,128)(2,1)S(1)}, bf16[128,1536]{1,0:T(8,128)(2,1)S(1)}, u32[]{:S(2)}, u32[]{:S(2)}) %collective-permute-start.6) | collective-permute-done | bytes 393248 | tf_op jit(solution)/shard_map/last_rows/ppermute | solution.py:471
  40.6 1.6 %later_block.9 = (bf16[144,768]{1,0:T(8,128)(2,1)S(1)}, bf16[128,768]{1,0:T(8,128)(2,1)S(1)}, f32[128,1536]{1,0:T(8,128)S(1)}, bf16[128,1536]{1,0:T(8,128)(2,1)S(1)}, f32[1,256]{1,0:T(1,128)S(1)}) custom-call(bf16[128,1536]{1,0:T(8,128)(2,1)S(1)} %collective-permute-done.3.refs_0_, bf16[128,1536]{1,0:T(8,128)(2,1)S(1)} %collective-permute-done.6.refs_1_, ...), custom_call_target="tpu_custom_call" | custom-call | flops 1207959552 | bytes 1024 | tf_op jit(solution)/shard_map/later_block/pallas_call | solution.py:265
  42.3 0.5 collective-permute-start.15
  42.8 0.1 collective-permute-start.19
  42.9 0.4 collective-permute-start.20
  43.3 0.7 collective-permute-done.15.second
  44.0 0.1 chip_sum.7
  44.1 0.6 collective-permute-start.18
  44.8 1.4 %later_block.10 = (bf16[128,1536]{1,0:T(8,128)(2,1)S(1)}, f32[128,1536]{1,0:T(8,128)S(1)}) custom-call(bf16[128,1536]{1,0:T(8,128)(2,1)S(1)} %get-tuple-element.120.left, bf16[1536,1536]{1,0:T(8,128)(2,1)S(1)} %get-tuple-element.106.give_held, bf16[1536,1536]{1,0:T(8,128)(2,1)S(1)} %get-tuple-element.107.keep_held), custom_call_target="tpu_custom_call" | custom-call | flops 1207959552 | bytes 1024 | tf_op jit(solution)/shard_map/later_block/pallas_call | solution.py:265
  46.3 1.4 %later_block.11 = (bf16[128,768]{1,0:T(8,128)(2,1)S(1)}, bf16[128,768]{1,0:T(8,128)(2,1)S(1)}, f32[128,1536]{1,0:T(8,128)S(1)}) custom-call(bf16[128,1536]{1,0:T(8,128)(2,1)S(1)} %get-tuple-element.122.left, bf16[1536,1536]{1,0:T(8,128)(2,1)S(1)} %get-tuple-element.106.give_held, bf16[1536,1536]{1,0:T(8,128)(2,1)S(1)} %get-tuple-element.107.keep_held), custom_call_target="tpu_custom_call" | custom-call | flops 1207959552 | bytes 1024 | tf_op jit(solution)/shard_map/later_block/pallas_call | solution.py:265
  47.7 0.5 collective-permute-start.16
  48.2 0.1 collective-permute-start.17
  48.3 1.0 %pool.3.refs_7_ = f32[1,1536]{1,0:T(1,128)S(1)} custom-call(f32[128,1536]{1,0:T(8,128)S(1)} %get-tuple-element.88.refs_0_, bf16[144,1536]{1,0:T(8,128)(2,1)S(1)} %collective-permute-done.19.refs_1_, bf16[136,1536]{1,0:T(8,128)(2,1)S(1)} %collective-permute-done.10.refs_2_, f32[1,6144]{1,0:T(1,128)S(1)} %bitcast.8, f32[8,1536]{1,0:T(8,128)S(1)} %all_gains.1.refs_4_.refs_5_, ...), custom_call_target="tpu_custom_call" | custom-call | flops 1024 | bytes 1024 | tf_op jit(solution)/shard_map/pool/pallas_call | solution.py:348
  49.4 1.1 %pool.4.refs_8_ = f32[1,1536]{1,0:T(1,128)S(1)} custom-call(f32[128,1536]{1,0:T(8,128)S(1)} %get-tuple-element.130.refs_0_, bf16[128,1536]{1,0:T(8,128)(2,1)S(1)} %collective-permute-done.20.refs_1_, bf16[136,1536]{1,0:T(8,128)(2,1)S(1)} %collective-permute-done.7.refs_2_, f32[1,6144]{1,0:T(1,128)S(1)} %bitcast.9, f32[8,1536]{1,0:T(8,128)S(1)} %all_gains.1.refs_4_.refs_5_, ...), custom_call_target="tpu_custom_call" | custom-call | flops 1024 | bytes 1024 | tf_op jit(solution)/shard_map/pool/pallas_call | solution.py:348
  50.4 1.1 %pool.5.refs_9_ = f32[1,1536]{1,0:T(1,128)S(1)} custom-call(f32[128,1536]{1,0:T(8,128)S(1)} %get-tuple-element.132.refs_0_, bf16[128,1536]{1,0:T(8,128)(2,1)S(1)} %collective-permute-done.21.refs_1_, bf16[136,1536]{1,0:T(8,128)(2,1)S(1)} %collective-permute-done.13.refs_2_, f32[1,6144]{1,0:T(1,128)S(1)} %bitcast.10, f32[8,1536]{1,0:T(8,128)S(1)} %all_gains.1.refs_4_.refs_5_, ...), custom_call_target="tpu_custom_call" | custom-call | flops 1024 | bytes 1024 | tf_op jit(solution)/shard_map/pool/pallas_call | solution.py:348
  51.5 4.4 %collective-permute-done.18.refs_3_ = bf16[136,1536]{1,0:T(8,128)(2,1)S(1)} collective-permute-done((bf16[136,1536]{1,0:T(8,128)(2,1)S(1)}, bf16[136,1536]{1,0:T(8,128)(2,1)S(1)}, u32[]{:S(2)}, u32[]{:S(2)}) %collective-permute-start.18) | collective-permute-done | bytes 417824 | tf_op jit(solution)/shard_map/chip_sum_3/ppermute | solution.py:461
  56.0 1.3 %pool_all.1.refs_0_ = f32[2,1536]{1,0:T(2,128)S(1)} custom-call(f32[128,1536]{1,0:T(8,128)S(1)} %get-tuple-element.123.refs_0_, bf16[128,768]{1,0:T(8,128)(2,1)S(1)} %collective-permute-done.16.refs_1_, bf16[128,768]{1,0:T(8,128)(2,1)S(1)} %collective-permute-done.17.refs_2_, bf16[136,1536]{1,0:T(8,128)(2,1)S(1)} %collective-permute-done.18.refs_3_, ...), custom_call_target="tpu_custom_call" | custom-call | flops 1024 | bytes 1024 | tf_op jit(solution)/shard_map/pool_all/pallas_call | solution.py:374
  57.3 0.6 collective-permute-start.22
  57.9 1.3 %collective-permute-start.23 = (f32[2,1536]{1,0:T(2,128)S(1)}, f32[2,1536]{1,0:T(2,128)S(1)}, u32[]{:S(2)}, u32[]{:S(2)}) collective-permute-start(f32[2,1536]{1,0:T(2,128)S(1)} %pool_all.1.refs_0_), channel_id=1, source_target_pairs={{0,3},{1,2},{2,1},{3,0},{4,7},{5,6},{6,5},{7,4},{8,11},{9,10},{10,... | collective-permute-start | bytes 36872 | tf_op jit(solution)/shard_map/both_pool/ppermute | solution.py:466
  59.2 1.3 %mix.2.refs_2_ = f32[2,1536]{1,0:T(2,128)S(1)} custom-call(f32[2,1536]{1,0:T(2,128)S(1)} %pool_all.1.refs_0_, f32[2,1536]{1,0:T(2,128)S(1)} %collective-permute-done.24.refs_1_, f32[1,1536]{1,0:T(1,128)S(1)} %get-tuple-element.134.refs_2_, bf16[6144,1536]{1,0:T(8,128)(2,1)S(1)} %bitcast.7), custom_call_target="tpu_custom_call" | custom-call | flops 1024 | bytes 1024 | tf_op jit(solution)/shard_map/mix/pallas_call | solution.py:406
  60.6 0.6 collective-permute-done.22.refs_0_
  61.2 1.3 %mix.3 = f32[2,1536]{1,0:T(2,128)S(1)} custom-call(f32[2,1536]{1,0:T(2,128)S(1)} %collective-permute-done.22.refs_0_, f32[2,1536]{1,0:T(2,128)S(1)} %collective-permute-done.23.refs_1_, f32[2,1536]{1,0:T(2,128)S(1)} %mix.2.refs_2_, bf16[6144,1536]{1,0:T(8,128)(2,1)S(1)} %bitcast.7), custom_call_target="tpu_custom_call" | custom-call | flops 1024 | bytes 1024 | tf_op jit(solution)/shard_map/mix/pallas_call | solution.py:406
  62.5 1.0 %collective-permute-start.25 = (f32[2,1536]{1,0:T(2,128)S(1)}, f32[2,1536]{1,0:T(2,128)S(1)}, u32[]{:S(2)}, u32[]{:S(2)}) collective-permute-start(f32[2,1536]{1,0:T(2,128)S(1)} %mix.3), channel_id=1, source_target_pairs={{0,4},{4,0},{8,12},{12,8},{1,5},{5,1},{9,13},{13,9},{2,6},{6,2},{1... | collective-permute-start | bytes 36872 | tf_op jit(solution)/shard_map/swap_mixed/ppermute | solution.py:471
  63.5 0.9 %collective-permute-start.26 = (f32[2,1536]{1,0:T(2,128)S(1)}, f32[2,1536]{1,0:T(2,128)S(1)}, u32[]{:S(2)}, u32[]{:S(2)}) collective-permute-start(f32[2,1536]{1,0:T(2,128)S(1)} %mix.3), channel_id=1, source_target_pairs={{0,8},{8,0},{4,12},{12,4},{1,9},{9,1},{5,13},{13,5},{2,10},{10,2},... | collective-permute-start | bytes 36872 | tf_op jit(solution)/shard_map/skip_mixed/ppermute | solution.py:471
  64.4 2.5 %collective-permute-start.27 = (f32[2,1536]{1,0:T(2,128)S(1)}, f32[2,1536]{1,0:T(2,128)S(1)}, u32[]{:S(2)}, u32[]{:S(2)}) collective-permute-start(f32[2,1536]{1,0:T(2,128)S(1)} %mix.3), channel_id=1, source_target_pairs={{0,12},{12,0},{4,8},{8,4},{1,13},{13,1},{5,9},{9,5},{2,14},{14,2},... | collective-permute-start | bytes 36872 | tf_op jit(solution)/shard_map/ends_mixed/ppermute | solution.py:471
  66.9 0.3 multiply_reduce_fusion
  67.2 1.0 %collective-permute-done.26 = f32[2,1536]{1,0:T(2,128)S(1)} collective-permute-done((f32[2,1536]{1,0:T(2,128)S(1)}, f32[2,1536]{1,0:T(2,128)S(1)}, u32[]{:S(2)}, u32[]{:S(2)}) %collective-permute-start.26) | collective-permute-done | bytes 12320 | tf_op jit(solution)/shard_map/skip_mixed/ppermute | solution.py:471
  68.2 1.7 %collective-permute-done.27 = f32[2,1536]{1,0:T(2,128)S(1)} collective-permute-done((f32[2,1536]{1,0:T(2,128)S(1)}, f32[2,1536]{1,0:T(2,128)S(1)}, u32[]{:S(2)}, u32[]{:S(2)}) %collective-permute-start.27) | collective-permute-done | bytes 12320 | tf_op jit(solution)/shard_map/ends_mixed/ppermute | solution.py:471
  69.9 0.1 collective-permute-start.28
  70.0 1.3 %collective-permute-start.29 = (f32[2,1536]{1,0:T(2,128)S(1)}, f32[2,1536]{1,0:T(2,128)S(1)}, u32[]{:S(2)}, u32[]{:S(2)}) collective-permute-start(f32[2,1536]{1,0:T(2,128)S(1)} %add_add_fusion.own), channel_id=1, source_target_pairs={{0,2},{2,0},{1,3},{3,1},{4,6},{6,4},{5,7},{7,5},{8,10},{10,8},{9,1... | collective-permute-start | bytes 36872 | tf_op jit(solution)/shard_map/chip_embed/ppermute | solution.py:461
  71.3 0.6 collective-permute-start.30
  71.9 1.9 %collective-permute-done.29.across = f32[2,1536]{1,0:T(2,128)S(1)} collective-permute-done((f32[2,1536]{1,0:T(2,128)S(1)}, f32[2,1536]{1,0:T(2,128)S(1)}, u32[]{:S(2)}, u32[]{:S(2)}) %collective-permute-start.29) | collective-permute-done | bytes 12320 | tf_op jit(solution)/shard_map/chip_embed/ppermute | solution.py:461
  73.8 0.6 collective-permute-done.30.both
  74.4 1.0 %score.1 = f32[1,64]{1,0:T(1,128)} custom-call(f32[2,1536]{1,0:T(2,128)S(1)} %add_add_fusion.own, f32[2,1536]{1,0:T(2,128)S(1)} %collective-permute-done.28.core, f32[2,1536]{1,0:T(2,128)S(1)} %collective-permute-done.29.across, f32[2,1536]{1,0:T(2,128)S(1)} %collective-permute-done.30.both, f32[1,6144]{1,0:T(1,128)S(1)} %bitcast.12, ...), custom_call_target="tpu_custom_call" | custom-call | flops 1024 | bytes 1024 | tf_op jit(solution)/shard_map/score/pallas_call | solution.py:443
  (43 shorter events, 0.4 us)
Async XLA Ops:
  0.0 12.3 %collective-permute-start = (bf16[128,1536]{1,0:T(8,128)(2,1)}, bf16[128,1536]{1,0:T(8,128)(2,1)S(1)}, u32[]{:S(2)}, u32[]{:S(2)}) collective-permute-start(bf16[128,1536]{1,0:T(8,128)(2,1)} %tokens.3), channel_id=1, source_target_pairs={{0,4},{4,0},{8,12},{12,8},{1,5},{5,1},{9,13},{13,9},{2,6},{6,2},{1... | collective-permute-start | bytes 1179656 | tf_op jit(solution)/shard_map/near_rows/ppermute | solution.py:471
  3.0 9.3 %collective-permute-start.8 = (bf16[128,1536]{1,0:T(8,128)(2,1)}, bf16[128,1536]{1,0:T(8,128)(2,1)S(1)}, u32[]{:S(2)}, u32[]{:S(2)}) collective-permute-start(bf16[128,1536]{1,0:T(8,128)(2,1)} %tokens.3), channel_id=1, source_target_pairs={{4,8},{8,4},{5,9},{9,5},{6,10},{10,6},{7,11},{11,7},{20,24},{24,20... | collective-permute-start | bytes 1179656 | tf_op jit(solution)/shard_map/middle_rows/ppermute | solution.py:471
  8.5 1.5 %collective-permute-start.1 = (bf16[144,768]{1,0:T(8,128)(2,1)S(1)}, bf16[144,768]{1,0:T(8,128)(2,1)S(1)}, u32[]{:S(2)}, u32[]{:S(2)}) collective-permute-start(bf16[144,768]{1,0:T(8,128)(2,1)S(1)} %get-tuple-element.72), channel_id=1, source_target_pairs={{0,1},{1,0},{2,3},{3,2},{4,5},{5,4},{6,7},{7,6},{8,9},{9,8},{10,11... | collective-permute-start | bytes 663560 | tf_op jit(solution)/shard_map/core_sum_0a/ppermute | solution.py:456
  8.6 1.8 %collective-permute-start.2 = (bf16[144,768]{1,0:T(8,128)(2,1)S(1)}, bf16[144,768]{1,0:T(8,128)(2,1)S(1)}, u32[]{:S(2)}, u32[]{:S(2)}) collective-permute-start(bf16[144,768]{1,0:T(8,128)(2,1)S(1)} %get-tuple-element.73), channel_id=1, source_target_pairs={{0,1},{1,0},{2,3},{3,2},{4,5},{5,4},{6,7},{7,6},{8,9},{9,8},{10,11... | collective-permute-start | bytes 663560 | tf_op jit(solution)/shard_map/core_sum_0a/ppermute | solution.py:456
  10.5 12.5 %collective-permute-start.10 = (bf16[136,1536]{1,0:T(8,128)(2,1)S(1)}, bf16[136,1536]{1,0:T(8,128)(2,1)S(1)}, u32[]{:S(2)}, u32[]{:S(2)}) collective-permute-start(bf16[136,1536]{1,0:T(8,128)(2,1)S(1)} %get-tuple-element.76), channel_id=1, source_target_pairs={{0,2},{2,0},{1,3},{3,1},{4,6},{6,4},{5,7},{7,5},{8,10},{10,8},{9,1... | collective-permute-start | bytes 1253384 | tf_op jit(solution)/shard_map/chip_sum_0/ppermute | solution.py:461
  12.3 14.5 %collective-permute-start.9 = (bf16[128,1536]{1,0:T(8,128)(2,1)S(1)}, bf16[128,1536]{1,0:T(8,128)(2,1)S(1)}, u32[]{:S(2)}, u32[]{:S(2)}) collective-permute-start(bf16[128,1536]{1,0:T(8,128)(2,1)S(1)} %collective-permute-done.8.refs_0_), channel_id=1, source_target_pairs={{4,0},{8,12},{5,1},{9,13},{6,2},{10,14},{7,3},{11,15},{20,16},{24,... | collective-permute-start | bytes 1179656 | tf_op jit(solution)/shard_map/passed_rows/ppermute | solution.py:471
  13.6 13.2 %collective-permute-start.3 = (bf16[128,1536]{1,0:T(8,128)(2,1)S(1)}, bf16[128,1536]{1,0:T(8,128)(2,1)S(1)}, u32[]{:S(2)}, u32[]{:S(2)}) collective-permute-start(bf16[128,1536]{1,0:T(8,128)(2,1)S(1)} %collective-permute-done.refs_0_), channel_id=1, source_target_pairs={{4,8},{8,4},{5,9},{9,5},{6,10},{10,6},{7,11},{11,7},{20,24},{24,20... | collective-permute-start | bytes 1179656 | tf_op jit(solution)/shard_map/crossed_rows/ppermute | solution.py:471
  14.3 5.3 %copy-start = (bf16[128,1536]{1,0:T(8,128)(2,1)S(1)}, bf16[128,1536]{1,0:T(8,128)(2,1)}, u32[]{:S(2)}) copy-start(bf16[128,1536]{1,0:T(8,128)(2,1)} %tokens.3) | copy-start | bytes 1179652
  15.9 1.8 %collective-permute-start.4 = (bf16[144,768]{1,0:T(8,128)(2,1)S(1)}, bf16[144,768]{1,0:T(8,128)(2,1)S(1)}, u32[]{:S(2)}, u32[]{:S(2)}) collective-permute-start(bf16[144,768]{1,0:T(8,128)(2,1)S(1)} %get-tuple-element.81), channel_id=1, source_target_pairs={{0,1},{1,0},{2,3},{3,2},{4,5},{5,4},{6,7},{7,6},{8,9},{9,8},{10,11... | collective-permute-start | bytes 663560 | tf_op jit(solution)/shard_map/core_sum_1a/ppermute | solution.py:456
  16.0 1.7 %collective-permute-start.5 = (bf16[128,768]{1,0:T(8,128)(2,1)S(1)}, bf16[128,768]{1,0:T(8,128)(2,1)S(1)}, u32[]{:S(2)}, u32[]{:S(2)}) collective-permute-start(bf16[128,768]{1,0:T(8,128)(2,1)S(1)} %get-tuple-element.82), channel_id=1, source_target_pairs={{0,1},{1,0},{2,3},{3,2},{4,5},{5,4},{6,7},{7,6},{8,9},{9,8},{10,11... | collective-permute-start | bytes 589832 | tf_op jit(solution)/shard_map/core_sum_1a/ppermute | solution.py:456
  17.9 18.4 %collective-permute-start.7 = (bf16[136,1536]{1,0:T(8,128)(2,1)S(1)}, bf16[136,1536]{1,0:T(8,128)(2,1)S(1)}, u32[]{:S(2)}, u32[]{:S(2)}) collective-permute-start(bf16[136,1536]{1,0:T(8,128)(2,1)S(1)} %get-tuple-element.86), channel_id=1, source_target_pairs={{0,2},{2,0},{1,3},{3,1},{4,6},{6,4},{5,7},{7,5},{8,10},{10,8},{9,1... | collective-permute-start | bytes 1253384 | tf_op jit(solution)/shard_map/chip_sum_1/ppermute | solution.py:461
  26.9 13.7 %collective-permute-start.6 = (bf16[128,1536]{1,0:T(8,128)(2,1)S(1)}, bf16[128,1536]{1,0:T(8,128)(2,1)S(1)}, u32[]{:S(2)}, u32[]{:S(2)}) collective-permute-start(bf16[128,1536]{1,0:T(8,128)(2,1)S(1)} %collective-permute-done.3.refs_0_), channel_id=1, source_target_pairs={{4,0},{8,12},{5,1},{9,13},{6,2},{10,14},{7,3},{11,15},{20,16},{24,... | collective-permute-start | bytes 1179656 | tf_op jit(solution)/shard_map/last_rows/ppermute | solution.py:471
  30.0 1.8 %collective-permute-start.11 = (bf16[144,768]{1,0:T(8,128)(2,1)S(1)}, bf16[144,768]{1,0:T(8,128)(2,1)S(1)}, u32[]{:S(2)}, u32[]{:S(2)}) collective-permute-start(bf16[144,768]{1,0:T(8,128)(2,1)S(1)} %get-tuple-element.96), channel_id=1, source_target_pairs={{0,1},{1,0},{2,3},{3,2},{4,5},{5,4},{6,7},{7,6},{8,9},{9,8},{10,11... | collective-permute-start | bytes 663560 | tf_op jit(solution)/shard_map/core_sum_2a/ppermute | solution.py:456
  30.0 1.7 %collective-permute-start.12 = (bf16[128,768]{1,0:T(8,128)(2,1)S(1)}, bf16[128,768]{1,0:T(8,128)(2,1)S(1)}, u32[]{:S(2)}, u32[]{:S(2)}) collective-permute-start(bf16[128,768]{1,0:T(8,128)(2,1)S(1)} %get-tuple-element.97), channel_id=1, source_target_pairs={{0,1},{1,0},{2,3},{3,2},{4,5},{5,4},{6,7},{7,6},{8,9},{9,8},{10,11... | collective-permute-start | bytes 589832 | tf_op jit(solution)/shard_map/core_sum_2a/ppermute | solution.py:456
  31.9 12.8 %collective-permute-start.13 = (bf16[136,1536]{1,0:T(8,128)(2,1)S(1)}, bf16[136,1536]{1,0:T(8,128)(2,1)S(1)}, u32[]{:S(2)}, u32[]{:S(2)}) collective-permute-start(bf16[136,1536]{1,0:T(8,128)(2,1)S(1)} %get-tuple-element.101), channel_id=1, source_target_pairs={{0,2},{2,0},{1,3},{3,1},{4,6},{6,4},{5,7},{7,5},{8,10},{10,8},{9,1... | collective-permute-start | bytes 1253384 | tf_op jit(solution)/shard_map/chip_sum_2/ppermute | solution.py:461
  40.6 18.6 %slice-start = ((s8[18874368]{0:T(1024)(128)(4,1)}), s8[2097152]{0:T(1024)(128)(4,1)S(1)}, s32[]{:S(2)}) async-start(s8[18874368]{0:T(1024)(128)(4,1)} %bitcast.6), calls=%async_computation | async-start | bytes 4194304
  40.6 18.6 %slice-start.1 = ((s8[18874368]{0:T(1024)(128)(4,1)}), s8[4194304]{0:T(1024)(128)(4,1)S(1)}, s32[]{:S(2)}) async-start(s8[18874368]{0:T(1024)(128)(4,1)} %bitcast.6), calls=%async_computation.1 | async-start | bytes 8388608
  42.2 1.8 %collective-permute-start.14 = (bf16[144,768]{1,0:T(8,128)(2,1)S(1)}, bf16[144,768]{1,0:T(8,128)(2,1)S(1)}, u32[]{:S(2)}, u32[]{:S(2)}) collective-permute-start(bf16[144,768]{1,0:T(8,128)(2,1)S(1)} %get-tuple-element.113), channel_id=1, source_target_pairs={{0,1},{1,0},{2,3},{3,2},{4,5},{5,4},{6,7},{7,6},{8,9},{9,8},{10,11... | collective-permute-start | bytes 663560 | tf_op jit(solution)/shard_map/core_sum_3a/ppermute | solution.py:456
  42.3 1.7 %collective-permute-start.15 = (bf16[128,768]{1,0:T(8,128)(2,1)S(1)}, bf16[128,768]{1,0:T(8,128)(2,1)S(1)}, u32[]{:S(2)}, u32[]{:S(2)}) collective-permute-start(bf16[128,768]{1,0:T(8,128)(2,1)S(1)} %get-tuple-element.114), channel_id=1, source_target_pairs={{0,1},{1,0},{2,3},{3,2},{4,5},{5,4},{6,7},{7,6},{8,9},{9,8},{10,11... | collective-permute-start | bytes 589832 | tf_op jit(solution)/shard_map/core_sum_3a/ppermute | solution.py:456
  42.8 5.4 %collective-permute-start.19 = (bf16[144,1536]{1,0:T(8,128)(2,1)S(1)}, bf16[144,1536]{1,0:T(8,128)(2,1)S(1)}, u32[]{:S(2)}, u32[]{:S(2)}) collective-permute-start(bf16[144,1536]{1,0:T(8,128)(2,1)S(1)} %get-tuple-element.103), channel_id=1, source_target_pairs={{0,1},{1,0},{2,3},{3,2},{4,5},{5,4},{6,7},{7,6},{8,9},{9,8},{10,11... | collective-permute-start | bytes 1327112 | tf_op jit(solution)/shard_map/core_sum_0b/ppermute | solution.py:456
  42.9 6.5 %collective-permute-start.20 = (bf16[128,1536]{1,0:T(8,128)(2,1)S(1)}, bf16[128,1536]{1,0:T(8,128)(2,1)S(1)}, u32[]{:S(2)}, u32[]{:S(2)}) collective-permute-start(bf16[128,1536]{1,0:T(8,128)(2,1)S(1)} %get-tuple-element.108), channel_id=1, source_target_pairs={{0,1},{1,0},{2,3},{3,2},{4,5},{5,4},{6,7},{7,6},{8,9},{9,8},{10,11... | collective-permute-start | bytes 1179656 | tf_op jit(solution)/shard_map/core_sum_1b/ppermute | solution.py:456
  44.1 11.8 %collective-permute-start.18 = (bf16[136,1536]{1,0:T(8,128)(2,1)S(1)}, bf16[136,1536]{1,0:T(8,128)(2,1)S(1)}, u32[]{:S(2)}, u32[]{:S(2)}) collective-permute-start(bf16[136,1536]{1,0:T(8,128)(2,1)S(1)} %get-tuple-element.118), channel_id=1, source_target_pairs={{0,2},{2,0},{1,3},{3,1},{4,6},{6,4},{5,7},{7,5},{8,10},{10,8},{9,1... | collective-permute-start | bytes 1253384 | tf_op jit(solution)/shard_map/chip_sum_3/ppermute | solution.py:461
  44.8 14.4 %slice-start.2 = ((s8[18874368]{0:T(1024)(128)(4,1)}), s8[4194304]{0:T(1024)(128)(4,1)S(1)}, s32[]{:S(2)}) async-start(s8[18874368]{0:T(1024)(128)(4,1)} %bitcast.6), calls=%async_computation.2 | async-start | bytes 8388608
  46.1 4.3 %collective-permute-start.21 = (bf16[128,1536]{1,0:T(8,128)(2,1)S(1)}, bf16[128,1536]{1,0:T(8,128)(2,1)S(1)}, u32[]{:S(2)}, u32[]{:S(2)}) collective-permute-start(bf16[128,1536]{1,0:T(8,128)(2,1)S(1)} %get-tuple-element.121), channel_id=1, source_target_pairs={{0,1},{1,0},{2,3},{3,2},{4,5},{5,4},{6,7},{7,6},{8,9},{9,8},{10,11... | collective-permute-start | bytes 1179656 | tf_op jit(solution)/shard_map/core_sum_2b/ppermute | solution.py:456
  46.2 2.1 %copy-start.2 = (f32[6144]{0:T(1024)S(1)}, f32[6144]{0:T(1024)}, u32[]{:S(2)}) copy-start(f32[6144]{0:T(1024)} %param.11) | copy-start | bytes 73732
  46.2 13.0 %slice-start.3 = ((s8[18874368]{0:T(1024)(128)(4,1)}), s8[4194304]{0:T(1024)(128)(4,1)S(1)}, s32[]{:S(2)}) async-start(s8[18874368]{0:T(1024)(128)(4,1)} %bitcast.6), calls=%async_computation.3 | async-start | bytes 8388608
  46.2 13.0 %slice-start.4 = ((s8[18874368]{0:T(1024)(128)(4,1)}), s8[4194304]{0:T(1024)(128)(4,1)S(1)}, s32[]{:S(2)}) async-start(s8[18874368]{0:T(1024)(128)(4,1)} %bitcast.6), calls=%async_computation.4 | async-start | bytes 8388608
  47.7 3.9 %collective-permute-start.16 = (bf16[128,768]{1,0:T(8,128)(2,1)S(1)}, bf16[128,768]{1,0:T(8,128)(2,1)S(1)}, u32[]{:S(2)}, u32[]{:S(2)}) collective-permute-start(bf16[128,768]{1,0:T(8,128)(2,1)S(1)} %get-tuple-element.124), channel_id=1, source_target_pairs={{0,1},{1,0},{2,3},{3,2},{4,5},{5,4},{6,7},{7,6},{8,9},{9,8},{10,11... | collective-permute-start | bytes 589832 | tf_op jit(solution)/shard_map/core_sum_3b/ppermute | solution.py:456
  48.2 3.3 %collective-permute-start.17 = (bf16[128,768]{1,0:T(8,128)(2,1)S(1)}, bf16[128,768]{1,0:T(8,128)(2,1)S(1)}, u32[]{:S(2)}, u32[]{:S(2)}) collective-permute-start(bf16[128,768]{1,0:T(8,128)(2,1)S(1)} %get-tuple-element.125), channel_id=1, source_target_pairs={{0,1},{1,0},{2,3},{3,2},{4,5},{5,4},{6,7},{7,6},{8,9},{9,8},{10,11... | collective-permute-start | bytes 589832 | tf_op jit(solution)/shard_map/core_sum_3b/ppermute | solution.py:456
  57.2 1.9 %collective-permute-start.24 = (f32[2,1536]{1,0:T(2,128)S(1)}, f32[2,1536]{1,0:T(2,128)S(1)}, u32[]{:S(2)}, u32[]{:S(2)}) collective-permute-start(f32[2,1536]{1,0:T(2,128)S(1)} %pool_all.1.refs_0_), channel_id=1, source_target_pairs={{0,1},{1,0},{2,3},{3,2},{4,5},{5,4},{6,7},{7,6},{8,9},{9,8},{10,11... | collective-permute-start | bytes 36872 | tf_op jit(solution)/shard_map/core_pool/ppermute | solution.py:456
  57.3 3.9 %collective-permute-start.22 = (f32[2,1536]{1,0:T(2,128)S(1)}, f32[2,1536]{1,0:T(2,128)S(1)}, u32[]{:S(2)}, u32[]{:S(2)}) collective-permute-start(f32[2,1536]{1,0:T(2,128)S(1)} %pool_all.1.refs_0_), channel_id=1, source_target_pairs={{0,2},{2,0},{1,3},{3,1},{4,6},{6,4},{5,7},{7,5},{8,10},{10,8},{9,1... | collective-permute-start | bytes 36872 | tf_op jit(solution)/shard_map/chip_pool/ppermute | solution.py:461
  57.9 3.3 %collective-permute-start.23 = (f32[2,1536]{1,0:T(2,128)S(1)}, f32[2,1536]{1,0:T(2,128)S(1)}, u32[]{:S(2)}, u32[]{:S(2)}) collective-permute-start(f32[2,1536]{1,0:T(2,128)S(1)} %pool_all.1.refs_0_), channel_id=1, source_target_pairs={{0,3},{1,2},{2,1},{3,0},{4,7},{5,6},{6,5},{7,4},{8,11},{9,10},{10,... | collective-permute-start | bytes 36872 | tf_op jit(solution)/shard_map/both_pool/ppermute | solution.py:466
  60.6 6.3 %copy-start.1 = (bf16[64,6144]{1,0:T(8,128)(2,1)S(1)}, bf16[64,6144]{1,0:T(8,128)(2,1)}, u32[]{:S(2)}) copy-start(bf16[64,6144]{1,0:T(8,128)(2,1)} %captions.1) | copy-start | bytes 2359300
  60.6 13.8 %copy-start.3 = (f32[6144]{0:T(1024)S(1)}, f32[6144]{0:T(1024)}, u32[]{:S(2)}) copy-start(f32[6144]{0:T(1024)} %param.13) | copy-start | bytes 73732
  60.6 13.8 %copy-start.4 = (s32[64]{0:T(128)S(1)}, s32[64]{0:T(128)}, u32[]{:S(2)}) copy-start(s32[64]{0:T(128)} %param.15) | copy-start | bytes 772
  62.5 4.7 %collective-permute-start.25 = (f32[2,1536]{1,0:T(2,128)S(1)}, f32[2,1536]{1,0:T(2,128)S(1)}, u32[]{:S(2)}, u32[]{:S(2)}) collective-permute-start(f32[2,1536]{1,0:T(2,128)S(1)} %mix.3), channel_id=1, source_target_pairs={{0,4},{4,0},{8,12},{12,8},{1,5},{5,1},{9,13},{13,9},{2,6},{6,2},{1... | collective-permute-start | bytes 36872 | tf_op jit(solution)/shard_map/swap_mixed/ppermute | solution.py:471
  63.5 4.7 %collective-permute-start.26 = (f32[2,1536]{1,0:T(2,128)S(1)}, f32[2,1536]{1,0:T(2,128)S(1)}, u32[]{:S(2)}, u32[]{:S(2)}) collective-permute-start(f32[2,1536]{1,0:T(2,128)S(1)} %mix.3), channel_id=1, source_target_pairs={{0,8},{8,0},{4,12},{12,4},{1,9},{9,1},{5,13},{13,5},{2,10},{10,2},... | collective-permute-start | bytes 36872 | tf_op jit(solution)/shard_map/skip_mixed/ppermute | solution.py:471
  64.4 5.5 %collective-permute-start.27 = (f32[2,1536]{1,0:T(2,128)S(1)}, f32[2,1536]{1,0:T(2,128)S(1)}, u32[]{:S(2)}, u32[]{:S(2)}) collective-permute-start(f32[2,1536]{1,0:T(2,128)S(1)} %mix.3), channel_id=1, source_target_pairs={{0,12},{12,0},{4,8},{8,4},{1,13},{13,1},{5,9},{9,5},{2,14},{14,2},... | collective-permute-start | bytes 36872 | tf_op jit(solution)/shard_map/ends_mixed/ppermute | solution.py:471
  69.9 1.9 %collective-permute-start.28 = (f32[2,1536]{1,0:T(2,128)S(1)}, f32[2,1536]{1,0:T(2,128)S(1)}, u32[]{:S(2)}, u32[]{:S(2)}) collective-permute-start(f32[2,1536]{1,0:T(2,128)S(1)} %add_add_fusion.own), channel_id=1, source_target_pairs={{0,1},{1,0},{2,3},{3,2},{4,5},{5,4},{6,7},{7,6},{8,9},{9,8},{10,11... | collective-permute-start | bytes 36872 | tf_op jit(solution)/shard_map/core_embed/ppermute | solution.py:456
  70.0 3.8 %collective-permute-start.29 = (f32[2,1536]{1,0:T(2,128)S(1)}, f32[2,1536]{1,0:T(2,128)S(1)}, u32[]{:S(2)}, u32[]{:S(2)}) collective-permute-start(f32[2,1536]{1,0:T(2,128)S(1)} %add_add_fusion.own), channel_id=1, source_target_pairs={{0,2},{2,0},{1,3},{3,1},{4,6},{6,4},{5,7},{7,5},{8,10},{10,8},{9,1... | collective-permute-start | bytes 36872 | tf_op jit(solution)/shard_map/chip_embed/ppermute | solution.py:461
  71.3 3.1 %collective-permute-start.30 = (f32[2,1536]{1,0:T(2,128)S(1)}, f32[2,1536]{1,0:T(2,128)S(1)}, u32[]{:S(2)}, u32[]{:S(2)}) collective-permute-start(f32[2,1536]{1,0:T(2,128)S(1)} %add_add_fusion.own), channel_id=1, source_target_pairs={{0,3},{1,2},{2,1},{3,0},{4,7},{5,6},{6,5},{7,4},{8,11},{9,10},{10,... | collective-permute-start | bytes 36872 | tf_op jit(solution)/shard_map/both_embed/ppermute | solution.py:466

commit v5 on v4

--- a/solution.py
+++ b/solution.py
@@ -77,7 +77,7 @@
     return ((values - mean) * gain).astype(BF16)
 
 
-PIECES = 4
+PIECES = 2
 NOTE_ROWS = 8
 
 
@@ -505,7 +505,8 @@
     *gives_a, keep_a, keep_gain, sums, held_a, gain = first_a(tokens, ln_gain, w_in)
     gots_a = [other_core("core_sum_0a", give_a) for give_a in gives_a]
     chip_0, note_0, far_0 = chip_sum(0, keep_a, gots_a, sums, keep_gain)
-    near, middle = after(near, chip_0), after(middle, chip_0)
+    near = after(near, chip_0)
+    middle = after(middle, near)
     passed = along("passed_rows", middle, OUTWARD)
     crossed = along("crossed_rows", near, MIDDLE)
 
@@ -542,7 +543,7 @@
         w_in,
         (struct((rows, share)), struct((1, share)), pltpu.VMEM((depth, share), BF16)),
     )
-    passed, crossed, far_0 = after(passed, keep_0), after(crossed, keep_0), after(far_0, keep_0)
+    crossed = after(crossed, keep_0)
     last = along("last_rows", crossed, OUTWARD)
 
     ready_2, chip_2, note_2, far_2 = later_a(2, (middle, passed), far_0)

time: 75.6 us -> 73.9 us (0.978)
  waiting for transfers between devices: 22.4 us -> 21.5 us
    ppermute x6, starting transfers between devices: 7.06 us -> 5.82 us  [other_chip(): return lax.ppermute(value, 'mcol', [(0, 1), (1, 0)])]
  transfers between devices with their start and end apart: 31 -> 31, of which waited for: 15 -> 16; matrix products, arithmetic and copies ran while one was open for 0% -> 0% of each run, Pallas kernels for 33% -> 34%
where the time goes in v5:
time: 73.9 us; the launch traced here: 73.7 us
  Pallas kernels  28.2 us (38%)
  starting transfers between devices  23.3 us (32%)
  waiting for transfers between devices  21.5 us (29%)
    ppermute x8, starting transfers between devices, along(): return lax.ppermute(value, 'mrow', list(pairs))  11.5 us
    ppermute x8, waiting for transfers between devices, along(): return lax.ppermute(value, 'mrow', list(pairs))  9.73 us
    pallas_call x6, Pallas kernels, later_block(): pl.pallas_call(kernel, name='later_block', out_shape=out, in_specs=[WHOLE...  8.94 us
    ppermute x6, waiting for transfers between devices, other_chip(): return lax.ppermute(value, 'mcol', [(0, 1), (1, 0)])  7.13 us
    pallas_call x2, Pallas kernels, first_part(): pl.pallas_call(kernel, name=name, out_shape=shapes, in_specs=[WHOLE, WHOL...  6.23 us
    ppermute x6, starting transfers between devices, other_chip(): return lax.ppermute(value, 'mcol', [(0, 1), (1, 0)])  5.82 us
    pallas_call x1, Pallas kernels, first_a(): pl.pallas_call(first_a_kernel, name='first_a', out_shape=(struct((rows +...  4.66 us
    ppermute x15, waiting for transfers between devices, other_core(): return lax.ppermute(value, 'sub', [(0, 1), (1, 0)])  4.54 us
  transfers between devices with their start and end apart: 31, of which 16 were waited for; matrix products, arithmetic and copies ran while one was open for 0% of the time, Pallas kernels for 34%

profile of v5, /device:TPU:0, one launch (start us, length us, event | category | flops | bytes accessed | tf_op | source)
XLA Modules:
  0.0 73.7 jit_solution(11569255515047480618)
XLA Ops:
  0.0 3.0 %collective-permute-start = (bf16[128,1536]{1,0:T(8,128)(2,1)}, bf16[128,1536]{1,0:T(8,128)(2,1)S(1)}, u32[]{:S(2)}, u32[]{:S(2)}) collective-permute-start(bf16[128,1536]{1,0:T(8,128)(2,1)} %tokens.3), channel_id=1, source_target_pairs={{0,4},{4,0},{8,12},{12,8},{1,5},{5,1},{9,13},{13,9},{2,6},{6,2},{1... | collective-permute-start | bytes 1179656 | tf_op jit(solution)/shard_map/near_rows/ppermute | solution.py:471
  3.0 0.7 collective-permute-start.8
  3.7 4.7 %first_a.1 = (bf16[144,768]{1,0:T(8,128)(2,1)S(1)}, bf16[144,768]{1,0:T(8,128)(2,1)S(1)}, f32[128,1536]{1,0:T(8,128)S(1)}, f32[1,1536]{1,0:T(1,128)S(1)}, f32[1,...) custom-call(bf16[128,1536]{1,0:T(8,128)(2,1)} %tokens.3, f32[1536]{0:T(1024)} %gain.1, ...), custom_call_target="tpu_custom_call" | custom-call | flops 1024 | bytes 1024 | tf_op jit(solution)/shard_map/first_a/pallas_call | solution.py:173
  8.5 0.5 collective-permute-start.2
  9.0 1.0 %collective-permute-done.1.first = bf16[144,768]{1,0:T(8,128)(2,1)S(1)} collective-permute-done((bf16[144,768]{1,0:T(8,128)(2,1)S(1)}, bf16[144,768]{1,0:T(8,128)(2,1)S(1)}, u32[]{:S(2)}, u32[]{:S(2)}) %collective-permute-start.1) | collective-permute-done | bytes 221216 | tf_op jit(solution)/shard_map/core_sum_0a/ppermute | solution.py:456
  9.9 0.3 collective-permute-done.2.second
  10.2 0.1 chip_sum.4
  10.4 1.6 %collective-permute-start.10 = (bf16[136,1536]{1,0:T(8,128)(2,1)S(1)}, bf16[136,1536]{1,0:T(8,128)(2,1)S(1)}, u32[]{:S(2)}, u32[]{:S(2)}) collective-permute-start(bf16[136,1536]{1,0:T(8,128)(2,1)S(1)} %get-tuple-element.74), channel_id=1, source_target_pairs={{0,2},{2,0},{1,3},{3,1},{4,6},{6,4},{5,7},{7,5},{8,10},{10,8},{9,1... | collective-permute-start | bytes 1253384 | tf_op jit(solution)/shard_map/chip_sum_0/ppermute | solution.py:461
  11.9 0.4 collective-permute-done.refs_0_
  12.3 0.7 collective-permute-start.3
  13.0 1.3 %collective-permute-start.9 = (bf16[128,1536]{1,0:T(8,128)(2,1)S(1)}, bf16[128,1536]{1,0:T(8,128)(2,1)S(1)}, u32[]{:S(2)}, u32[]{:S(2)}) collective-permute-start(bf16[128,1536]{1,0:T(8,128)(2,1)S(1)} %collective-permute-done.8.refs_0_), channel_id=1, source_target_pairs={{4,0},{8,12},{5,1},{9,13},{6,2},{10,14},{7,3},{11,15},{20,16},{24,... | collective-permute-start | bytes 1179656 | tf_op jit(solution)/shard_map/passed_rows/ppermute | solution.py:471
  14.4 1.6 %later_block.6 = (bf16[144,768]{1,0:T(8,128)(2,1)S(1)}, bf16[128,768]{1,0:T(8,128)(2,1)S(1)}, f32[128,1536]{1,0:T(8,128)S(1)}, bf16[128,1536]{1,0:T(8,128)(2,1)S(1)}, f32[1,256]{1,0:T(1,128)S(1)}) custom-call(bf16[128,1536]{1,0:T(8,128)(2,1)S(1)} %collective-permute-done.refs_0_, f32[1,1536]{1,0:T(1,128)S(1)} %get-tuple-element.105.refs_1_.gain.refs_2_, ...), custom_call_target="tpu_custom_call" | custom-call | flops 1207959552 | bytes 1024 | tf_op jit(solution)/shard_map/later_block/pallas_call | solution.py:265
  15.9 0.1 collective-permute-start.4
  16.0 0.5 collective-permute-start.5
  16.5 1.2 %collective-permute-done.5.second = bf16[128,768]{1,0:T(8,128)(2,1)S(1)} collective-permute-done((bf16[128,768]{1,0:T(8,128)(2,1)S(1)}, bf16[128,768]{1,0:T(8,128)(2,1)S(1)}, u32[]{:S(2)}, u32[]{:S(2)}) %collective-permute-start.5) | collective-permute-done | bytes 196640 | tf_op jit(solution)/shard_map/core_sum_1a/ppermute | solution.py:456
  17.8 0.1 chip_sum.5
  17.9 1.7 %collective-permute-start.7 = (bf16[136,1536]{1,0:T(8,128)(2,1)S(1)}, bf16[136,1536]{1,0:T(8,128)(2,1)S(1)}, u32[]{:S(2)}, u32[]{:S(2)}) collective-permute-start(bf16[136,1536]{1,0:T(8,128)(2,1)S(1)} %get-tuple-element.84), channel_id=1, source_target_pairs={{0,2},{2,0},{1,3},{3,1},{4,6},{6,4},{5,7},{7,5},{8,10},{10,8},{9,1... | collective-permute-start | bytes 1253384 | tf_op jit(solution)/shard_map/chip_sum_1/ppermute | solution.py:461
  19.6 3.1 %first_keep.1 = (f32[128,1536]{1,0:T(8,128)S(1)}, f32[1,1536]{1,0:T(1,128)S(1)}, bf16[1536,1536]{1,0:T(8,128)(2,1)S(1)}) custom-call(bf16[128,1536]{1,0:T(8,128)(2,1)S(1)} %copy-done, f32[1,1536]{1,0:T(1,128)S(1)} %get-tuple-element.105.refs_1_.gain.refs_2_, bf16[1536,6144]{1,0:T(8,128)(2,1)} %w.5), custom_call_target="tpu_custom_call" | custom-call | flops 1024 | bytes 1024 | tf_op jit(solution)/shard_map/first_keep/pallas_call | solution.py:219
  22.7 0.2 collective-permute-done.10.refs_2_
  22.9 1.5 %collective-permute-start.6 = (bf16[128,1536]{1,0:T(8,128)(2,1)S(1)}, bf16[128,1536]{1,0:T(8,128)(2,1)S(1)}, u32[]{:S(2)}, u32[]{:S(2)}) collective-permute-start(bf16[128,1536]{1,0:T(8,128)(2,1)S(1)} %collective-permute-done.3.refs_0_), channel_id=1, source_target_pairs={{4,0},{8,12},{5,1},{9,13},{6,2},{10,14},{7,3},{11,15},{20,16},{24,... | collective-permute-start | bytes 1179656 | tf_op jit(solution)/shard_map/last_rows/ppermute | solution.py:471
  24.4 4.3 %collective-permute-done.9.refs_1_ = bf16[128,1536]{1,0:T(8,128)(2,1)S(1)} collective-permute-done((bf16[128,1536]{1,0:T(8,128)(2,1)S(1)}, bf16[128,1536]{1,0:T(8,128)(2,1)S(1)}, u32[]{:S(2)}, u32[]{:S(2)}) %collective-permute-start.9) | collective-permute-done | bytes 393248 | tf_op jit(solution)/shard_map/passed_rows/ppermute | solution.py:471
  28.7 1.6 %later_block.7 = (bf16[144,768]{1,0:T(8,128)(2,1)S(1)}, bf16[128,768]{1,0:T(8,128)(2,1)S(1)}, f32[128,1536]{1,0:T(8,128)S(1)}, bf16[128,1536]{1,0:T(8,128)(2,1)S(1)}, f32[1,256]{1,0:T(1,128)S(1)}) custom-call(bf16[128,1536]{1,0:T(8,128)(2,1)S(1)} %collective-permute-done.8.refs_0_, bf16[128,1536]{1,0:T(8,128)(2,1)S(1)} %collective-permute-done.9.refs_1_, ...), custom_call_target="tpu_custom_call" | custom-call | flops 1207959552 | bytes 1024 | tf_op jit(solution)/shard_map/later_block/pallas_call | solution.py:265
  30.3 0.1 collective-permute-start.11
  30.4 0.5 collective-permute-start.12
  30.9 1.2 %collective-permute-done.12.second = bf16[128,768]{1,0:T(8,128)(2,1)S(1)} collective-permute-done((bf16[128,768]{1,0:T(8,128)(2,1)S(1)}, bf16[128,768]{1,0:T(8,128)(2,1)S(1)}, u32[]{:S(2)}, u32[]{:S(2)}) %collective-permute-start.12) | collective-permute-done | bytes 196640 | tf_op jit(solution)/shard_map/core_sum_2a/ppermute | solution.py:456
  32.1 0.1 chip_sum.6
  32.2 0.6 collective-permute-start.13
  32.8 3.2 %first_give.1 = (bf16[144,1536]{1,0:T(8,128)(2,1)S(1)}, bf16[1536,1536]{1,0:T(8,128)(2,1)S(1)}, f32[1,1536]{1,0:T(1,128)S(1)}) custom-call(bf16[128,1536]{1,0:T(8,128)(2,1)S(1)} %copy-done, f32[1,1536]{1,0:T(1,128)S(1)} %get-tuple-element.105.refs_1_.gain.refs_2_, bf16[1536,6144]{1,0:T(8,128)(2,1)} %w.5), custom_call_target="tpu_custom_call" | custom-call | flops 1024 | bytes 1024 | tf_op jit(solution)/shard_map/first_give/pallas_call | solution.py:219
  36.0 1.4 %later_block.8 = (bf16[128,1536]{1,0:T(8,128)(2,1)S(1)}, f32[128,1536]{1,0:T(8,128)S(1)}) custom-call(bf16[128,1536]{1,0:T(8,128)(2,1)S(1)} %get-tuple-element.101.left, bf16[1536,1536]{1,0:T(8,128)(2,1)S(1)} %get-tuple-element.102.give_held, bf16[1536,1536]{1,0:T(8,128)(2,1)S(1)} %get-tuple-element.103.keep_held), custom_call_target="tpu_custom_call" | custom-call | flops 1207959552 | bytes 1024 | tf_op jit(solution)/shard_map/later_block/pallas_call | solution.py:265
  37.4 1.3 %collective-permute-done.6.refs_1_ = bf16[128,1536]{1,0:T(8,128)(2,1)S(1)} collective-permute-done((bf16[128,1536]{1,0:T(8,128)(2,1)S(1)}, bf16[128,1536]{1,0:T(8,128)(2,1)S(1)}, u32[]{:S(2)}, u32[]{:S(2)}) %collective-permute-start.6) | collective-permute-done | bytes 393248 | tf_op jit(solution)/shard_map/last_rows/ppermute | solution.py:471
  38.7 1.6 %later_block.9 = (bf16[144,768]{1,0:T(8,128)(2,1)S(1)}, bf16[128,768]{1,0:T(8,128)(2,1)S(1)}, f32[128,1536]{1,0:T(8,128)S(1)}, bf16[128,1536]{1,0:T(8,128)(2,1)S(1)}, f32[1,256]{1,0:T(1,128)S(1)}) custom-call(bf16[128,1536]{1,0:T(8,128)(2,1)S(1)} %collective-permute-done.3.refs_0_, bf16[128,1536]{1,0:T(8,128)(2,1)S(1)} %collective-permute-done.6.refs_1_, ...), custom_call_target="tpu_custom_call" | custom-call | flops 1207959552 | bytes 1024 | tf_op jit(solution)/shard_map/later_block/pallas_call | solution.py:265
  40.3 0.1 collective-permute-start.14
  40.4 0.5 collective-permute-start.15
  40.9 0.1 collective-permute-start.19
  41.0 0.4 collective-permute-start.20
  41.4 0.7 collective-permute-done.15.second
  42.2 0.1 chip_sum.7
  42.3 0.6 collective-permute-start.18
  42.9 1.2 %collective-permute-done.13.refs_2_ = bf16[136,1536]{1,0:T(8,128)(2,1)S(1)} collective-permute-done((bf16[136,1536]{1,0:T(8,128)(2,1)S(1)}, bf16[136,1536]{1,0:T(8,128)(2,1)S(1)}, u32[]{:S(2)}, u32[]{:S(2)}) %collective-permute-start.13) | collective-permute-done | bytes 417824 | tf_op jit(solution)/shard_map/chip_sum_2/ppermute | solution.py:461
  44.1 1.4 %later_block.10 = (bf16[128,1536]{1,0:T(8,128)(2,1)S(1)}, f32[128,1536]{1,0:T(8,128)S(1)}) custom-call(bf16[128,1536]{1,0:T(8,128)(2,1)S(1)} %get-tuple-element.116.left, bf16[1536,1536]{1,0:T(8,128)(2,1)S(1)} %get-tuple-element.102.give_held, bf16[1536,1536]{1,0:T(8,128)(2,1)S(1)} %get-tuple-element.103.keep_held), custom_call_target="tpu_custom_call" | custom-call | flops 1207959552 | bytes 1024 | tf_op jit(solution)/shard_map/later_block/pallas_call | solution.py:265
  45.6 1.4 %later_block.11 = (bf16[128,768]{1,0:T(8,128)(2,1)S(1)}, bf16[128,768]{1,0:T(8,128)(2,1)S(1)}, f32[128,1536]{1,0:T(8,128)S(1)}) custom-call(bf16[128,1536]{1,0:T(8,128)(2,1)S(1)} %get-tuple-element.118.left, bf16[1536,1536]{1,0:T(8,128)(2,1)S(1)} %get-tuple-element.102.give_held, bf16[1536,1536]{1,0:T(8,128)(2,1)S(1)} %get-tuple-element.103.keep_held), custom_call_target="tpu_custom_call" | custom-call | flops 1207959552 | bytes 1024 | tf_op jit(solution)/shard_map/later_block/pallas_call | solution.py:265
  47.0 0.5 collective-permute-start.16
  47.5 0.1 collective-permute-start.17
  47.6 1.0 %pool.3.refs_7_ = f32[1,1536]{1,0:T(1,128)S(1)} custom-call(f32[128,1536]{1,0:T(8,128)S(1)} %get-tuple-element.86.refs_0_, bf16[144,1536]{1,0:T(8,128)(2,1)S(1)} %collective-permute-done.19.refs_1_, bf16[136,1536]{1,0:T(8,128)(2,1)S(1)} %collective-permute-done.10.refs_2_, f32[1,6144]{1,0:T(1,128)S(1)} %bitcast.8, f32[8,1536]{1,0:T(8,128)S(1)} %all_gains.1.refs_4_.refs_5_, ...), custom_call_target="tpu_custom_call" | custom-call | flops 1024 | bytes 1024 | tf_op jit(solution)/shard_map/pool/pallas_call | solution.py:348
  48.7 1.1 %pool.4.refs_8_ = f32[1,1536]{1,0:T(1,128)S(1)} custom-call(f32[128,1536]{1,0:T(8,128)S(1)} %get-tuple-element.126.refs_0_, bf16[128,1536]{1,0:T(8,128)(2,1)S(1)} %collective-permute-done.20.refs_1_, bf16[136,1536]{1,0:T(8,128)(2,1)S(1)} %collective-permute-done.7.refs_2_, f32[1,6144]{1,0:T(1,128)S(1)} %bitcast.9, f32[8,1536]{1,0:T(8,128)S(1)} %all_gains.1.refs_4_.refs_5_, ...), custom_call_target="tpu_custom_call" | custom-call | flops 1024 | bytes 1024 | tf_op jit(solution)/shard_map/pool/pallas_call | solution.py:348
  49.7 1.1 %pool.5.refs_9_ = f32[1,1536]{1,0:T(1,128)S(1)} custom-call(f32[128,1536]{1,0:T(8,128)S(1)} %get-tuple-element.128.refs_0_, bf16[128,1536]{1,0:T(8,128)(2,1)S(1)} %collective-permute-done.21.refs_1_, bf16[136,1536]{1,0:T(8,128)(2,1)S(1)} %collective-permute-done.13.refs_2_, f32[1,6144]{1,0:T(1,128)S(1)} %bitcast.10, f32[8,1536]{1,0:T(8,128)S(1)} %all_gains.1.refs_4_.refs_5_, ...), custom_call_target="tpu_custom_call" | custom-call | flops 1024 | bytes 1024 | tf_op jit(solution)/shard_map/pool/pallas_call | solution.py:348
  50.8 3.2 %collective-permute-done.18.refs_3_ = bf16[136,1536]{1,0:T(8,128)(2,1)S(1)} collective-permute-done((bf16[136,1536]{1,0:T(8,128)(2,1)S(1)}, bf16[136,1536]{1,0:T(8,128)(2,1)S(1)}, u32[]{:S(2)}, u32[]{:S(2)}) %collective-permute-start.18) | collective-permute-done | bytes 417824 | tf_op jit(solution)/shard_map/chip_sum_3/ppermute | solution.py:461
  54.1 1.1 %pool_all.1.refs_0_ = f32[2,1536]{1,0:T(2,128)S(1)} custom-call(f32[128,1536]{1,0:T(8,128)S(1)} %get-tuple-element.119.refs_0_, bf16[128,768]{1,0:T(8,128)(2,1)S(1)} %collective-permute-done.16.refs_1_, bf16[128,768]{1,0:T(8,128)(2,1)S(1)} %collective-permute-done.17.refs_2_, bf16[136,1536]{1,0:T(8,128)(2,1)S(1)} %collective-permute-done.18.refs_3_, ...), custom_call_target="tpu_custom_call" | custom-call | flops 1024 | bytes 1024 | tf_op jit(solution)/shard_map/pool_all/pallas_call | solution.py:374
  55.2 0.6 collective-permute-start.22
  55.8 1.3 %collective-permute-start.23 = (f32[2,1536]{1,0:T(2,128)S(1)}, f32[2,1536]{1,0:T(2,128)S(1)}, u32[]{:S(2)}, u32[]{:S(2)}) collective-permute-start(f32[2,1536]{1,0:T(2,128)S(1)} %pool_all.1.refs_0_), channel_id=1, source_target_pairs={{0,3},{1,2},{2,1},{3,0},{4,7},{5,6},{6,5},{7,4},{8,11},{9,10},{10,... | collective-permute-start | bytes 36872 | tf_op jit(solution)/shard_map/both_pool/ppermute | solution.py:466
  57.1 1.3 %mix.2.refs_2_ = f32[2,1536]{1,0:T(2,128)S(1)} custom-call(f32[2,1536]{1,0:T(2,128)S(1)} %pool_all.1.refs_0_, f32[2,1536]{1,0:T(2,128)S(1)} %collective-permute-done.24.refs_1_, f32[1,1536]{1,0:T(1,128)S(1)} %get-tuple-element.130.refs_2_, bf16[6144,1536]{1,0:T(8,128)(2,1)S(1)} %bitcast.7), custom_call_target="tpu_custom_call" | custom-call | flops 1024 | bytes 1024 | tf_op jit(solution)/shard_map/mix/pallas_call | solution.py:406
  58.5 0.6 collective-permute-done.22.refs_0_
  59.1 1.3 %mix.3 = f32[2,1536]{1,0:T(2,128)S(1)} custom-call(f32[2,1536]{1,0:T(2,128)S(1)} %collective-permute-done.22.refs_0_, f32[2,1536]{1,0:T(2,128)S(1)} %collective-permute-done.23.refs_1_, f32[2,1536]{1,0:T(2,128)S(1)} %mix.2.refs_2_, bf16[6144,1536]{1,0:T(8,128)(2,1)S(1)} %bitcast.7), custom_call_target="tpu_custom_call" | custom-call | flops 1024 | bytes 1024 | tf_op jit(solution)/shard_map/mix/pallas_call | solution.py:406
  60.4 1.5 %collective-permute-start.25 = (f32[2,1536]{1,0:T(2,128)S(1)}, f32[2,1536]{1,0:T(2,128)S(1)}, u32[]{:S(2)}, u32[]{:S(2)}) collective-permute-start(f32[2,1536]{1,0:T(2,128)S(1)} %mix.3), channel_id=1, source_target_pairs={{0,4},{4,0},{8,12},{12,8},{1,5},{5,1},{9,13},{13,9},{2,6},{6,2},{1... | collective-permute-start | bytes 36872 | tf_op jit(solution)/shard_map/swap_mixed/ppermute | solution.py:471
  61.9 1.4 %collective-permute-start.26 = (f32[2,1536]{1,0:T(2,128)S(1)}, f32[2,1536]{1,0:T(2,128)S(1)}, u32[]{:S(2)}, u32[]{:S(2)}) collective-permute-start(f32[2,1536]{1,0:T(2,128)S(1)} %mix.3), channel_id=1, source_target_pairs={{0,8},{8,0},{4,12},{12,4},{1,9},{9,1},{5,13},{13,5},{2,10},{10,2},... | collective-permute-start | bytes 36872 | tf_op jit(solution)/shard_map/skip_mixed/ppermute | solution.py:471
  63.3 1.5 %collective-permute-start.27 = (f32[2,1536]{1,0:T(2,128)S(1)}, f32[2,1536]{1,0:T(2,128)S(1)}, u32[]{:S(2)}, u32[]{:S(2)}) collective-permute-start(f32[2,1536]{1,0:T(2,128)S(1)} %mix.3), channel_id=1, source_target_pairs={{0,12},{12,0},{4,8},{8,4},{1,13},{13,1},{5,9},{9,5},{2,14},{14,2},... | collective-permute-start | bytes 36872 | tf_op jit(solution)/shard_map/ends_mixed/ppermute | solution.py:471
  64.8 0.3 multiply_reduce_fusion
  65.1 1.5 %collective-permute-done.26 = f32[2,1536]{1,0:T(2,128)S(1)} collective-permute-done((f32[2,1536]{1,0:T(2,128)S(1)}, f32[2,1536]{1,0:T(2,128)S(1)}, u32[]{:S(2)}, u32[]{:S(2)}) %collective-permute-start.26) | collective-permute-done | bytes 12320 | tf_op jit(solution)/shard_map/skip_mixed/ppermute | solution.py:471
  66.6 2.1 %collective-permute-done.27 = f32[2,1536]{1,0:T(2,128)S(1)} collective-permute-done((f32[2,1536]{1,0:T(2,128)S(1)}, f32[2,1536]{1,0:T(2,128)S(1)}, u32[]{:S(2)}, u32[]{:S(2)}) %collective-permute-start.27) | collective-permute-done | bytes 12320 | tf_op jit(solution)/shard_map/ends_mixed/ppermute | solution.py:471
  68.8 0.8 %collective-permute-start.29 = (f32[2,1536]{1,0:T(2,128)S(1)}, f32[2,1536]{1,0:T(2,128)S(1)}, u32[]{:S(2)}, u32[]{:S(2)}) collective-permute-start(f32[2,1536]{1,0:T(2,128)S(1)} %add_add_fusion.own), channel_id=1, source_target_pairs={{0,2},{2,0},{1,3},{3,1},{4,6},{6,4},{5,7},{7,5},{8,10},{10,8},{9,1... | collective-permute-start | bytes 36872 | tf_op jit(solution)/shard_map/chip_embed/ppermute | solution.py:461
  69.6 1.1 %collective-permute-start.30 = (f32[2,1536]{1,0:T(2,128)S(1)}, f32[2,1536]{1,0:T(2,128)S(1)}, u32[]{:S(2)}, u32[]{:S(2)}) collective-permute-start(f32[2,1536]{1,0:T(2,128)S(1)} %add_add_fusion.own), channel_id=1, source_target_pairs={{0,3},{1,2},{2,1},{3,0},{4,7},{5,6},{6,5},{7,4},{8,11},{9,10},{10,... | collective-permute-start | bytes 36872 | tf_op jit(solution)/shard_map/both_embed/ppermute | solution.py:466
  70.7 1.9 %collective-permute-done.29.across = f32[2,1536]{1,0:T(2,128)S(1)} collective-permute-done((f32[2,1536]{1,0:T(2,128)S(1)}, f32[2,1536]{1,0:T(2,128)S(1)}, u32[]{:S(2)}, u32[]{:S(2)}) %collective-permute-start.29) | collective-permute-done | bytes 12320 | tf_op jit(solution)/shard_map/chip_embed/ppermute | solution.py:461
  72.6 0.1 collective-permute-done.30.both
  72.7 1.0 %score.1 = f32[1,64]{1,0:T(1,128)} custom-call(f32[2,1536]{1,0:T(2,128)S(1)} %add_add_fusion.own, f32[2,1536]{1,0:T(2,128)S(1)} %collective-permute-done.28.core, f32[2,1536]{1,0:T(2,128)S(1)} %collective-permute-done.29.across, f32[2,1536]{1,0:T(2,128)S(1)} %collective-permute-done.30.both, f32[1,6144]{1,0:T(1,128)S(1)} %bitcast.12, ...), custom_call_target="tpu_custom_call" | custom-call | flops 1024 | bytes 1024 | tf_op jit(solution)/shard_map/score/pallas_call | solution.py:443
  (43 shorter events, 0.4 us)
Async XLA Ops:
  0.0 12.3 %collective-permute-start = (bf16[128,1536]{1,0:T(8,128)(2,1)}, bf16[128,1536]{1,0:T(8,128)(2,1)S(1)}, u32[]{:S(2)}, u32[]{:S(2)}) collective-permute-start(bf16[128,1536]{1,0:T(8,128)(2,1)} %tokens.3), channel_id=1, source_target_pairs={{0,4},{4,0},{8,12},{12,8},{1,5},{5,1},{9,13},{13,9},{2,6},{6,2},{1... | collective-permute-start | bytes 1179656 | tf_op jit(solution)/shard_map/near_rows/ppermute | solution.py:471
  3.0 10.0 %collective-permute-start.8 = (bf16[128,1536]{1,0:T(8,128)(2,1)}, bf16[128,1536]{1,0:T(8,128)(2,1)S(1)}, u32[]{:S(2)}, u32[]{:S(2)}) collective-permute-start(bf16[128,1536]{1,0:T(8,128)(2,1)} %tokens.3), channel_id=1, source_target_pairs={{4,8},{8,4},{5,9},{9,5},{6,10},{10,6},{7,11},{11,7},{20,24},{24,20... | collective-permute-start | bytes 1179656 | tf_op jit(solution)/shard_map/middle_rows/ppermute | solution.py:471
  8.4 1.5 %collective-permute-start.1 = (bf16[144,768]{1,0:T(8,128)(2,1)S(1)}, bf16[144,768]{1,0:T(8,128)(2,1)S(1)}, u32[]{:S(2)}, u32[]{:S(2)}) collective-permute-start(bf16[144,768]{1,0:T(8,128)(2,1)S(1)} %get-tuple-element.70), channel_id=1, source_target_pairs={{0,1},{1,0},{2,3},{3,2},{4,5},{5,4},{6,7},{7,6},{8,9},{9,8},{10,11... | collective-permute-start | bytes 663560 | tf_op jit(solution)/shard_map/core_sum_0a/ppermute | solution.py:456
  8.5 1.8 %collective-permute-start.2 = (bf16[144,768]{1,0:T(8,128)(2,1)S(1)}, bf16[144,768]{1,0:T(8,128)(2,1)S(1)}, u32[]{:S(2)}, u32[]{:S(2)}) collective-permute-start(bf16[144,768]{1,0:T(8,128)(2,1)S(1)} %get-tuple-element.71), channel_id=1, source_target_pairs={{0,1},{1,0},{2,3},{3,2},{4,5},{5,4},{6,7},{7,6},{8,9},{9,8},{10,11... | collective-permute-start | bytes 663560 | tf_op jit(solution)/shard_map/core_sum_0a/ppermute | solution.py:456
  10.4 12.5 %collective-permute-start.10 = (bf16[136,1536]{1,0:T(8,128)(2,1)S(1)}, bf16[136,1536]{1,0:T(8,128)(2,1)S(1)}, u32[]{:S(2)}, u32[]{:S(2)}) collective-permute-start(bf16[136,1536]{1,0:T(8,128)(2,1)S(1)} %get-tuple-element.74), channel_id=1, source_target_pairs={{0,2},{2,0},{1,3},{3,1},{4,6},{6,4},{5,7},{7,5},{8,10},{10,8},{9,1... | collective-permute-start | bytes 1253384 | tf_op jit(solution)/shard_map/chip_sum_0/ppermute | solution.py:461
  12.3 10.6 %collective-permute-start.3 = (bf16[128,1536]{1,0:T(8,128)(2,1)S(1)}, bf16[128,1536]{1,0:T(8,128)(2,1)S(1)}, u32[]{:S(2)}, u32[]{:S(2)}) collective-permute-start(bf16[128,1536]{1,0:T(8,128)(2,1)S(1)} %collective-permute-done.refs_0_), channel_id=1, source_target_pairs={{4,8},{8,4},{5,9},{9,5},{6,10},{10,6},{7,11},{11,7},{20,24},{24,20... | collective-permute-start | bytes 1179656 | tf_op jit(solution)/shard_map/crossed_rows/ppermute | solution.py:471
  13.0 15.7 %collective-permute-start.9 = (bf16[128,1536]{1,0:T(8,128)(2,1)S(1)}, bf16[128,1536]{1,0:T(8,128)(2,1)S(1)}, u32[]{:S(2)}, u32[]{:S(2)}) collective-permute-start(bf16[128,1536]{1,0:T(8,128)(2,1)S(1)} %collective-permute-done.8.refs_0_), channel_id=1, source_target_pairs={{4,0},{8,12},{5,1},{9,13},{6,2},{10,14},{7,3},{11,15},{20,16},{24,... | collective-permute-start | bytes 1179656 | tf_op jit(solution)/shard_map/passed_rows/ppermute | solution.py:471
  14.3 5.3 %copy-start = (bf16[128,1536]{1,0:T(8,128)(2,1)S(1)}, bf16[128,1536]{1,0:T(8,128)(2,1)}, u32[]{:S(2)}) copy-start(bf16[128,1536]{1,0:T(8,128)(2,1)} %tokens.3) | copy-start | bytes 1179652
  15.9 1.8 %collective-permute-start.4 = (bf16[144,768]{1,0:T(8,128)(2,1)S(1)}, bf16[144,768]{1,0:T(8,128)(2,1)S(1)}, u32[]{:S(2)}, u32[]{:S(2)}) collective-permute-start(bf16[144,768]{1,0:T(8,128)(2,1)S(1)} %get-tuple-element.79), channel_id=1, source_target_pairs={{0,1},{1,0},{2,3},{3,2},{4,5},{5,4},{6,7},{7,6},{8,9},{9,8},{10,11... | collective-permute-start | bytes 663560 | tf_op jit(solution)/shard_map/core_sum_1a/ppermute | solution.py:456
  16.0 1.7 %collective-permute-start.5 = (bf16[128,768]{1,0:T(8,128)(2,1)S(1)}, bf16[128,768]{1,0:T(8,128)(2,1)S(1)}, u32[]{:S(2)}, u32[]{:S(2)}) collective-permute-start(bf16[128,768]{1,0:T(8,128)(2,1)S(1)} %get-tuple-element.80), channel_id=1, source_target_pairs={{0,1},{1,0},{2,3},{3,2},{4,5},{5,4},{6,7},{7,6},{8,9},{9,8},{10,11... | collective-permute-start | bytes 589832 | tf_op jit(solution)/shard_map/core_sum_1a/ppermute | solution.py:456
  17.9 18.1 %collective-permute-start.7 = (bf16[136,1536]{1,0:T(8,128)(2,1)S(1)}, bf16[136,1536]{1,0:T(8,128)(2,1)S(1)}, u32[]{:S(2)}, u32[]{:S(2)}) collective-permute-start(bf16[136,1536]{1,0:T(8,128)(2,1)S(1)} %get-tuple-element.84), channel_id=1, source_target_pairs={{0,2},{2,0},{1,3},{3,1},{4,6},{6,4},{5,7},{7,5},{8,10},{10,8},{9,1... | collective-permute-start | bytes 1253384 | tf_op jit(solution)/shard_map/chip_sum_1/ppermute | solution.py:461
  22.9 15.8 %collective-permute-start.6 = (bf16[128,1536]{1,0:T(8,128)(2,1)S(1)}, bf16[128,1536]{1,0:T(8,128)(2,1)S(1)}, u32[]{:S(2)}, u32[]{:S(2)}) collective-permute-start(bf16[128,1536]{1,0:T(8,128)(2,1)S(1)} %collective-permute-done.3.refs_0_), channel_id=1, source_target_pairs={{4,0},{8,12},{5,1},{9,13},{6,2},{10,14},{7,3},{11,15},{20,16},{24,... | collective-permute-start | bytes 1179656 | tf_op jit(solution)/shard_map/last_rows/ppermute | solution.py:471
  30.3 1.8 %collective-permute-start.11 = (bf16[144,768]{1,0:T(8,128)(2,1)S(1)}, bf16[144,768]{1,0:T(8,128)(2,1)S(1)}, u32[]{:S(2)}, u32[]{:S(2)}) collective-permute-start(bf16[144,768]{1,0:T(8,128)(2,1)S(1)} %get-tuple-element.92), channel_id=1, source_target_pairs={{0,1},{1,0},{2,3},{3,2},{4,5},{5,4},{6,7},{7,6},{8,9},{9,8},{10,11... | collective-permute-start | bytes 663560 | tf_op jit(solution)/shard_map/core_sum_2a/ppermute | solution.py:456
  30.4 1.7 %collective-permute-start.12 = (bf16[128,768]{1,0:T(8,128)(2,1)S(1)}, bf16[128,768]{1,0:T(8,128)(2,1)S(1)}, u32[]{:S(2)}, u32[]{:S(2)}) collective-permute-start(bf16[128,768]{1,0:T(8,128)(2,1)S(1)} %get-tuple-element.93), channel_id=1, source_target_pairs={{0,1},{1,0},{2,3},{3,2},{4,5},{5,4},{6,7},{7,6},{8,9},{9,8},{10,11... | collective-permute-start | bytes 589832 | tf_op jit(solution)/shard_map/core_sum_2a/ppermute | solution.py:456
  32.2 11.8 %collective-permute-start.13 = (bf16[136,1536]{1,0:T(8,128)(2,1)S(1)}, bf16[136,1536]{1,0:T(8,128)(2,1)S(1)}, u32[]{:S(2)}, u32[]{:S(2)}) collective-permute-start(bf16[136,1536]{1,0:T(8,128)(2,1)S(1)} %get-tuple-element.97), channel_id=1, source_target_pairs={{0,2},{2,0},{1,3},{3,1},{4,6},{6,4},{5,7},{7,5},{8,10},{10,8},{9,1... | collective-permute-start | bytes 1253384 | tf_op jit(solution)/shard_map/chip_sum_2/ppermute | solution.py:461
  38.7 18.4 %slice-start = ((s8[18874368]{0:T(1024)(128)(4,1)}), s8[2097152]{0:T(1024)(128)(4,1)S(1)}, s32[]{:S(2)}) async-start(s8[18874368]{0:T(1024)(128)(4,1)} %bitcast.6), calls=%async_computation | async-start | bytes 4194304
  38.7 18.4 %slice-start.1 = ((s8[18874368]{0:T(1024)(128)(4,1)}), s8[4194304]{0:T(1024)(128)(4,1)S(1)}, s32[]{:S(2)}) async-start(s8[18874368]{0:T(1024)(128)(4,1)} %bitcast.6), calls=%async_computation.1 | async-start | bytes 8388608
  40.3 1.8 %collective-permute-start.14 = (bf16[144,768]{1,0:T(8,128)(2,1)S(1)}, bf16[144,768]{1,0:T(8,128)(2,1)S(1)}, u32[]{:S(2)}, u32[]{:S(2)}) collective-permute-start(bf16[144,768]{1,0:T(8,128)(2,1)S(1)} %get-tuple-element.109), channel_id=1, source_target_pairs={{0,1},{1,0},{2,3},{3,2},{4,5},{5,4},{6,7},{7,6},{8,9},{9,8},{10,11... | collective-permute-start | bytes 663560 | tf_op jit(solution)/shard_map/core_sum_3a/ppermute | solution.py:456
  40.4 1.7 %collective-permute-start.15 = (bf16[128,768]{1,0:T(8,128)(2,1)S(1)}, bf16[128,768]{1,0:T(8,128)(2,1)S(1)}, u32[]{:S(2)}, u32[]{:S(2)}) collective-permute-start(bf16[128,768]{1,0:T(8,128)(2,1)S(1)} %get-tuple-element.110), channel_id=1, source_target_pairs={{0,1},{1,0},{2,3},{3,2},{4,5},{5,4},{6,7},{7,6},{8,9},{9,8},{10,11... | collective-permute-start | bytes 589832 | tf_op jit(solution)/shard_map/core_sum_3a/ppermute | solution.py:456
  40.9 6.6 %collective-permute-start.19 = (bf16[144,1536]{1,0:T(8,128)(2,1)S(1)}, bf16[144,1536]{1,0:T(8,128)(2,1)S(1)}, u32[]{:S(2)}, u32[]{:S(2)}) collective-permute-start(bf16[144,1536]{1,0:T(8,128)(2,1)S(1)} %get-tuple-element.99), channel_id=1, source_target_pairs={{0,1},{1,0},{2,3},{3,2},{4,5},{5,4},{6,7},{7,6},{8,9},{9,8},{10,11... | collective-permute-start | bytes 1327112 | tf_op jit(solution)/shard_map/core_sum_0b/ppermute | solution.py:456
  41.0 7.7 %collective-permute-start.20 = (bf16[128,1536]{1,0:T(8,128)(2,1)S(1)}, bf16[128,1536]{1,0:T(8,128)(2,1)S(1)}, u32[]{:S(2)}, u32[]{:S(2)}) collective-permute-start(bf16[128,1536]{1,0:T(8,128)(2,1)S(1)} %get-tuple-element.104), channel_id=1, source_target_pairs={{0,1},{1,0},{2,3},{3,2},{4,5},{5,4},{6,7},{7,6},{8,9},{9,8},{10,11... | collective-permute-start | bytes 1179656 | tf_op jit(solution)/shard_map/core_sum_1b/ppermute | solution.py:456
  42.3 11.8 %collective-permute-start.18 = (bf16[136,1536]{1,0:T(8,128)(2,1)S(1)}, bf16[136,1536]{1,0:T(8,128)(2,1)S(1)}, u32[]{:S(2)}, u32[]{:S(2)}) collective-permute-start(bf16[136,1536]{1,0:T(8,128)(2,1)S(1)} %get-tuple-element.114), channel_id=1, source_target_pairs={{0,2},{2,0},{1,3},{3,1},{4,6},{6,4},{5,7},{7,5},{8,10},{10,8},{9,1... | collective-permute-start | bytes 1253384 | tf_op jit(solution)/shard_map/chip_sum_3/ppermute | solution.py:461
  44.1 13.0 %slice-start.2 = ((s8[18874368]{0:T(1024)(128)(4,1)}), s8[4194304]{0:T(1024)(128)(4,1)S(1)}, s32[]{:S(2)}) async-start(s8[18874368]{0:T(1024)(128)(4,1)} %bitcast.6), calls=%async_computation.2 | async-start | bytes 8388608
  45.4 4.3 %collective-permute-start.21 = (bf16[128,1536]{1,0:T(8,128)(2,1)S(1)}, bf16[128,1536]{1,0:T(8,128)(2,1)S(1)}, u32[]{:S(2)}, u32[]{:S(2)}) collective-permute-start(bf16[128,1536]{1,0:T(8,128)(2,1)S(1)} %get-tuple-element.117), channel_id=1, source_target_pairs={{0,1},{1,0},{2,3},{3,2},{4,5},{5,4},{6,7},{7,6},{8,9},{9,8},{10,11... | collective-permute-start | bytes 1179656 | tf_op jit(solution)/shard_map/core_sum_2b/ppermute | solution.py:456
  45.5 2.1 %copy-start.2 = (f32[6144]{0:T(1024)S(1)}, f32[6144]{0:T(1024)}, u32[]{:S(2)}) copy-start(f32[6144]{0:T(1024)} %param.11) | copy-start | bytes 73732
  45.5 11.6 %slice-start.3 = ((s8[18874368]{0:T(1024)(128)(4,1)}), s8[4194304]{0:T(1024)(128)(4,1)S(1)}, s32[]{:S(2)}) async-start(s8[18874368]{0:T(1024)(128)(4,1)} %bitcast.6), calls=%async_computation.3 | async-start | bytes 8388608
  45.5 11.6 %slice-start.4 = ((s8[18874368]{0:T(1024)(128)(4,1)}), s8[4194304]{0:T(1024)(128)(4,1)S(1)}, s32[]{:S(2)}) async-start(s8[18874368]{0:T(1024)(128)(4,1)} %bitcast.6), calls=%async_computation.4 | async-start | bytes 8388608
  47.0 3.9 %collective-permute-start.16 = (bf16[128,768]{1,0:T(8,128)(2,1)S(1)}, bf16[128,768]{1,0:T(8,128)(2,1)S(1)}, u32[]{:S(2)}, u32[]{:S(2)}) collective-permute-start(bf16[128,768]{1,0:T(8,128)(2,1)S(1)} %get-tuple-element.120), channel_id=1, source_target_pairs={{0,1},{1,0},{2,3},{3,2},{4,5},{5,4},{6,7},{7,6},{8,9},{9,8},{10,11... | collective-permute-start | bytes 589832 | tf_op jit(solution)/shard_map/core_sum_3b/ppermute | solution.py:456
  47.5 3.3 %collective-permute-start.17 = (bf16[128,768]{1,0:T(8,128)(2,1)S(1)}, bf16[128,768]{1,0:T(8,128)(2,1)S(1)}, u32[]{:S(2)}, u32[]{:S(2)}) collective-permute-start(bf16[128,768]{1,0:T(8,128)(2,1)S(1)} %get-tuple-element.121), channel_id=1, source_target_pairs={{0,1},{1,0},{2,3},{3,2},{4,5},{5,4},{6,7},{7,6},{8,9},{9,8},{10,11... | collective-permute-start | bytes 589832 | tf_op jit(solution)/shard_map/core_sum_3b/ppermute | solution.py:456
  55.1 1.9 %collective-permute-start.24 = (f32[2,1536]{1,0:T(2,128)S(1)}, f32[2,1536]{1,0:T(2,128)S(1)}, u32[]{:S(2)}, u32[]{:S(2)}) collective-permute-start(f32[2,1536]{1,0:T(2,128)S(1)} %pool_all.1.refs_0_), channel_id=1, source_target_pairs={{0,1},{1,0},{2,3},{3,2},{4,5},{5,4},{6,7},{7,6},{8,9},{9,8},{10,11... | collective-permute-start | bytes 36872 | tf_op jit(solution)/shard_map/core_pool/ppermute | solution.py:456
  55.2 3.8 %collective-permute-start.22 = (f32[2,1536]{1,0:T(2,128)S(1)}, f32[2,1536]{1,0:T(2,128)S(1)}, u32[]{:S(2)}, u32[]{:S(2)}) collective-permute-start(f32[2,1536]{1,0:T(2,128)S(1)} %pool_all.1.refs_0_), channel_id=1, source_target_pairs={{0,2},{2,0},{1,3},{3,1},{4,6},{6,4},{5,7},{7,5},{8,10},{10,8},{9,1... | collective-permute-start | bytes 36872 | tf_op jit(solution)/shard_map/chip_pool/ppermute | solution.py:461
  55.8 3.3 %collective-permute-start.23 = (f32[2,1536]{1,0:T(2,128)S(1)}, f32[2,1536]{1,0:T(2,128)S(1)}, u32[]{:S(2)}, u32[]{:S(2)}) collective-permute-start(f32[2,1536]{1,0:T(2,128)S(1)} %pool_all.1.refs_0_), channel_id=1, source_target_pairs={{0,3},{1,2},{2,1},{3,0},{4,7},{5,6},{6,5},{7,4},{8,11},{9,10},{10,... | collective-permute-start | bytes 36872 | tf_op jit(solution)/shard_map/both_pool/ppermute | solution.py:466
  58.5 6.3 %copy-start.1 = (bf16[64,6144]{1,0:T(8,128)(2,1)S(1)}, bf16[64,6144]{1,0:T(8,128)(2,1)}, u32[]{:S(2)}) copy-start(bf16[64,6144]{1,0:T(8,128)(2,1)} %captions.1) | copy-start | bytes 2359300
  58.5 14.3 %copy-start.3 = (f32[6144]{0:T(1024)S(1)}, f32[6144]{0:T(1024)}, u32[]{:S(2)}) copy-start(f32[6144]{0:T(1024)} %param.13) | copy-start | bytes 73732
  58.5 14.2 %copy-start.4 = (s32[64]{0:T(128)S(1)}, s32[64]{0:T(128)}, u32[]{:S(2)}) copy-start(s32[64]{0:T(128)} %param.15) | copy-start | bytes 772
  60.4 4.7 %collective-permute-start.25 = (f32[2,1536]{1,0:T(2,128)S(1)}, f32[2,1536]{1,0:T(2,128)S(1)}, u32[]{:S(2)}, u32[]{:S(2)}) collective-permute-start(f32[2,1536]{1,0:T(2,128)S(1)} %mix.3), channel_id=1, source_target_pairs={{0,4},{4,0},{8,12},{12,8},{1,5},{5,1},{9,13},{13,9},{2,6},{6,2},{1... | collective-permute-start | bytes 36872 | tf_op jit(solution)/shard_map/swap_mixed/ppermute | solution.py:471
  61.9 4.7 %collective-permute-start.26 = (f32[2,1536]{1,0:T(2,128)S(1)}, f32[2,1536]{1,0:T(2,128)S(1)}, u32[]{:S(2)}, u32[]{:S(2)}) collective-permute-start(f32[2,1536]{1,0:T(2,128)S(1)} %mix.3), channel_id=1, source_target_pairs={{0,8},{8,0},{4,12},{12,4},{1,9},{9,1},{5,13},{13,5},{2,10},{10,2},... | collective-permute-start | bytes 36872 | tf_op jit(solution)/shard_map/skip_mixed/ppermute | solution.py:471
  63.3 5.5 %collective-permute-start.27 = (f32[2,1536]{1,0:T(2,128)S(1)}, f32[2,1536]{1,0:T(2,128)S(1)}, u32[]{:S(2)}, u32[]{:S(2)}) collective-permute-start(f32[2,1536]{1,0:T(2,128)S(1)} %mix.3), channel_id=1, source_target_pairs={{0,12},{12,0},{4,8},{8,4},{1,13},{13,1},{5,9},{9,5},{2,14},{14,2},... | collective-permute-start | bytes 36872 | tf_op jit(solution)/shard_map/ends_mixed/ppermute | solution.py:471
  68.8 1.9 %collective-permute-start.28 = (f32[2,1536]{1,0:T(2,128)S(1)}, f32[2,1536]{1,0:T(2,128)S(1)}, u32[]{:S(2)}, u32[]{:S(2)}) collective-permute-start(f32[2,1536]{1,0:T(2,128)S(1)} %add_add_fusion.own), channel_id=1, source_target_pairs={{0,1},{1,0},{2,3},{3,2},{4,5},{5,4},{6,7},{7,6},{8,9},{9,8},{10,11... | collective-permute-start | bytes 36872 | tf_op jit(solution)/shard_map/core_embed/ppermute | solution.py:456
  68.8 3.8 %collective-permute-start.29 = (f32[2,1536]{1,0:T(2,128)S(1)}, f32[2,1536]{1,0:T(2,128)S(1)}, u32[]{:S(2)}, u32[]{:S(2)}) collective-permute-start(f32[2,1536]{1,0:T(2,128)S(1)} %add_add_fusion.own), channel_id=1, source_target_pairs={{0,2},{2,0},{1,3},{3,1},{4,6},{6,4},{5,7},{7,5},{8,10},{10,8},{9,1... | collective-permute-start | bytes 36872 | tf_op jit(solution)/shard_map/chip_embed/ppermute | solution.py:461
  69.6 3.1 %collective-permute-start.30 = (f32[2,1536]{1,0:T(2,128)S(1)}, f32[2,1536]{1,0:T(2,128)S(1)}, u32[]{:S(2)}, u32[]{:S(2)}) collective-permute-start(f32[2,1536]{1,0:T(2,128)S(1)} %add_add_fusion.own), channel_id=1, source_target_pairs={{0,3},{1,2},{2,1},{3,0},{4,7},{5,6},{6,5},{7,4},{8,11},{9,10},{10,... | collective-permute-start | bytes 36872 | tf_op jit(solution)/shard_map/both_embed/ppermute | solution.py:466

commit v6 on v5

--- a/solution.py
+++ b/solution.py
@@ -19,8 +19,8 @@
     return pltpu.CompilerParams(vmem_limit_bytes=mib * MIB)
 
 
-def cost(flops, moved):
-    return pl.CostEstimate(flops=1024, bytes_accessed=1024, transcendentals=0)
+def cost(flops=1024):
+    return pl.CostEstimate(flops=flops, bytes_accessed=1024, transcendentals=0)
 
 
 def struct(shape, dtype=F32):
@@ -186,7 +186,7 @@
         out_specs=(WHOLE,) * 7,
         scratch_shapes=[VMEM((rows, depth), BF16), VMEM((depth,), F32), pltpu.SemaphoreType.DMA((2 * PIECES + 2,))],
         compiler_params=params(8),
-        cost_estimate=cost(4 * rows * depth * share, 4 * depth * share),
+        cost_estimate=cost(),
     )(*(pltpu.with_memory_space_constraint(value, pltpu.HBM) for value in (tokens, gain, w)))
 
 
@@ -224,7 +224,7 @@
         out_specs=(WHOLE,) * len(shapes),
         scratch_shapes=[pltpu.SemaphoreType.DMA((PIECES,))],
         compiler_params=params(8),
-        cost_estimate=cost(2 * rows * depth * share, 2 * depth * share),
+        cost_estimate=cost(),
     )(tokens, gain, pltpu.with_memory_space_constraint(w, pltpu.HBM))
 
 
@@ -269,12 +269,12 @@
         in_specs=[WHOLE] * len(args),
         out_specs=(WHOLE,) * len(out),
         compiler_params=params(8),
-        cost_estimate=pl.CostEstimate(flops=flops, bytes_accessed=1024, transcendentals=0),
+        cost_estimate=cost(flops),
     )(*args)
 
 
-def chip_sum_kernel(kept, first, second, own, *refs):
-    kept_gain, (out, note) = refs[:-2], refs[-2:]
+def chip_sum_kernel(slot, kept, first, second, own, *refs):
+    *extra, out, note = refs
     rows, share = kept.shape
     half = share // 2
     for index, got in enumerate((first, second)):
@@ -283,8 +283,12 @@
     sums = jnp.concatenate([own[...], rejoined(first[rows : rows + 3, 0 : 2 * rows])], axis=1)
     note[...] = sums
     below = list(thirds(sums))
-    if kept_gain:
-        below.extend(thirds(kept_gain[0][...])[:2])
+    if slot == 1:
+        return
+    if slot == 2:
+        below.extend(thirds(extra[0][...]))
+    if slot == 0:
+        below.extend(thirds(extra[0][...])[:2])
         got_gain = jnp.concatenate([rejoined(got[rows + 3 : rows + 6, :]) for got in (first, second)], axis=1)
         below.extend(thirds(got_gain)[:2])
     out[rows:, :] = row_block(below, (NOTE_ROWS, share))
@@ -307,14 +311,14 @@
         in_specs=[WHOLE] * len(args),
         out_specs=jax.tree.map(lambda _: WHOLE, out),
         compiler_params=params(4),
-        cost_estimate=cost(0, 0),
+        cost_estimate=cost(),
     )(*args)
 
 
-def pool_pieces(width, kept, nears, far, bias, gains, note, out):
+def pool_pieces(width, row, kept, nears, far, told, bias, gains, note, out):
     rows, share = kept.shape
     depth = width // 4
-    all_sums = jnp.concatenate([note[...], rejoined(far[rows : rows + 3, 0 : 4 * rows])], axis=1)
+    all_sums = jnp.concatenate([note[...], rejoined(told[rows + row : rows + row + 3, 0 : 4 * rows])], axis=1)
     lines = [all_sums[:, index * rows : (index + 1) * rows] for index in range(8)]
     columns = jnp.concatenate([*lines, jnp.zeros((120, rows), F32)], axis=0).T
     totals = [columns[:, 2 * k : 2 * k + 1] for k in range(4)]
@@ -338,27 +342,27 @@
         out[:, cols] = jnp.sum(hidden, axis=0, keepdims=True)
 
 
-def pool_kernel(width, count, kept, *refs):
-    pool_pieces(width, kept, refs[:count], *refs[count:])
-
-
-def pool(width, kept, nears, far, bias, gains, note):
+def pool_kernel(width, row, count, kept, *refs):
+    pool_pieces(width, row, kept, refs[:count], *refs[count:])
+
+
+def pool(width, row, kept, nears, far, told, bias, gains, note):
     share = kept.shape[1]
-    args = (kept, *nears, far, bias, gains, note)
-    return pl.pallas_call(
-        lambda *refs: pool_kernel(width, len(nears), *refs),
+    args = (kept, *nears, far, told, bias, gains, note)
+    return pl.pallas_call(
+        lambda *refs: pool_kernel(width, row, len(nears), *refs),
         name="pool",
         out_shape=struct((1, share)),
         in_specs=[WHOLE] * len(args),
         out_specs=WHOLE,
         compiler_params=params(6),
-        cost_estimate=cost(20 * kept.size, 8 * kept.size),
+        cost_estimate=cost(),
     )(*args)
 
 
 def pool_all_kernel(width, count, kept, *refs):
     nears, (far, bias, gains, note, first, second, third, out, part) = refs[:count], refs[count:]
-    pool_pieces(width, kept, nears, far, bias, gains, note, part)
+    pool_pieces(width, 0, kept, nears, far, far, bias, gains, note, part)
     z = lax.axis_index("mrow")
     sources = (z, z ^ 1, jnp.where(z < 2, 2, 1), jnp.where(z < 2, 3, 0))
     image = lax.broadcasted_iota(jnp.int32, out.shape, 0)
@@ -379,7 +383,7 @@
         out_specs=WHOLE,
         scratch_shapes=[VMEM((1, share), F32)],
         compiler_params=params(6),
-        cost_estimate=cost(20 * kept.size, 8 * kept.size),
+        cost_estimate=cost(),
     )(*args)
 
 
@@ -410,7 +414,7 @@
         in_specs=[WHOLE] * 4,
         out_specs=WHOLE,
         compiler_params=params(8),
-        cost_estimate=cost(16 * w.size, 8 * w.shape[0]),
+        cost_estimate=cost(),
     )(first, second, other, w)
 
 
@@ -447,7 +451,7 @@
         in_specs=[WHOLE] * 8,
         out_specs=WHOLE,
         compiler_params=params(8),
-        cost_estimate=cost(4 * captions.size, 2 * captions.size),
+        cost_estimate=cost(),
     )(own, core, across, both, bias, captions, text_scale, pairs)
 
 
@@ -493,9 +497,9 @@
 
     def chip_sum(index, keep, gots, *others):
         chip, note = small(
-            chip_sum_kernel,
+            lambda *refs: chip_sum_kernel(index, *refs),
             "chip_sum",
-            (struct((rows + NOTE_ROWS, share), BF16), struct((1, 4 * rows))),
+            (struct((rows + (0 if index == 1 else NOTE_ROWS), share), BF16), struct((1, 4 * rows))),
             keep,
             *gots,
             *others,
@@ -510,7 +514,7 @@
     passed = along("passed_rows", middle, OUTWARD)
     crossed = along("crossed_rows", near, MIDDLE)
 
-    def later_a(index, rows_of, ready_after, sums_after=()):
+    def later_a(index, rows_of, ready_after, *others):
         halves = (struct((rows + 16, share // 2), BF16), struct((rows, share // 2), BF16))
         *gives, keep, ready, own = later_block(
             lambda *refs: later_a_kernel(len(rows_of), *refs),
@@ -518,8 +522,8 @@
             (*halves, struct((rows, share)), struct((rows, depth), BF16), struct((1, 2 * rows))),
             4 * rows * depth * share,
         )
-        gots = after([other_core(f"core_sum_{index}a", give) for give in gives], sums_after)
-        return ready, *chip_sum(index, keep, gots, own)
+        gots = [other_core(f"core_sum_{index}a", give) for give in gives]
+        return ready, *chip_sum(index, keep, gots, own, *others)
 
     def later_b(index, ready, *others):
         ready = lax.optimization_barrier((ready, others))[0]
@@ -546,7 +550,7 @@
     crossed = after(crossed, keep_0)
     last = along("last_rows", crossed, OUTWARD)
 
-    ready_2, chip_2, note_2, far_2 = later_a(2, (middle, passed), far_0)
+    ready_2, chip_2, note_2, far_2 = later_a(2, (middle, passed), far_0, note_1)
     give_0, give_held, resid = first_part(
         first_give_kernel,
         "first_give",
@@ -572,9 +576,9 @@
         far_0,
     )
     parts = [
-        pool(width, keep_0, nears_0, far_0, bias, gains, note_0),
-        pool(width, keep_1, nears_1, far_1, bias, gains, note_1),
-        pool(width, keep_2, nears_2, far_2, bias, gains, note_2),
+        pool(width, 0, keep_0, nears_0, far_0, far_0, bias, gains, note_0),
+        pool(width, 3, keep_1, nears_1, far_1, far_2, bias, gains, note_1),
+        pool(width, 0, keep_2, nears_2, far_2, far_2, bias, gains, note_2),
     ]
     pooled = pool_all(width, keep_3, nears_3, far_3, bias, gains, note_3, parts)
 
@@ -609,6 +613,7 @@
             and PATCHES % rows == 0
             and depth % 256 == 0
             and w_in.shape[1] % 1024 == 0
+            and w_in.shape[1] >= 16 * rows
         )
         return (staged if fits else plain)(tokens, ln_gain, w_in, *rest)
 

time: 73.9 us -> 73.9 us (level)
  no operation moved by 1% of the time
where the time goes in v6:
time: 73.9 us; the launch traced here: 73.7 us
  Pallas kernels  28.1 us (38%)
  starting transfers between devices  23.3 us (32%)
  waiting for transfers between devices  21.6 us (29%)
    ppermute x8, starting transfers between devices, along(): return lax.ppermute(value, 'mrow', list(pairs))  11.5 us
    ppermute x8, waiting for transfers between devices, along(): return lax.ppermute(value, 'mrow', list(pairs))  9.74 us
    pallas_call x6, Pallas kernels, later_block(): pl.pallas_call(kernel, name='later_block', out_shape=out, in_specs=[WHOLE...  8.94 us
    ppermute x6, waiting for transfers between devices, other_chip(): return lax.ppermute(value, 'mcol', [(0, 1), (1, 0)])  7.17 us
    pallas_call x2, Pallas kernels, first_part(): pl.pallas_call(kernel, name=name, out_shape=shapes, in_specs=[WHOLE, WHOL...  6.22 us
    ppermute x6, starting transfers between devices, other_chip(): return lax.ppermute(value, 'mcol', [(0, 1), (1, 0)])  5.82 us
    pallas_call x1, Pallas kernels, first_a(): pl.pallas_call(first_a_kernel, name='first_a', out_shape=(struct((rows +...  4.66 us
    ppermute x15, waiting for transfers between devices, other_core(): return lax.ppermute(value, 'sub', [(0, 1), (1, 0)])  4.54 us
  transfers between devices with their start and end apart: 31, of which 16 were waited for; matrix products, arithmetic and copies ran while one was open for 0% of the time, Pallas kernels for 34%

profile of v6, /device:TPU:0, one launch (start us, length us, event | category | flops | bytes accessed | tf_op | source)
XLA Modules:
  0.0 73.7 jit_solution(14592593375456207014)
XLA Ops:
  0.0 3.0 %collective-permute-start = (bf16[128,1536]{1,0:T(8,128)(2,1)}, bf16[128,1536]{1,0:T(8,128)(2,1)S(1)}, u32[]{:S(2)}, u32[]{:S(2)}) collective-permute-start(bf16[128,1536]{1,0:T(8,128)(2,1)} %tokens.3), channel_id=1, source_target_pairs={{0,4},{4,0},{8,12},{12,8},{1,5},{5,1},{9,13},{13,9},{2,6},{6,2},{1... | collective-permute-start | bytes 1179656 | tf_op jit(solution)/shard_map/near_rows/ppermute | solution.py:475
  3.0 0.7 collective-permute-start.8
  3.7 4.7 %first_a.1 = (bf16[144,768]{1,0:T(8,128)(2,1)S(1)}, bf16[144,768]{1,0:T(8,128)(2,1)S(1)}, f32[128,1536]{1,0:T(8,128)S(1)}, f32[1,1536]{1,0:T(1,128)S(1)}, f32[1,...) custom-call(bf16[128,1536]{1,0:T(8,128)(2,1)} %tokens.3, f32[1536]{0:T(1024)} %gain.1, ...), custom_call_target="tpu_custom_call" | custom-call | flops 1024 | bytes 1024 | tf_op jit(solution)/shard_map/first_a/pallas_call | solution.py:173
  8.4 0.1 collective-permute-start.1
  8.5 0.5 collective-permute-start.2
  9.0 1.0 %collective-permute-done.1.refs_1_ = bf16[144,768]{1,0:T(8,128)(2,1)S(1)} collective-permute-done((bf16[144,768]{1,0:T(8,128)(2,1)S(1)}, bf16[144,768]{1,0:T(8,128)(2,1)S(1)}, u32[]{:S(2)}, u32[]{:S(2)}) %collective-permute-start.1) | collective-permute-done | bytes 221216 | tf_op jit(solution)/shard_map/core_sum_0a/ppermute | solution.py:460
  9.9 0.3 collective-permute-done.2.refs_2_
  10.2 0.1 chip_sum.4
  10.4 1.6 %collective-permute-start.10 = (bf16[136,1536]{1,0:T(8,128)(2,1)S(1)}, bf16[136,1536]{1,0:T(8,128)(2,1)S(1)}, u32[]{:S(2)}, u32[]{:S(2)}) collective-permute-start(bf16[136,1536]{1,0:T(8,128)(2,1)S(1)} %get-tuple-element.68), channel_id=1, source_target_pairs={{0,2},{2,0},{1,3},{3,1},{4,6},{6,4},{5,7},{7,5},{8,10},{10,8},{9,1... | collective-permute-start | bytes 1253384 | tf_op jit(solution)/shard_map/chip_sum_0/ppermute | solution.py:465
  11.9 0.4 collective-permute-done.refs_0_
  12.3 0.7 collective-permute-start.3
  13.0 1.3 %collective-permute-start.9 = (bf16[128,1536]{1,0:T(8,128)(2,1)S(1)}, bf16[128,1536]{1,0:T(8,128)(2,1)S(1)}, u32[]{:S(2)}, u32[]{:S(2)}) collective-permute-start(bf16[128,1536]{1,0:T(8,128)(2,1)S(1)} %collective-permute-done.8.refs_0_), channel_id=1, source_target_pairs={{4,0},{8,12},{5,1},{9,13},{6,2},{10,14},{7,3},{11,15},{20,16},{24,... | collective-permute-start | bytes 1179656 | tf_op jit(solution)/shard_map/passed_rows/ppermute | solution.py:475
  14.4 1.6 %later_block.6 = (bf16[144,768]{1,0:T(8,128)(2,1)S(1)}, bf16[128,768]{1,0:T(8,128)(2,1)S(1)}, f32[128,1536]{1,0:T(8,128)S(1)}, bf16[128,1536]{1,0:T(8,128)(2,1)S(1)}, f32[1,256]{1,0:T(1,128)S(1)}) custom-call(bf16[128,1536]{1,0:T(8,128)(2,1)S(1)} %collective-permute-done.refs_0_, f32[1,1536]{1,0:T(1,128)S(1)} %get-tuple-element.96.refs_1_.gain.refs_2_, ...), custom_call_target="tpu_custom_call" | custom-call | flops 1207959552 | bytes 1024 | tf_op jit(solution)/shard_map/later_block/pallas_call | solution.py:265
  15.9 0.1 collective-permute-start.4
  16.0 0.5 collective-permute-start.5
  16.5 1.2 %collective-permute-done.5.refs_2_ = bf16[128,768]{1,0:T(8,128)(2,1)S(1)} collective-permute-done((bf16[128,768]{1,0:T(8,128)(2,1)S(1)}, bf16[128,768]{1,0:T(8,128)(2,1)S(1)}, u32[]{:S(2)}, u32[]{:S(2)}) %collective-permute-start.5) | collective-permute-done | bytes 196640 | tf_op jit(solution)/shard_map/core_sum_1a/ppermute | solution.py:460
  17.8 0.1 chip_sum.5
  17.9 1.7 %collective-permute-start.7 = (bf16[128,1536]{1,0:T(8,128)(2,1)S(1)}, bf16[128,1536]{1,0:T(8,128)(2,1)S(1)}, u32[]{:S(2)}, u32[]{:S(2)}) collective-permute-start(bf16[128,1536]{1,0:T(8,128)(2,1)S(1)} %get-tuple-element.76), channel_id=1, source_target_pairs={{0,2},{2,0},{1,3},{3,1},{4,6},{6,4},{5,7},{7,5},{8,10},{10,8},{9,1... | collective-permute-start | bytes 1179656 | tf_op jit(solution)/shard_map/chip_sum_1/ppermute | solution.py:465
  19.6 3.1 %first_keep.1 = (f32[128,1536]{1,0:T(8,128)S(1)}, f32[1,1536]{1,0:T(1,128)S(1)}, bf16[1536,1536]{1,0:T(8,128)(2,1)S(1)}) custom-call(bf16[128,1536]{1,0:T(8,128)(2,1)S(1)} %copy-done, f32[1,1536]{1,0:T(1,128)S(1)} %get-tuple-element.96.refs_1_.gain.refs_2_, bf16[1536,6144]{1,0:T(8,128)(2,1)} %w.5), custom_call_target="tpu_custom_call" | custom-call | flops 1024 | bytes 1024 | tf_op jit(solution)/shard_map/first_keep/pallas_call | solution.py:219
  22.7 0.3 collective-permute-done.10.refs_2_.refs_3_
  22.9 1.5 %collective-permute-start.6 = (bf16[128,1536]{1,0:T(8,128)(2,1)S(1)}, bf16[128,1536]{1,0:T(8,128)(2,1)S(1)}, u32[]{:S(2)}, u32[]{:S(2)}) collective-permute-start(bf16[128,1536]{1,0:T(8,128)(2,1)S(1)} %collective-permute-done.3.refs_0_), channel_id=1, source_target_pairs={{4,0},{8,12},{5,1},{9,13},{6,2},{10,14},{7,3},{11,15},{20,16},{24,... | collective-permute-start | bytes 1179656 | tf_op jit(solution)/shard_map/last_rows/ppermute | solution.py:475
  24.4 4.3 %collective-permute-done.9.refs_1_ = bf16[128,1536]{1,0:T(8,128)(2,1)S(1)} collective-permute-done((bf16[128,1536]{1,0:T(8,128)(2,1)S(1)}, bf16[128,1536]{1,0:T(8,128)(2,1)S(1)}, u32[]{:S(2)}, u32[]{:S(2)}) %collective-permute-start.9) | collective-permute-done | bytes 393248 | tf_op jit(solution)/shard_map/passed_rows/ppermute | solution.py:475
  28.7 1.6 %later_block.7 = (bf16[144,768]{1,0:T(8,128)(2,1)S(1)}, bf16[128,768]{1,0:T(8,128)(2,1)S(1)}, f32[128,1536]{1,0:T(8,128)S(1)}, bf16[128,1536]{1,0:T(8,128)(2,1)S(1)}, f32[1,256]{1,0:T(1,128)S(1)}) custom-call(bf16[128,1536]{1,0:T(8,128)(2,1)S(1)} %collective-permute-done.8.refs_0_, bf16[128,1536]{1,0:T(8,128)(2,1)S(1)} %collective-permute-done.9.refs_1_, ...), custom_call_target="tpu_custom_call" | custom-call | flops 1207959552 | bytes 1024 | tf_op jit(solution)/shard_map/later_block/pallas_call | solution.py:265
  30.4 0.5 collective-permute-start.12
  30.9 1.2 %collective-permute-done.12.refs_2_ = bf16[128,768]{1,0:T(8,128)(2,1)S(1)} collective-permute-done((bf16[128,768]{1,0:T(8,128)(2,1)S(1)}, bf16[128,768]{1,0:T(8,128)(2,1)S(1)}, u32[]{:S(2)}, u32[]{:S(2)}) %collective-permute-start.12) | collective-permute-done | bytes 196640 | tf_op jit(solution)/shard_map/core_sum_2a/ppermute | solution.py:460
  32.1 0.1 chip_sum.6
  32.2 0.6 collective-permute-start.13
  32.8 3.2 %first_give.1 = (bf16[144,1536]{1,0:T(8,128)(2,1)S(1)}, bf16[1536,1536]{1,0:T(8,128)(2,1)S(1)}, f32[1,1536]{1,0:T(1,128)S(1)}) custom-call(bf16[128,1536]{1,0:T(8,128)(2,1)S(1)} %copy-done, f32[1,1536]{1,0:T(1,128)S(1)} %get-tuple-element.96.refs_1_.gain.refs_2_, bf16[1536,6144]{1,0:T(8,128)(2,1)} %w.5), custom_call_target="tpu_custom_call" | custom-call | flops 1024 | bytes 1024 | tf_op jit(solution)/shard_map/first_give/pallas_call | solution.py:219
  36.0 1.4 %later_block.8 = (bf16[128,1536]{1,0:T(8,128)(2,1)S(1)}, f32[128,1536]{1,0:T(8,128)S(1)}) custom-call(bf16[128,1536]{1,0:T(8,128)(2,1)S(1)} %get-tuple-element.92.left, bf16[1536,1536]{1,0:T(8,128)(2,1)S(1)} %get-tuple-element.93.give_held, bf16[1536,1536]{1,0:T(8,128)(2,1)S(1)} %get-tuple-element.94.keep_held), custom_call_target="tpu_custom_call" | custom-call | flops 1207959552 | bytes 1024 | tf_op jit(solution)/shard_map/later_block/pallas_call | solution.py:265
  37.4 1.3 %collective-permute-done.6.refs_1_ = bf16[128,1536]{1,0:T(8,128)(2,1)S(1)} collective-permute-done((bf16[128,1536]{1,0:T(8,128)(2,1)S(1)}, bf16[128,1536]{1,0:T(8,128)(2,1)S(1)}, u32[]{:S(2)}, u32[]{:S(2)}) %collective-permute-start.6) | collective-permute-done | bytes 393248 | tf_op jit(solution)/shard_map/last_rows/ppermute | solution.py:475
  38.7 1.6 %later_block.9 = (bf16[144,768]{1,0:T(8,128)(2,1)S(1)}, bf16[128,768]{1,0:T(8,128)(2,1)S(1)}, f32[128,1536]{1,0:T(8,128)S(1)}, bf16[128,1536]{1,0:T(8,128)(2,1)S(1)}, f32[1,256]{1,0:T(1,128)S(1)}) custom-call(bf16[128,1536]{1,0:T(8,128)(2,1)S(1)} %collective-permute-done.3.refs_0_, bf16[128,1536]{1,0:T(8,128)(2,1)S(1)} %collective-permute-done.6.refs_1_, ...), custom_call_target="tpu_custom_call" | custom-call | flops 1207959552 | bytes 1024 | tf_op jit(solution)/shard_map/later_block/pallas_call | solution.py:265
  40.3 0.1 collective-permute-start.14
  40.4 0.5 collective-permute-start.15
  40.9 0.1 collective-permute-start.19
  41.0 0.4 collective-permute-start.20
  41.4 0.7 collective-permute-done.15.refs_2_
  42.2 0.1 chip_sum.7
  42.2 0.6 collective-permute-start.18
  42.8 1.2 %collective-permute-done.13.refs_3_.refs_2_ = bf16[136,1536]{1,0:T(8,128)(2,1)S(1)} collective-permute-done((bf16[136,1536]{1,0:T(8,128)(2,1)S(1)}, bf16[136,1536]{1,0:T(8,128)(2,1)S(1)}, u32[]{:S(2)}, u32[]{:S(2)}) %collective-permute-start.13) | collective-permute-done | bytes 417824 | tf_op jit(solution)/shard_map/chip_sum_2/ppermute | solution.py:465
  44.0 1.4 %later_block.10 = (bf16[128,1536]{1,0:T(8,128)(2,1)S(1)}, f32[128,1536]{1,0:T(8,128)S(1)}) custom-call(bf16[128,1536]{1,0:T(8,128)(2,1)S(1)} %get-tuple-element.105.left, bf16[1536,1536]{1,0:T(8,128)(2,1)S(1)} %get-tuple-element.93.give_held, bf16[1536,1536]{1,0:T(8,128)(2,1)S(1)} %get-tuple-element.94.keep_held), custom_call_target="tpu_custom_call" | custom-call | flops 1207959552 | bytes 1024 | tf_op jit(solution)/shard_map/later_block/pallas_call | solution.py:265
  45.5 1.4 %later_block.11 = (bf16[128,768]{1,0:T(8,128)(2,1)S(1)}, bf16[128,768]{1,0:T(8,128)(2,1)S(1)}, f32[128,1536]{1,0:T(8,128)S(1)}) custom-call(bf16[128,1536]{1,0:T(8,128)(2,1)S(1)} %get-tuple-element.107.left, bf16[1536,1536]{1,0:T(8,128)(2,1)S(1)} %get-tuple-element.93.give_held, bf16[1536,1536]{1,0:T(8,128)(2,1)S(1)} %get-tuple-element.94.keep_held), custom_call_target="tpu_custom_call" | custom-call | flops 1207959552 | bytes 1024 | tf_op jit(solution)/shard_map/later_block/pallas_call | solution.py:265
  46.9 0.5 collective-permute-start.16
  47.5 0.1 collective-permute-start.17
  47.6 1.0 %pool.3.refs_7_ = f32[1,1536]{1,0:T(1,128)S(1)} custom-call(f32[128,1536]{1,0:T(8,128)S(1)} %get-tuple-element.78.refs_0_, bf16[144,1536]{1,0:T(8,128)(2,1)S(1)} %collective-permute-done.19.refs_1_, bf16[136,1536]{1,0:T(8,128)(2,1)S(1)} %collective-permute-done.10.refs_2_.refs_3_, bf16[136,1536]{1,0:T(8,128)(2,1)S(1)} %collective-permute-done.10.refs_2_.refs_3_, ...), custom_call_target="tpu_custom_call" | custom-call | flops 1024 | bytes 1024 | tf_op jit(solution)/shard_map/pool/pallas_call | solution.py:352
  48.7 1.0 %pool.4.refs_8_ = f32[1,1536]{1,0:T(1,128)S(1)} custom-call(f32[128,1536]{1,0:T(8,128)S(1)} %get-tuple-element.115.refs_0_, bf16[128,1536]{1,0:T(8,128)(2,1)S(1)} %collective-permute-done.20.refs_1_, bf16[128,1536]{1,0:T(8,128)(2,1)S(1)} %collective-permute-done.7.refs_2_, bf16[136,1536]{1,0:T(8,128)(2,1)S(1)} %collective-permute-done.13.refs_3_.refs_2_, ...), custom_call_target="tpu_custom_call" | custom-call | flops 1024 | bytes 1024 | tf_op jit(solution)/shard_map/pool/pallas_call | solution.py:352
  49.7 1.0 %pool.5.refs_9_ = f32[1,1536]{1,0:T(1,128)S(1)} custom-call(f32[128,1536]{1,0:T(8,128)S(1)} %get-tuple-element.116.refs_0_, bf16[128,1536]{1,0:T(8,128)(2,1)S(1)} %collective-permute-done.21.refs_1_, bf16[136,1536]{1,0:T(8,128)(2,1)S(1)} %collective-permute-done.13.refs_3_.refs_2_, bf16[136,1536]{1,0:T(8,128)(2,1)S(1)} %collective-permute-done.13.refs_3_.refs_2_, ...), custom_call_target="tpu_custom_call" | custom-call | flops 1024 | bytes 1024 | tf_op jit(solution)/shard_map/pool/pallas_call | solution.py:352
  50.8 3.3 %collective-permute-done.18.refs_3_ = bf16[136,1536]{1,0:T(8,128)(2,1)S(1)} collective-permute-done((bf16[136,1536]{1,0:T(8,128)(2,1)S(1)}, bf16[136,1536]{1,0:T(8,128)(2,1)S(1)}, u32[]{:S(2)}, u32[]{:S(2)}) %collective-permute-start.18) | collective-permute-done | bytes 417824 | tf_op jit(solution)/shard_map/chip_sum_3/ppermute | solution.py:465
  54.1 1.1 %pool_all.1.refs_0_ = f32[2,1536]{1,0:T(2,128)S(1)} custom-call(f32[128,1536]{1,0:T(8,128)S(1)} %get-tuple-element.108.refs_0_, bf16[128,768]{1,0:T(8,128)(2,1)S(1)} %collective-permute-done.16.refs_1_, bf16[128,768]{1,0:T(8,128)(2,1)S(1)} %collective-permute-done.17.refs_2_, bf16[136,1536]{1,0:T(8,128)(2,1)S(1)} %collective-permute-done.18.refs_3_, ...), custom_call_target="tpu_custom_call" | custom-call | flops 1024 | bytes 1024 | tf_op jit(solution)/shard_map/pool_all/pallas_call | solution.py:378
  55.2 0.6 collective-permute-start.22
  55.8 1.3 %collective-permute-start.23 = (f32[2,1536]{1,0:T(2,128)S(1)}, f32[2,1536]{1,0:T(2,128)S(1)}, u32[]{:S(2)}, u32[]{:S(2)}) collective-permute-start(f32[2,1536]{1,0:T(2,128)S(1)} %pool_all.1.refs_0_), channel_id=1, source_target_pairs={{0,3},{1,2},{2,1},{3,0},{4,7},{5,6},{6,5},{7,4},{8,11},{9,10},{10,... | collective-permute-start | bytes 36872 | tf_op jit(solution)/shard_map/both_pool/ppermute | solution.py:470
  57.1 1.3 %mix.2.refs_2_ = f32[2,1536]{1,0:T(2,128)S(1)} custom-call(f32[2,1536]{1,0:T(2,128)S(1)} %pool_all.1.refs_0_, f32[2,1536]{1,0:T(2,128)S(1)} %collective-permute-done.24.refs_1_, f32[1,1536]{1,0:T(1,128)S(1)} %get-tuple-element.118.refs_2_, bf16[6144,1536]{1,0:T(8,128)(2,1)S(1)} %bitcast.7), custom_call_target="tpu_custom_call" | custom-call | flops 1024 | bytes 1024 | tf_op jit(solution)/shard_map/mix/pallas_call | solution.py:410
  58.5 0.6 collective-permute-done.22.refs_0_
  59.1 1.3 %mix.3 = f32[2,1536]{1,0:T(2,128)S(1)} custom-call(f32[2,1536]{1,0:T(2,128)S(1)} %collective-permute-done.22.refs_0_, f32[2,1536]{1,0:T(2,128)S(1)} %collective-permute-done.23.refs_1_, f32[2,1536]{1,0:T(2,128)S(1)} %mix.2.refs_2_, bf16[6144,1536]{1,0:T(8,128)(2,1)S(1)} %bitcast.7), custom_call_target="tpu_custom_call" | custom-call | flops 1024 | bytes 1024 | tf_op jit(solution)/shard_map/mix/pallas_call | solution.py:410
  60.4 1.5 %collective-permute-start.25 = (f32[2,1536]{1,0:T(2,128)S(1)}, f32[2,1536]{1,0:T(2,128)S(1)}, u32[]{:S(2)}, u32[]{:S(2)}) collective-permute-start(f32[2,1536]{1,0:T(2,128)S(1)} %mix.3), channel_id=1, source_target_pairs={{0,4},{4,0},{8,12},{12,8},{1,5},{5,1},{9,13},{13,9},{2,6},{6,2},{1... | collective-permute-start | bytes 36872 | tf_op jit(solution)/shard_map/swap_mixed/ppermute | solution.py:475
  61.9 1.4 %collective-permute-start.26 = (f32[2,1536]{1,0:T(2,128)S(1)}, f32[2,1536]{1,0:T(2,128)S(1)}, u32[]{:S(2)}, u32[]{:S(2)}) collective-permute-start(f32[2,1536]{1,0:T(2,128)S(1)} %mix.3), channel_id=1, source_target_pairs={{0,8},{8,0},{4,12},{12,4},{1,9},{9,1},{5,13},{13,5},{2,10},{10,2},... | collective-permute-start | bytes 36872 | tf_op jit(solution)/shard_map/skip_mixed/ppermute | solution.py:475
  63.2 1.6 %collective-permute-start.27 = (f32[2,1536]{1,0:T(2,128)S(1)}, f32[2,1536]{1,0:T(2,128)S(1)}, u32[]{:S(2)}, u32[]{:S(2)}) collective-permute-start(f32[2,1536]{1,0:T(2,128)S(1)} %mix.3), channel_id=1, source_target_pairs={{0,12},{12,0},{4,8},{8,4},{1,13},{13,1},{5,9},{9,5},{2,14},{14,2},... | collective-permute-start | bytes 36872 | tf_op jit(solution)/shard_map/ends_mixed/ppermute | solution.py:475
  64.8 0.3 multiply_reduce_fusion
  65.1 1.5 %collective-permute-done.26 = f32[2,1536]{1,0:T(2,128)S(1)} collective-permute-done((f32[2,1536]{1,0:T(2,128)S(1)}, f32[2,1536]{1,0:T(2,128)S(1)}, u32[]{:S(2)}, u32[]{:S(2)}) %collective-permute-start.26) | collective-permute-done | bytes 12320 | tf_op jit(solution)/shard_map/skip_mixed/ppermute | solution.py:475
  66.6 2.1 %collective-permute-done.27 = f32[2,1536]{1,0:T(2,128)S(1)} collective-permute-done((f32[2,1536]{1,0:T(2,128)S(1)}, f32[2,1536]{1,0:T(2,128)S(1)}, u32[]{:S(2)}, u32[]{:S(2)}) %collective-permute-start.27) | collective-permute-done | bytes 12320 | tf_op jit(solution)/shard_map/ends_mixed/ppermute | solution.py:475
  68.8 0.8 %collective-permute-start.29 = (f32[2,1536]{1,0:T(2,128)S(1)}, f32[2,1536]{1,0:T(2,128)S(1)}, u32[]{:S(2)}, u32[]{:S(2)}) collective-permute-start(f32[2,1536]{1,0:T(2,128)S(1)} %add_add_fusion.own), channel_id=1, source_target_pairs={{0,2},{2,0},{1,3},{3,1},{4,6},{6,4},{5,7},{7,5},{8,10},{10,8},{9,1... | collective-permute-start | bytes 36872 | tf_op jit(solution)/shard_map/chip_embed/ppermute | solution.py:465
  69.6 1.1 %collective-permute-start.30 = (f32[2,1536]{1,0:T(2,128)S(1)}, f32[2,1536]{1,0:T(2,128)S(1)}, u32[]{:S(2)}, u32[]{:S(2)}) collective-permute-start(f32[2,1536]{1,0:T(2,128)S(1)} %add_add_fusion.own), channel_id=1, source_target_pairs={{0,3},{1,2},{2,1},{3,0},{4,7},{5,6},{6,5},{7,4},{8,11},{9,10},{10,... | collective-permute-start | bytes 36872 | tf_op jit(solution)/shard_map/both_embed/ppermute | solution.py:470
  70.7 1.9 %collective-permute-done.29.across = f32[2,1536]{1,0:T(2,128)S(1)} collective-permute-done((f32[2,1536]{1,0:T(2,128)S(1)}, f32[2,1536]{1,0:T(2,128)S(1)}, u32[]{:S(2)}, u32[]{:S(2)}) %collective-permute-start.29) | collective-permute-done | bytes 12320 | tf_op jit(solution)/shard_map/chip_embed/ppermute | solution.py:465
  72.6 0.1 collective-permute-done.30.both
  72.7 1.0 %score.1 = f32[1,64]{1,0:T(1,128)} custom-call(f32[2,1536]{1,0:T(2,128)S(1)} %add_add_fusion.own, f32[2,1536]{1,0:T(2,128)S(1)} %collective-permute-done.28.core, f32[2,1536]{1,0:T(2,128)S(1)} %collective-permute-done.29.across, f32[2,1536]{1,0:T(2,128)S(1)} %collective-permute-done.30.both, f32[1,6144]{1,0:T(1,128)S(1)} %bitcast.12, ...), custom_call_target="tpu_custom_call" | custom-call | flops 1024 | bytes 1024 | tf_op jit(solution)/shard_map/score/pallas_call | solution.py:447
  (43 shorter events, 0.4 us)
Async XLA Ops:
  0.0 12.3 %collective-permute-start = (bf16[128,1536]{1,0:T(8,128)(2,1)}, bf16[128,1536]{1,0:T(8,128)(2,1)S(1)}, u32[]{:S(2)}, u32[]{:S(2)}) collective-permute-start(bf16[128,1536]{1,0:T(8,128)(2,1)} %tokens.3), channel_id=1, source_target_pairs={{0,4},{4,0},{8,12},{12,8},{1,5},{5,1},{9,13},{13,9},{2,6},{6,2},{1... | collective-permute-start | bytes 1179656 | tf_op jit(solution)/shard_map/near_rows/ppermute | solution.py:475
  3.0 10.0 %collective-permute-start.8 = (bf16[128,1536]{1,0:T(8,128)(2,1)}, bf16[128,1536]{1,0:T(8,128)(2,1)S(1)}, u32[]{:S(2)}, u32[]{:S(2)}) collective-permute-start(bf16[128,1536]{1,0:T(8,128)(2,1)} %tokens.3), channel_id=1, source_target_pairs={{4,8},{8,4},{5,9},{9,5},{6,10},{10,6},{7,11},{11,7},{20,24},{24,20... | collective-permute-start | bytes 1179656 | tf_op jit(solution)/shard_map/middle_rows/ppermute | solution.py:475
  8.4 1.5 %collective-permute-start.1 = (bf16[144,768]{1,0:T(8,128)(2,1)S(1)}, bf16[144,768]{1,0:T(8,128)(2,1)S(1)}, u32[]{:S(2)}, u32[]{:S(2)}) collective-permute-start(bf16[144,768]{1,0:T(8,128)(2,1)S(1)} %get-tuple-element.64), channel_id=1, source_target_pairs={{0,1},{1,0},{2,3},{3,2},{4,5},{5,4},{6,7},{7,6},{8,9},{9,8},{10,11... | collective-permute-start | bytes 663560 | tf_op jit(solution)/shard_map/core_sum_0a/ppermute | solution.py:460
  8.5 1.8 %collective-permute-start.2 = (bf16[144,768]{1,0:T(8,128)(2,1)S(1)}, bf16[144,768]{1,0:T(8,128)(2,1)S(1)}, u32[]{:S(2)}, u32[]{:S(2)}) collective-permute-start(bf16[144,768]{1,0:T(8,128)(2,1)S(1)} %get-tuple-element.65), channel_id=1, source_target_pairs={{0,1},{1,0},{2,3},{3,2},{4,5},{5,4},{6,7},{7,6},{8,9},{9,8},{10,11... | collective-permute-start | bytes 663560 | tf_op jit(solution)/shard_map/core_sum_0a/ppermute | solution.py:460
  10.4 12.5 %collective-permute-start.10 = (bf16[136,1536]{1,0:T(8,128)(2,1)S(1)}, bf16[136,1536]{1,0:T(8,128)(2,1)S(1)}, u32[]{:S(2)}, u32[]{:S(2)}) collective-permute-start(bf16[136,1536]{1,0:T(8,128)(2,1)S(1)} %get-tuple-element.68), channel_id=1, source_target_pairs={{0,2},{2,0},{1,3},{3,1},{4,6},{6,4},{5,7},{7,5},{8,10},{10,8},{9,1... | collective-permute-start | bytes 1253384 | tf_op jit(solution)/shard_map/chip_sum_0/ppermute | solution.py:465
  12.3 10.6 %collective-permute-start.3 = (bf16[128,1536]{1,0:T(8,128)(2,1)S(1)}, bf16[128,1536]{1,0:T(8,128)(2,1)S(1)}, u32[]{:S(2)}, u32[]{:S(2)}) collective-permute-start(bf16[128,1536]{1,0:T(8,128)(2,1)S(1)} %collective-permute-done.refs_0_), channel_id=1, source_target_pairs={{4,8},{8,4},{5,9},{9,5},{6,10},{10,6},{7,11},{11,7},{20,24},{24,20... | collective-permute-start | bytes 1179656 | tf_op jit(solution)/shard_map/crossed_rows/ppermute | solution.py:475
  13.0 15.7 %collective-permute-start.9 = (bf16[128,1536]{1,0:T(8,128)(2,1)S(1)}, bf16[128,1536]{1,0:T(8,128)(2,1)S(1)}, u32[]{:S(2)}, u32[]{:S(2)}) collective-permute-start(bf16[128,1536]{1,0:T(8,128)(2,1)S(1)} %collective-permute-done.8.refs_0_), channel_id=1, source_target_pairs={{4,0},{8,12},{5,1},{9,13},{6,2},{10,14},{7,3},{11,15},{20,16},{24,... | collective-permute-start | bytes 1179656 | tf_op jit(solution)/shard_map/passed_rows/ppermute | solution.py:475
  14.3 5.2 %copy-start = (bf16[128,1536]{1,0:T(8,128)(2,1)S(1)}, bf16[128,1536]{1,0:T(8,128)(2,1)}, u32[]{:S(2)}) copy-start(bf16[128,1536]{1,0:T(8,128)(2,1)} %tokens.3) | copy-start | bytes 1179652
  15.9 1.8 %collective-permute-start.4 = (bf16[144,768]{1,0:T(8,128)(2,1)S(1)}, bf16[144,768]{1,0:T(8,128)(2,1)S(1)}, u32[]{:S(2)}, u32[]{:S(2)}) collective-permute-start(bf16[144,768]{1,0:T(8,128)(2,1)S(1)} %get-tuple-element.73), channel_id=1, source_target_pairs={{0,1},{1,0},{2,3},{3,2},{4,5},{5,4},{6,7},{7,6},{8,9},{9,8},{10,11... | collective-permute-start | bytes 663560 | tf_op jit(solution)/shard_map/core_sum_1a/ppermute | solution.py:460
  16.0 1.7 %collective-permute-start.5 = (bf16[128,768]{1,0:T(8,128)(2,1)S(1)}, bf16[128,768]{1,0:T(8,128)(2,1)S(1)}, u32[]{:S(2)}, u32[]{:S(2)}) collective-permute-start(bf16[128,768]{1,0:T(8,128)(2,1)S(1)} %get-tuple-element.74), channel_id=1, source_target_pairs={{0,1},{1,0},{2,3},{3,2},{4,5},{5,4},{6,7},{7,6},{8,9},{9,8},{10,11... | collective-permute-start | bytes 589832 | tf_op jit(solution)/shard_map/core_sum_1a/ppermute | solution.py:460
  17.9 18.1 %collective-permute-start.7 = (bf16[128,1536]{1,0:T(8,128)(2,1)S(1)}, bf16[128,1536]{1,0:T(8,128)(2,1)S(1)}, u32[]{:S(2)}, u32[]{:S(2)}) collective-permute-start(bf16[128,1536]{1,0:T(8,128)(2,1)S(1)} %get-tuple-element.76), channel_id=1, source_target_pairs={{0,2},{2,0},{1,3},{3,1},{4,6},{6,4},{5,7},{7,5},{8,10},{10,8},{9,1... | collective-permute-start | bytes 1179656 | tf_op jit(solution)/shard_map/chip_sum_1/ppermute | solution.py:465
  22.9 15.8 %collective-permute-start.6 = (bf16[128,1536]{1,0:T(8,128)(2,1)S(1)}, bf16[128,1536]{1,0:T(8,128)(2,1)S(1)}, u32[]{:S(2)}, u32[]{:S(2)}) collective-permute-start(bf16[128,1536]{1,0:T(8,128)(2,1)S(1)} %collective-permute-done.3.refs_0_), channel_id=1, source_target_pairs={{4,0},{8,12},{5,1},{9,13},{6,2},{10,14},{7,3},{11,15},{20,16},{24,... | collective-permute-start | bytes 1179656 | tf_op jit(solution)/shard_map/last_rows/ppermute | solution.py:475
  30.3 1.8 %collective-permute-start.11 = (bf16[144,768]{1,0:T(8,128)(2,1)S(1)}, bf16[144,768]{1,0:T(8,128)(2,1)S(1)}, u32[]{:S(2)}, u32[]{:S(2)}) collective-permute-start(bf16[144,768]{1,0:T(8,128)(2,1)S(1)} %get-tuple-element.84), channel_id=1, source_target_pairs={{0,1},{1,0},{2,3},{3,2},{4,5},{5,4},{6,7},{7,6},{8,9},{9,8},{10,11... | collective-permute-start | bytes 663560 | tf_op jit(solution)/shard_map/core_sum_2a/ppermute | solution.py:460
  30.4 1.7 %collective-permute-start.12 = (bf16[128,768]{1,0:T(8,128)(2,1)S(1)}, bf16[128,768]{1,0:T(8,128)(2,1)S(1)}, u32[]{:S(2)}, u32[]{:S(2)}) collective-permute-start(bf16[128,768]{1,0:T(8,128)(2,1)S(1)} %get-tuple-element.85), channel_id=1, source_target_pairs={{0,1},{1,0},{2,3},{3,2},{4,5},{5,4},{6,7},{7,6},{8,9},{9,8},{10,11... | collective-permute-start | bytes 589832 | tf_op jit(solution)/shard_map/core_sum_2a/ppermute | solution.py:460
  32.2 11.8 %collective-permute-start.13 = (bf16[136,1536]{1,0:T(8,128)(2,1)S(1)}, bf16[136,1536]{1,0:T(8,128)(2,1)S(1)}, u32[]{:S(2)}, u32[]{:S(2)}) collective-permute-start(bf16[136,1536]{1,0:T(8,128)(2,1)S(1)} %get-tuple-element.88), channel_id=1, source_target_pairs={{0,2},{2,0},{1,3},{3,1},{4,6},{6,4},{5,7},{7,5},{8,10},{10,8},{9,1... | collective-permute-start | bytes 1253384 | tf_op jit(solution)/shard_map/chip_sum_2/ppermute | solution.py:465
  38.7 18.4 %slice-start = ((s8[18874368]{0:T(1024)(128)(4,1)}), s8[2097152]{0:T(1024)(128)(4,1)S(1)}, s32[]{:S(2)}) async-start(s8[18874368]{0:T(1024)(128)(4,1)} %bitcast.6), calls=%async_computation | async-start | bytes 4194304
  38.7 18.4 %slice-start.1 = ((s8[18874368]{0:T(1024)(128)(4,1)}), s8[4194304]{0:T(1024)(128)(4,1)S(1)}, s32[]{:S(2)}) async-start(s8[18874368]{0:T(1024)(128)(4,1)} %bitcast.6), calls=%async_computation.1 | async-start | bytes 8388608
  40.3 1.8 %collective-permute-start.14 = (bf16[144,768]{1,0:T(8,128)(2,1)S(1)}, bf16[144,768]{1,0:T(8,128)(2,1)S(1)}, u32[]{:S(2)}, u32[]{:S(2)}) collective-permute-start(bf16[144,768]{1,0:T(8,128)(2,1)S(1)} %get-tuple-element.100), channel_id=1, source_target_pairs={{0,1},{1,0},{2,3},{3,2},{4,5},{5,4},{6,7},{7,6},{8,9},{9,8},{10,11... | collective-permute-start | bytes 663560 | tf_op jit(solution)/shard_map/core_sum_3a/ppermute | solution.py:460
  40.4 1.7 %collective-permute-start.15 = (bf16[128,768]{1,0:T(8,128)(2,1)S(1)}, bf16[128,768]{1,0:T(8,128)(2,1)S(1)}, u32[]{:S(2)}, u32[]{:S(2)}) collective-permute-start(bf16[128,768]{1,0:T(8,128)(2,1)S(1)} %get-tuple-element.101), channel_id=1, source_target_pairs={{0,1},{1,0},{2,3},{3,2},{4,5},{5,4},{6,7},{7,6},{8,9},{9,8},{10,11... | collective-permute-start | bytes 589832 | tf_op jit(solution)/shard_map/core_sum_3a/ppermute | solution.py:460
  40.9 6.6 %collective-permute-start.19 = (bf16[144,1536]{1,0:T(8,128)(2,1)S(1)}, bf16[144,1536]{1,0:T(8,128)(2,1)S(1)}, u32[]{:S(2)}, u32[]{:S(2)}) collective-permute-start(bf16[144,1536]{1,0:T(8,128)(2,1)S(1)} %get-tuple-element.90), channel_id=1, source_target_pairs={{0,1},{1,0},{2,3},{3,2},{4,5},{5,4},{6,7},{7,6},{8,9},{9,8},{10,11... | collective-permute-start | bytes 1327112 | tf_op jit(solution)/shard_map/core_sum_0b/ppermute | solution.py:460
  41.0 7.7 %collective-permute-start.20 = (bf16[128,1536]{1,0:T(8,128)(2,1)S(1)}, bf16[128,1536]{1,0:T(8,128)(2,1)S(1)}, u32[]{:S(2)}, u32[]{:S(2)}) collective-permute-start(bf16[128,1536]{1,0:T(8,128)(2,1)S(1)} %get-tuple-element.95), channel_id=1, source_target_pairs={{0,1},{1,0},{2,3},{3,2},{4,5},{5,4},{6,7},{7,6},{8,9},{9,8},{10,11... | collective-permute-start | bytes 1179656 | tf_op jit(solution)/shard_map/core_sum_1b/ppermute | solution.py:460
  42.2 11.8 %collective-permute-start.18 = (bf16[136,1536]{1,0:T(8,128)(2,1)S(1)}, bf16[136,1536]{1,0:T(8,128)(2,1)S(1)}, u32[]{:S(2)}, u32[]{:S(2)}) collective-permute-start(bf16[136,1536]{1,0:T(8,128)(2,1)S(1)} %get-tuple-element.103), channel_id=1, source_target_pairs={{0,2},{2,0},{1,3},{3,1},{4,6},{6,4},{5,7},{7,5},{8,10},{10,8},{9,1... | collective-permute-start | bytes 1253384 | tf_op jit(solution)/shard_map/chip_sum_3/ppermute | solution.py:465
  44.0 13.0 %slice-start.2 = ((s8[18874368]{0:T(1024)(128)(4,1)}), s8[4194304]{0:T(1024)(128)(4,1)S(1)}, s32[]{:S(2)}) async-start(s8[18874368]{0:T(1024)(128)(4,1)} %bitcast.6), calls=%async_computation.2 | async-start | bytes 8388608
  45.4 4.3 %collective-permute-start.21 = (bf16[128,1536]{1,0:T(8,128)(2,1)S(1)}, bf16[128,1536]{1,0:T(8,128)(2,1)S(1)}, u32[]{:S(2)}, u32[]{:S(2)}) collective-permute-start(bf16[128,1536]{1,0:T(8,128)(2,1)S(1)} %get-tuple-element.106), channel_id=1, source_target_pairs={{0,1},{1,0},{2,3},{3,2},{4,5},{5,4},{6,7},{7,6},{8,9},{9,8},{10,11... | collective-permute-start | bytes 1179656 | tf_op jit(solution)/shard_map/core_sum_2b/ppermute | solution.py:460
  45.5 2.1 %copy-start.2 = (f32[6144]{0:T(1024)S(1)}, f32[6144]{0:T(1024)}, u32[]{:S(2)}) copy-start(f32[6144]{0:T(1024)} %param.11) | copy-start | bytes 73732
  45.5 11.6 %slice-start.3 = ((s8[18874368]{0:T(1024)(128)(4,1)}), s8[4194304]{0:T(1024)(128)(4,1)S(1)}, s32[]{:S(2)}) async-start(s8[18874368]{0:T(1024)(128)(4,1)} %bitcast.6), calls=%async_computation.3 | async-start | bytes 8388608
  46.9 3.8 %collective-permute-start.16 = (bf16[128,768]{1,0:T(8,128)(2,1)S(1)}, bf16[128,768]{1,0:T(8,128)(2,1)S(1)}, u32[]{:S(2)}, u32[]{:S(2)}) collective-permute-start(bf16[128,768]{1,0:T(8,128)(2,1)S(1)} %get-tuple-element.109), channel_id=1, source_target_pairs={{0,1},{1,0},{2,3},{3,2},{4,5},{5,4},{6,7},{7,6},{8,9},{9,8},{10,11... | collective-permute-start | bytes 589832 | tf_op jit(solution)/shard_map/core_sum_3b/ppermute | solution.py:460
  47.5 3.3 %collective-permute-start.17 = (bf16[128,768]{1,0:T(8,128)(2,1)S(1)}, bf16[128,768]{1,0:T(8,128)(2,1)S(1)}, u32[]{:S(2)}, u32[]{:S(2)}) collective-permute-start(bf16[128,768]{1,0:T(8,128)(2,1)S(1)} %get-tuple-element.110), channel_id=1, source_target_pairs={{0,1},{1,0},{2,3},{3,2},{4,5},{5,4},{6,7},{7,6},{8,9},{9,8},{10,11... | collective-permute-start | bytes 589832 | tf_op jit(solution)/shard_map/core_sum_3b/ppermute | solution.py:460
  47.6 9.5 %slice-start.4 = ((s8[18874368]{0:T(1024)(128)(4,1)}), s8[4194304]{0:T(1024)(128)(4,1)S(1)}, s32[]{:S(2)}) async-start(s8[18874368]{0:T(1024)(128)(4,1)} %bitcast.6), calls=%async_computation.4 | async-start | bytes 8388608
  55.1 1.9 %collective-permute-start.24 = (f32[2,1536]{1,0:T(2,128)S(1)}, f32[2,1536]{1,0:T(2,128)S(1)}, u32[]{:S(2)}, u32[]{:S(2)}) collective-permute-start(f32[2,1536]{1,0:T(2,128)S(1)} %pool_all.1.refs_0_), channel_id=1, source_target_pairs={{0,1},{1,0},{2,3},{3,2},{4,5},{5,4},{6,7},{7,6},{8,9},{9,8},{10,11... | collective-permute-start | bytes 36872 | tf_op jit(solution)/shard_map/core_pool/ppermute | solution.py:460
  55.2 3.8 %collective-permute-start.22 = (f32[2,1536]{1,0:T(2,128)S(1)}, f32[2,1536]{1,0:T(2,128)S(1)}, u32[]{:S(2)}, u32[]{:S(2)}) collective-permute-start(f32[2,1536]{1,0:T(2,128)S(1)} %pool_all.1.refs_0_), channel_id=1, source_target_pairs={{0,2},{2,0},{1,3},{3,1},{4,6},{6,4},{5,7},{7,5},{8,10},{10,8},{9,1... | collective-permute-start | bytes 36872 | tf_op jit(solution)/shard_map/chip_pool/ppermute | solution.py:465
  55.8 3.3 %collective-permute-start.23 = (f32[2,1536]{1,0:T(2,128)S(1)}, f32[2,1536]{1,0:T(2,128)S(1)}, u32[]{:S(2)}, u32[]{:S(2)}) collective-permute-start(f32[2,1536]{1,0:T(2,128)S(1)} %pool_all.1.refs_0_), channel_id=1, source_target_pairs={{0,3},{1,2},{2,1},{3,0},{4,7},{5,6},{6,5},{7,4},{8,11},{9,10},{10,... | collective-permute-start | bytes 36872 | tf_op jit(solution)/shard_map/both_pool/ppermute | solution.py:470
  58.5 6.3 %copy-start.1 = (bf16[64,6144]{1,0:T(8,128)(2,1)S(1)}, bf16[64,6144]{1,0:T(8,128)(2,1)}, u32[]{:S(2)}) copy-start(bf16[64,6144]{1,0:T(8,128)(2,1)} %captions.1) | copy-start | bytes 2359300
  58.5 14.2 %copy-start.3 = (f32[6144]{0:T(1024)S(1)}, f32[6144]{0:T(1024)}, u32[]{:S(2)}) copy-start(f32[6144]{0:T(1024)} %param.13) | copy-start | bytes 73732
  58.5 14.2 %copy-start.4 = (s32[64]{0:T(128)S(1)}, s32[64]{0:T(128)}, u32[]{:S(2)}) copy-start(s32[64]{0:T(128)} %param.15) | copy-start | bytes 772
  60.4 4.7 %collective-permute-start.25 = (f32[2,1536]{1,0:T(2,128)S(1)}, f32[2,1536]{1,0:T(2,128)S(1)}, u32[]{:S(2)}, u32[]{:S(2)}) collective-permute-start(f32[2,1536]{1,0:T(2,128)S(1)} %mix.3), channel_id=1, source_target_pairs={{0,4},{4,0},{8,12},{12,8},{1,5},{5,1},{9,13},{13,9},{2,6},{6,2},{1... | collective-permute-start | bytes 36872 | tf_op jit(solution)/shard_map/swap_mixed/ppermute | solution.py:475
  61.9 4.7 %collective-permute-start.26 = (f32[2,1536]{1,0:T(2,128)S(1)}, f32[2,1536]{1,0:T(2,128)S(1)}, u32[]{:S(2)}, u32[]{:S(2)}) collective-permute-start(f32[2,1536]{1,0:T(2,128)S(1)} %mix.3), channel_id=1, source_target_pairs={{0,8},{8,0},{4,12},{12,4},{1,9},{9,1},{5,13},{13,5},{2,10},{10,2},... | collective-permute-start | bytes 36872 | tf_op jit(solution)/shard_map/skip_mixed/ppermute | solution.py:475
  63.2 5.5 %collective-permute-start.27 = (f32[2,1536]{1,0:T(2,128)S(1)}, f32[2,1536]{1,0:T(2,128)S(1)}, u32[]{:S(2)}, u32[]{:S(2)}) collective-permute-start(f32[2,1536]{1,0:T(2,128)S(1)} %mix.3), channel_id=1, source_target_pairs={{0,12},{12,0},{4,8},{8,4},{1,13},{13,1},{5,9},{9,5},{2,14},{14,2},... | collective-permute-start | bytes 36872 | tf_op jit(solution)/shard_map/ends_mixed/ppermute | solution.py:475
  68.7 1.9 %collective-permute-start.28 = (f32[2,1536]{1,0:T(2,128)S(1)}, f32[2,1536]{1,0:T(2,128)S(1)}, u32[]{:S(2)}, u32[]{:S(2)}) collective-permute-start(f32[2,1536]{1,0:T(2,128)S(1)} %add_add_fusion.own), channel_id=1, source_target_pairs={{0,1},{1,0},{2,3},{3,2},{4,5},{5,4},{6,7},{7,6},{8,9},{9,8},{10,11... | collective-permute-start | bytes 36872 | tf_op jit(solution)/shard_map/core_embed/ppermute | solution.py:460
  68.8 3.8 %collective-permute-start.29 = (f32[2,1536]{1,0:T(2,128)S(1)}, f32[2,1536]{1,0:T(2,128)S(1)}, u32[]{:S(2)}, u32[]{:S(2)}) collective-permute-start(f32[2,1536]{1,0:T(2,128)S(1)} %add_add_fusion.own), channel_id=1, source_target_pairs={{0,2},{2,0},{1,3},{3,1},{4,6},{6,4},{5,7},{7,5},{8,10},{10,8},{9,1... | collective-permute-start | bytes 36872 | tf_op jit(solution)/shard_map/chip_embed/ppermute | solution.py:465
  69.6 3.1 %collective-permute-start.30 = (f32[2,1536]{1,0:T(2,128)S(1)}, f32[2,1536]{1,0:T(2,128)S(1)}, u32[]{:S(2)}, u32[]{:S(2)}) collective-permute-start(f32[2,1536]{1,0:T(2,128)S(1)} %add_add_fusion.own), channel_id=1, source_target_pairs={{0,3},{1,2},{2,1},{3,0},{4,7},{5,6},{6,5},{7,4},{8,11},{9,10},{10,... | collective-permute-start | bytes 36872 | tf_op jit(solution)/shard_map/both_embed/ppermute | solution.py:470

commit v7 on v6

--- a/solution.py
+++ b/solution.py
@@ -430,13 +430,14 @@
         pooled = ref[...] + bias[:, pl.ds(start, depth)]
         total = total + jnp.sum(pooled * pooled, axis=1, keepdims=True)
         pieces.append((start, pooled))
+    terms = jnp.zeros((16, captions.shape[0]), F32)
+    for start, pooled in pieces:
+        left = jnp.concatenate([*thirds(pooled), jnp.zeros((10, depth), BF16)], axis=0)
+        terms = terms + lax.dot_general(
+            left, captions[:, pl.ds(start, depth)], (((1,), (1,)), ((), ())), preferred_element_type=F32
+        )
     scale = lax.rsqrt(total / width + 1e-06)
-    similar = jnp.zeros((IMAGES, captions.shape[0]), F32)
-    for start, pooled in pieces:
-        embedding = (pooled * scale).astype(BF16)
-        similar = similar + lax.dot_general(
-            embedding, captions[:, pl.ds(start, depth)], (((1,), (1,)), ((), ())), preferred_element_type=F32
-        )
+    similar = (terms[0:2] + (terms[2:4] + terms[4:6])) * scale
     chosen = lax.broadcasted_iota(jnp.int32, similar.shape, 0) == pairs[...]
     picked = jnp.sum(jnp.where(chosen, similar, 0.0), axis=0, keepdims=True)
     out[...] = 100.0 * picked * text_scale[...] / width

time: 73.9 us -> 73.8 us (level)
  no operation moved by 1% of the time
where the time goes in v7:
time: 73.8 us; the launch traced here: 73.6 us
  Pallas kernels  28.2 us (38%)
  starting transfers between devices  23.3 us (32%)
  waiting for transfers between devices  21.4 us (29%)
    ppermute x8, starting transfers between devices, along(): return lax.ppermute(value, 'mrow', list(pairs))  11.5 us
    ppermute x8, waiting for transfers between devices, along(): return lax.ppermute(value, 'mrow', list(pairs))  9.74 us
    pallas_call x6, Pallas kernels, later_block(): pl.pallas_call(kernel, name='later_block', out_shape=out, in_specs=[WHOLE...  8.94 us
    ppermute x6, waiting for transfers between devices, other_chip(): return lax.ppermute(value, 'mcol', [(0, 1), (1, 0)])  6.95 us
    pallas_call x2, Pallas kernels, first_part(): pl.pallas_call(kernel, name=name, out_shape=shapes, in_specs=[WHOLE, WHOL...  6.22 us
    ppermute x6, starting transfers between devices, other_chip(): return lax.ppermute(value, 'mcol', [(0, 1), (1, 0)])  5.82 us
    pallas_call x1, Pallas kernels, first_a(): pl.pallas_call(first_a_kernel, name='first_a', out_shape=(struct((rows +...  4.66 us
    ppermute x15, waiting for transfers between devices, other_core(): return lax.ppermute(value, 'sub', [(0, 1), (1, 0)])  4.54 us
  transfers between devices with their start and end apart: 31, of which 16 were waited for; matrix products, arithmetic and copies ran while one was open for 0% of the time, Pallas kernels for 34%

profile of v7, /device:TPU:0, one launch (start us, length us, event | category | flops | bytes accessed | tf_op | source)
XLA Modules:
  0.0 73.6 jit_solution(2122322950521479663)
XLA Ops:
  0.0 3.0 %collective-permute-start = (bf16[128,1536]{1,0:T(8,128)(2,1)}, bf16[128,1536]{1,0:T(8,128)(2,1)S(1)}, u32[]{:S(2)}, u32[]{:S(2)}) collective-permute-start(bf16[128,1536]{1,0:T(8,128)(2,1)} %tokens.3), channel_id=1, source_target_pairs={{0,4},{4,0},{8,12},{12,8},{1,5},{5,1},{9,13},{13,9},{2,6},{6,2},{1... | collective-permute-start | bytes 1179656 | tf_op jit(solution)/shard_map/near_rows/ppermute | solution.py:476
  3.0 0.7 collective-permute-start.8
  3.7 4.7 %first_a.1 = (bf16[144,768]{1,0:T(8,128)(2,1)S(1)}, bf16[144,768]{1,0:T(8,128)(2,1)S(1)}, f32[128,1536]{1,0:T(8,128)S(1)}, f32[1,1536]{1,0:T(1,128)S(1)}, f32[1,...) custom-call(bf16[128,1536]{1,0:T(8,128)(2,1)} %tokens.3, f32[1536]{0:T(1024)} %gain.1, ...), custom_call_target="tpu_custom_call" | custom-call | flops 1024 | bytes 1024 | tf_op jit(solution)/shard_map/first_a/pallas_call | solution.py:173
  8.4 0.1 collective-permute-start.1
  8.5 0.5 collective-permute-start.2
  9.0 1.0 %collective-permute-done.1.refs_1_ = bf16[144,768]{1,0:T(8,128)(2,1)S(1)} collective-permute-done((bf16[144,768]{1,0:T(8,128)(2,1)S(1)}, bf16[144,768]{1,0:T(8,128)(2,1)S(1)}, u32[]{:S(2)}, u32[]{:S(2)}) %collective-permute-start.1) | collective-permute-done | bytes 221216 | tf_op jit(solution)/shard_map/core_sum_0a/ppermute | solution.py:461
  9.9 0.3 collective-permute-done.2.refs_2_
  10.2 0.1 chip_sum.4
  10.4 1.6 %collective-permute-start.10 = (bf16[136,1536]{1,0:T(8,128)(2,1)S(1)}, bf16[136,1536]{1,0:T(8,128)(2,1)S(1)}, u32[]{:S(2)}, u32[]{:S(2)}) collective-permute-start(bf16[136,1536]{1,0:T(8,128)(2,1)S(1)} %get-tuple-element.68), channel_id=1, source_target_pairs={{0,2},{2,0},{1,3},{3,1},{4,6},{6,4},{5,7},{7,5},{8,10},{10,8},{9,1... | collective-permute-start | bytes 1253384 | tf_op jit(solution)/shard_map/chip_sum_0/ppermute | solution.py:466
  11.9 0.4 collective-permute-done.refs_0_
  12.3 0.7 collective-permute-start.3
  13.0 1.3 %collective-permute-start.9 = (bf16[128,1536]{1,0:T(8,128)(2,1)S(1)}, bf16[128,1536]{1,0:T(8,128)(2,1)S(1)}, u32[]{:S(2)}, u32[]{:S(2)}) collective-permute-start(bf16[128,1536]{1,0:T(8,128)(2,1)S(1)} %collective-permute-done.8.refs_0_), channel_id=1, source_target_pairs={{4,0},{8,12},{5,1},{9,13},{6,2},{10,14},{7,3},{11,15},{20,16},{24,... | collective-permute-start | bytes 1179656 | tf_op jit(solution)/shard_map/passed_rows/ppermute | solution.py:476
  14.4 1.6 %later_block.6 = (bf16[144,768]{1,0:T(8,128)(2,1)S(1)}, bf16[128,768]{1,0:T(8,128)(2,1)S(1)}, f32[128,1536]{1,0:T(8,128)S(1)}, bf16[128,1536]{1,0:T(8,128)(2,1)S(1)}, f32[1,256]{1,0:T(1,128)S(1)}) custom-call(bf16[128,1536]{1,0:T(8,128)(2,1)S(1)} %collective-permute-done.refs_0_, f32[1,1536]{1,0:T(1,128)S(1)} %get-tuple-element.96.refs_1_.gain.refs_2_, ...), custom_call_target="tpu_custom_call" | custom-call | flops 1207959552 | bytes 1024 | tf_op jit(solution)/shard_map/later_block/pallas_call | solution.py:265
  15.9 0.1 collective-permute-start.4
  16.0 0.5 collective-permute-start.5
  16.5 1.2 %collective-permute-done.5.refs_2_ = bf16[128,768]{1,0:T(8,128)(2,1)S(1)} collective-permute-done((bf16[128,768]{1,0:T(8,128)(2,1)S(1)}, bf16[128,768]{1,0:T(8,128)(2,1)S(1)}, u32[]{:S(2)}, u32[]{:S(2)}) %collective-permute-start.5) | collective-permute-done | bytes 196640 | tf_op jit(solution)/shard_map/core_sum_1a/ppermute | solution.py:461
  17.8 0.1 chip_sum.5
  17.9 1.7 %collective-permute-start.7 = (bf16[128,1536]{1,0:T(8,128)(2,1)S(1)}, bf16[128,1536]{1,0:T(8,128)(2,1)S(1)}, u32[]{:S(2)}, u32[]{:S(2)}) collective-permute-start(bf16[128,1536]{1,0:T(8,128)(2,1)S(1)} %get-tuple-element.76), channel_id=1, source_target_pairs={{0,2},{2,0},{1,3},{3,1},{4,6},{6,4},{5,7},{7,5},{8,10},{10,8},{9,1... | collective-permute-start | bytes 1179656 | tf_op jit(solution)/shard_map/chip_sum_1/ppermute | solution.py:466
  19.6 3.1 %first_keep.1 = (f32[128,1536]{1,0:T(8,128)S(1)}, f32[1,1536]{1,0:T(1,128)S(1)}, bf16[1536,1536]{1,0:T(8,128)(2,1)S(1)}) custom-call(bf16[128,1536]{1,0:T(8,128)(2,1)S(1)} %copy-done, f32[1,1536]{1,0:T(1,128)S(1)} %get-tuple-element.96.refs_1_.gain.refs_2_, bf16[1536,6144]{1,0:T(8,128)(2,1)} %w.5), custom_call_target="tpu_custom_call" | custom-call | flops 1024 | bytes 1024 | tf_op jit(solution)/shard_map/first_keep/pallas_call | solution.py:219
  22.7 0.3 collective-permute-done.10.refs_2_.refs_3_
  22.9 1.5 %collective-permute-start.6 = (bf16[128,1536]{1,0:T(8,128)(2,1)S(1)}, bf16[128,1536]{1,0:T(8,128)(2,1)S(1)}, u32[]{:S(2)}, u32[]{:S(2)}) collective-permute-start(bf16[128,1536]{1,0:T(8,128)(2,1)S(1)} %collective-permute-done.3.refs_0_), channel_id=1, source_target_pairs={{4,0},{8,12},{5,1},{9,13},{6,2},{10,14},{7,3},{11,15},{20,16},{24,... | collective-permute-start | bytes 1179656 | tf_op jit(solution)/shard_map/last_rows/ppermute | solution.py:476
  24.4 4.3 %collective-permute-done.9.refs_1_ = bf16[128,1536]{1,0:T(8,128)(2,1)S(1)} collective-permute-done((bf16[128,1536]{1,0:T(8,128)(2,1)S(1)}, bf16[128,1536]{1,0:T(8,128)(2,1)S(1)}, u32[]{:S(2)}, u32[]{:S(2)}) %collective-permute-start.9) | collective-permute-done | bytes 393248 | tf_op jit(solution)/shard_map/passed_rows/ppermute | solution.py:476
  28.7 1.6 %later_block.7 = (bf16[144,768]{1,0:T(8,128)(2,1)S(1)}, bf16[128,768]{1,0:T(8,128)(2,1)S(1)}, f32[128,1536]{1,0:T(8,128)S(1)}, bf16[128,1536]{1,0:T(8,128)(2,1)S(1)}, f32[1,256]{1,0:T(1,128)S(1)}) custom-call(bf16[128,1536]{1,0:T(8,128)(2,1)S(1)} %collective-permute-done.8.refs_0_, bf16[128,1536]{1,0:T(8,128)(2,1)S(1)} %collective-permute-done.9.refs_1_, ...), custom_call_target="tpu_custom_call" | custom-call | flops 1207959552 | bytes 1024 | tf_op jit(solution)/shard_map/later_block/pallas_call | solution.py:265
  30.4 0.5 collective-permute-start.12
  30.9 1.2 %collective-permute-done.12.refs_2_ = bf16[128,768]{1,0:T(8,128)(2,1)S(1)} collective-permute-done((bf16[128,768]{1,0:T(8,128)(2,1)S(1)}, bf16[128,768]{1,0:T(8,128)(2,1)S(1)}, u32[]{:S(2)}, u32[]{:S(2)}) %collective-permute-start.12) | collective-permute-done | bytes 196640 | tf_op jit(solution)/shard_map/core_sum_2a/ppermute | solution.py:461
  32.1 0.1 chip_sum.6
  32.2 0.6 collective-permute-start.13
  32.8 3.2 %first_give.1 = (bf16[144,1536]{1,0:T(8,128)(2,1)S(1)}, bf16[1536,1536]{1,0:T(8,128)(2,1)S(1)}, f32[1,1536]{1,0:T(1,128)S(1)}) custom-call(bf16[128,1536]{1,0:T(8,128)(2,1)S(1)} %copy-done, f32[1,1536]{1,0:T(1,128)S(1)} %get-tuple-element.96.refs_1_.gain.refs_2_, bf16[1536,6144]{1,0:T(8,128)(2,1)} %w.5), custom_call_target="tpu_custom_call" | custom-call | flops 1024 | bytes 1024 | tf_op jit(solution)/shard_map/first_give/pallas_call | solution.py:219
  36.0 1.4 %later_block.8 = (bf16[128,1536]{1,0:T(8,128)(2,1)S(1)}, f32[128,1536]{1,0:T(8,128)S(1)}) custom-call(bf16[128,1536]{1,0:T(8,128)(2,1)S(1)} %get-tuple-element.92.left, bf16[1536,1536]{1,0:T(8,128)(2,1)S(1)} %get-tuple-element.93.give_held, bf16[1536,1536]{1,0:T(8,128)(2,1)S(1)} %get-tuple-element.94.keep_held), custom_call_target="tpu_custom_call" | custom-call | flops 1207959552 | bytes 1024 | tf_op jit(solution)/shard_map/later_block/pallas_call | solution.py:265
  37.4 1.3 %collective-permute-done.6.refs_1_ = bf16[128,1536]{1,0:T(8,128)(2,1)S(1)} collective-permute-done((bf16[128,1536]{1,0:T(8,128)(2,1)S(1)}, bf16[128,1536]{1,0:T(8,128)(2,1)S(1)}, u32[]{:S(2)}, u32[]{:S(2)}) %collective-permute-start.6) | collective-permute-done | bytes 393248 | tf_op jit(solution)/shard_map/last_rows/ppermute | solution.py:476
  38.7 1.6 %later_block.9 = (bf16[144,768]{1,0:T(8,128)(2,1)S(1)}, bf16[128,768]{1,0:T(8,128)(2,1)S(1)}, f32[128,1536]{1,0:T(8,128)S(1)}, bf16[128,1536]{1,0:T(8,128)(2,1)S(1)}, f32[1,256]{1,0:T(1,128)S(1)}) custom-call(bf16[128,1536]{1,0:T(8,128)(2,1)S(1)} %collective-permute-done.3.refs_0_, bf16[128,1536]{1,0:T(8,128)(2,1)S(1)} %collective-permute-done.6.refs_1_, ...), custom_call_target="tpu_custom_call" | custom-call | flops 1207959552 | bytes 1024 | tf_op jit(solution)/shard_map/later_block/pallas_call | solution.py:265
  40.3 0.1 collective-permute-start.14
  40.4 0.5 collective-permute-start.15
  40.9 0.1 collective-permute-start.19
  41.0 0.4 collective-permute-start.20
  41.4 0.7 %collective-permute-done.15.refs_2_ = bf16[128,768]{1,0:T(8,128)(2,1)S(1)} collective-permute-done((bf16[128,768]{1,0:T(8,128)(2,1)S(1)}, bf16[128,768]{1,0:T(8,128)(2,1)S(1)}, u32[]{:S(2)}, u32[]{:S(2)}) %collective-permute-start.15) | collective-permute-done | bytes 196640 | tf_op jit(solution)/shard_map/core_sum_3a/ppermute | solution.py:461
  42.2 0.1 chip_sum.7
  42.2 0.6 collective-permute-start.18
  42.8 1.2 %collective-permute-done.13.refs_3_.refs_2_ = bf16[136,1536]{1,0:T(8,128)(2,1)S(1)} collective-permute-done((bf16[136,1536]{1,0:T(8,128)(2,1)S(1)}, bf16[136,1536]{1,0:T(8,128)(2,1)S(1)}, u32[]{:S(2)}, u32[]{:S(2)}) %collective-permute-start.13) | collective-permute-done | bytes 417824 | tf_op jit(solution)/shard_map/chip_sum_2/ppermute | solution.py:466
  44.0 1.4 %later_block.10 = (bf16[128,1536]{1,0:T(8,128)(2,1)S(1)}, f32[128,1536]{1,0:T(8,128)S(1)}) custom-call(bf16[128,1536]{1,0:T(8,128)(2,1)S(1)} %get-tuple-element.105.left, bf16[1536,1536]{1,0:T(8,128)(2,1)S(1)} %get-tuple-element.93.give_held, bf16[1536,1536]{1,0:T(8,128)(2,1)S(1)} %get-tuple-element.94.keep_held), custom_call_target="tpu_custom_call" | custom-call | flops 1207959552 | bytes 1024 | tf_op jit(solution)/shard_map/later_block/pallas_call | solution.py:265
  45.5 1.4 %later_block.11 = (bf16[128,768]{1,0:T(8,128)(2,1)S(1)}, bf16[128,768]{1,0:T(8,128)(2,1)S(1)}, f32[128,1536]{1,0:T(8,128)S(1)}) custom-call(bf16[128,1536]{1,0:T(8,128)(2,1)S(1)} %get-tuple-element.107.left, bf16[1536,1536]{1,0:T(8,128)(2,1)S(1)} %get-tuple-element.93.give_held, bf16[1536,1536]{1,0:T(8,128)(2,1)S(1)} %get-tuple-element.94.keep_held), custom_call_target="tpu_custom_call" | custom-call | flops 1207959552 | bytes 1024 | tf_op jit(solution)/shard_map/later_block/pallas_call | solution.py:265
  46.9 0.5 collective-permute-start.16
  47.5 0.1 collective-permute-start.17
  47.6 1.0 %pool.3.refs_7_ = f32[1,1536]{1,0:T(1,128)S(1)} custom-call(f32[128,1536]{1,0:T(8,128)S(1)} %get-tuple-element.78.refs_0_, bf16[144,1536]{1,0:T(8,128)(2,1)S(1)} %collective-permute-done.19.refs_1_, bf16[136,1536]{1,0:T(8,128)(2,1)S(1)} %collective-permute-done.10.refs_2_.refs_3_, bf16[136,1536]{1,0:T(8,128)(2,1)S(1)} %collective-permute-done.10.refs_2_.refs_3_, ...), custom_call_target="tpu_custom_call" | custom-call | flops 1024 | bytes 1024 | tf_op jit(solution)/shard_map/pool/pallas_call | solution.py:352
  48.7 1.0 %pool.4.refs_8_ = f32[1,1536]{1,0:T(1,128)S(1)} custom-call(f32[128,1536]{1,0:T(8,128)S(1)} %get-tuple-element.115.refs_0_, bf16[128,1536]{1,0:T(8,128)(2,1)S(1)} %collective-permute-done.20.refs_1_, bf16[128,1536]{1,0:T(8,128)(2,1)S(1)} %collective-permute-done.7.refs_2_, bf16[136,1536]{1,0:T(8,128)(2,1)S(1)} %collective-permute-done.13.refs_3_.refs_2_, ...), custom_call_target="tpu_custom_call" | custom-call | flops 1024 | bytes 1024 | tf_op jit(solution)/shard_map/pool/pallas_call | solution.py:352
  49.7 1.0 %pool.5.refs_9_ = f32[1,1536]{1,0:T(1,128)S(1)} custom-call(f32[128,1536]{1,0:T(8,128)S(1)} %get-tuple-element.116.refs_0_, bf16[128,1536]{1,0:T(8,128)(2,1)S(1)} %collective-permute-done.21.refs_1_, bf16[136,1536]{1,0:T(8,128)(2,1)S(1)} %collective-permute-done.13.refs_3_.refs_2_, bf16[136,1536]{1,0:T(8,128)(2,1)S(1)} %collective-permute-done.13.refs_3_.refs_2_, ...), custom_call_target="tpu_custom_call" | custom-call | flops 1024 | bytes 1024 | tf_op jit(solution)/shard_map/pool/pallas_call | solution.py:352
  50.8 3.3 %collective-permute-done.18.refs_3_ = bf16[136,1536]{1,0:T(8,128)(2,1)S(1)} collective-permute-done((bf16[136,1536]{1,0:T(8,128)(2,1)S(1)}, bf16[136,1536]{1,0:T(8,128)(2,1)S(1)}, u32[]{:S(2)}, u32[]{:S(2)}) %collective-permute-start.18) | collective-permute-done | bytes 417824 | tf_op jit(solution)/shard_map/chip_sum_3/ppermute | solution.py:466
  54.1 1.1 %pool_all.1.refs_0_ = f32[2,1536]{1,0:T(2,128)S(1)} custom-call(f32[128,1536]{1,0:T(8,128)S(1)} %get-tuple-element.108.refs_0_, bf16[128,768]{1,0:T(8,128)(2,1)S(1)} %collective-permute-done.16.refs_1_, bf16[128,768]{1,0:T(8,128)(2,1)S(1)} %collective-permute-done.17.refs_2_, bf16[136,1536]{1,0:T(8,128)(2,1)S(1)} %collective-permute-done.18.refs_3_, ...), custom_call_target="tpu_custom_call" | custom-call | flops 1024 | bytes 1024 | tf_op jit(solution)/shard_map/pool_all/pallas_call | solution.py:378
  55.2 0.6 collective-permute-start.22
  55.8 1.3 %collective-permute-start.23 = (f32[2,1536]{1,0:T(2,128)S(1)}, f32[2,1536]{1,0:T(2,128)S(1)}, u32[]{:S(2)}, u32[]{:S(2)}) collective-permute-start(f32[2,1536]{1,0:T(2,128)S(1)} %pool_all.1.refs_0_), channel_id=1, source_target_pairs={{0,3},{1,2},{2,1},{3,0},{4,7},{5,6},{6,5},{7,4},{8,11},{9,10},{10,... | collective-permute-start | bytes 36872 | tf_op jit(solution)/shard_map/both_pool/ppermute | solution.py:471
  57.1 1.6 %mix.2.refs_2_ = f32[2,1536]{1,0:T(2,128)S(1)} custom-call(f32[2,1536]{1,0:T(2,128)S(1)} %pool_all.1.refs_0_, f32[2,1536]{1,0:T(2,128)S(1)} %collective-permute-done.24.refs_1_, f32[1,1536]{1,0:T(1,128)S(1)} %get-tuple-element.118.refs_2_, bf16[6144,1536]{1,0:T(8,128)(2,1)S(1)} %bitcast.7), custom_call_target="tpu_custom_call" | custom-call | flops 1024 | bytes 1024 | tf_op jit(solution)/shard_map/mix/pallas_call | solution.py:410
  58.7 0.3 collective-permute-done.22.refs_0_
  59.1 1.3 %mix.3 = f32[2,1536]{1,0:T(2,128)S(1)} custom-call(f32[2,1536]{1,0:T(2,128)S(1)} %collective-permute-done.22.refs_0_, f32[2,1536]{1,0:T(2,128)S(1)} %collective-permute-done.23.refs_1_, f32[2,1536]{1,0:T(2,128)S(1)} %mix.2.refs_2_, bf16[6144,1536]{1,0:T(8,128)(2,1)S(1)} %bitcast.7), custom_call_target="tpu_custom_call" | custom-call | flops 1024 | bytes 1024 | tf_op jit(solution)/shard_map/mix/pallas_call | solution.py:410
  60.4 1.5 %collective-permute-start.25 = (f32[2,1536]{1,0:T(2,128)S(1)}, f32[2,1536]{1,0:T(2,128)S(1)}, u32[]{:S(2)}, u32[]{:S(2)}) collective-permute-start(f32[2,1536]{1,0:T(2,128)S(1)} %mix.3), channel_id=1, source_target_pairs={{0,4},{4,0},{8,12},{12,8},{1,5},{5,1},{9,13},{13,9},{2,6},{6,2},{1... | collective-permute-start | bytes 36872 | tf_op jit(solution)/shard_map/swap_mixed/ppermute | solution.py:476
  61.9 1.4 %collective-permute-start.26 = (f32[2,1536]{1,0:T(2,128)S(1)}, f32[2,1536]{1,0:T(2,128)S(1)}, u32[]{:S(2)}, u32[]{:S(2)}) collective-permute-start(f32[2,1536]{1,0:T(2,128)S(1)} %mix.3), channel_id=1, source_target_pairs={{0,8},{8,0},{4,12},{12,4},{1,9},{9,1},{5,13},{13,5},{2,10},{10,2},... | collective-permute-start | bytes 36872 | tf_op jit(solution)/shard_map/skip_mixed/ppermute | solution.py:476
  63.2 1.6 %collective-permute-start.27 = (f32[2,1536]{1,0:T(2,128)S(1)}, f32[2,1536]{1,0:T(2,128)S(1)}, u32[]{:S(2)}, u32[]{:S(2)}) collective-permute-start(f32[2,1536]{1,0:T(2,128)S(1)} %mix.3), channel_id=1, source_target_pairs={{0,12},{12,0},{4,8},{8,4},{1,13},{13,1},{5,9},{9,5},{2,14},{14,2},... | collective-permute-start | bytes 36872 | tf_op jit(solution)/shard_map/ends_mixed/ppermute | solution.py:476
  64.8 0.3 multiply_reduce_fusion
  65.1 1.5 %collective-permute-done.26 = f32[2,1536]{1,0:T(2,128)S(1)} collective-permute-done((f32[2,1536]{1,0:T(2,128)S(1)}, f32[2,1536]{1,0:T(2,128)S(1)}, u32[]{:S(2)}, u32[]{:S(2)}) %collective-permute-start.26) | collective-permute-done | bytes 12320 | tf_op jit(solution)/shard_map/skip_mixed/ppermute | solution.py:476
  66.6 2.1 %collective-permute-done.27 = f32[2,1536]{1,0:T(2,128)S(1)} collective-permute-done((f32[2,1536]{1,0:T(2,128)S(1)}, f32[2,1536]{1,0:T(2,128)S(1)}, u32[]{:S(2)}, u32[]{:S(2)}) %collective-permute-start.27) | collective-permute-done | bytes 12320 | tf_op jit(solution)/shard_map/ends_mixed/ppermute | solution.py:476
  68.8 0.8 %collective-permute-start.29 = (f32[2,1536]{1,0:T(2,128)S(1)}, f32[2,1536]{1,0:T(2,128)S(1)}, u32[]{:S(2)}, u32[]{:S(2)}) collective-permute-start(f32[2,1536]{1,0:T(2,128)S(1)} %add_add_fusion.own), channel_id=1, source_target_pairs={{0,2},{2,0},{1,3},{3,1},{4,6},{6,4},{5,7},{7,5},{8,10},{10,8},{9,1... | collective-permute-start | bytes 36872 | tf_op jit(solution)/shard_map/chip_embed/ppermute | solution.py:466
  69.6 1.1 %collective-permute-start.30 = (f32[2,1536]{1,0:T(2,128)S(1)}, f32[2,1536]{1,0:T(2,128)S(1)}, u32[]{:S(2)}, u32[]{:S(2)}) collective-permute-start(f32[2,1536]{1,0:T(2,128)S(1)} %add_add_fusion.own), channel_id=1, source_target_pairs={{0,3},{1,2},{2,1},{3,0},{4,7},{5,6},{6,5},{7,4},{8,11},{9,10},{10,... | collective-permute-start | bytes 36872 | tf_op jit(solution)/shard_map/both_embed/ppermute | solution.py:471
  70.7 1.9 %collective-permute-done.29.across = f32[2,1536]{1,0:T(2,128)S(1)} collective-permute-done((f32[2,1536]{1,0:T(2,128)S(1)}, f32[2,1536]{1,0:T(2,128)S(1)}, u32[]{:S(2)}, u32[]{:S(2)}) %collective-permute-start.29) | collective-permute-done | bytes 12320 | tf_op jit(solution)/shard_map/chip_embed/ppermute | solution.py:466
  72.6 0.1 collective-permute-done.30.both
  72.7 0.9 %score.1 = f32[1,64]{1,0:T(1,128)} custom-call(f32[2,1536]{1,0:T(2,128)S(1)} %add_add_fusion.own, f32[2,1536]{1,0:T(2,128)S(1)} %collective-permute-done.28.core, f32[2,1536]{1,0:T(2,128)S(1)} %collective-permute-done.29.across, f32[2,1536]{1,0:T(2,128)S(1)} %collective-permute-done.30.both, f32[1,6144]{1,0:T(1,128)S(1)} %bitcast.12, ...), custom_call_target="tpu_custom_call" | custom-call | flops 1024 | bytes 1024 | tf_op jit(solution)/shard_map/score/pallas_call | solution.py:448
  (43 shorter events, 0.4 us)
Async XLA Ops:
  0.0 12.3 %collective-permute-start = (bf16[128,1536]{1,0:T(8,128)(2,1)}, bf16[128,1536]{1,0:T(8,128)(2,1)S(1)}, u32[]{:S(2)}, u32[]{:S(2)}) collective-permute-start(bf16[128,1536]{1,0:T(8,128)(2,1)} %tokens.3), channel_id=1, source_target_pairs={{0,4},{4,0},{8,12},{12,8},{1,5},{5,1},{9,13},{13,9},{2,6},{6,2},{1... | collective-permute-start | bytes 1179656 | tf_op jit(solution)/shard_map/near_rows/ppermute | solution.py:476
  3.0 10.0 %collective-permute-start.8 = (bf16[128,1536]{1,0:T(8,128)(2,1)}, bf16[128,1536]{1,0:T(8,128)(2,1)S(1)}, u32[]{:S(2)}, u32[]{:S(2)}) collective-permute-start(bf16[128,1536]{1,0:T(8,128)(2,1)} %tokens.3), channel_id=1, source_target_pairs={{4,8},{8,4},{5,9},{9,5},{6,10},{10,6},{7,11},{11,7},{20,24},{24,20... | collective-permute-start | bytes 1179656 | tf_op jit(solution)/shard_map/middle_rows/ppermute | solution.py:476
  8.4 1.5 %collective-permute-start.1 = (bf16[144,768]{1,0:T(8,128)(2,1)S(1)}, bf16[144,768]{1,0:T(8,128)(2,1)S(1)}, u32[]{:S(2)}, u32[]{:S(2)}) collective-permute-start(bf16[144,768]{1,0:T(8,128)(2,1)S(1)} %get-tuple-element.64), channel_id=1, source_target_pairs={{0,1},{1,0},{2,3},{3,2},{4,5},{5,4},{6,7},{7,6},{8,9},{9,8},{10,11... | collective-permute-start | bytes 663560 | tf_op jit(solution)/shard_map/core_sum_0a/ppermute | solution.py:461
  8.5 1.8 %collective-permute-start.2 = (bf16[144,768]{1,0:T(8,128)(2,1)S(1)}, bf16[144,768]{1,0:T(8,128)(2,1)S(1)}, u32[]{:S(2)}, u32[]{:S(2)}) collective-permute-start(bf16[144,768]{1,0:T(8,128)(2,1)S(1)} %get-tuple-element.65), channel_id=1, source_target_pairs={{0,1},{1,0},{2,3},{3,2},{4,5},{5,4},{6,7},{7,6},{8,9},{9,8},{10,11... | collective-permute-start | bytes 663560 | tf_op jit(solution)/shard_map/core_sum_0a/ppermute | solution.py:461
  10.4 12.5 %collective-permute-start.10 = (bf16[136,1536]{1,0:T(8,128)(2,1)S(1)}, bf16[136,1536]{1,0:T(8,128)(2,1)S(1)}, u32[]{:S(2)}, u32[]{:S(2)}) collective-permute-start(bf16[136,1536]{1,0:T(8,128)(2,1)S(1)} %get-tuple-element.68), channel_id=1, source_target_pairs={{0,2},{2,0},{1,3},{3,1},{4,6},{6,4},{5,7},{7,5},{8,10},{10,8},{9,1... | collective-permute-start | bytes 1253384 | tf_op jit(solution)/shard_map/chip_sum_0/ppermute | solution.py:466
  12.3 10.6 %collective-permute-start.3 = (bf16[128,1536]{1,0:T(8,128)(2,1)S(1)}, bf16[128,1536]{1,0:T(8,128)(2,1)S(1)}, u32[]{:S(2)}, u32[]{:S(2)}) collective-permute-start(bf16[128,1536]{1,0:T(8,128)(2,1)S(1)} %collective-permute-done.refs_0_), channel_id=1, source_target_pairs={{4,8},{8,4},{5,9},{9,5},{6,10},{10,6},{7,11},{11,7},{20,24},{24,20... | collective-permute-start | bytes 1179656 | tf_op jit(solution)/shard_map/crossed_rows/ppermute | solution.py:476
  13.0 15.7 %collective-permute-start.9 = (bf16[128,1536]{1,0:T(8,128)(2,1)S(1)}, bf16[128,1536]{1,0:T(8,128)(2,1)S(1)}, u32[]{:S(2)}, u32[]{:S(2)}) collective-permute-start(bf16[128,1536]{1,0:T(8,128)(2,1)S(1)} %collective-permute-done.8.refs_0_), channel_id=1, source_target_pairs={{4,0},{8,12},{5,1},{9,13},{6,2},{10,14},{7,3},{11,15},{20,16},{24,... | collective-permute-start | bytes 1179656 | tf_op jit(solution)/shard_map/passed_rows/ppermute | solution.py:476
  14.3 5.2 %copy-start = (bf16[128,1536]{1,0:T(8,128)(2,1)S(1)}, bf16[128,1536]{1,0:T(8,128)(2,1)}, u32[]{:S(2)}) copy-start(bf16[128,1536]{1,0:T(8,128)(2,1)} %tokens.3) | copy-start | bytes 1179652
  15.9 1.8 %collective-permute-start.4 = (bf16[144,768]{1,0:T(8,128)(2,1)S(1)}, bf16[144,768]{1,0:T(8,128)(2,1)S(1)}, u32[]{:S(2)}, u32[]{:S(2)}) collective-permute-start(bf16[144,768]{1,0:T(8,128)(2,1)S(1)} %get-tuple-element.73), channel_id=1, source_target_pairs={{0,1},{1,0},{2,3},{3,2},{4,5},{5,4},{6,7},{7,6},{8,9},{9,8},{10,11... | collective-permute-start | bytes 663560 | tf_op jit(solution)/shard_map/core_sum_1a/ppermute | solution.py:461
  16.0 1.7 %collective-permute-start.5 = (bf16[128,768]{1,0:T(8,128)(2,1)S(1)}, bf16[128,768]{1,0:T(8,128)(2,1)S(1)}, u32[]{:S(2)}, u32[]{:S(2)}) collective-permute-start(bf16[128,768]{1,0:T(8,128)(2,1)S(1)} %get-tuple-element.74), channel_id=1, source_target_pairs={{0,1},{1,0},{2,3},{3,2},{4,5},{5,4},{6,7},{7,6},{8,9},{9,8},{10,11... | collective-permute-start | bytes 589832 | tf_op jit(solution)/shard_map/core_sum_1a/ppermute | solution.py:461
  17.9 18.1 %collective-permute-start.7 = (bf16[128,1536]{1,0:T(8,128)(2,1)S(1)}, bf16[128,1536]{1,0:T(8,128)(2,1)S(1)}, u32[]{:S(2)}, u32[]{:S(2)}) collective-permute-start(bf16[128,1536]{1,0:T(8,128)(2,1)S(1)} %get-tuple-element.76), channel_id=1, source_target_pairs={{0,2},{2,0},{1,3},{3,1},{4,6},{6,4},{5,7},{7,5},{8,10},{10,8},{9,1... | collective-permute-start | bytes 1179656 | tf_op jit(solution)/shard_map/chip_sum_1/ppermute | solution.py:466
  22.9 15.8 %collective-permute-start.6 = (bf16[128,1536]{1,0:T(8,128)(2,1)S(1)}, bf16[128,1536]{1,0:T(8,128)(2,1)S(1)}, u32[]{:S(2)}, u32[]{:S(2)}) collective-permute-start(bf16[128,1536]{1,0:T(8,128)(2,1)S(1)} %collective-permute-done.3.refs_0_), channel_id=1, source_target_pairs={{4,0},{8,12},{5,1},{9,13},{6,2},{10,14},{7,3},{11,15},{20,16},{24,... | collective-permute-start | bytes 1179656 | tf_op jit(solution)/shard_map/last_rows/ppermute | solution.py:476
  30.3 1.8 %collective-permute-start.11 = (bf16[144,768]{1,0:T(8,128)(2,1)S(1)}, bf16[144,768]{1,0:T(8,128)(2,1)S(1)}, u32[]{:S(2)}, u32[]{:S(2)}) collective-permute-start(bf16[144,768]{1,0:T(8,128)(2,1)S(1)} %get-tuple-element.84), channel_id=1, source_target_pairs={{0,1},{1,0},{2,3},{3,2},{4,5},{5,4},{6,7},{7,6},{8,9},{9,8},{10,11... | collective-permute-start | bytes 663560 | tf_op jit(solution)/shard_map/core_sum_2a/ppermute | solution.py:461
  30.4 1.7 %collective-permute-start.12 = (bf16[128,768]{1,0:T(8,128)(2,1)S(1)}, bf16[128,768]{1,0:T(8,128)(2,1)S(1)}, u32[]{:S(2)}, u32[]{:S(2)}) collective-permute-start(bf16[128,768]{1,0:T(8,128)(2,1)S(1)} %get-tuple-element.85), channel_id=1, source_target_pairs={{0,1},{1,0},{2,3},{3,2},{4,5},{5,4},{6,7},{7,6},{8,9},{9,8},{10,11... | collective-permute-start | bytes 589832 | tf_op jit(solution)/shard_map/core_sum_2a/ppermute | solution.py:461
  32.2 11.8 %collective-permute-start.13 = (bf16[136,1536]{1,0:T(8,128)(2,1)S(1)}, bf16[136,1536]{1,0:T(8,128)(2,1)S(1)}, u32[]{:S(2)}, u32[]{:S(2)}) collective-permute-start(bf16[136,1536]{1,0:T(8,128)(2,1)S(1)} %get-tuple-element.88), channel_id=1, source_target_pairs={{0,2},{2,0},{1,3},{3,1},{4,6},{6,4},{5,7},{7,5},{8,10},{10,8},{9,1... | collective-permute-start | bytes 1253384 | tf_op jit(solution)/shard_map/chip_sum_2/ppermute | solution.py:466
  38.7 18.4 %slice-start = ((s8[18874368]{0:T(1024)(128)(4,1)}), s8[2097152]{0:T(1024)(128)(4,1)S(1)}, s32[]{:S(2)}) async-start(s8[18874368]{0:T(1024)(128)(4,1)} %bitcast.6), calls=%async_computation | async-start | bytes 4194304
  38.7 18.4 %slice-start.1 = ((s8[18874368]{0:T(1024)(128)(4,1)}), s8[4194304]{0:T(1024)(128)(4,1)S(1)}, s32[]{:S(2)}) async-start(s8[18874368]{0:T(1024)(128)(4,1)} %bitcast.6), calls=%async_computation.1 | async-start | bytes 8388608
  40.3 1.8 %collective-permute-start.14 = (bf16[144,768]{1,0:T(8,128)(2,1)S(1)}, bf16[144,768]{1,0:T(8,128)(2,1)S(1)}, u32[]{:S(2)}, u32[]{:S(2)}) collective-permute-start(bf16[144,768]{1,0:T(8,128)(2,1)S(1)} %get-tuple-element.100), channel_id=1, source_target_pairs={{0,1},{1,0},{2,3},{3,2},{4,5},{5,4},{6,7},{7,6},{8,9},{9,8},{10,11... | collective-permute-start | bytes 663560 | tf_op jit(solution)/shard_map/core_sum_3a/ppermute | solution.py:461
  40.4 1.7 %collective-permute-start.15 = (bf16[128,768]{1,0:T(8,128)(2,1)S(1)}, bf16[128,768]{1,0:T(8,128)(2,1)S(1)}, u32[]{:S(2)}, u32[]{:S(2)}) collective-permute-start(bf16[128,768]{1,0:T(8,128)(2,1)S(1)} %get-tuple-element.101), channel_id=1, source_target_pairs={{0,1},{1,0},{2,3},{3,2},{4,5},{5,4},{6,7},{7,6},{8,9},{9,8},{10,11... | collective-permute-start | bytes 589832 | tf_op jit(solution)/shard_map/core_sum_3a/ppermute | solution.py:461
  40.9 6.6 %collective-permute-start.19 = (bf16[144,1536]{1,0:T(8,128)(2,1)S(1)}, bf16[144,1536]{1,0:T(8,128)(2,1)S(1)}, u32[]{:S(2)}, u32[]{:S(2)}) collective-permute-start(bf16[144,1536]{1,0:T(8,128)(2,1)S(1)} %get-tuple-element.90), channel_id=1, source_target_pairs={{0,1},{1,0},{2,3},{3,2},{4,5},{5,4},{6,7},{7,6},{8,9},{9,8},{10,11... | collective-permute-start | bytes 1327112 | tf_op jit(solution)/shard_map/core_sum_0b/ppermute | solution.py:461
  41.0 7.7 %collective-permute-start.20 = (bf16[128,1536]{1,0:T(8,128)(2,1)S(1)}, bf16[128,1536]{1,0:T(8,128)(2,1)S(1)}, u32[]{:S(2)}, u32[]{:S(2)}) collective-permute-start(bf16[128,1536]{1,0:T(8,128)(2,1)S(1)} %get-tuple-element.95), channel_id=1, source_target_pairs={{0,1},{1,0},{2,3},{3,2},{4,5},{5,4},{6,7},{7,6},{8,9},{9,8},{10,11... | collective-permute-start | bytes 1179656 | tf_op jit(solution)/shard_map/core_sum_1b/ppermute | solution.py:461
  42.2 11.8 %collective-permute-start.18 = (bf16[136,1536]{1,0:T(8,128)(2,1)S(1)}, bf16[136,1536]{1,0:T(8,128)(2,1)S(1)}, u32[]{:S(2)}, u32[]{:S(2)}) collective-permute-start(bf16[136,1536]{1,0:T(8,128)(2,1)S(1)} %get-tuple-element.103), channel_id=1, source_target_pairs={{0,2},{2,0},{1,3},{3,1},{4,6},{6,4},{5,7},{7,5},{8,10},{10,8},{9,1... | collective-permute-start | bytes 1253384 | tf_op jit(solution)/shard_map/chip_sum_3/ppermute | solution.py:466
  44.0 13.0 %slice-start.2 = ((s8[18874368]{0:T(1024)(128)(4,1)}), s8[4194304]{0:T(1024)(128)(4,1)S(1)}, s32[]{:S(2)}) async-start(s8[18874368]{0:T(1024)(128)(4,1)} %bitcast.6), calls=%async_computation.2 | async-start | bytes 8388608
  45.4 4.3 %collective-permute-start.21 = (bf16[128,1536]{1,0:T(8,128)(2,1)S(1)}, bf16[128,1536]{1,0:T(8,128)(2,1)S(1)}, u32[]{:S(2)}, u32[]{:S(2)}) collective-permute-start(bf16[128,1536]{1,0:T(8,128)(2,1)S(1)} %get-tuple-element.106), channel_id=1, source_target_pairs={{0,1},{1,0},{2,3},{3,2},{4,5},{5,4},{6,7},{7,6},{8,9},{9,8},{10,11... | collective-permute-start | bytes 1179656 | tf_op jit(solution)/shard_map/core_sum_2b/ppermute | solution.py:461
  45.5 2.1 %copy-start.2 = (f32[6144]{0:T(1024)S(1)}, f32[6144]{0:T(1024)}, u32[]{:S(2)}) copy-start(f32[6144]{0:T(1024)} %param.11) | copy-start | bytes 73732
  45.5 11.6 %slice-start.3 = ((s8[18874368]{0:T(1024)(128)(4,1)}), s8[4194304]{0:T(1024)(128)(4,1)S(1)}, s32[]{:S(2)}) async-start(s8[18874368]{0:T(1024)(128)(4,1)} %bitcast.6), calls=%async_computation.3 | async-start | bytes 8388608
  46.9 3.8 %collective-permute-start.16 = (bf16[128,768]{1,0:T(8,128)(2,1)S(1)}, bf16[128,768]{1,0:T(8,128)(2,1)S(1)}, u32[]{:S(2)}, u32[]{:S(2)}) collective-permute-start(bf16[128,768]{1,0:T(8,128)(2,1)S(1)} %get-tuple-element.109), channel_id=1, source_target_pairs={{0,1},{1,0},{2,3},{3,2},{4,5},{5,4},{6,7},{7,6},{8,9},{9,8},{10,11... | collective-permute-start | bytes 589832 | tf_op jit(solution)/shard_map/core_sum_3b/ppermute | solution.py:461
  47.5 3.3 %collective-permute-start.17 = (bf16[128,768]{1,0:T(8,128)(2,1)S(1)}, bf16[128,768]{1,0:T(8,128)(2,1)S(1)}, u32[]{:S(2)}, u32[]{:S(2)}) collective-permute-start(bf16[128,768]{1,0:T(8,128)(2,1)S(1)} %get-tuple-element.110), channel_id=1, source_target_pairs={{0,1},{1,0},{2,3},{3,2},{4,5},{5,4},{6,7},{7,6},{8,9},{9,8},{10,11... | collective-permute-start | bytes 589832 | tf_op jit(solution)/shard_map/core_sum_3b/ppermute | solution.py:461
  47.6 9.5 %slice-start.4 = ((s8[18874368]{0:T(1024)(128)(4,1)}), s8[4194304]{0:T(1024)(128)(4,1)S(1)}, s32[]{:S(2)}) async-start(s8[18874368]{0:T(1024)(128)(4,1)} %bitcast.6), calls=%async_computation.4 | async-start | bytes 8388608
  55.1 1.9 %collective-permute-start.24 = (f32[2,1536]{1,0:T(2,128)S(1)}, f32[2,1536]{1,0:T(2,128)S(1)}, u32[]{:S(2)}, u32[]{:S(2)}) collective-permute-start(f32[2,1536]{1,0:T(2,128)S(1)} %pool_all.1.refs_0_), channel_id=1, source_target_pairs={{0,1},{1,0},{2,3},{3,2},{4,5},{5,4},{6,7},{7,6},{8,9},{9,8},{10,11... | collective-permute-start | bytes 36872 | tf_op jit(solution)/shard_map/core_pool/ppermute | solution.py:461
  55.2 3.8 %collective-permute-start.22 = (f32[2,1536]{1,0:T(2,128)S(1)}, f32[2,1536]{1,0:T(2,128)S(1)}, u32[]{:S(2)}, u32[]{:S(2)}) collective-permute-start(f32[2,1536]{1,0:T(2,128)S(1)} %pool_all.1.refs_0_), channel_id=1, source_target_pairs={{0,2},{2,0},{1,3},{3,1},{4,6},{6,4},{5,7},{7,5},{8,10},{10,8},{9,1... | collective-permute-start | bytes 36872 | tf_op jit(solution)/shard_map/chip_pool/ppermute | solution.py:466
  55.8 3.3 %collective-permute-start.23 = (f32[2,1536]{1,0:T(2,128)S(1)}, f32[2,1536]{1,0:T(2,128)S(1)}, u32[]{:S(2)}, u32[]{:S(2)}) collective-permute-start(f32[2,1536]{1,0:T(2,128)S(1)} %pool_all.1.refs_0_), channel_id=1, source_target_pairs={{0,3},{1,2},{2,1},{3,0},{4,7},{5,6},{6,5},{7,4},{8,11},{9,10},{10,... | collective-permute-start | bytes 36872 | tf_op jit(solution)/shard_map/both_pool/ppermute | solution.py:471
  58.7 6.1 %copy-start.1 = (bf16[64,6144]{1,0:T(8,128)(2,1)S(1)}, bf16[64,6144]{1,0:T(8,128)(2,1)}, u32[]{:S(2)}) copy-start(bf16[64,6144]{1,0:T(8,128)(2,1)} %captions.1) | copy-start | bytes 2359300
  58.7 14.0 %copy-start.3 = (f32[6144]{0:T(1024)S(1)}, f32[6144]{0:T(1024)}, u32[]{:S(2)}) copy-start(f32[6144]{0:T(1024)} %param.13) | copy-start | bytes 73732
  58.7 14.0 %copy-start.4 = (s32[64]{0:T(128)S(1)}, s32[64]{0:T(128)}, u32[]{:S(2)}) copy-start(s32[64]{0:T(128)} %param.15) | copy-start | bytes 772
  60.4 4.7 %collective-permute-start.25 = (f32[2,1536]{1,0:T(2,128)S(1)}, f32[2,1536]{1,0:T(2,128)S(1)}, u32[]{:S(2)}, u32[]{:S(2)}) collective-permute-start(f32[2,1536]{1,0:T(2,128)S(1)} %mix.3), channel_id=1, source_target_pairs={{0,4},{4,0},{8,12},{12,8},{1,5},{5,1},{9,13},{13,9},{2,6},{6,2},{1... | collective-permute-start | bytes 36872 | tf_op jit(solution)/shard_map/swap_mixed/ppermute | solution.py:476
  61.9 4.7 %collective-permute-start.26 = (f32[2,1536]{1,0:T(2,128)S(1)}, f32[2,1536]{1,0:T(2,128)S(1)}, u32[]{:S(2)}, u32[]{:S(2)}) collective-permute-start(f32[2,1536]{1,0:T(2,128)S(1)} %mix.3), channel_id=1, source_target_pairs={{0,8},{8,0},{4,12},{12,4},{1,9},{9,1},{5,13},{13,5},{2,10},{10,2},... | collective-permute-start | bytes 36872 | tf_op jit(solution)/shard_map/skip_mixed/ppermute | solution.py:476
  63.2 5.5 %collective-permute-start.27 = (f32[2,1536]{1,0:T(2,128)S(1)}, f32[2,1536]{1,0:T(2,128)S(1)}, u32[]{:S(2)}, u32[]{:S(2)}) collective-permute-start(f32[2,1536]{1,0:T(2,128)S(1)} %mix.3), channel_id=1, source_target_pairs={{0,12},{12,0},{4,8},{8,4},{1,13},{13,1},{5,9},{9,5},{2,14},{14,2},... | collective-permute-start | bytes 36872 | tf_op jit(solution)/shard_map/ends_mixed/ppermute | solution.py:476
  68.7 1.9 %collective-permute-start.28 = (f32[2,1536]{1,0:T(2,128)S(1)}, f32[2,1536]{1,0:T(2,128)S(1)}, u32[]{:S(2)}, u32[]{:S(2)}) collective-permute-start(f32[2,1536]{1,0:T(2,128)S(1)} %add_add_fusion.own), channel_id=1, source_target_pairs={{0,1},{1,0},{2,3},{3,2},{4,5},{5,4},{6,7},{7,6},{8,9},{9,8},{10,11... | collective-permute-start | bytes 36872 | tf_op jit(solution)/shard_map/core_embed/ppermute | solution.py:461
  68.8 3.8 %collective-permute-start.29 = (f32[2,1536]{1,0:T(2,128)S(1)}, f32[2,1536]{1,0:T(2,128)S(1)}, u32[]{:S(2)}, u32[]{:S(2)}) collective-permute-start(f32[2,1536]{1,0:T(2,128)S(1)} %add_add_fusion.own), channel_id=1, source_target_pairs={{0,2},{2,0},{1,3},{3,1},{4,6},{6,4},{5,7},{7,5},{8,10},{10,8},{9,1... | collective-permute-start | bytes 36872 | tf_op jit(solution)/shard_map/chip_embed/ppermute | solution.py:466
  69.6 3.1 %collective-permute-start.30 = (f32[2,1536]{1,0:T(2,128)S(1)}, f32[2,1536]{1,0:T(2,128)S(1)}, u32[]{:S(2)}, u32[]{:S(2)}) collective-permute-start(f32[2,1536]{1,0:T(2,128)S(1)} %add_add_fusion.own), channel_id=1, source_target_pairs={{0,3},{1,2},{2,1},{3,0},{4,7},{5,6},{6,5},{7,4},{8,11},{9,10},{10,... | collective-permute-start | bytes 36872 | tf_op jit(solution)/shard_map/both_embed/ppermute | solution.py:471

commit v8 on v6

--- a/solution.py
+++ b/solution.py
@@ -387,35 +387,35 @@
     )(*args)
 
 
-def mix_kernel(rows, distant, *refs):
+def mix_kernel(rows, places, *refs):
     *shares, other, w, out = refs
     share = shares[0].shape[1]
     mine_x, mine_c = lax.axis_index("mcol"), lax.axis_index("sub")
-    x = 1 - mine_x if distant else mine_x
     total = jnp.zeros((16, w.shape[1]), F32)
-    for ref, c in zip(shares, (mine_c, 1 - mine_c)):
+    for ref, (dx, dc) in zip(shares, places):
+        x, c = (1 - mine_x if dx else mine_x), (1 - mine_c if dc else mine_c)
         start = pl.multiple_of((c * 2 + x) * share, 128)
         terms = jnp.concatenate([*thirds(ref[...] / PATCHES), jnp.zeros((10, share), BF16)], axis=0)
         total = total + jnp.dot(terms, w[pl.ds(start, share), :], preferred_element_type=F32)
     mixed = total[0:2] + (total[2:4] + total[4:6])
-    if distant:
-        out[...] = mixed + other[...]
-    else:
+    if places[0] == (0, 0):
         image = lax.axis_index("mrow") * rows // PATCHES
         row = lax.broadcasted_iota(jnp.int32, mixed.shape, 0)
         out[...] = mixed + jnp.where(row == image, other[...], 0.0)
-
-
-def mix(rows, distant, first, second, other, w):
-    return pl.pallas_call(
-        lambda *refs: mix_kernel(rows, distant, *refs),
+    else:
+        out[...] = mixed + other[...]
+
+
+def mix(rows, places, shares, other, w):
+    return pl.pallas_call(
+        lambda *refs: mix_kernel(rows, places, *refs),
         name="mix",
         out_shape=struct((IMAGES, w.shape[1])),
-        in_specs=[WHOLE] * 4,
+        in_specs=[WHOLE] * (len(shares) + 2),
         out_specs=WHOLE,
         compiler_params=params(8),
         cost_estimate=cost(),
-    )(first, second, other, w)
+    )(*shares, other, w)
 
 
 def score_kernel(own, core, across, both, bias, captions, text_scale, pairs, out):
@@ -583,9 +583,10 @@
     pooled = pool_all(width, keep_3, nears_3, far_3, bias, gains, note_3, parts)
 
     core, across, both = other_core("core_pool", pooled), other_chip("chip_pool", pooled), other_both("both_pool", pooled)
-    near_mix = mix(rows, False, pooled, core, resid, w_out)
-    across, both = after((across, both), near_mix)
-    mixed = mix(rows, True, across, both, near_mix, w_out)
+    mixed = mix(rows, ((0, 0), (0, 1)), (pooled, core), resid, w_out)
+    across, both = after(across, mixed), after(both, mixed)
+    mixed = mix(rows, ((1, 0),), (across,), mixed, w_out)
+    mixed = mix(rows, ((1, 1),), (after(both, mixed),), mixed, w_out)
     own = mixed + along("swap_mixed", mixed, SWAP) + along("skip_mixed", mixed, SKIP) + along("ends_mixed", mixed, ENDS)
     text_vals = captions.astype(F32)
     text_scale = lax.rsqrt(jnp.mean(text_vals * text_vals, axis=1) + 1e-06)

time: 73.9 us -> 74 us (level)
    ppermute x8, waiting for transfers between devices: 9.74 us -> 8.91 us  [along(): return lax.ppermute(value, 'mrow', list(pairs))]
    pallas_call x2 -> x3, Pallas kernels: 2.68 us -> 3.02 us  [mix(): pl.pallas_call(lambda *refs: mix_kernel(rows, places, *refs), name='mix',...]
  transfers between devices with their start and end apart: 31 -> 31, of which waited for: 16 -> 16; matrix products, arithmetic and copies ran while one was open for 0% -> 0% of each run, Pallas kernels for 34% -> 35%
where the time goes in v8:
time: 74 us; the launch traced here: 73.8 us
  Pallas kernels  28.6 us (39%)
  starting transfers between devices  23.3 us (31%)
  waiting for transfers between devices  21.2 us (29%)
    ppermute x8, starting transfers between devices, along(): return lax.ppermute(value, 'mrow', list(pairs))  11.5 us
    pallas_call x6, Pallas kernels, later_block(): pl.pallas_call(kernel, name='later_block', out_shape=out, in_specs=[WHOLE...  9.04 us
    ppermute x8, waiting for transfers between devices, along(): return lax.ppermute(value, 'mrow', list(pairs))  8.91 us
    ppermute x6, waiting for transfers between devices, other_chip(): return lax.ppermute(value, 'mcol', [(0, 1), (1, 0)])  6.94 us
    ppermute x6, starting transfers between devices, other_chip(): return lax.ppermute(value, 'mcol', [(0, 1), (1, 0)])  6.49 us
    pallas_call x2, Pallas kernels, first_part(): pl.pallas_call(kernel, name=name, out_shape=shapes, in_specs=[WHOLE, WHOL...  6.25 us
    pallas_call x1, Pallas kernels, first_a(): pl.pallas_call(first_a_kernel, name='first_a', out_shape=(struct((rows +...  4.66 us
    ppermute x15, waiting for transfers between devices, other_core(): return lax.ppermute(value, 'sub', [(0, 1), (1, 0)])  4.54 us
  transfers between devices with their start and end apart: 31, of which 16 were waited for; matrix products, arithmetic and copies ran while one was open for 0% of the time, Pallas kernels for 35%

profile of v8, /device:TPU:0, one launch (start us, length us, event | category | flops | bytes accessed | tf_op | source)
XLA Modules:
  0.0 73.8 jit_solution(3490460528148348723)
XLA Ops:
  0.0 3.0 %collective-permute-start = (bf16[128,1536]{1,0:T(8,128)(2,1)}, bf16[128,1536]{1,0:T(8,128)(2,1)S(1)}, u32[]{:S(2)}, u32[]{:S(2)}) collective-permute-start(bf16[128,1536]{1,0:T(8,128)(2,1)} %tokens.3), channel_id=1, source_target_pairs={{0,4},{4,0},{8,12},{12,8},{1,5},{5,1},{9,13},{13,9},{2,6},{6,2},{1... | collective-permute-start | bytes 1179656 | tf_op jit(solution)/shard_map/near_rows/ppermute | solution.py:475
  3.0 0.7 collective-permute-start.8
  3.7 4.7 %first_a.1 = (bf16[144,768]{1,0:T(8,128)(2,1)S(1)}, bf16[144,768]{1,0:T(8,128)(2,1)S(1)}, f32[128,1536]{1,0:T(8,128)S(1)}, f32[1,1536]{1,0:T(1,128)S(1)}, f32[1,...) custom-call(bf16[128,1536]{1,0:T(8,128)(2,1)} %tokens.3, f32[1536]{0:T(1024)} %gain.1, ...), custom_call_target="tpu_custom_call" | custom-call | flops 1024 | bytes 1024 | tf_op jit(solution)/shard_map/first_a/pallas_call | solution.py:173
  8.5 0.5 collective-permute-start.2
  9.0 1.0 %collective-permute-done.1.refs_1_ = bf16[144,768]{1,0:T(8,128)(2,1)S(1)} collective-permute-done((bf16[144,768]{1,0:T(8,128)(2,1)S(1)}, bf16[144,768]{1,0:T(8,128)(2,1)S(1)}, u32[]{:S(2)}, u32[]{:S(2)}) %collective-permute-start.1) | collective-permute-done | bytes 221216 | tf_op jit(solution)/shard_map/core_sum_0a/ppermute | solution.py:460
  9.9 0.3 collective-permute-done.2.refs_2_
  10.2 0.1 chip_sum.4
  10.4 1.6 %collective-permute-start.10 = (bf16[136,1536]{1,0:T(8,128)(2,1)S(1)}, bf16[136,1536]{1,0:T(8,128)(2,1)S(1)}, u32[]{:S(2)}, u32[]{:S(2)}) collective-permute-start(bf16[136,1536]{1,0:T(8,128)(2,1)S(1)} %get-tuple-element.69), channel_id=1, source_target_pairs={{0,2},{2,0},{1,3},{3,1},{4,6},{6,4},{5,7},{7,5},{8,10},{10,8},{9,1... | collective-permute-start | bytes 1253384 | tf_op jit(solution)/shard_map/chip_sum_0/ppermute | solution.py:465
  11.9 0.4 collective-permute-done.refs_0_
  12.3 0.7 collective-permute-start.3
  13.0 1.3 %collective-permute-start.9 = (bf16[128,1536]{1,0:T(8,128)(2,1)S(1)}, bf16[128,1536]{1,0:T(8,128)(2,1)S(1)}, u32[]{:S(2)}, u32[]{:S(2)}) collective-permute-start(bf16[128,1536]{1,0:T(8,128)(2,1)S(1)} %collective-permute-done.8.refs_0_), channel_id=1, source_target_pairs={{4,0},{8,12},{5,1},{9,13},{6,2},{10,14},{7,3},{11,15},{20,16},{24,... | collective-permute-start | bytes 1179656 | tf_op jit(solution)/shard_map/passed_rows/ppermute | solution.py:475
  14.4 1.6 %later_block.6 = (bf16[144,768]{1,0:T(8,128)(2,1)S(1)}, bf16[128,768]{1,0:T(8,128)(2,1)S(1)}, f32[128,1536]{1,0:T(8,128)S(1)}, bf16[128,1536]{1,0:T(8,128)(2,1)S(1)}, f32[1,256]{1,0:T(1,128)S(1)}) custom-call(bf16[128,1536]{1,0:T(8,128)(2,1)S(1)} %collective-permute-done.refs_0_, f32[1,1536]{1,0:T(1,128)S(1)} %get-tuple-element.97.refs_1_.gain.refs_2_, ...), custom_call_target="tpu_custom_call" | custom-call | flops 1207959552 | bytes 1024 | tf_op jit(solution)/shard_map/later_block/pallas_call | solution.py:265
  16.0 0.5 collective-permute-start.5
  16.5 1.2 %collective-permute-done.5.refs_2_ = bf16[128,768]{1,0:T(8,128)(2,1)S(1)} collective-permute-done((bf16[128,768]{1,0:T(8,128)(2,1)S(1)}, bf16[128,768]{1,0:T(8,128)(2,1)S(1)}, u32[]{:S(2)}, u32[]{:S(2)}) %collective-permute-start.5) | collective-permute-done | bytes 196640 | tf_op jit(solution)/shard_map/core_sum_1a/ppermute | solution.py:460
  17.8 0.1 chip_sum.5
  17.9 1.7 %collective-permute-start.7 = (bf16[128,1536]{1,0:T(8,128)(2,1)S(1)}, bf16[128,1536]{1,0:T(8,128)(2,1)S(1)}, u32[]{:S(2)}, u32[]{:S(2)}) collective-permute-start(bf16[128,1536]{1,0:T(8,128)(2,1)S(1)} %get-tuple-element.77), channel_id=1, source_target_pairs={{0,2},{2,0},{1,3},{3,1},{4,6},{6,4},{5,7},{7,5},{8,10},{10,8},{9,1... | collective-permute-start | bytes 1179656 | tf_op jit(solution)/shard_map/chip_sum_1/ppermute | solution.py:465
  19.6 3.1 %first_keep.1 = (f32[128,1536]{1,0:T(8,128)S(1)}, f32[1,1536]{1,0:T(1,128)S(1)}, bf16[1536,1536]{1,0:T(8,128)(2,1)S(1)}) custom-call(bf16[128,1536]{1,0:T(8,128)(2,1)S(1)} %copy-done, f32[1,1536]{1,0:T(1,128)S(1)} %get-tuple-element.97.refs_1_.gain.refs_2_, bf16[1536,6144]{1,0:T(8,128)(2,1)} %w.5), custom_call_target="tpu_custom_call" | custom-call | flops 1024 | bytes 1024 | tf_op jit(solution)/shard_map/first_keep/pallas_call | solution.py:219
  22.7 0.2 collective-permute-done.10.refs_2_.refs_3_
  22.9 1.5 %collective-permute-start.6 = (bf16[128,1536]{1,0:T(8,128)(2,1)S(1)}, bf16[128,1536]{1,0:T(8,128)(2,1)S(1)}, u32[]{:S(2)}, u32[]{:S(2)}) collective-permute-start(bf16[128,1536]{1,0:T(8,128)(2,1)S(1)} %collective-permute-done.3.refs_0_), channel_id=1, source_target_pairs={{4,0},{8,12},{5,1},{9,13},{6,2},{10,14},{7,3},{11,15},{20,16},{24,... | collective-permute-start | bytes 1179656 | tf_op jit(solution)/shard_map/last_rows/ppermute | solution.py:475
  24.4 4.3 %collective-permute-done.9.refs_1_ = bf16[128,1536]{1,0:T(8,128)(2,1)S(1)} collective-permute-done((bf16[128,1536]{1,0:T(8,128)(2,1)S(1)}, bf16[128,1536]{1,0:T(8,128)(2,1)S(1)}, u32[]{:S(2)}, u32[]{:S(2)}) %collective-permute-start.9) | collective-permute-done | bytes 393248 | tf_op jit(solution)/shard_map/passed_rows/ppermute | solution.py:475
  28.7 1.6 %later_block.7 = (bf16[144,768]{1,0:T(8,128)(2,1)S(1)}, bf16[128,768]{1,0:T(8,128)(2,1)S(1)}, f32[128,1536]{1,0:T(8,128)S(1)}, bf16[128,1536]{1,0:T(8,128)(2,1)S(1)}, f32[1,256]{1,0:T(1,128)S(1)}) custom-call(bf16[128,1536]{1,0:T(8,128)(2,1)S(1)} %collective-permute-done.8.refs_0_, bf16[128,1536]{1,0:T(8,128)(2,1)S(1)} %collective-permute-done.9.refs_1_, ...), custom_call_target="tpu_custom_call" | custom-call | flops 1207959552 | bytes 1024 | tf_op jit(solution)/shard_map/later_block/pallas_call | solution.py:265
  30.3 0.1 collective-permute-start.11
  30.4 0.5 collective-permute-start.12
  30.9 1.2 %collective-permute-done.12.refs_2_ = bf16[128,768]{1,0:T(8,128)(2,1)S(1)} collective-permute-done((bf16[128,768]{1,0:T(8,128)(2,1)S(1)}, bf16[128,768]{1,0:T(8,128)(2,1)S(1)}, u32[]{:S(2)}, u32[]{:S(2)}) %collective-permute-start.12) | collective-permute-done | bytes 196640 | tf_op jit(solution)/shard_map/core_sum_2a/ppermute | solution.py:460
  32.1 0.1 chip_sum.6
  32.3 0.6 collective-permute-start.13
  32.9 3.2 %first_give.1 = (bf16[144,1536]{1,0:T(8,128)(2,1)S(1)}, bf16[1536,1536]{1,0:T(8,128)(2,1)S(1)}, f32[1,1536]{1,0:T(1,128)S(1)}) custom-call(bf16[128,1536]{1,0:T(8,128)(2,1)S(1)} %copy-done, f32[1,1536]{1,0:T(1,128)S(1)} %get-tuple-element.97.refs_1_.gain.refs_2_, bf16[1536,6144]{1,0:T(8,128)(2,1)} %w.5), custom_call_target="tpu_custom_call" | custom-call | flops 1024 | bytes 1024 | tf_op jit(solution)/shard_map/first_give/pallas_call | solution.py:219
  36.0 1.4 %later_block.8 = (bf16[128,1536]{1,0:T(8,128)(2,1)S(1)}, f32[128,1536]{1,0:T(8,128)S(1)}) custom-call(bf16[128,1536]{1,0:T(8,128)(2,1)S(1)} %get-tuple-element.93.left, bf16[1536,1536]{1,0:T(8,128)(2,1)S(1)} %get-tuple-element.94.give_held, bf16[1536,1536]{1,0:T(8,128)(2,1)S(1)} %get-tuple-element.95.keep_held), custom_call_target="tpu_custom_call" | custom-call | flops 1207959552 | bytes 1024 | tf_op jit(solution)/shard_map/later_block/pallas_call | solution.py:265
  37.5 1.3 %collective-permute-done.6.refs_1_ = bf16[128,1536]{1,0:T(8,128)(2,1)S(1)} collective-permute-done((bf16[128,1536]{1,0:T(8,128)(2,1)S(1)}, bf16[128,1536]{1,0:T(8,128)(2,1)S(1)}, u32[]{:S(2)}, u32[]{:S(2)}) %collective-permute-start.6) | collective-permute-done | bytes 393248 | tf_op jit(solution)/shard_map/last_rows/ppermute | solution.py:475
  38.7 1.6 %later_block.9 = (bf16[144,768]{1,0:T(8,128)(2,1)S(1)}, bf16[128,768]{1,0:T(8,128)(2,1)S(1)}, f32[128,1536]{1,0:T(8,128)S(1)}, bf16[128,1536]{1,0:T(8,128)(2,1)S(1)}, f32[1,256]{1,0:T(1,128)S(1)}) custom-call(bf16[128,1536]{1,0:T(8,128)(2,1)S(1)} %collective-permute-done.3.refs_0_, bf16[128,1536]{1,0:T(8,128)(2,1)S(1)} %collective-permute-done.6.refs_1_, ...), custom_call_target="tpu_custom_call" | custom-call | flops 1207959552 | bytes 1024 | tf_op jit(solution)/shard_map/later_block/pallas_call | solution.py:265
  40.3 0.1 collective-permute-start.14
  40.4 0.5 collective-permute-start.15
  40.9 0.1 collective-permute-start.19
  41.0 0.4 collective-permute-start.20
  41.4 0.7 collective-permute-done.15.refs_2_
  42.2 0.1 chip_sum.7
  42.3 0.6 collective-permute-start.18
  42.9 1.2 %collective-permute-done.13.refs_3_.refs_2_ = bf16[136,1536]{1,0:T(8,128)(2,1)S(1)} collective-permute-done((bf16[136,1536]{1,0:T(8,128)(2,1)S(1)}, bf16[136,1536]{1,0:T(8,128)(2,1)S(1)}, u32[]{:S(2)}, u32[]{:S(2)}) %collective-permute-start.13) | collective-permute-done | bytes 417824 | tf_op jit(solution)/shard_map/chip_sum_2/ppermute | solution.py:465
  44.1 1.4 %later_block.10 = (bf16[128,1536]{1,0:T(8,128)(2,1)S(1)}, f32[128,1536]{1,0:T(8,128)S(1)}) custom-call(bf16[128,1536]{1,0:T(8,128)(2,1)S(1)} %get-tuple-element.106.left, bf16[1536,1536]{1,0:T(8,128)(2,1)S(1)} %get-tuple-element.94.give_held, bf16[1536,1536]{1,0:T(8,128)(2,1)S(1)} %get-tuple-element.95.keep_held), custom_call_target="tpu_custom_call" | custom-call | flops 1207959552 | bytes 1024 | tf_op jit(solution)/shard_map/later_block/pallas_call | solution.py:265
  45.6 1.4 %later_block.11 = (bf16[128,768]{1,0:T(8,128)(2,1)S(1)}, bf16[128,768]{1,0:T(8,128)(2,1)S(1)}, f32[128,1536]{1,0:T(8,128)S(1)}) custom-call(bf16[128,1536]{1,0:T(8,128)(2,1)S(1)} %get-tuple-element.108.left, bf16[1536,1536]{1,0:T(8,128)(2,1)S(1)} %get-tuple-element.94.give_held, bf16[1536,1536]{1,0:T(8,128)(2,1)S(1)} %get-tuple-element.95.keep_held), custom_call_target="tpu_custom_call" | custom-call | flops 1207959552 | bytes 1024 | tf_op jit(solution)/shard_map/later_block/pallas_call | solution.py:265
  47.0 0.5 collective-permute-start.16
  47.5 0.1 collective-permute-start.17
  47.7 1.1 %pool.3.refs_7_ = f32[1,1536]{1,0:T(1,128)S(1)} custom-call(f32[128,1536]{1,0:T(8,128)S(1)} %get-tuple-element.79.refs_0_, bf16[144,1536]{1,0:T(8,128)(2,1)S(1)} %collective-permute-done.19.refs_1_, bf16[136,1536]{1,0:T(8,128)(2,1)S(1)} %collective-permute-done.10.refs_2_.refs_3_, bf16[136,1536]{1,0:T(8,128)(2,1)S(1)} %collective-permute-done.10.refs_2_.refs_3_, ...), custom_call_target="tpu_custom_call" | custom-call | flops 1024 | bytes 1024 | tf_op jit(solution)/shard_map/pool/pallas_call | solution.py:352
  48.8 1.0 %pool.4.refs_8_ = f32[1,1536]{1,0:T(1,128)S(1)} custom-call(f32[128,1536]{1,0:T(8,128)S(1)} %get-tuple-element.116.refs_0_, bf16[128,1536]{1,0:T(8,128)(2,1)S(1)} %collective-permute-done.20.refs_1_, bf16[128,1536]{1,0:T(8,128)(2,1)S(1)} %collective-permute-done.7.refs_2_, bf16[136,1536]{1,0:T(8,128)(2,1)S(1)} %collective-permute-done.13.refs_3_.refs_2_, ...), custom_call_target="tpu_custom_call" | custom-call | flops 1024 | bytes 1024 | tf_op jit(solution)/shard_map/pool/pallas_call | solution.py:352
  49.8 1.0 %pool.5.refs_9_ = f32[1,1536]{1,0:T(1,128)S(1)} custom-call(f32[128,1536]{1,0:T(8,128)S(1)} %get-tuple-element.117.refs_0_, bf16[128,1536]{1,0:T(8,128)(2,1)S(1)} %collective-permute-done.21.refs_1_, bf16[136,1536]{1,0:T(8,128)(2,1)S(1)} %collective-permute-done.13.refs_3_.refs_2_, bf16[136,1536]{1,0:T(8,128)(2,1)S(1)} %collective-permute-done.13.refs_3_.refs_2_, ...), custom_call_target="tpu_custom_call" | custom-call | flops 1024 | bytes 1024 | tf_op jit(solution)/shard_map/pool/pallas_call | solution.py:352
  50.9 3.2 %collective-permute-done.18.refs_3_ = bf16[136,1536]{1,0:T(8,128)(2,1)S(1)} collective-permute-done((bf16[136,1536]{1,0:T(8,128)(2,1)S(1)}, bf16[136,1536]{1,0:T(8,128)(2,1)S(1)}, u32[]{:S(2)}, u32[]{:S(2)}) %collective-permute-start.18) | collective-permute-done | bytes 417824 | tf_op jit(solution)/shard_map/chip_sum_3/ppermute | solution.py:465
  54.1 1.1 %pool_all.1.refs_0_ = f32[2,1536]{1,0:T(2,128)S(1)} custom-call(f32[128,1536]{1,0:T(8,128)S(1)} %get-tuple-element.109.refs_0_, bf16[128,768]{1,0:T(8,128)(2,1)S(1)} %collective-permute-done.16.refs_1_, bf16[128,768]{1,0:T(8,128)(2,1)S(1)} %collective-permute-done.17.refs_2_, bf16[136,1536]{1,0:T(8,128)(2,1)S(1)} %collective-permute-done.18.refs_3_, ...), custom_call_target="tpu_custom_call" | custom-call | flops 1024 | bytes 1024 | tf_op jit(solution)/shard_map/pool_all/pallas_call | solution.py:378
  55.2 0.6 collective-permute-start.24
  55.8 1.3 %collective-permute-start.22 = (f32[2,1536]{1,0:T(2,128)S(1)}, f32[2,1536]{1,0:T(2,128)S(1)}, u32[]{:S(2)}, u32[]{:S(2)}) collective-permute-start(f32[2,1536]{1,0:T(2,128)S(1)} %pool_all.1.refs_0_), channel_id=1, source_target_pairs={{0,3},{1,2},{2,1},{3,0},{4,7},{5,6},{6,5},{7,4},{8,11},{9,10},{10,... | collective-permute-start | bytes 36872 | tf_op jit(solution)/shard_map/both_pool/ppermute | solution.py:470
  57.1 1.6 %mix.3.refs_1_ = f32[2,1536]{1,0:T(2,128)S(1)} custom-call(f32[2,1536]{1,0:T(2,128)S(1)} %pool_all.1.refs_0_, f32[2,1536]{1,0:T(2,128)S(1)} %collective-permute-done.23.refs_1_, f32[1,1536]{1,0:T(1,128)S(1)} %get-tuple-element.119.refs_2_, bf16[6144,1536]{1,0:T(8,128)(2,1)S(1)} %bitcast.7), custom_call_target="tpu_custom_call" | custom-call | flops 1024 | bytes 1024 | tf_op jit(solution)/shard_map/mix/pallas_call | solution.py:410
  58.7 0.4 collective-permute-done.24.refs_0_
  59.1 0.7 mix.4.refs_1_
  59.8 0.7 mix.5
  60.6 0.8 %collective-permute-start.25 = (f32[2,1536]{1,0:T(2,128)S(1)}, f32[2,1536]{1,0:T(2,128)S(1)}, u32[]{:S(2)}, u32[]{:S(2)}) collective-permute-start(f32[2,1536]{1,0:T(2,128)S(1)} %mix.5), channel_id=1, source_target_pairs={{0,4},{4,0},{8,12},{12,8},{1,5},{5,1},{9,13},{13,9},{2,6},{6,2},{1... | collective-permute-start | bytes 36872 | tf_op jit(solution)/shard_map/swap_mixed/ppermute | solution.py:475
  61.4 1.3 %collective-permute-start.26 = (f32[2,1536]{1,0:T(2,128)S(1)}, f32[2,1536]{1,0:T(2,128)S(1)}, u32[]{:S(2)}, u32[]{:S(2)}) collective-permute-start(f32[2,1536]{1,0:T(2,128)S(1)} %mix.5), channel_id=1, source_target_pairs={{0,8},{8,0},{4,12},{12,4},{1,9},{9,1},{5,13},{13,5},{2,10},{10,2},... | collective-permute-start | bytes 36872 | tf_op jit(solution)/shard_map/skip_mixed/ppermute | solution.py:475
  62.7 2.3 %collective-permute-start.27 = (f32[2,1536]{1,0:T(2,128)S(1)}, f32[2,1536]{1,0:T(2,128)S(1)}, u32[]{:S(2)}, u32[]{:S(2)}) collective-permute-start(f32[2,1536]{1,0:T(2,128)S(1)} %mix.5), channel_id=1, source_target_pairs={{0,12},{12,0},{4,8},{8,4},{1,13},{13,1},{5,9},{9,5},{2,14},{14,2},... | collective-permute-start | bytes 36872 | tf_op jit(solution)/shard_map/ends_mixed/ppermute | solution.py:475
  65.0 0.3 multiply_reduce_fusion
  65.2 0.7 %collective-permute-done.26 = f32[2,1536]{1,0:T(2,128)S(1)} collective-permute-done((f32[2,1536]{1,0:T(2,128)S(1)}, f32[2,1536]{1,0:T(2,128)S(1)}, u32[]{:S(2)}, u32[]{:S(2)}) %collective-permute-start.26) | collective-permute-done | bytes 12320 | tf_op jit(solution)/shard_map/skip_mixed/ppermute | solution.py:475
  66.0 2.2 %collective-permute-done.27 = f32[2,1536]{1,0:T(2,128)S(1)} collective-permute-done((f32[2,1536]{1,0:T(2,128)S(1)}, f32[2,1536]{1,0:T(2,128)S(1)}, u32[]{:S(2)}, u32[]{:S(2)}) %collective-permute-start.27) | collective-permute-done | bytes 12320 | tf_op jit(solution)/shard_map/ends_mixed/ppermute | solution.py:475
  68.3 1.4 %collective-permute-start.29 = (f32[2,1536]{1,0:T(2,128)S(1)}, f32[2,1536]{1,0:T(2,128)S(1)}, u32[]{:S(2)}, u32[]{:S(2)}) collective-permute-start(f32[2,1536]{1,0:T(2,128)S(1)} %add_add_fusion.own), channel_id=1, source_target_pairs={{0,2},{2,0},{1,3},{3,1},{4,6},{6,4},{5,7},{7,5},{8,10},{10,8},{9,1... | collective-permute-start | bytes 36872 | tf_op jit(solution)/shard_map/chip_embed/ppermute | solution.py:465
  69.7 0.4 collective-permute-start.30
  70.1 1.9 %collective-permute-done.29.across = f32[2,1536]{1,0:T(2,128)S(1)} collective-permute-done((f32[2,1536]{1,0:T(2,128)S(1)}, f32[2,1536]{1,0:T(2,128)S(1)}, u32[]{:S(2)}, u32[]{:S(2)}) %collective-permute-start.29) | collective-permute-done | bytes 12320 | tf_op jit(solution)/shard_map/chip_embed/ppermute | solution.py:465
  72.0 0.8 %collective-permute-done.30.both = f32[2,1536]{1,0:T(2,128)S(1)} collective-permute-done((f32[2,1536]{1,0:T(2,128)S(1)}, f32[2,1536]{1,0:T(2,128)S(1)}, u32[]{:S(2)}, u32[]{:S(2)}) %collective-permute-start.30) | collective-permute-done | bytes 12320 | tf_op jit(solution)/shard_map/both_embed/ppermute | solution.py:470
  72.8 1.0 %score.1 = f32[1,64]{1,0:T(1,128)} custom-call(f32[2,1536]{1,0:T(2,128)S(1)} %add_add_fusion.own, f32[2,1536]{1,0:T(2,128)S(1)} %collective-permute-done.28.core, f32[2,1536]{1,0:T(2,128)S(1)} %collective-permute-done.29.across, f32[2,1536]{1,0:T(2,128)S(1)} %collective-permute-done.30.both, f32[1,6144]{1,0:T(1,128)S(1)} %bitcast.12, ...), custom_call_target="tpu_custom_call" | custom-call | flops 1024 | bytes 1024 | tf_op jit(solution)/shard_map/score/pallas_call | solution.py:447
  (44 shorter events, 0.5 us)
Async XLA Ops:
  0.0 12.3 %collective-permute-start = (bf16[128,1536]{1,0:T(8,128)(2,1)}, bf16[128,1536]{1,0:T(8,128)(2,1)S(1)}, u32[]{:S(2)}, u32[]{:S(2)}) collective-permute-start(bf16[128,1536]{1,0:T(8,128)(2,1)} %tokens.3), channel_id=1, source_target_pairs={{0,4},{4,0},{8,12},{12,8},{1,5},{5,1},{9,13},{13,9},{2,6},{6,2},{1... | collective-permute-start | bytes 1179656 | tf_op jit(solution)/shard_map/near_rows/ppermute | solution.py:475
  3.0 10.0 %collective-permute-start.8 = (bf16[128,1536]{1,0:T(8,128)(2,1)}, bf16[128,1536]{1,0:T(8,128)(2,1)S(1)}, u32[]{:S(2)}, u32[]{:S(2)}) collective-permute-start(bf16[128,1536]{1,0:T(8,128)(2,1)} %tokens.3), channel_id=1, source_target_pairs={{4,8},{8,4},{5,9},{9,5},{6,10},{10,6},{7,11},{11,7},{20,24},{24,20... | collective-permute-start | bytes 1179656 | tf_op jit(solution)/shard_map/middle_rows/ppermute | solution.py:475
  8.4 1.5 %collective-permute-start.1 = (bf16[144,768]{1,0:T(8,128)(2,1)S(1)}, bf16[144,768]{1,0:T(8,128)(2,1)S(1)}, u32[]{:S(2)}, u32[]{:S(2)}) collective-permute-start(bf16[144,768]{1,0:T(8,128)(2,1)S(1)} %get-tuple-element.65), channel_id=1, source_target_pairs={{0,1},{1,0},{2,3},{3,2},{4,5},{5,4},{6,7},{7,6},{8,9},{9,8},{10,11... | collective-permute-start | bytes 663560 | tf_op jit(solution)/shard_map/core_sum_0a/ppermute | solution.py:460
  8.5 1.8 %collective-permute-start.2 = (bf16[144,768]{1,0:T(8,128)(2,1)S(1)}, bf16[144,768]{1,0:T(8,128)(2,1)S(1)}, u32[]{:S(2)}, u32[]{:S(2)}) collective-permute-start(bf16[144,768]{1,0:T(8,128)(2,1)S(1)} %get-tuple-element.66), channel_id=1, source_target_pairs={{0,1},{1,0},{2,3},{3,2},{4,5},{5,4},{6,7},{7,6},{8,9},{9,8},{10,11... | collective-permute-start | bytes 663560 | tf_op jit(solution)/shard_map/core_sum_0a/ppermute | solution.py:460
  10.4 12.5 %collective-permute-start.10 = (bf16[136,1536]{1,0:T(8,128)(2,1)S(1)}, bf16[136,1536]{1,0:T(8,128)(2,1)S(1)}, u32[]{:S(2)}, u32[]{:S(2)}) collective-permute-start(bf16[136,1536]{1,0:T(8,128)(2,1)S(1)} %get-tuple-element.69), channel_id=1, source_target_pairs={{0,2},{2,0},{1,3},{3,1},{4,6},{6,4},{5,7},{7,5},{8,10},{10,8},{9,1... | collective-permute-start | bytes 1253384 | tf_op jit(solution)/shard_map/chip_sum_0/ppermute | solution.py:465
  12.3 10.6 %collective-permute-start.3 = (bf16[128,1536]{1,0:T(8,128)(2,1)S(1)}, bf16[128,1536]{1,0:T(8,128)(2,1)S(1)}, u32[]{:S(2)}, u32[]{:S(2)}) collective-permute-start(bf16[128,1536]{1,0:T(8,128)(2,1)S(1)} %collective-permute-done.refs_0_), channel_id=1, source_target_pairs={{4,8},{8,4},{5,9},{9,5},{6,10},{10,6},{7,11},{11,7},{20,24},{24,20... | collective-permute-start | bytes 1179656 | tf_op jit(solution)/shard_map/crossed_rows/ppermute | solution.py:475
  13.0 15.7 %collective-permute-start.9 = (bf16[128,1536]{1,0:T(8,128)(2,1)S(1)}, bf16[128,1536]{1,0:T(8,128)(2,1)S(1)}, u32[]{:S(2)}, u32[]{:S(2)}) collective-permute-start(bf16[128,1536]{1,0:T(8,128)(2,1)S(1)} %collective-permute-done.8.refs_0_), channel_id=1, source_target_pairs={{4,0},{8,12},{5,1},{9,13},{6,2},{10,14},{7,3},{11,15},{20,16},{24,... | collective-permute-start | bytes 1179656 | tf_op jit(solution)/shard_map/passed_rows/ppermute | solution.py:475
  14.3 5.2 %copy-start = (bf16[128,1536]{1,0:T(8,128)(2,1)S(1)}, bf16[128,1536]{1,0:T(8,128)(2,1)}, u32[]{:S(2)}) copy-start(bf16[128,1536]{1,0:T(8,128)(2,1)} %tokens.3) | copy-start | bytes 1179652
  15.9 1.8 %collective-permute-start.4 = (bf16[144,768]{1,0:T(8,128)(2,1)S(1)}, bf16[144,768]{1,0:T(8,128)(2,1)S(1)}, u32[]{:S(2)}, u32[]{:S(2)}) collective-permute-start(bf16[144,768]{1,0:T(8,128)(2,1)S(1)} %get-tuple-element.74), channel_id=1, source_target_pairs={{0,1},{1,0},{2,3},{3,2},{4,5},{5,4},{6,7},{7,6},{8,9},{9,8},{10,11... | collective-permute-start | bytes 663560 | tf_op jit(solution)/shard_map/core_sum_1a/ppermute | solution.py:460
  16.0 1.7 %collective-permute-start.5 = (bf16[128,768]{1,0:T(8,128)(2,1)S(1)}, bf16[128,768]{1,0:T(8,128)(2,1)S(1)}, u32[]{:S(2)}, u32[]{:S(2)}) collective-permute-start(bf16[128,768]{1,0:T(8,128)(2,1)S(1)} %get-tuple-element.75), channel_id=1, source_target_pairs={{0,1},{1,0},{2,3},{3,2},{4,5},{5,4},{6,7},{7,6},{8,9},{9,8},{10,11... | collective-permute-start | bytes 589832 | tf_op jit(solution)/shard_map/core_sum_1a/ppermute | solution.py:460
  17.9 18.2 %collective-permute-start.7 = (bf16[128,1536]{1,0:T(8,128)(2,1)S(1)}, bf16[128,1536]{1,0:T(8,128)(2,1)S(1)}, u32[]{:S(2)}, u32[]{:S(2)}) collective-permute-start(bf16[128,1536]{1,0:T(8,128)(2,1)S(1)} %get-tuple-element.77), channel_id=1, source_target_pairs={{0,2},{2,0},{1,3},{3,1},{4,6},{6,4},{5,7},{7,5},{8,10},{10,8},{9,1... | collective-permute-start | bytes 1179656 | tf_op jit(solution)/shard_map/chip_sum_1/ppermute | solution.py:465
  22.9 15.8 %collective-permute-start.6 = (bf16[128,1536]{1,0:T(8,128)(2,1)S(1)}, bf16[128,1536]{1,0:T(8,128)(2,1)S(1)}, u32[]{:S(2)}, u32[]{:S(2)}) collective-permute-start(bf16[128,1536]{1,0:T(8,128)(2,1)S(1)} %collective-permute-done.3.refs_0_), channel_id=1, source_target_pairs={{4,0},{8,12},{5,1},{9,13},{6,2},{10,14},{7,3},{11,15},{20,16},{24,... | collective-permute-start | bytes 1179656 | tf_op jit(solution)/shard_map/last_rows/ppermute | solution.py:475
  30.3 1.8 %collective-permute-start.11 = (bf16[144,768]{1,0:T(8,128)(2,1)S(1)}, bf16[144,768]{1,0:T(8,128)(2,1)S(1)}, u32[]{:S(2)}, u32[]{:S(2)}) collective-permute-start(bf16[144,768]{1,0:T(8,128)(2,1)S(1)} %get-tuple-element.85), channel_id=1, source_target_pairs={{0,1},{1,0},{2,3},{3,2},{4,5},{5,4},{6,7},{7,6},{8,9},{9,8},{10,11... | collective-permute-start | bytes 663560 | tf_op jit(solution)/shard_map/core_sum_2a/ppermute | solution.py:460
  30.4 1.7 %collective-permute-start.12 = (bf16[128,768]{1,0:T(8,128)(2,1)S(1)}, bf16[128,768]{1,0:T(8,128)(2,1)S(1)}, u32[]{:S(2)}, u32[]{:S(2)}) collective-permute-start(bf16[128,768]{1,0:T(8,128)(2,1)S(1)} %get-tuple-element.86), channel_id=1, source_target_pairs={{0,1},{1,0},{2,3},{3,2},{4,5},{5,4},{6,7},{7,6},{8,9},{9,8},{10,11... | collective-permute-start | bytes 589832 | tf_op jit(solution)/shard_map/core_sum_2a/ppermute | solution.py:460
  32.3 11.8 %collective-permute-start.13 = (bf16[136,1536]{1,0:T(8,128)(2,1)S(1)}, bf16[136,1536]{1,0:T(8,128)(2,1)S(1)}, u32[]{:S(2)}, u32[]{:S(2)}) collective-permute-start(bf16[136,1536]{1,0:T(8,128)(2,1)S(1)} %get-tuple-element.89), channel_id=1, source_target_pairs={{0,2},{2,0},{1,3},{3,1},{4,6},{6,4},{5,7},{7,5},{8,10},{10,8},{9,1... | collective-permute-start | bytes 1253384 | tf_op jit(solution)/shard_map/chip_sum_2/ppermute | solution.py:465
  38.7 18.4 %slice-start = ((s8[18874368]{0:T(1024)(128)(4,1)}), s8[4194304]{0:T(1024)(128)(4,1)S(1)}, s32[]{:S(2)}) async-start(s8[18874368]{0:T(1024)(128)(4,1)} %bitcast.6), calls=%async_computation | async-start | bytes 8388608
  38.7 18.4 %slice-start.1 = ((s8[18874368]{0:T(1024)(128)(4,1)}), s8[4194304]{0:T(1024)(128)(4,1)S(1)}, s32[]{:S(2)}) async-start(s8[18874368]{0:T(1024)(128)(4,1)} %bitcast.6), calls=%async_computation.1 | async-start | bytes 8388608
  40.3 1.8 %collective-permute-start.14 = (bf16[144,768]{1,0:T(8,128)(2,1)S(1)}, bf16[144,768]{1,0:T(8,128)(2,1)S(1)}, u32[]{:S(2)}, u32[]{:S(2)}) collective-permute-start(bf16[144,768]{1,0:T(8,128)(2,1)S(1)} %get-tuple-element.101), channel_id=1, source_target_pairs={{0,1},{1,0},{2,3},{3,2},{4,5},{5,4},{6,7},{7,6},{8,9},{9,8},{10,11... | collective-permute-start | bytes 663560 | tf_op jit(solution)/shard_map/core_sum_3a/ppermute | solution.py:460
  40.4 1.7 %collective-permute-start.15 = (bf16[128,768]{1,0:T(8,128)(2,1)S(1)}, bf16[128,768]{1,0:T(8,128)(2,1)S(1)}, u32[]{:S(2)}, u32[]{:S(2)}) collective-permute-start(bf16[128,768]{1,0:T(8,128)(2,1)S(1)} %get-tuple-element.102), channel_id=1, source_target_pairs={{0,1},{1,0},{2,3},{3,2},{4,5},{5,4},{6,7},{7,6},{8,9},{9,8},{10,11... | collective-permute-start | bytes 589832 | tf_op jit(solution)/shard_map/core_sum_3a/ppermute | solution.py:460
  40.9 6.6 %collective-permute-start.19 = (bf16[144,1536]{1,0:T(8,128)(2,1)S(1)}, bf16[144,1536]{1,0:T(8,128)(2,1)S(1)}, u32[]{:S(2)}, u32[]{:S(2)}) collective-permute-start(bf16[144,1536]{1,0:T(8,128)(2,1)S(1)} %get-tuple-element.91), channel_id=1, source_target_pairs={{0,1},{1,0},{2,3},{3,2},{4,5},{5,4},{6,7},{7,6},{8,9},{9,8},{10,11... | collective-permute-start | bytes 1327112 | tf_op jit(solution)/shard_map/core_sum_0b/ppermute | solution.py:460
  41.0 7.8 %collective-permute-start.20 = (bf16[128,1536]{1,0:T(8,128)(2,1)S(1)}, bf16[128,1536]{1,0:T(8,128)(2,1)S(1)}, u32[]{:S(2)}, u32[]{:S(2)}) collective-permute-start(bf16[128,1536]{1,0:T(8,128)(2,1)S(1)} %get-tuple-element.96), channel_id=1, source_target_pairs={{0,1},{1,0},{2,3},{3,2},{4,5},{5,4},{6,7},{7,6},{8,9},{9,8},{10,11... | collective-permute-start | bytes 1179656 | tf_op jit(solution)/shard_map/core_sum_1b/ppermute | solution.py:460
  42.3 11.8 %collective-permute-start.18 = (bf16[136,1536]{1,0:T(8,128)(2,1)S(1)}, bf16[136,1536]{1,0:T(8,128)(2,1)S(1)}, u32[]{:S(2)}, u32[]{:S(2)}) collective-permute-start(bf16[136,1536]{1,0:T(8,128)(2,1)S(1)} %get-tuple-element.104), channel_id=1, source_target_pairs={{0,2},{2,0},{1,3},{3,1},{4,6},{6,4},{5,7},{7,5},{8,10},{10,8},{9,1... | collective-permute-start | bytes 1253384 | tf_op jit(solution)/shard_map/chip_sum_3/ppermute | solution.py:465
  44.1 13.0 %slice-start.2 = ((s8[18874368]{0:T(1024)(128)(4,1)}), s8[4194304]{0:T(1024)(128)(4,1)S(1)}, s32[]{:S(2)}) async-start(s8[18874368]{0:T(1024)(128)(4,1)} %bitcast.6), calls=%async_computation.2 | async-start | bytes 8388608
  45.5 4.3 %collective-permute-start.21 = (bf16[128,1536]{1,0:T(8,128)(2,1)S(1)}, bf16[128,1536]{1,0:T(8,128)(2,1)S(1)}, u32[]{:S(2)}, u32[]{:S(2)}) collective-permute-start(bf16[128,1536]{1,0:T(8,128)(2,1)S(1)} %get-tuple-element.107), channel_id=1, source_target_pairs={{0,1},{1,0},{2,3},{3,2},{4,5},{5,4},{6,7},{7,6},{8,9},{9,8},{10,11... | collective-permute-start | bytes 1179656 | tf_op jit(solution)/shard_map/core_sum_2b/ppermute | solution.py:460
  45.6 2.1 %copy-start.2 = (f32[6144]{0:T(1024)S(1)}, f32[6144]{0:T(1024)}, u32[]{:S(2)}) copy-start(f32[6144]{0:T(1024)} %param.11) | copy-start | bytes 73732
  45.6 11.5 %slice-start.3 = ((s8[18874368]{0:T(1024)(128)(4,1)}), s8[4194304]{0:T(1024)(128)(4,1)S(1)}, s32[]{:S(2)}) async-start(s8[18874368]{0:T(1024)(128)(4,1)} %bitcast.6), calls=%async_computation.3 | async-start | bytes 8388608
  47.0 3.8 %collective-permute-start.16 = (bf16[128,768]{1,0:T(8,128)(2,1)S(1)}, bf16[128,768]{1,0:T(8,128)(2,1)S(1)}, u32[]{:S(2)}, u32[]{:S(2)}) collective-permute-start(bf16[128,768]{1,0:T(8,128)(2,1)S(1)} %get-tuple-element.110), channel_id=1, source_target_pairs={{0,1},{1,0},{2,3},{3,2},{4,5},{5,4},{6,7},{7,6},{8,9},{9,8},{10,11... | collective-permute-start | bytes 589832 | tf_op jit(solution)/shard_map/core_sum_3b/ppermute | solution.py:460
  47.5 3.3 %collective-permute-start.17 = (bf16[128,768]{1,0:T(8,128)(2,1)S(1)}, bf16[128,768]{1,0:T(8,128)(2,1)S(1)}, u32[]{:S(2)}, u32[]{:S(2)}) collective-permute-start(bf16[128,768]{1,0:T(8,128)(2,1)S(1)} %get-tuple-element.111), channel_id=1, source_target_pairs={{0,1},{1,0},{2,3},{3,2},{4,5},{5,4},{6,7},{7,6},{8,9},{9,8},{10,11... | collective-permute-start | bytes 589832 | tf_op jit(solution)/shard_map/core_sum_3b/ppermute | solution.py:460
  47.7 9.4 %slice-start.4 = ((s8[18874368]{0:T(1024)(128)(4,1)}), s8[2097152]{0:T(1024)(128)(4,1)S(1)}, s32[]{:S(2)}) async-start(s8[18874368]{0:T(1024)(128)(4,1)} %bitcast.6), calls=%async_computation.4 | async-start | bytes 4194304
  55.1 1.9 %collective-permute-start.23 = (f32[2,1536]{1,0:T(2,128)S(1)}, f32[2,1536]{1,0:T(2,128)S(1)}, u32[]{:S(2)}, u32[]{:S(2)}) collective-permute-start(f32[2,1536]{1,0:T(2,128)S(1)} %pool_all.1.refs_0_), channel_id=1, source_target_pairs={{0,1},{1,0},{2,3},{3,2},{4,5},{5,4},{6,7},{7,6},{8,9},{9,8},{10,11... | collective-permute-start | bytes 36872 | tf_op jit(solution)/shard_map/core_pool/ppermute | solution.py:460
  55.2 3.8 %collective-permute-start.24 = (f32[2,1536]{1,0:T(2,128)S(1)}, f32[2,1536]{1,0:T(2,128)S(1)}, u32[]{:S(2)}, u32[]{:S(2)}) collective-permute-start(f32[2,1536]{1,0:T(2,128)S(1)} %pool_all.1.refs_0_), channel_id=1, source_target_pairs={{0,2},{2,0},{1,3},{3,1},{4,6},{6,4},{5,7},{7,5},{8,10},{10,8},{9,1... | collective-permute-start | bytes 36872 | tf_op jit(solution)/shard_map/chip_pool/ppermute | solution.py:465
  55.8 4.0 %collective-permute-start.22 = (f32[2,1536]{1,0:T(2,128)S(1)}, f32[2,1536]{1,0:T(2,128)S(1)}, u32[]{:S(2)}, u32[]{:S(2)}) collective-permute-start(f32[2,1536]{1,0:T(2,128)S(1)} %pool_all.1.refs_0_), channel_id=1, source_target_pairs={{0,3},{1,2},{2,1},{3,0},{4,7},{5,6},{6,5},{7,4},{8,11},{9,10},{10,... | collective-permute-start | bytes 36872 | tf_op jit(solution)/shard_map/both_pool/ppermute | solution.py:470
  59.8 5.2 %copy-start.1 = (bf16[64,6144]{1,0:T(8,128)(2,1)S(1)}, bf16[64,6144]{1,0:T(8,128)(2,1)}, u32[]{:S(2)}) copy-start(bf16[64,6144]{1,0:T(8,128)(2,1)} %captions.1) | copy-start | bytes 2359300
  59.8 13.0 %copy-start.3 = (f32[6144]{0:T(1024)S(1)}, f32[6144]{0:T(1024)}, u32[]{:S(2)}) copy-start(f32[6144]{0:T(1024)} %param.13) | copy-start | bytes 73732
  59.8 13.0 %copy-start.4 = (s32[64]{0:T(128)S(1)}, s32[64]{0:T(128)}, u32[]{:S(2)}) copy-start(s32[64]{0:T(128)} %param.15) | copy-start | bytes 772
  60.6 4.7 %collective-permute-start.25 = (f32[2,1536]{1,0:T(2,128)S(1)}, f32[2,1536]{1,0:T(2,128)S(1)}, u32[]{:S(2)}, u32[]{:S(2)}) collective-permute-start(f32[2,1536]{1,0:T(2,128)S(1)} %mix.5), channel_id=1, source_target_pairs={{0,4},{4,0},{8,12},{12,8},{1,5},{5,1},{9,13},{13,9},{2,6},{6,2},{1... | collective-permute-start | bytes 36872 | tf_op jit(solution)/shard_map/swap_mixed/ppermute | solution.py:475
  61.4 4.6 %collective-permute-start.26 = (f32[2,1536]{1,0:T(2,128)S(1)}, f32[2,1536]{1,0:T(2,128)S(1)}, u32[]{:S(2)}, u32[]{:S(2)}) collective-permute-start(f32[2,1536]{1,0:T(2,128)S(1)} %mix.5), channel_id=1, source_target_pairs={{0,8},{8,0},{4,12},{12,4},{1,9},{9,1},{5,13},{13,5},{2,10},{10,2},... | collective-permute-start | bytes 36872 | tf_op jit(solution)/shard_map/skip_mixed/ppermute | solution.py:475
  62.7 5.5 %collective-permute-start.27 = (f32[2,1536]{1,0:T(2,128)S(1)}, f32[2,1536]{1,0:T(2,128)S(1)}, u32[]{:S(2)}, u32[]{:S(2)}) collective-permute-start(f32[2,1536]{1,0:T(2,128)S(1)} %mix.5), channel_id=1, source_target_pairs={{0,12},{12,0},{4,8},{8,4},{1,13},{13,1},{5,9},{9,5},{2,14},{14,2},... | collective-permute-start | bytes 36872 | tf_op jit(solution)/shard_map/ends_mixed/ppermute | solution.py:475
  68.2 1.9 %collective-permute-start.28 = (f32[2,1536]{1,0:T(2,128)S(1)}, f32[2,1536]{1,0:T(2,128)S(1)}, u32[]{:S(2)}, u32[]{:S(2)}) collective-permute-start(f32[2,1536]{1,0:T(2,128)S(1)} %add_add_fusion.own), channel_id=1, source_target_pairs={{0,1},{1,0},{2,3},{3,2},{4,5},{5,4},{6,7},{7,6},{8,9},{9,8},{10,11... | collective-permute-start | bytes 36872 | tf_op jit(solution)/shard_map/core_embed/ppermute | solution.py:460
  68.3 3.8 %collective-permute-start.29 = (f32[2,1536]{1,0:T(2,128)S(1)}, f32[2,1536]{1,0:T(2,128)S(1)}, u32[]{:S(2)}, u32[]{:S(2)}) collective-permute-start(f32[2,1536]{1,0:T(2,128)S(1)} %add_add_fusion.own), channel_id=1, source_target_pairs={{0,2},{2,0},{1,3},{3,1},{4,6},{6,4},{5,7},{7,5},{8,10},{10,8},{9,1... | collective-permute-start | bytes 36872 | tf_op jit(solution)/shard_map/chip_embed/ppermute | solution.py:465
  69.7 3.1 %collective-permute-start.30 = (f32[2,1536]{1,0:T(2,128)S(1)}, f32[2,1536]{1,0:T(2,128)S(1)}, u32[]{:S(2)}, u32[]{:S(2)}) collective-permute-start(f32[2,1536]{1,0:T(2,128)S(1)} %add_add_fusion.own), channel_id=1, source_target_pairs={{0,3},{1,2},{2,1},{3,0},{4,7},{5,6},{6,5},{7,4},{8,11},{9,10},{10,... | collective-permute-start | bytes 36872 | tf_op jit(solution)/shard_map/both_embed/ppermute | solution.py:470
